TPU v7x, 512 devices: a whole 4x8x8 slice. The times are simulated.
512 devices in a mesh: dp: 4 (over x), ctx: 8 (over z), expert: 16 (over y, core).
Axes of the slice: x: 4, y: 8, z: 8, core: 2. Of those that a mesh axis runs over, the one named last changes fastest.
Arguments:
- projected: bfloat16 [64, 3, 1024, 1536], P(('dp', 'expert'), None, 'ctx'), may hold values from -6 to 6
- residual_in: bfloat16 [64, 1024, 1536], P(('dp', 'expert'), 'ctx'), may hold values from -6 to 6
- modulation_scale: float32 [64, 1536], P(('dp', 'expert')), may hold values from -3 to 3
- modulation_shift: float32 [64, 1536], P(('dp', 'expert')), may hold values from -3 to 3
- expert_choice: int32 [64, 1024, 2], P(('dp', 'expert'), 'ctx'), may hold values from 0 to 15, all different within a row; in each aligned block of 128 rows (0 to 127, 128 to 255, ..., all dimensions but the last counted through in order) at most 20 rows name the same one
- gate_values: float32 [64, 1024, 2], P(('dp', 'expert'), 'ctx'), may hold values from 0.2 to 1
- expert_in: bfloat16 [16, 3072, 1536], P('expert', ('dp', 'ctx')), may hold values from -0.15625 to 0.15625
- expert_out: bfloat16 [16, 3072, 1536], P('expert', ('dp', 'ctx')), may hold values from -0.109375 to 0.109375
Outputs:
- block_out: bfloat16 [64, 1024, 1536], P(('dp', 'expert'), 'ctx')
Inputs may be any that keep to these rules, and one draw needn't show every extreme that they name: `expert_choice`: a token's 2 experts differ; in the rows of one device no expert is named by more than 20 rows, and some device reaches 20.
All inputs are finite; a program needn't handle non-finite values.
Results may differ from a plain program's by a relative error of at most 0.01.
Values may be sent and summed in bfloat16 or wider, within the bound.
No kernel may reach another device: no remote copies, remote signals or barrier semaphores. Data moves between devices by JAX's collectives and lax.ppermute only.
A program may use at most 64 MiB of HBM per device.

v0:
```python
import jax
import jax.numpy as jnp
from jax import lax
from jax.sharding import PartitionSpec as P

HD = 64
TOP = 2


def per_device(
    projected,
    residual_in,
    modulation_scale,
    modulation_shift,
    expert_choice,
    gate_values,
    expert_in,
    expert_out,
):
    local_tokens = projected.shape[2]
    width = projected.shape[3]
    ctx_size = lax.axis_size("ctx")
    scaling = HD ** (-0.5)
    mixed = lax.all_to_all(projected, "ctx", split_axis=3, concat_axis=2, tiled=True)
    length = local_tokens * ctx_size
    local_heads = width // ctx_size // HD
    queries = mixed[0, 0].reshape(length, local_heads, HD)
    key_heads = mixed[0, 1].reshape(length, local_heads, HD)
    value_heads = mixed[0, 2].reshape(length, local_heads, HD)
    block_rows = min(512, length)
    query_blocks = queries.reshape(length // block_rows, block_rows, local_heads, HD)

    def attend_block(query_block):
        scores = (
            jnp.einsum("qhd,khd->hqk", query_block, key_heads, preferred_element_type=jnp.float32)
            * scaling
        )
        top_score = jnp.max(scores, axis=-1, keepdims=True)
        probs = jnp.exp(scores - top_score)
        totals = jnp.sum(probs, axis=-1)
        weighted = jnp.einsum(
            "hqk,khd->qhd",
            probs.astype(jnp.bfloat16),
            value_heads,
            preferred_element_type=jnp.float32,
        )
        result = weighted / jnp.transpose(totals)[:, :, None]
        return result.astype(jnp.bfloat16).reshape(block_rows, local_heads * HD)

    head_output = lax.map(attend_block, query_blocks).reshape(1, length, local_heads * HD)
    attended = lax.all_to_all(head_output, "ctx", split_axis=1, concat_axis=2, tiled=True)[0]
    stream = residual_in[0].astype(jnp.float32) + attended.astype(jnp.float32)
    mean_square = jnp.mean(stream * stream, axis=-1, keepdims=True)
    normed = (
        stream / jnp.sqrt(mean_square + 1e-06) * (1.0 + modulation_scale[0][None, :])
        + modulation_shift[0][None, :]
    )
    normed = normed.astype(jnp.bfloat16)
    experts = lax.axis_size("expert")
    capacity = 5 * local_tokens * TOP // (4 * experts)
    choice_flat = expert_choice[0].reshape(local_tokens * TOP)
    onehot = (choice_flat[:, None] == jnp.arange(experts, dtype=jnp.int32)[None, :]).astype(
        jnp.int32
    )
    earlier = jnp.cumsum(onehot, axis=0) - onehot
    target = choice_flat * capacity + jnp.sum(earlier * onehot, axis=1)
    send_buffer = (
        jnp.zeros((experts * capacity, width), jnp.bfloat16)
        .at[target]
        .set(jnp.repeat(normed, TOP, axis=0))
    )
    send_blocks = send_buffer.reshape(experts, capacity, width)
    dp_size = lax.axis_size("dp")
    tiled = jnp.broadcast_to(send_blocks[None], (dp_size, experts, capacity, width)).reshape(
        dp_size * experts, capacity, width
    )
    arrived_rows = lax.all_to_all(tiled, ("dp", "expert"), split_axis=0, concat_axis=0, tiled=True)
    arrived_rows = arrived_rows.reshape(-1, width)
    weight_in, weight_out = (
        lax.all_gather(expert_in[0], "ctx", axis=0, tiled=True),
        lax.all_gather(expert_out[0], "ctx", axis=0, tiled=True),
    )
    pre_act = lax.dot_general(
        arrived_rows, weight_in, (((1,), (1,)), ((), ())), preferred_element_type=jnp.float32
    )
    hidden = jax.nn.gelu(pre_act, approximate=True).astype(jnp.bfloat16)
    summed = lax.psum_scatter(
        jnp.dot(hidden, weight_out, preferred_element_type=jnp.float32).astype(jnp.bfloat16),
        "dp",
        scatter_dimension=0,
        tiled=True,
    )
    expert_result = summed.reshape(experts, capacity, width)
    returned_rows = lax.all_to_all(
        expert_result, "expert", split_axis=0, concat_axis=0, tiled=True
    ).reshape(experts * capacity, width)
    picked = returned_rows[target].reshape(local_tokens, TOP, width).astype(jnp.float32)
    mixture = jnp.sum(gate_values[0][..., None] * picked, axis=1)
    return (stream + mixture).astype(jnp.bfloat16)[None]


def solution(mesh):
    return jax.shard_map(
        per_device,
        mesh=mesh,
        in_specs=(
            P(("dp", "expert"), None, "ctx", None),
            P(("dp", "expert"), "ctx", None),
            P(("dp", "expert"), None),
            P(("dp", "expert"), None),
            P(("dp", "expert"), "ctx", None),
            P(("dp", "expert"), "ctx", None),
            P("expert", ("dp", "ctx"), None),
            P("expert", ("dp", "ctx"), None),
        ),
        out_specs=P(("dp", "expert"), "ctx", None),
        check_vma=False,
    )
```

profile of v0, /device:TPU:7, one launch (start us, length us, event | category | flops | bytes accessed | tf_op | source)
XLA Modules:
  0.0 343.5 jit_solution(7869001802821175676)
XLA Ops:
  6.5 3.6 %copy.54 = bf16[1,3,128,1536]{2,1,0,3:T(4,128)(2,1)} copy(bf16[1,3,128,1536]{3,2,1,0:T(8,128)(2,1)} %param.10) | data formatting | bytes 2359296 | tf_op args[0]
  10.1 10.0 %all-to-all-start = ((bf16[1,3,128,1536]{2,1,0,3:T(4,128)(2,1)}), bf16[1,3,128,1536]{2,1,0,3:T(4,128)(2,1)S(1)}, u32[]{:S(2)}, u32[]{:S(2)}) async-start(bf16[1,3,128,1536]{2,1,0,3:T(4,128)(2,1)} %copy.54), calls=%async_computation | async-start | bytes 3145728 | tf_op jit(solution)/shard_map/all_to_all | solution.py:24
  20.2 0.0 all-gather.5.cloned.1.call-start
  20.2 0.7 all-gather.5.cloned.1.call-update
  20.9 0.1 copy.65
  21.0 0.1 eq.29
  21.2 0.6 reduce-window.6
  21.8 47.7 %all-to-all-done = bf16[1,3,128,1536]{2,1,0,3:T(4,128)(2,1)S(1)} async-done(((bf16[1,3,128,1536]{2,1,0,3:T(4,128)(2,1)}), bf16[1,3,128,1536]{2,1,0,3:T(4,128)(2,1)S(1)}, u32[]{:S(2)}, u32[]{:S(2)}) %all-to-all-start) | async-done | bytes 1179680 | tf_op jit(solution)/shard_map/all_to_all | solution.py:24
  69.5 0.2 copy.55
  69.7 0.3 copy.77
  70.0 0.1 fusion.46
  70.1 0.3 reshape_reshape_squeeze.3
  70.4 7.6 %while.10 = (s32[]{:T(128)}, bf16[2,512,192]{1,2,0:T(8,128)(2,1)S(1)}, bf16[2,512,3,64]{1,3,2,0:T(8,128)(2,1)S(1)}, bf16[1024,3,64]{0,2,1:T(8,128)(2,1)S(1)}, bf16[1024,3,64]{0,2,1:T(8,128)(2,1)S(1)}, /*index=5*/s32[]{:T(128)}) while((s32[]{:T(128)}, bf16[2,512,192]{1,2,0:T(8,128)(2,1)S(1)}, bf16[2,512,3,64]{1,3,2,0:T(8,128)(2,1)S(1)}, ...), condition=%wide.region_3.4_spmd, body=%wide.region_0.3_spmd.sunk | while | flops 415429632 | bytes 20478028 | solution.py:50
  70.5 1.1 multiply_reduce_fusion.4
  71.6 1.3 fusion.58
  72.9 1.3 fusion.59
  74.2 1.1 multiply_reduce_fusion.4
  75.4 1.3 fusion.58
  76.7 1.3 fusion.59
  78.0 0.0 copy-start.3
  78.0 0.2 copy.70
  78.2 0.3 reshape.133
  78.5 0.5 broadcast.85
  79.0 4.0 %reduce.5 = bf16[1024,192]{1,0:T(8,128)(2,1)S(1)} reduce(bf16[1024,1,192]{2,1,0:T(2,128)(2,1)S(1)} %bitcast.104, bf16[]{:T(256)} %broadcast.85), dimensions={1}, to_apply=%bitcast.76.reduce_sub_computation | reduce | bytes 786434
  83.1 1.3 reshape.139
  84.4 3.6 %all-to-all-start.1 = ((bf16[8,2,12288]{2,1,0:T(2,128)(2,1)}), bf16[8,2,12288]{2,1,0:T(2,128)(2,1)S(1)}, u32[]{:S(2)}, u32[]{:S(2)}) async-start(bf16[8,2,12288]{2,1,0:T(2,128)(2,1)} %reshape.139), calls=%async_computation.1 | async-start | bytes 786432 | tf_op jit(solution)/shard_map/all_to_all | solution.py:51
  88.1 0.2 slice_reduce_fusion
  88.2 0.1 eq.25
  88.4 0.1 copy.64
  88.5 0.1 mul.70
  88.8 0.1 fusion.40
  88.9 13.5 %all-to-all-done.1 = bf16[8,2,12288]{2,1,0:T(2,128)(2,1)S(1)} async-done(((bf16[8,2,12288]{2,1,0:T(2,128)(2,1)}), bf16[8,2,12288]{2,1,0:T(2,128)(2,1)S(1)}, u32[]{:S(2)}, u32[]{:S(2)}) %all-to-all-start.1) | async-done | bytes 393248 | tf_op jit(solution)/shard_map/all_to_all | solution.py:51
  102.3 0.7 reshape.140
  103.1 0.6 copy.60
  103.7 0.1 convert_bitcast_fusion.1
  103.8 0.1 copy.74
  103.9 0.2 copy.61
  104.1 0.3 copy.69
  104.4 0.2 multiply_reduce_fusion.2
  104.6 0.2 add_convert_fusion
  104.8 0.4 broadcast_in_dim.29
  105.2 1.2 reshape.127
  106.4 2.7 scatter_custom_fusion
  109.0 0.3 broadcast_in_dim.30
  109.3 2.6 broadcast_in_dim.31
  111.9 11.8 %all-to-all-start.2 = ((bf16[64,20,1536]{2,1,0:T(8,128)(2,1)}), bf16[64,20,1536]{2,1,0:T(8,128)(2,1)}, u32[]{:S(2)}, u32[]{:S(2)}) async-start(bf16[64,20,1536]{2,1,0:T(8,128)(2,1)} %bitcast.97), calls=%async_computation.2 | async-start | bytes 9437184 | tf_op jit(solution)/shard_map/all_to_all | solution.py:77
  123.6 0.0 all-gather.7.cloned.1.call-start
  123.7 0.7 all-gather.7.cloned.1.call-update
  124.4 0.0 reduce-scatter.2.cloned.1.call-start
  124.4 106.2 %all-to-all-done.2 = bf16[64,20,1536]{2,1,0:T(8,128)(2,1)} async-done(((bf16[64,20,1536]{2,1,0:T(8,128)(2,1)}), bf16[64,20,1536]{2,1,0:T(8,128)(2,1)}, u32[]{:S(2)}, u32[]{:S(2)}) %all-to-all-start.2) | async-done | bytes 3932192 | tf_op jit(solution)/shard_map/all_to_all | solution.py:77
  230.6 6.9 %reshape.106 = bf16[1280,1536]{1,0:T(8,128)(2,1)} reshape(bf16[64,20,1536]{2,1,0:T(8,128)(2,1)} %all-to-all-done.2) | data formatting | bytes 7864320 | tf_op jit(solution)/shard_map/reshape | solution.py:78
  237.5 12.3 %convolution_convert_fusion = bf16[1280,1536]{1,0:T(8,128)(2,1)} fusion(bf16[1,768,1536]{2,1,0:T(8,128)(2,1)} %all-gather.7.cloned.1.call-done, bf16[1280,1536]{1,0:T(8,128)(2,1)} %reshape.106, bf16[1,768,1536]{2,1,0:T(8,128)(2,1)} %all-gather.5.cloned.1.call-done), kind=kOutput, calls=%fused_computation.16 | convolution fusion | flops 6050611200 | bytes 12582912 | tf_op jit(solution)/shard_map/dot_general | solution.py:88
  249.9 0.0 reduce-scatter.2.cloned.1.call-update
  249.9 39.4 %reduce-scatter.2.cloned.1.call-done = bf16[320,1536]{1,0:T(8,128)(2,1)} async-done(((bf16[1280,1536]{1,0:T(8,128)(2,1)}), bf16[320,1536]{1,0:T(8,128)(2,1)}) %reduce-scatter.2.cloned.1.call-update) | async-done | bytes 983056 | tf_op jit(solution)/shard_map/reduce_scatter | solution.py:87
  289.2 2.1 reshape.107
  291.4 7.4 %all-to-all-start.3 = ((bf16[16,20,1536]{2,1,0:T(8,128)(2,1)}), bf16[16,20,1536]{2,1,0:T(8,128)(2,1)S(1)}, u32[]{:S(2)}, u32[]{:S(2)}) async-start(bf16[16,20,1536]{2,1,0:T(8,128)(2,1)} %reshape.107), calls=%async_computation.4 | async-start | bytes 2359296 | tf_op jit(solution)/shard_map/all_to_all | solution.py:94
  298.8 0.1 copy.63
  298.9 1.2 copy.62
  300.1 29.2 %all-to-all-done.3 = bf16[16,20,1536]{2,1,0:T(8,128)(2,1)S(1)} async-done(((bf16[16,20,1536]{2,1,0:T(8,128)(2,1)}), bf16[16,20,1536]{2,1,0:T(8,128)(2,1)S(1)}, u32[]{:S(2)}, u32[]{:S(2)}) %all-to-all-start.3) | async-done | bytes 983072 | tf_op jit(solution)/shard_map/all_to_all | solution.py:94
  329.3 0.2 reshape.108
  329.6 2.1 gather_fusion
  331.7 2.2 reshape.112
  333.9 2.2 multiply_reduce_fusion.1
  336.1 0.9 fusion.34
  (26 shorter events, 0.2 us)
Async XLA Ops:
  6.5 14.4 %copy-start.4 = (s32[1,128,2]{1,2,0:T(2,128)S(1)}, s32[1,128,2]{1,2,0:T(2,128)}, u32[]{:S(2)}) copy-start(s32[1,128,2]{1,2,0:T(2,128)} %param.14) | copy-start | bytes 3076
  10.1 59.4 %all-to-all-start = ((bf16[1,3,128,1536]{2,1,0,3:T(4,128)(2,1)}), bf16[1,3,128,1536]{2,1,0,3:T(4,128)(2,1)S(1)}, u32[]{:S(2)}, u32[]{:S(2)}) async-start(bf16[1,3,128,1536]{2,1,0,3:T(4,128)(2,1)} %copy.54), calls=%async_computation | async-start | bytes 3145728 | tf_op jit(solution)/shard_map/all_to_all | solution.py:24
  20.2 217.4 %all-gather.5.cloned.1.call-start = ((), (), s32[]{:S(2)}) async-start(), calls=%async_computation.6 | async-start | bytes 2654208 | tf_op jit(solution)/shard_map/all_gather | solution.py:80
  78.0 10.7 %copy-start.3 = (f32[1,1536]{1,0:T(1,128)S(1)}, f32[1,1536]{1,0:T(1,128)}, u32[]{:S(2)}) copy-start(f32[1,1536]{1,0:T(1,128)} %param.13) | copy-start | bytes 18436
  78.0 10.7 %copy-start.2 = (f32[1,1536]{1,0:T(1,128)S(1)}, f32[1,1536]{1,0:T(1,128)}, u32[]{:S(2)}) copy-start(f32[1,1536]{1,0:T(1,128)} %param.12) | copy-start | bytes 18436
  84.4 17.9 %all-to-all-start.1 = ((bf16[8,2,12288]{2,1,0:T(2,128)(2,1)}), bf16[8,2,12288]{2,1,0:T(2,128)(2,1)S(1)}, u32[]{:S(2)}, u32[]{:S(2)}) async-start(bf16[8,2,12288]{2,1,0:T(2,128)(2,1)} %reshape.139), calls=%async_computation.1 | async-start | bytes 786432 | tf_op jit(solution)/shard_map/all_to_all | solution.py:51
  103.1 1.3 copy-start
  111.9 118.8 %all-to-all-start.2 = ((bf16[64,20,1536]{2,1,0:T(8,128)(2,1)}), bf16[64,20,1536]{2,1,0:T(8,128)(2,1)}, u32[]{:S(2)}, u32[]{:S(2)}) async-start(bf16[64,20,1536]{2,1,0:T(8,128)(2,1)} %bitcast.97), calls=%async_computation.2 | async-start | bytes 9437184 | tf_op jit(solution)/shard_map/all_to_all | solution.py:77
  123.6 113.9 %all-gather.7.cloned.1.call-start = ((), (), s32[]{:S(2)}) async-start(), calls=%async_computation.7 | async-start | bytes 2654208 | tf_op jit(solution)/shard_map/all_gather | solution.py:81
  124.4 164.9 %reduce-scatter.2.cloned.1.call-start = ((), (), s32[]{:S(2)}) async-start(), calls=%async_computation.5 | async-start | bytes 4915200 | tf_op jit(solution)/shard_map/reduce_scatter | solution.py:87
  249.9 48.9 %copy-start.5 = (f32[1,128,2]{1,2,0:T(2,128)S(1)}, f32[1,128,2]{1,2,0:T(2,128)}, u32[]{:S(2)}) copy-start(f32[1,128,2]{1,2,0:T(2,128)} %param.15) | copy-start | bytes 3076
  291.4 37.9 %all-to-all-start.3 = ((bf16[16,20,1536]{2,1,0:T(8,128)(2,1)}), bf16[16,20,1536]{2,1,0:T(8,128)(2,1)S(1)}, u32[]{:S(2)}, u32[]{:S(2)}) async-start(bf16[16,20,1536]{2,1,0:T(8,128)(2,1)} %reshape.107), calls=%async_computation.4 | async-start | bytes 2359296 | tf_op jit(solution)/shard_map/all_to_all | solution.py:94
  331.7 4.4 %copy-start.1 = (f32[1,128,1536]{2,1,0:T(8,128)S(1)}, f32[1,128,1536]{2,1,0:T(8,128)}, u32[]{:S(2)}) copy-start(f32[1,128,1536]{2,1,0:T(8,128)} %copy.62) | copy-start | bytes 2359300
Sparse Core Ops, SparseCore 0:
  23.1 58.3 all-gather.4
  126.5 37.1 all-gather.6
  250.0 39.1 reduce-scatter.1
where the time goes:
time: 347 us; the launch traced here: 344 us
  waiting for transfers between devices  237 us (68%)
  starting transfers between devices  32.9 us (9%)
  local copies, waits for them, and re-layouts  31.7 us (9%)
  matrix products  17.2 us (5%)
  between operations  13.4 us (4%)
  other arithmetic  10.9 us (3%)
    all_to_all x1, waiting for transfers between devices, per_device(): lax.all_to_all(tiled, ('dp', 'expert'), split_axis=0, concat_axis=0, tile...  106 us
    all_to_all x1, waiting for transfers between devices, per_device(): lax.all_to_all(projected, 'ctx', split_axis=3, concat_axis=2, tiled=True)  47.7 us
    reduce_scatter x1, waiting for transfers between devices, per_device(): lax.psum_scatter(jnp.dot(hidden, weight_out, preferred_element_type=jnp.f...  39.4 us
    all_to_all x1, waiting for transfers between devices, per_device(): lax.all_to_all(expert_result, 'expert', split_axis=0, concat_axis=0, tile...  29.2 us
    all_to_all x1, waiting for transfers between devices, per_device(): lax.all_to_all(head_output, 'ctx', split_axis=1, concat_axis=2, tiled=True)  13.5 us
    dot_general x1, matrix products, per_device(): jnp.dot(hidden, weight_out, preferred_element_type=jnp.float32)  12.3 us
    all_to_all x1, starting transfers between devices, per_device(): lax.all_to_all(tiled, ('dp', 'expert'), split_axis=0, concat_axis=0, tile...  11.8 us
    all_to_all x1, starting transfers between devices, per_device(): lax.all_to_all(projected, 'ctx', split_axis=3, concat_axis=2, tiled=True)  10 us
  transfers between devices with their start and end apart: 7, of which 5 were waited for; matrix products, arithmetic and copies ran while one was open for 10% of the time, Pallas kernels for 0%

commit v1 on v0

v1 whole, which is shorter than its diff:
```python
import functools

import jax
import jax.numpy as jnp
from jax import lax
from jax.experimental import pallas as pl
from jax.experimental.pallas import tpu as pltpu
from jax.sharding import PartitionSpec as P

HD = 64
CHUNKS = 1
BF = jnp.bfloat16
F32 = jnp.float32
LIMIT = 48 * 1024 * 1024


def swap(x):
    return jnp.concatenate([x[:, HD:], x[:, :HD]], axis=1)


def low_lanes(rows):
    return lax.broadcasted_iota(jnp.int32, (rows, 2 * HD), 1) < HD


def pack_kernel(x_ref, o_ref):
    n = o_ref.shape[0]
    t = x_ref.shape[2]
    half = t // 2
    low, low_half = low_lanes(t), low_lanes(half)
    for j in range(n):
        for part in range(3):
            o_ref[j, part * t : (part + 1) * t, :] = x_ref[0, part, :, 128 * j : 128 * (j + 1)]
        at = 128 * (n + j // 2)
        q, k, v = (x_ref[0, part, :, at : at + 128] for part in range(3))
        if j % 2 == 0:
            o_ref[j, 3 * t : 4 * t, :] = jnp.where(low, q, swap(k))
            o_ref[j, 4 * t :, :] = jnp.where(low_half, v[:half], swap(v[half:]))
        else:
            o_ref[j, 3 * t : 4 * t, :] = jnp.where(low, swap(q), k)
            o_ref[j, 4 * t :, :] = jnp.where(low_half, swap(v[:half]), v[half:])


def attend_kernel(m_ref, o_ref, v2_ref):
    n, _, _ = m_ref.shape
    t = m_ref.shape[1] * 2 // 9
    half = t // 2
    group = o_ref.shape[0]
    step = pl.program_id(0)

    @pl.when(step == 0)
    def _():
        for z in range(n):
            block = m_ref[z, 4 * t :, :]
            v2_ref[z * t : z * t + half, :] = block
            v2_ref[z * t + half : (z + 1) * t, :] = swap(block)

    rows = group * t
    low = low_lanes(rows)
    mine = pl.ds(step * group, group)
    q01 = m_ref[mine, 0:t, :].reshape(rows, 128)
    q2 = swap(m_ref[mine, 3 * t : 4 * t, :].reshape(rows, 128))
    k01 = m_ref[:, t : 2 * t, :].reshape(n * t, 128)
    k2 = m_ref[:, 3 * t : 4 * t, :].reshape(n * t, 128)
    v01 = m_ref[:, 2 * t : 3 * t, :].reshape(n * t, 128)
    v2 = v2_ref[...]
    zero = jnp.zeros_like(q01)

    def head(q, k, v):
        scores = lax.dot_general(q, k, (((1,), (1,)), ((), ())), preferred_element_type=F32)
        scores = scores * HD ** (-0.5)
        probs = jnp.exp(scores - jnp.max(scores, axis=-1, keepdims=True))
        totals = jnp.sum(probs, axis=-1, keepdims=True)
        return jnp.dot(probs.astype(BF), v, preferred_element_type=F32) / totals

    a = head(jnp.where(low, q01, zero), k01, v01)
    b = head(jnp.where(low, zero, q01), k01, v01)
    c = head(jnp.where(low, zero, q2), k2, v2).astype(BF)
    pair = jnp.where(low, a, b).astype(BF)
    low_half = low_lanes(half)
    for g in range(group):
        o_ref[g, 0:t, :] = pair[g * t : (g + 1) * t]
        o_ref[g, t:, :] = jnp.where(
            low_half, c[g * t : g * t + half], swap(c[g * t + half : (g + 1) * t])
        )


def dispatch_kernel(experts, cap, b_ref, r_ref, scale_ref, shift_ref, choice_ref, s_ref, *sends):
    n = b_ref.shape[0]
    t, width = r_ref.shape
    half = t // 2
    low_half = low_lanes(half)
    tiles = [b_ref[j, 0:t, :] for j in range(n)]
    for m in range(n // 2):
        even, odd = b_ref[2 * m, t:, :], b_ref[2 * m + 1, t:, :]
        top = jnp.where(low_half, even, swap(odd))
        bottom = jnp.where(low_half, swap(even), odd)
        tiles.append(jnp.concatenate([top, bottom], axis=0))
    attended = jnp.concatenate(tiles, axis=1)
    stream = r_ref[...].astype(F32) + attended.astype(F32)
    s_ref[...] = stream
    mean_square = jnp.mean(stream * stream, axis=-1, keepdims=True)
    normed = (
        stream / jnp.sqrt(mean_square + 1e-06) * (1.0 + scale_ref[...]) + shift_ref[...]
    ).astype(BF)
    choices = choice_ref[...]
    expert_at = lax.broadcasted_iota(jnp.int32, (experts, t), 0)
    first, second = expert_at == choices[0:1], expert_at == choices[1:2]
    earlier = lax.broadcasted_iota(jnp.int32, (t, t), 0) < lax.broadcasted_iota(
        jnp.int32, (t, t), 1
    )
    before = jnp.dot(
        (first | second).astype(F32).astype(BF),
        earlier.astype(F32).astype(BF),
        preferred_element_type=F32,
    ).astype(jnp.int32)
    keys = [
        choices[k : k + 1] * 32 + jnp.sum(jnp.where(named, before, 0), axis=0, keepdims=True)
        for k, named in enumerate((first, second))
    ]
    part = cap // len(sends)
    main, extra = part * 4 // 5, part // 5
    rows = experts * main
    at = lax.broadcasted_iota(jnp.int32, (rows, 1), 0)
    quarter = width // 4
    for c, send in enumerate(sends):
        main_key = at // main * 32 + c * part + at % main
        pick = ((main_key == keys[0]) | (main_key == keys[1])).astype(F32).astype(BF)
        send[:, :width] = jnp.dot(pick, normed, preferred_element_type=F32).astype(BF)
        extra_key = at // main * 32 + c * part + main + at % main // 4
        matches = (extra_key == keys[0]) | (extra_key == keys[1])
        total = jnp.zeros((rows, quarter), F32)
        for q in range(4):
            pick = (matches & (at % 4 == q)).astype(F32).astype(BF)
            total += jnp.dot(
                pick, normed[:, q * quarter : (q + 1) * quarter], preferred_element_type=F32
            )
        send[:, width:] = total.astype(BF)


def expert_kernel(x_ref, in_ref, out_ref, y_ref, rows_ref):
    rows = x_ref.shape[0]
    width = in_ref.shape[1]
    quarter = width // 4
    extras = rows // 4
    rows_ref[:rows, :] = x_ref[:, :width]
    packed = x_ref[:, width:]
    row_at = lax.broadcasted_iota(jnp.int32, (extras, rows), 0)
    source = lax.broadcasted_iota(jnp.int32, (extras, rows), 1)
    for q in range(4):
        pick = (source == 4 * row_at + q).astype(F32).astype(BF)
        rows_ref[rows:, q * quarter : (q + 1) * quarter] = jnp.dot(
            pick, packed, preferred_element_type=F32
        ).astype(BF)
    pre_act = lax.dot_general(
        rows_ref[...], in_ref[...], (((1,), (1,)), ((), ())), preferred_element_type=F32
    )
    hidden = jax.nn.gelu(pre_act, approximate=True).astype(BF)
    partial = jnp.dot(hidden, out_ref[...], preferred_element_type=F32).astype(BF)
    y_ref[:, :width] = partial[:rows]
    to = lax.broadcasted_iota(jnp.int32, (rows, extras), 0)
    origin = lax.broadcasted_iota(jnp.int32, (rows, extras), 1)
    total = jnp.zeros((rows, quarter), F32)
    for q in range(4):
        pick = (to == 4 * origin + q).astype(F32).astype(BF)
        total += jnp.dot(
            pick, partial[rows:, q * quarter : (q + 1) * quarter], preferred_element_type=F32
        )
    y_ref[:, width:] = total.astype(BF)


def combine_kernel(experts, cap, s_ref, choice_ref, gate_ref, *refs):
    returned, o_ref = refs[:-1], refs[-1]
    t, width = s_ref.shape
    choices = choice_ref[...]
    expert_at = lax.broadcasted_iota(jnp.int32, (t, 128), 1)
    first, second = expert_at == choices[:, 0:1], expert_at == choices[:, 1:2]
    earlier = lax.broadcasted_iota(jnp.int32, (t, t), 1) < lax.broadcasted_iota(
        jnp.int32, (t, t), 0
    )
    before = jnp.dot(
        earlier.astype(F32).astype(BF),
        (first | second).astype(F32).astype(BF),
        preferred_element_type=F32,
    ).astype(jnp.int32)
    keys = jnp.concatenate(
        [
            choices[:, k : k + 1] * 32
            + jnp.sum(jnp.where(named, before, 0), axis=1, keepdims=True)
            for k, named in enumerate((first, second))
        ],
        axis=0,
    )
    part = cap // len(returned)
    main, extra = part * 4 // 5, part // 5
    rows = experts * main
    at = lax.broadcasted_iota(jnp.int32, (1, rows), 1)
    quarter = width // 4
    picked = jnp.zeros((2 * t, width), F32)
    for c, back in enumerate(returned):
        main_key = at // main * 32 + c * part + at % main
        pick = (main_key == keys).astype(F32).astype(BF)
        picked += jnp.dot(pick, back[:, :width], preferred_element_type=F32)
        extra_key = at // main * 32 + c * part + main + at % main // 4
        parts = []
        for q in range(4):
            pick = ((extra_key == keys) & (at % 4 == q)).astype(F32).astype(BF)
            parts.append(jnp.dot(pick, back[:, width:], preferred_element_type=F32))
        picked += jnp.concatenate(parts, axis=1)
    gates = gate_ref[...]
    mixture = gates[:, 0:1] * picked[:t] + gates[:, 1:2] * picked[t:]
    o_ref[0] = (s_ref[...] + mixture).astype(BF)


def local(kernel, out_shape, scratch=(), **more):
    return pl.pallas_call(
        kernel,
        out_shape=out_shape,
        scratch_shapes=scratch,
        compiler_params=pltpu.CompilerParams(vmem_limit_bytes=LIMIT),
        **more,
    )


def run_experts(x, weight_in, weight_out):
    rows, wide = x.shape
    hidden, width = weight_in.shape
    work = rows * 5 // 4
    return local(
        expert_kernel,
        jax.ShapeDtypeStruct((rows, wide), BF),
        [pltpu.VMEM((work, width), BF)],
        cost_estimate=pl.CostEstimate(
            flops=4 * work * hidden * width,
            bytes_accessed=4 * hidden * width + 4 * rows * wide,
            transcendentals=work * hidden,
        ),
    )(x, weight_in, weight_out)


def add(a, b):
    return (a.astype(F32) + b.astype(F32)).astype(BF)


def expert_layer(x, weights):
    right = [(i, (i + 1) % 4) for i in range(4)]
    left = [(i, (i + 3) % 4) for i in range(4)]
    half = x.shape[0] // 2
    from_left = lax.ppermute(x, "dp", right)
    from_right = lax.ppermute(x, "dp", left)
    across = jnp.concatenate(
        [
            lax.ppermute(from_left[:half], "dp", right),
            lax.ppermute(from_right[half:], "dp", left),
        ]
    )
    own = run_experts(x, *weights)
    for_left = run_experts(from_left, *weights)
    for_right = run_experts(from_right, *weights)
    for_across = run_experts(across, *weights)
    via_left = lax.ppermute(for_across[:half], "dp", right)
    via_right = lax.ppermute(for_across[half:], "dp", left)
    to_right = jnp.concatenate([add(for_right[:half], via_left), for_right[half:]])
    to_left = jnp.concatenate([for_left[:half], add(for_left[half:], via_right)])
    one = lax.ppermute(to_right, "dp", right)
    two = lax.ppermute(to_left, "dp", left)
    return (own.astype(F32) + one.astype(F32) + two.astype(F32)).astype(BF)


def per_device(
    projected,
    residual_in,
    modulation_scale,
    modulation_shift,
    expert_choice,
    gate_values,
    expert_in,
    expert_out,
):
    _, _, t, width = projected.shape
    n = lax.axis_size("ctx")
    experts = lax.axis_size("expert")
    cap = 5 * t * 2 // (4 * experts)
    packed = local(pack_kernel, jax.ShapeDtypeStruct((n, t * 9 // 2, 128), BF))(projected)
    mixed = lax.all_to_all(packed, "ctx", 0, 0, tiled=True)
    mixed, expert_in, expert_out = lax.optimization_barrier((mixed, expert_in, expert_out))
    weights = (
        lax.all_gather(expert_in[0], "ctx", axis=0, tiled=True),
        lax.all_gather(expert_out[0], "ctx", axis=0, tiled=True),
    )
    group = 2
    head_output = local(
        attend_kernel,
        jax.ShapeDtypeStruct((n, t * 3 // 2, 128), BF),
        [pltpu.VMEM((n * t, 128), BF)],
        grid=(n // group,),
        in_specs=[pl.BlockSpec((n, t * 9 // 2, 128), lambda i: (0, 0, 0))],
        out_specs=pl.BlockSpec((group, t * 3 // 2, 128), lambda i: (i, 0, 0)),
    )(mixed)
    back = lax.all_to_all(head_output, "ctx", 0, 0, tiled=True)
    part = cap // CHUNKS
    wide = (experts * part * 4 // 5, width * 5 // 4)
    stream, *sends = local(
        functools.partial(dispatch_kernel, experts, cap),
        [jax.ShapeDtypeStruct((t, width), F32)] + [jax.ShapeDtypeStruct(wide, BF)] * CHUNKS,
    )(back, residual_in[0], modulation_scale, modulation_shift, expert_choice[0].T)
    arrived = [lax.all_to_all(x, "expert", 0, 0, tiled=True) for x in sends]
    sums = [expert_layer(x, weights) for x in arrived]
    returned = [lax.all_to_all(x, "expert", 0, 0, tiled=True) for x in sums]
    return local(
        functools.partial(combine_kernel, experts, cap),
        jax.ShapeDtypeStruct((1, t, width), BF),
    )(stream, expert_choice[0], gate_values[0], *returned)


def solution(mesh):
    return jax.shard_map(
        per_device,
        mesh=mesh,
        in_specs=(
            P(("dp", "expert"), None, "ctx", None),
            P(("dp", "expert"), "ctx", None),
            P(("dp", "expert"), None),
            P(("dp", "expert"), None),
            P(("dp", "expert"), "ctx", None),
            P(("dp", "expert"), "ctx", None),
            P("expert", ("dp", "ctx"), None),
            P("expert", ("dp", "ctx"), None),
        ),
        out_specs=P(("dp", "expert"), "ctx", None),
        check_vma=False,
    )
```

time: 347 us -> 255 us (0.73)
  waiting for transfers between devices: 237 us -> 98.9 us
  blocking collectives: 0 us -> 77.5 us
  local copies, waits for them, and re-layouts: 31.7 us -> 3.47 us
  Pallas kernels: 0 us -> 27.6 us
  matrix products: 17.2 us -> 0 us
  other arithmetic: 10.9 us -> 1.78 us
    all_to_all x4 -> x2, waiting for transfers between devices: 197 us -> 43 us  [the longest x1 26.5 us: per_device(): returned = [lax.all_to_all(x, 'expert', 0, 0, tiled=True) for x in sums]]
    all_to_all x0 -> x2, blocking collectives: none -> 77.5 us  [the longest x1 40.2 us: per_device(): mixed = lax.all_to_all(packed, 'ctx', 0, 0, tiled=True)]
    ppermute x0 -> x8, waiting for transfers between devices: none -> 55.2 us  [the longest x1 19.9 us: expert_layer(): from_left = lax.ppermute(x, 'dp', right)]
    reduce_scatter x1 -> x0, waiting for transfers between devices: 39.4 us -> none  [per_device(): lax.psum_scatter(jnp.dot(hidden, weight_out, preferred_element_type=jnp.f...]
    pallas_call x0 -> x8, Pallas kernels: none -> 27.6 us  [the longest x4 17 us: run_experts(): local(expert_kernel, jax.ShapeDtypeStruct((rows, wide), BF), [pltpu.VMEM(...]
    all_to_all x4 -> x2, starting transfers between devices: 32.8 us -> 9.96 us  [the longest x1 6.51 us: per_device(): returned = [lax.all_to_all(x, 'expert', 0, 0, tiled=True) for x in sums]]
    ppermute x0 -> x8, starting transfers between devices: none -> 21.4 us  [the longest x1 3.38 us: expert_layer(): lax.ppermute(from_left[:half], 'dp', right)]
    dot_general x5 -> x0, matrix products: 17.2 us -> none  [the longest x1 12.3 us: per_device(): jnp.dot(hidden, weight_out, preferred_element_type=jnp.float32)]
  transfers between devices with their start and end apart: 7 -> 12, of which waited for: 5 -> 8; matrix products, arithmetic and copies ran while one was open for 10% -> 0% of each run, Pallas kernels for 0% -> 8%
where the time goes in v1:
time: 255 us; the launch traced here: 254 us
  waiting for transfers between devices  98.9 us (39%)
  blocking collectives  77.5 us (30%)
  starting transfers between devices  31.4 us (12%)
  Pallas kernels  27.6 us (11%)
  between operations  13.7 us (5%)
  local copies, waits for them, and re-layouts  3.47 us (1%)
    all_to_all x1, blocking collectives, per_device(): mixed = lax.all_to_all(packed, 'ctx', 0, 0, tiled=True)  40.2 us
    all_to_all x1, blocking collectives, per_device(): arrived = [lax.all_to_all(x, 'expert', 0, 0, tiled=True) for x in sends]  37.3 us
    all_to_all x1, waiting for transfers between devices, per_device(): returned = [lax.all_to_all(x, 'expert', 0, 0, tiled=True) for x in sums]  26.5 us
    ppermute x1, waiting for transfers between devices, expert_layer(): from_left = lax.ppermute(x, 'dp', right)  19.9 us
    pallas_call x4, Pallas kernels, run_experts(): local(expert_kernel, jax.ShapeDtypeStruct((rows, wide), BF), [pltpu.VMEM(...  17 us
    all_to_all x1, waiting for transfers between devices, per_device(): back = lax.all_to_all(head_output, 'ctx', 0, 0, tiled=True)  16.5 us
    ppermute x1, waiting for transfers between devices, expert_layer(): one = lax.ppermute(to_right, 'dp', right)  10.1 us
    ppermute x1, waiting for transfers between devices, expert_layer(): lax.ppermute(from_left[:half], 'dp', right)  9.25 us
  transfers between devices with their start and end apart: 12, of which 8 were waited for; matrix products, arithmetic and copies ran while one was open for 0% of the time, Pallas kernels for 8%

profile of v1, /device:TPU:7, one launch (start us, length us, event | category | flops | bytes accessed | tf_op | source)
XLA Modules:
  0.0 254.3 jit_solution(16319570024626229862)
XLA Ops:
  6.5 0.0 all-gather.5.cloned.1.call-start
  6.5 0.0 copy-start.4
  6.5 1.3 copy-done.4
  7.8 0.3 shard_map.82
  8.1 40.2 %all_to_all.32.m_ref = bf16[8,576,128]{2,1,0:T(8,128)(2,1)S(1)} all-to-all(bf16[8,576,128]{2,1,0:T(8,128)(2,1)S(1)} %shard_map.82), channel_id=1, replica_groups=mesh['dp'=4,'ctx'=8,'expert'=16] {'ctx'}, dimensions={0} | all-to-all | bytes 2359296 | tf_op jit(solution)/shard_map/all_to_all | solution.py:284
  48.3 0.0 copy-start.10
  48.3 0.0 copy-start.7
  48.3 0.0 all-gather.5.cloned.1.call-update
  48.3 7.6 %shard_map.83 = bf16[8,192,128]{2,1,0:T(8,128)(2,1)} custom-call(bf16[8,576,128]{2,1,0:T(8,128)(2,1)S(1)} %all_to_all.32.m_ref), custom_call_target="tpu_custom_call" | custom-call | tf_op jit(solution)/shard_map/pallas_call | solution.py:291
  56.0 3.5 %all-to-all-start.1 = ((bf16[8,192,128]{2,1,0:T(8,128)(2,1)}), bf16[8,192,128]{2,1,0:T(8,128)(2,1)S(1)}, u32[]{:S(2)}, u32[]{:S(2)}) async-start(bf16[8,192,128]{2,1,0:T(8,128)(2,1)} %shard_map.83), calls=%async_computation.1 | async-start | bytes 786432 | tf_op jit(solution)/shard_map/all_to_all | solution.py:299
  59.4 0.0 all-gather.7.cloned.1.call-start
  59.5 0.7 all-gather.7.cloned.1.call-update
  60.2 0.0 copy-done.10
  60.2 0.1 copy.9
  60.3 0.1 copy.10.choice_ref
  60.4 16.5 %all-to-all-done.1.b_ref = bf16[8,192,128]{2,1,0:T(8,128)(2,1)S(1)} async-done(((bf16[8,192,128]{2,1,0:T(8,128)(2,1)}), bf16[8,192,128]{2,1,0:T(8,128)(2,1)S(1)}, u32[]{:S(2)}, u32[]{:S(2)}) %all-to-all-start.1) | async-done | bytes 393248 | tf_op jit(solution)/shard_map/all_to_all | solution.py:299
  76.8 0.0 copy-done.7
  76.8 0.0 copy-done.8
  76.8 0.0 copy-done.9
  76.8 0.8 shard_map.84
  77.7 37.3 %all_to_all.33 = bf16[16,16,1920]{2,1,0:T(8,128)(2,1)S(1)} all-to-all(bf16[16,16,1920]{2,1,0:T(8,128)(2,1)S(1)} %bitcast.19), channel_id=1, replica_groups=mesh['dp'=4,'ctx'=8,'expert'=16] {'expert'}, dimensions={0} | all-to-all | bytes 1966080 | tf_op jit(solution)/shard_map/all_to_all | solution.py:306
  115.0 2.1 collective-permute-start.1
  117.1 3.2 %collective-permute-start = (bf16[256,1920]{1,0:T(8,128)(2,1)S(1)}, bf16[256,1920]{1,0:T(8,128)(2,1)S(1)}, u32[]{:S(2)}, u32[]{:S(2)}) collective-permute-start(bf16[256,1920]{1,0:T(8,128)(2,1)S(1)} %bitcast.16), channel_id=1, source_target_pairs={{0,384},{128,0},{256,128},{384,256},{1,385},{129,1},{257,129},{385... | collective-permute-start | bytes 2949128 | tf_op jit(solution)/shard_map/ppermute | solution.py:249
  120.3 19.9 %collective-permute-done.1.x_ref = bf16[256,1920]{1,0:T(8,128)(2,1)S(1)} collective-permute-done((bf16[256,1920]{1,0:T(8,128)(2,1)S(1)}, bf16[256,1920]{1,0:T(8,128)(2,1)S(1)}, u32[]{:S(2)}, u32[]{:S(2)}) %collective-permute-start.1) | collective-permute-done | bytes 983072 | tf_op jit(solution)/shard_map/ppermute | solution.py:248
  140.2 3.4 %collective-permute-start.2 = (bf16[128,1920]{1,0:T(8,128)(2,1)S(1)}, bf16[128,1920]{1,0:T(8,128)(2,1)S(1)}, u32[]{:S(2)}, u32[]{:S(2)}) collective-permute-start(bf16[128,1920]{1,0:T(8,128)(2,1)S(1)} %slice.33), channel_id=1, source_target_pairs={{0,128},{128,256},{256,384},{384,0},{1,129},{129,257},{257,385},{3... | collective-permute-start | bytes 1474568 | tf_op jit(solution)/shard_map/ppermute | solution.py:252
  143.6 0.0 collective-permute-done.x_ref
  143.6 0.0 copy-start.2
  143.6 0.0 copy-done.5
  143.7 2.1 collective-permute-start.3
  145.7 9.3 %collective-permute-done.2 = bf16[128,1920]{1,0:T(8,128)(2,1)S(1)} collective-permute-done((bf16[128,1920]{1,0:T(8,128)(2,1)S(1)}, bf16[128,1920]{1,0:T(8,128)(2,1)S(1)}, u32[]{:S(2)}, u32[]{:S(2)}) %collective-permute-start.2) | collective-permute-done | bytes 491552 | tf_op jit(solution)/shard_map/ppermute | solution.py:252
  155.0 0.0 copy-done.2
  155.0 4.3 %collective-permute-done.3 = bf16[128,1920]{1,0:T(8,128)(2,1)S(1)} collective-permute-done((bf16[128,1920]{1,0:T(8,128)(2,1)S(1)}, bf16[128,1920]{1,0:T(8,128)(2,1)S(1)}, u32[]{:S(2)}, u32[]{:S(2)}) %collective-permute-start.3) | collective-permute-done | bytes 491552 | tf_op jit(solution)/shard_map/ppermute | solution.py:253
  159.3 0.1 pad_maximum_fusion.x_ref
  159.4 0.0 all-gather.5.cloned.1.call-done
  159.4 0.0 all-gather.7.cloned.1.call-done
  159.4 0.0 copy-start
  159.4 1.7 copy-done
  161.1 4.4 %shard_map.87 = bf16[256,1920]{1,0:T(8,128)(2,1)S(1)} custom-call(bf16[256,1920]{1,0:T(8,128)(2,1)S(1)} %pad_maximum_fusion.x_ref, bf16[768,1536]{1,0:T(8,128)(2,1)S(1)} %bitcast.11, bf16[768,1536]{1,0:T(8,128)(2,1)} %bitcast.24), custom_call_target="tpu_custom_call" | custom-call | flops 1509949440 | bytes 6684672 | tf_op jit(solution)/shard_map/pallas_call | solution.py:228
  165.5 0.0 copy-start.3
  165.5 0.1 fusion
  165.6 2.1 collective-permute-start.4
  167.6 0.0 copy-done.1
  167.6 0.0 copy-done.3
  167.6 4.2 %shard_map.86 = bf16[256,1920]{1,0:T(8,128)(2,1)S(1)} custom-call(bf16[256,1920]{1,0:T(8,128)(2,1)S(1)} %copy-done.3, bf16[768,1536]{1,0:T(8,128)(2,1)S(1)} %bitcast.12, bf16[768,1536]{1,0:T(8,128)(2,1)} %bitcast.25), custom_call_target="tpu_custom_call" | custom-call | flops 1509949440 | bytes 6684672 | tf_op jit(solution)/shard_map/pallas_call | solution.py:228
  171.9 3.4 %collective-permute-start.6 = (bf16[128,1920]{1,0:T(8,128)(2,1)S(1)}, bf16[128,1920]{1,0:T(8,128)(2,1)S(1)}, u32[]{:S(2)}, u32[]{:S(2)}) collective-permute-start(bf16[128,1920]{1,0:T(8,128)(2,1)S(1)} %get-tuple-element.16), channel_id=1, source_target_pairs={{0,384},{128,0},{256,128},{384,256},{1,385},{129,1},{257,129},{385... | collective-permute-start | bytes 1474568 | tf_op jit(solution)/shard_map/ppermute | solution.py:261
  175.3 4.2 %shard_map.88 = bf16[256,1920]{1,0:T(8,128)(2,1)S(1)} custom-call(bf16[256,1920]{1,0:T(8,128)(2,1)S(1)} %collective-permute-done.1.x_ref, bf16[768,1536]{1,0:T(8,128)(2,1)S(1)} %bitcast.13, bf16[768,1536]{1,0:T(8,128)(2,1)} %bitcast.26), custom_call_target="tpu_custom_call" | custom-call | flops 1509949440 | bytes 6684672 | tf_op jit(solution)/shard_map/pallas_call | solution.py:228
  179.5 0.0 collective-permute-done.4
  179.5 0.1 add_convert_fusion.2
  179.7 0.1 pad_maximum_fusion.1
  179.8 3.1 %collective-permute-start.5 = (bf16[256,1920]{1,0:T(8,128)(2,1)S(1)}, bf16[256,1920]{1,0:T(8,128)(2,1)S(1)}, u32[]{:S(2)}, u32[]{:S(2)}) collective-permute-start(bf16[256,1920]{1,0:T(8,128)(2,1)S(1)} %pad_maximum_fusion.1), channel_id=1, source_target_pairs={{0,128},{128,256},{256,384},{384,0},{1,129},{129,257},{257,385},{3... | collective-permute-start | bytes 2949128 | tf_op jit(solution)/shard_map/ppermute | solution.py:264
  182.9 3.7 %collective-permute-done.6 = bf16[128,1920]{1,0:T(8,128)(2,1)S(1)} collective-permute-done((bf16[128,1920]{1,0:T(8,128)(2,1)S(1)}, bf16[128,1920]{1,0:T(8,128)(2,1)S(1)}, u32[]{:S(2)}, u32[]{:S(2)}) %collective-permute-start.6) | collective-permute-done | bytes 491552 | tf_op jit(solution)/shard_map/ppermute | solution.py:261
  186.6 0.1 add_convert_fusion.1
  186.7 0.1 pad_maximum_fusion.2
  186.8 2.1 collective-permute-start.7
  188.9 4.2 %shard_map.85 = bf16[256,1920]{1,0:T(8,128)(2,1)S(1)} custom-call(bf16[256,1920]{1,0:T(8,128)(2,1)S(1)} %bitcast.17, bf16[768,1536]{1,0:T(8,128)(2,1)S(1)} %bitcast.14, bf16[768,1536]{1,0:T(8,128)(2,1)} %bitcast.27), custom_call_target="tpu_custom_call" | custom-call | flops 1509949440 | bytes 6684672 | tf_op jit(solution)/shard_map/pallas_call | solution.py:228
  193.1 10.1 %collective-permute-done.5 = bf16[256,1920]{1,0:T(8,128)(2,1)S(1)} collective-permute-done((bf16[256,1920]{1,0:T(8,128)(2,1)S(1)}, bf16[256,1920]{1,0:T(8,128)(2,1)S(1)}, u32[]{:S(2)}, u32[]{:S(2)}) %collective-permute-start.5) | collective-permute-done | bytes 983072 | tf_op jit(solution)/shard_map/ppermute | solution.py:264
  203.2 7.9 %collective-permute-done.7 = bf16[256,1920]{1,0:T(8,128)(2,1)S(1)} collective-permute-done((bf16[256,1920]{1,0:T(8,128)(2,1)S(1)}, bf16[256,1920]{1,0:T(8,128)(2,1)S(1)}, u32[]{:S(2)}, u32[]{:S(2)}) %collective-permute-start.7) | collective-permute-done | bytes 983072 | tf_op jit(solution)/shard_map/ppermute | solution.py:265
  211.1 1.3 add_convert_fusion
  212.5 6.5 %all-to-all-start.3 = ((bf16[16,16,1920]{2,1,0:T(8,128)(2,1)}), bf16[16,16,1920]{2,1,0:T(8,128)(2,1)S(1)}, u32[]{:S(2)}, u32[]{:S(2)}) async-start(bf16[16,16,1920]{2,1,0:T(8,128)(2,1)} %bitcast.8), calls=%async_computation.3 | async-start | bytes 1966080 | tf_op jit(solution)/shard_map/all_to_all | solution.py:308
  219.0 0.0 copy-done.11
  219.0 0.1 copy.11
  219.1 26.5 %all-to-all-done.3 = bf16[16,16,1920]{2,1,0:T(8,128)(2,1)S(1)} async-done(((bf16[16,16,1920]{2,1,0:T(8,128)(2,1)}), bf16[16,16,1920]{2,1,0:T(8,128)(2,1)S(1)}, u32[]{:S(2)}, u32[]{:S(2)}) %all-to-all-start.3) | async-done | bytes 983072 | tf_op jit(solution)/shard_map/all_to_all | solution.py:308
  245.6 0.0 copy-done.6
  245.7 1.8 shard_map.89
  (10 shorter events, 0.2 us)
Async XLA Ops:
  6.5 152.9 %all-gather.5.cloned.1.call-start = ((), (), s32[]{:S(2)}) async-start(), calls=%async_computation.4 | async-start | bytes 2654208 | tf_op jit(solution)/shard_map/all_gather | solution.py:287
  6.5 1.3 copy-start.4
  48.3 11.9 %copy-start.10 = (s32[1,128,2]{1,2,0:T(2,128)S(1)}, s32[1,128,2]{1,2,0:T(2,128)}, u32[]{:S(2)}) copy-start(s32[1,128,2]{1,2,0:T(2,128)} %param.12) | copy-start | bytes 3076
  48.3 28.5 %copy-start.7 = (bf16[1,128,1536]{2,1,0:T(8,128)(2,1)S(1)}, bf16[1,128,1536]{2,1,0:T(8,128)(2,1)}, u32[]{:S(2)}) copy-start(bf16[1,128,1536]{2,1,0:T(8,128)(2,1)} %param.9) | copy-start | bytes 1179652
  48.3 28.5 %copy-start.8 = (f32[1,1536]{1,0:T(1,128)S(1)}, f32[1,1536]{1,0:T(1,128)}, u32[]{:S(2)}) copy-start(f32[1,1536]{1,0:T(1,128)} %scale_ref.1) | copy-start | bytes 18436
  48.3 28.5 %copy-start.9 = (f32[1,1536]{1,0:T(1,128)S(1)}, f32[1,1536]{1,0:T(1,128)}, u32[]{:S(2)}) copy-start(f32[1,1536]{1,0:T(1,128)} %shift_ref.1) | copy-start | bytes 18436
  56.0 20.9 %all-to-all-start.1 = ((bf16[8,192,128]{2,1,0:T(8,128)(2,1)}), bf16[8,192,128]{2,1,0:T(8,128)(2,1)S(1)}, u32[]{:S(2)}, u32[]{:S(2)}) async-start(bf16[8,192,128]{2,1,0:T(8,128)(2,1)} %shard_map.83), calls=%async_computation.1 | async-start | bytes 786432 | tf_op jit(solution)/shard_map/all_to_all | solution.py:299
  59.4 100.0 %all-gather.7.cloned.1.call-start = ((), (), s32[]{:S(2)}) async-start(), calls=%async_computation.5 | async-start | bytes 2654208 | tf_op jit(solution)/shard_map/all_gather | solution.py:288
  77.7 66.0 %copy-start.5 = (f32[128,1536]{1,0:T(8,128)}, f32[128,1536]{1,0:T(8,128)S(1)}, u32[]{:S(2)}) copy-start(f32[128,1536]{1,0:T(8,128)S(1)} %get-tuple-element.11.s_ref) | copy-start | bytes 2359300
  115.0 25.2 %collective-permute-start.1 = (bf16[256,1920]{1,0:T(8,128)(2,1)S(1)}, bf16[256,1920]{1,0:T(8,128)(2,1)S(1)}, u32[]{:S(2)}, u32[]{:S(2)}) collective-permute-start(bf16[256,1920]{1,0:T(8,128)(2,1)S(1)} %bitcast.15), channel_id=1, source_target_pairs={{0,128},{128,256},{256,384},{384,0},{1,129},{129,257},{257,385},{3... | collective-permute-start | bytes 2949128 | tf_op jit(solution)/shard_map/ppermute | solution.py:248
  117.1 26.5 %collective-permute-start = (bf16[256,1920]{1,0:T(8,128)(2,1)S(1)}, bf16[256,1920]{1,0:T(8,128)(2,1)S(1)}, u32[]{:S(2)}, u32[]{:S(2)}) collective-permute-start(bf16[256,1920]{1,0:T(8,128)(2,1)S(1)} %bitcast.16), channel_id=1, source_target_pairs={{0,384},{128,0},{256,128},{384,256},{1,385},{129,1},{257,129},{385... | collective-permute-start | bytes 2949128 | tf_op jit(solution)/shard_map/ppermute | solution.py:249
  140.2 14.8 %collective-permute-start.2 = (bf16[128,1920]{1,0:T(8,128)(2,1)S(1)}, bf16[128,1920]{1,0:T(8,128)(2,1)S(1)}, u32[]{:S(2)}, u32[]{:S(2)}) collective-permute-start(bf16[128,1920]{1,0:T(8,128)(2,1)S(1)} %slice.33), channel_id=1, source_target_pairs={{0,128},{128,256},{256,384},{384,0},{1,129},{129,257},{257,385},{3... | collective-permute-start | bytes 1474568 | tf_op jit(solution)/shard_map/ppermute | solution.py:252
  143.6 11.4 %copy-start.2 = (bf16[256,1920]{1,0:T(8,128)(2,1)}, bf16[256,1920]{1,0:T(8,128)(2,1)S(1)}, u32[]{:S(2)}) copy-start(bf16[256,1920]{1,0:T(8,128)(2,1)S(1)} %collective-permute-done.x_ref) | copy-start | bytes 2949124
  143.7 15.6 %collective-permute-start.3 = (bf16[128,1920]{1,0:T(8,128)(2,1)S(1)}, bf16[128,1920]{1,0:T(8,128)(2,1)S(1)}, u32[]{:S(2)}, u32[]{:S(2)}) collective-permute-start(bf16[128,1920]{1,0:T(8,128)(2,1)S(1)} %slice.34), channel_id=1, source_target_pairs={{0,384},{128,0},{256,128},{384,256},{1,385},{129,1},{257,129},{385... | collective-permute-start | bytes 1474568 | tf_op jit(solution)/shard_map/ppermute | solution.py:253
  159.4 1.7 copy-start
  161.1 6.5 %copy-start.1 = (bf16[1,768,1536]{2,1,0:T(8,128)(2,1)S(1)}, bf16[1,768,1536]{2,1,0:T(8,128)(2,1)}, u32[]{:S(2)}) copy-start(bf16[1,768,1536]{2,1,0:T(8,128)(2,1)} %all-gather.5.cloned.1.call-done) | copy-start | bytes 7077892
  165.5 2.2 copy-start.3
  165.6 14.0 %collective-permute-start.4 = (bf16[128,1920]{1,0:T(8,128)(2,1)S(1)}, bf16[128,1920]{1,0:T(8,128)(2,1)S(1)}, u32[]{:S(2)}, u32[]{:S(2)}) collective-permute-start(bf16[128,1920]{1,0:T(8,128)(2,1)S(1)} %get-tuple-element.15), channel_id=1, source_target_pairs={{0,128},{128,256},{256,384},{384,0},{1,129},{129,257},{257,385},{3... | collective-permute-start | bytes 1474568 | tf_op jit(solution)/shard_map/ppermute | solution.py:260
  171.9 14.7 %collective-permute-start.6 = (bf16[128,1920]{1,0:T(8,128)(2,1)S(1)}, bf16[128,1920]{1,0:T(8,128)(2,1)S(1)}, u32[]{:S(2)}, u32[]{:S(2)}) collective-permute-start(bf16[128,1920]{1,0:T(8,128)(2,1)S(1)} %get-tuple-element.16), channel_id=1, source_target_pairs={{0,384},{128,0},{256,128},{384,256},{1,385},{129,1},{257,129},{385... | collective-permute-start | bytes 1474568 | tf_op jit(solution)/shard_map/ppermute | solution.py:261
  179.8 23.5 %collective-permute-start.5 = (bf16[256,1920]{1,0:T(8,128)(2,1)S(1)}, bf16[256,1920]{1,0:T(8,128)(2,1)S(1)}, u32[]{:S(2)}, u32[]{:S(2)}) collective-permute-start(bf16[256,1920]{1,0:T(8,128)(2,1)S(1)} %pad_maximum_fusion.1), channel_id=1, source_target_pairs={{0,128},{128,256},{256,384},{384,0},{1,129},{129,257},{257,385},{3... | collective-permute-start | bytes 2949128 | tf_op jit(solution)/shard_map/ppermute | solution.py:264
  186.8 24.3 %collective-permute-start.7 = (bf16[256,1920]{1,0:T(8,128)(2,1)S(1)}, bf16[256,1920]{1,0:T(8,128)(2,1)S(1)}, u32[]{:S(2)}, u32[]{:S(2)}) collective-permute-start(bf16[256,1920]{1,0:T(8,128)(2,1)S(1)} %pad_maximum_fusion.2), channel_id=1, source_target_pairs={{0,384},{128,0},{256,128},{384,256},{1,385},{129,1},{257,129},{385... | collective-permute-start | bytes 2949128 | tf_op jit(solution)/shard_map/ppermute | solution.py:265
  212.5 6.5 %copy-start.11 = (f32[1,128,2]{1,2,0:T(2,128)S(1)}, f32[1,128,2]{1,2,0:T(2,128)}, u32[]{:S(2)}) copy-start(f32[1,128,2]{1,2,0:T(2,128)} %param.13) | copy-start | bytes 3076
  212.5 33.2 %copy-start.6 = (f32[128,1536]{1,0:T(8,128)S(1)}, f32[128,1536]{1,0:T(8,128)}, u32[]{:S(2)}) copy-start(f32[128,1536]{1,0:T(8,128)} %copy-done.5) | copy-start | bytes 2359300
  212.5 33.2 %all-to-all-start.3 = ((bf16[16,16,1920]{2,1,0:T(8,128)(2,1)}), bf16[16,16,1920]{2,1,0:T(8,128)(2,1)S(1)}, u32[]{:S(2)}, u32[]{:S(2)}) async-start(bf16[16,16,1920]{2,1,0:T(8,128)(2,1)} %bitcast.8), calls=%async_computation.3 | async-start | bytes 1966080 | tf_op jit(solution)/shard_map/all_to_all | solution.py:308
Sparse Core Ops, SparseCore 0:
  48.5 46.7 all-gather.4
  97.3 42.7 all-gather.6

commit v2 on v1

--- a/solution.py
+++ b/solution.py
@@ -22,7 +22,9 @@
     return lax.broadcasted_iota(jnp.int32, (rows, 2 * HD), 1) < HD
 
 
-def pack_kernel(x_ref, o_ref):
+def pack_kernel(x_ref, in_ref, out_ref, o_ref, w_ref):
+    w_ref[: in_ref.shape[1], :] = in_ref[0]
+    w_ref[in_ref.shape[1] :, :] = out_ref[0]
     n = o_ref.shape[0]
     t = x_ref.shape[2]
     half = t // 2
@@ -137,35 +139,51 @@
         send[:, width:] = total.astype(BF)
 
 
-def expert_kernel(x_ref, in_ref, out_ref, y_ref, rows_ref):
-    rows = x_ref.shape[0]
+def assemble_kernel(*refs):
+    blocks, (in_ref, out_ref) = refs[:-2], refs[-2:]
+    rows = in_ref.shape[0] // len(blocks)
+    for i, block in enumerate(blocks):
+        in_ref[i * rows : (i + 1) * rows, :] = block[:rows, :]
+        out_ref[i * rows : (i + 1) * rows, :] = block[rows:, :]
+
+
+def expert_kernel(pieces, in_ref, out_ref, *refs):
+    x_refs, y_refs, rows_ref = refs[:pieces], refs[pieces:-1], refs[-1]
+    rows = x_refs[0].shape[0]
     width = in_ref.shape[1]
     quarter = width // 4
     extras = rows // 4
-    rows_ref[:rows, :] = x_ref[:, :width]
-    packed = x_ref[:, width:]
+    every = rows + extras
     row_at = lax.broadcasted_iota(jnp.int32, (extras, rows), 0)
     source = lax.broadcasted_iota(jnp.int32, (extras, rows), 1)
-    for q in range(4):
-        pick = (source == 4 * row_at + q).astype(F32).astype(BF)
-        rows_ref[rows:, q * quarter : (q + 1) * quarter] = jnp.dot(
-            pick, packed, preferred_element_type=F32
-        ).astype(BF)
+    picks = [(source == 4 * row_at + q).astype(F32).astype(BF) for q in range(4)]
+    for p, x_ref in enumerate(x_refs):
+        base = p * every
+        rows_ref[base : base + rows, :] = x_ref[:, :width]
+        packed = x_ref[:, width:]
+        for q in range(4):
+            rows_ref[base + rows : base + every, q * quarter : (q + 1) * quarter] = jnp.dot(
+                picks[q], packed, preferred_element_type=F32
+            ).astype(BF)
     pre_act = lax.dot_general(
         rows_ref[...], in_ref[...], (((1,), (1,)), ((), ())), preferred_element_type=F32
     )
     hidden = jax.nn.gelu(pre_act, approximate=True).astype(BF)
     partial = jnp.dot(hidden, out_ref[...], preferred_element_type=F32).astype(BF)
-    y_ref[:, :width] = partial[:rows]
     to = lax.broadcasted_iota(jnp.int32, (rows, extras), 0)
     origin = lax.broadcasted_iota(jnp.int32, (rows, extras), 1)
-    total = jnp.zeros((rows, quarter), F32)
-    for q in range(4):
-        pick = (to == 4 * origin + q).astype(F32).astype(BF)
-        total += jnp.dot(
-            pick, partial[rows:, q * quarter : (q + 1) * quarter], preferred_element_type=F32
-        )
-    y_ref[:, width:] = total.astype(BF)
+    picks = [(to == 4 * origin + q).astype(F32).astype(BF) for q in range(4)]
+    for p, y_ref in enumerate(y_refs):
+        base = p * every
+        y_ref[:, :width] = partial[base : base + rows]
+        total = jnp.zeros((rows, quarter), F32)
+        for q in range(4):
+            total += jnp.dot(
+                picks[q],
+                partial[base + rows : base + every, q * quarter : (q + 1) * quarter],
+                preferred_element_type=F32,
+            )
+        y_ref[:, width:] = total.astype(BF)
 
 
 def combine_kernel(experts, cap, s_ref, choice_ref, gate_ref, *refs):
@@ -221,49 +239,51 @@
     )
 
 
-def run_experts(x, weight_in, weight_out):
-    rows, wide = x.shape
+def run_experts(pieces, weight_in, weight_out):
+    rows, wide = pieces[0].shape
     hidden, width = weight_in.shape
-    work = rows * 5 // 4
+    work = len(pieces) * rows * 5 // 4
     return local(
-        expert_kernel,
-        jax.ShapeDtypeStruct((rows, wide), BF),
+        functools.partial(expert_kernel, len(pieces)),
+        [jax.ShapeDtypeStruct((rows, wide), BF)] * len(pieces),
         [pltpu.VMEM((work, width), BF)],
         cost_estimate=pl.CostEstimate(
             flops=4 * work * hidden * width,
-            bytes_accessed=4 * hidden * width + 4 * rows * wide,
+            bytes_accessed=4 * hidden * width + 4 * len(pieces) * rows * wide,
             transcendentals=work * hidden,
         ),
-    )(x, weight_in, weight_out)
-
-
-def add(a, b):
-    return (a.astype(F32) + b.astype(F32)).astype(BF)
+    )(weight_in, weight_out, *pieces)
+
+
+def add(*parts):
+    return sum(p.astype(F32) for p in parts).astype(BF)
+
+
+def shift(x, axis, by):
+    n = lax.axis_size(axis)
+    return lax.ppermute(x, axis, [(i, (i + by) % n) for i in range(n)])
+
+
+def after(x, *others):
+    return lax.optimization_barrier((x, *others))[0]
 
 
 def expert_layer(x, weights):
-    right = [(i, (i + 1) % 4) for i in range(4)]
-    left = [(i, (i + 3) % 4) for i in range(4)]
     half = x.shape[0] // 2
-    from_left = lax.ppermute(x, "dp", right)
-    from_right = lax.ppermute(x, "dp", left)
-    across = jnp.concatenate(
-        [
-            lax.ppermute(from_left[:half], "dp", right),
-            lax.ppermute(from_right[half:], "dp", left),
-        ]
-    )
-    own = run_experts(x, *weights)
-    for_left = run_experts(from_left, *weights)
-    for_right = run_experts(from_right, *weights)
-    for_across = run_experts(across, *weights)
-    via_left = lax.ppermute(for_across[:half], "dp", right)
-    via_right = lax.ppermute(for_across[half:], "dp", left)
-    to_right = jnp.concatenate([add(for_right[:half], via_left), for_right[half:]])
-    to_left = jnp.concatenate([for_left[:half], add(for_left[half:], via_right)])
-    one = lax.ppermute(to_right, "dp", right)
-    two = lax.ppermute(to_left, "dp", left)
-    return (own.astype(F32) + one.astype(F32) + two.astype(F32)).astype(BF)
+    a, b = x[:half], x[half:]
+    left_a, right_b = shift(a, "dp", 1), shift(b, "dp", -1)
+    left_b, right_a = shift(b, "dp", 1), shift(a, "dp", -1)
+    across_a, across_b = shift(left_a, "dp", 1), shift(right_b, "dp", -1)
+    to_left_a, to_left_b, to_right_a, to_right_b = run_experts(
+        [left_a, left_b, right_a, right_b], *weights
+    )
+    got_a, got_b = shift(to_left_a, "dp", -1), shift(to_right_b, "dp", 1)
+    to_across_a, to_across_b = run_experts([across_a, across_b], *weights)
+    via_a, via_b = shift(to_across_a, "dp", 1), shift(to_across_b, "dp", -1)
+    own_a, own_b = run_experts([a, b], *weights)
+    sum_a = shift(add(to_right_a, via_a), "dp", 1)
+    sum_b = shift(add(to_left_b, via_b), "dp", -1)
+    return jnp.concatenate([add(own_a, got_a, sum_a), add(own_b, got_b, sum_b)])
 
 
 def per_device(
@@ -280,13 +300,17 @@
     n = lax.axis_size("ctx")
     experts = lax.axis_size("expert")
     cap = 5 * t * 2 // (4 * experts)
-    packed = local(pack_kernel, jax.ShapeDtypeStruct((n, t * 9 // 2, 128), BF))(projected)
+    slice_rows = expert_in.shape[1]
+    packed, block = local(
+        pack_kernel,
+        [
+            jax.ShapeDtypeStruct((n, t * 9 // 2, 128), BF),
+            jax.ShapeDtypeStruct((2 * slice_rows, width), BF),
+        ],
+    )(projected, expert_in, expert_out)
     mixed = lax.all_to_all(packed, "ctx", 0, 0, tiled=True)
-    mixed, expert_in, expert_out = lax.optimization_barrier((mixed, expert_in, expert_out))
-    weights = (
-        lax.all_gather(expert_in[0], "ctx", axis=0, tiled=True),
-        lax.all_gather(expert_out[0], "ctx", axis=0, tiled=True),
-    )
+    block = after(block, mixed)
+    up, down = [shift(block, "ctx", 1)], [shift(block, "ctx", -1)]
     group = 2
     head_output = local(
         attend_kernel,
@@ -303,6 +327,16 @@
         functools.partial(dispatch_kernel, experts, cap),
         [jax.ShapeDtypeStruct((t, width), F32)] + [jax.ShapeDtypeStruct(wide, BF)] * CHUNKS,
     )(back, residual_in[0], modulation_scale, modulation_shift, expert_choice[0].T)
+    up[0], down[0] = after(up[0], *sends), after(down[0], *sends)
+    for _ in range(n // 2 - 2):
+        up.append(shift(up[-1], "ctx", 1))
+        down.append(shift(down[-1], "ctx", -1))
+    far_in = shift(up[-1][:slice_rows], "ctx", 1)
+    far_out = shift(down[-1][slice_rows:], "ctx", -1)
+    far = jnp.concatenate([far_in, far_out])
+    weights = local(
+        assemble_kernel, [jax.ShapeDtypeStruct((n * slice_rows, width), BF)] * 2
+    )(block, *up, *down, far)
     arrived = [lax.all_to_all(x, "expert", 0, 0, tiled=True) for x in sends]
     sums = [expert_layer(x, weights) for x in arrived]
     returned = [lax.all_to_all(x, "expert", 0, 0, tiled=True) for x in sums]

time: 255 us -> 245 us (0.961)
  starting transfers between devices: 31.4 us -> 85 us
  blocking collectives: 77.5 us -> 40.2 us
  waiting for transfers between devices: 98.9 us -> 78.2 us
  between operations: 13.7 us -> 0.4 us
  local copies, waits for them, and re-layouts: 3.47 us -> 7.27 us
  Pallas kernels: 27.6 us -> 31 us
    all_to_all x1 -> x0, blocking collectives: 37.3 us -> none  [per_device(): arrived = [lax.all_to_all(x, 'expert', 0, 0, tiled=True) for x in sends]]
    ppermute x8 -> x20, starting transfers between devices: 21.4 us -> 57.6 us  [shift(): return lax.ppermute(x, axis, [(i, (i + by) % n) for i in range(n)])]
    ppermute x8 -> x20, waiting for transfers between devices: 55.2 us -> 39.8 us  [shift(): return lax.ppermute(x, axis, [(i, (i + by) % n) for i in range(n)])]
    all_to_all x0 -> x1, starting transfers between devices: none -> 10.5 us  [per_device(): arrived = [lax.all_to_all(x, 'expert', 0, 0, tiled=True) for x in sends]]
    all_to_all x1, starting transfers between devices: 6.51 us -> 13.4 us  [per_device(): returned = [lax.all_to_all(x, 'expert', 0, 0, tiled=True) for x in sums]]
    all_to_all x1, waiting for transfers between devices: 16.5 us -> 11.9 us  [per_device(): back = lax.all_to_all(head_output, 'ctx', 0, 0, tiled=True)]
    unnamed x26, local copies, waits for them, and re-layouts: 3.19 us -> 5.92 us
  transfers between devices with their start and end apart: 12 -> 23, of which waited for: 8 -> 9; matrix products, arithmetic and copies ran while one was open for 0% -> 1% of each run, Pallas kernels for 8% -> 8%
where the time goes in v2:
time: 245 us; the launch traced here: 244 us
  starting transfers between devices  85 us (35%)
  waiting for transfers between devices  78.2 us (32%)
  blocking collectives  40.2 us (16%)
  Pallas kernels  31 us (13%)
  local copies, waits for them, and re-layouts  7.27 us (3%)
    ppermute x20, starting transfers between devices, shift(): return lax.ppermute(x, axis, [(i, (i + by) % n) for i in range(n)])  57.6 us
    all_to_all x1, blocking collectives, per_device(): mixed = lax.all_to_all(packed, 'ctx', 0, 0, tiled=True)  40.2 us
    ppermute x20, waiting for transfers between devices, shift(): return lax.ppermute(x, axis, [(i, (i + by) % n) for i in range(n)])  39.8 us
    all_to_all x1, waiting for transfers between devices, per_device(): returned = [lax.all_to_all(x, 'expert', 0, 0, tiled=True) for x in sums]  26.5 us
    pallas_call x3, Pallas kernels, run_experts(): local(functools.partial(expert_kernel, len(pieces)), [jax.ShapeDtypeStruc...  15.8 us
    all_to_all x1, starting transfers between devices, per_device(): returned = [lax.all_to_all(x, 'expert', 0, 0, tiled=True) for x in sums]  13.4 us
    all_to_all x1, waiting for transfers between devices, per_device(): back = lax.all_to_all(head_output, 'ctx', 0, 0, tiled=True)  11.9 us
    all_to_all x1, starting transfers between devices, per_device(): arrived = [lax.all_to_all(x, 'expert', 0, 0, tiled=True) for x in sends]  10.5 us
  transfers between devices with their start and end apart: 23, of which 9 were waited for; matrix products, arithmetic and copies ran while one was open for 1% of the time, Pallas kernels for 8%

profile of v2, /device:TPU:7, one launch (start us, length us, event | category | flops | bytes accessed | tf_op | source)
XLA Modules:
  0.0 243.7 jit_solution(2874949432401319008)
XLA Ops:
  0.0 1.3 copy-done.2
  1.3 1.0 copy-done.6
  2.2 1.0 copy-done.7
  3.2 0.3 shard_map.82
  3.5 40.2 %all_to_all.30.m_ref = bf16[8,576,128]{2,1,0:T(8,128)(2,1)S(1)} all-to-all(bf16[8,576,128]{2,1,0:T(8,128)(2,1)S(1)} %get-tuple-element.22), channel_id=1, replica_groups=mesh['dp'=4,'ctx'=8,'expert'=16] {'ctx'}, dimensions={0} | all-to-all | bytes 2359296 | tf_op jit(solution)/shard_map/all_to_all | solution.py:311
  43.7 7.6 %shard_map.83 = bf16[8,192,128]{2,1,0:T(8,128)(2,1)} custom-call(bf16[8,576,128]{2,1,0:T(8,128)(2,1)S(1)} %all_to_all.30.m_ref), custom_call_target="tpu_custom_call" | custom-call | tf_op jit(solution)/shard_map/pallas_call | solution.py:315
  51.4 3.5 %all-to-all-start.1 = ((bf16[8,192,128]{2,1,0:T(8,128)(2,1)}), bf16[8,192,128]{2,1,0:T(8,128)(2,1)S(1)}, u32[]{:S(2)}, u32[]{:S(2)}) async-start(bf16[8,192,128]{2,1,0:T(8,128)(2,1)} %shard_map.83), calls=%async_computation.1 | async-start | bytes 786432 | tf_op jit(solution)/shard_map/all_to_all | solution.py:323
  54.8 0.1 copy.9
  54.9 0.1 copy.10.choice_ref
  55.0 11.9 %all-to-all-done.1.b_ref = bf16[8,192,128]{2,1,0:T(8,128)(2,1)S(1)} async-done(((bf16[8,192,128]{2,1,0:T(8,128)(2,1)}), bf16[8,192,128]{2,1,0:T(8,128)(2,1)S(1)}, u32[]{:S(2)}, u32[]{:S(2)}) %all-to-all-start.1) | async-done | bytes 393248 | tf_op jit(solution)/shard_map/all_to_all | solution.py:323
  67.0 1.8 shard_map.84
  68.7 10.5 %all-to-all-start.2 = ((bf16[16,16,1920]{2,1,0:T(8,128)(2,1)}), bf16[16,16,1920]{2,1,0:T(8,128)(2,1)}, u32[]{:S(2)}, u32[]{:S(2)}) async-start(bf16[16,16,1920]{2,1,0:T(8,128)(2,1)} %bitcast.4), calls=%async_computation.2 | async-start | bytes 1966080 | tf_op jit(solution)/shard_map/all_to_all | solution.py:340
  79.3 1.9 collective-permute-start.3
  81.2 3.4 %collective-permute-start = (bf16[192,1536]{1,0:T(8,128)(2,1)S(1)}, bf16[192,1536]{1,0:T(8,128)(2,1)S(1)}, u32[]{:S(2)}, u32[]{:S(2)}) collective-permute-start(bf16[192,1536]{1,0:T(8,128)(2,1)S(1)} %get-tuple-element.25.refs_0_), channel_id=1, source_target_pairs={{0,16},{16,32},{32,48},{48,64},{64,80},{80,96},{96,112},{112,0},{1... | collective-permute-start | bytes 1769480 | tf_op jit(solution)/shard_map/ppermute | solution.py:264
  84.6 11.5 %collective-permute-done.3.refs_4_ = bf16[192,1536]{1,0:T(8,128)(2,1)S(1)} collective-permute-done((bf16[192,1536]{1,0:T(8,128)(2,1)S(1)}, bf16[192,1536]{1,0:T(8,128)(2,1)S(1)}, u32[]{:S(2)}, u32[]{:S(2)}) %collective-permute-start.3) | collective-permute-done | bytes 589856 | tf_op jit(solution)/shard_map/ppermute | solution.py:264
  96.1 3.3 %collective-permute-start.4 = (bf16[192,1536]{1,0:T(8,128)(2,1)S(1)}, bf16[192,1536]{1,0:T(8,128)(2,1)}, u32[]{:S(2)}, u32[]{:S(2)}) collective-permute-start(bf16[192,1536]{1,0:T(8,128)(2,1)S(1)} %collective-permute-done.3.refs_4_), channel_id=1, source_target_pairs={{0,112},{16,0},{32,16},{48,32},{64,48},{80,64},{96,80},{112,96},{1... | collective-permute-start | bytes 1769480 | tf_op jit(solution)/shard_map/ppermute | solution.py:264
  99.4 1.9 collective-permute-start.1
  101.4 0.8 copy-done.3
  102.2 9.9 %collective-permute-done.4.refs_5_ = bf16[192,1536]{1,0:T(8,128)(2,1)} collective-permute-done((bf16[192,1536]{1,0:T(8,128)(2,1)S(1)}, bf16[192,1536]{1,0:T(8,128)(2,1)}, u32[]{:S(2)}, u32[]{:S(2)}) %collective-permute-start.4) | collective-permute-done | bytes 589856 | tf_op jit(solution)/shard_map/ppermute | solution.py:264
  112.0 4.8 %collective-permute-start.5 = (bf16[192,1536]{1,0:T(8,128)(2,1)}, bf16[192,1536]{1,0:T(8,128)(2,1)S(1)}, u32[]{:S(2)}, u32[]{:S(2)}) collective-permute-start(bf16[192,1536]{1,0:T(8,128)(2,1)} %collective-permute-done.4.refs_5_), channel_id=1, source_target_pairs={{0,112},{16,0},{32,16},{48,32},{64,48},{80,64},{96,80},{112,96},{1... | collective-permute-start | bytes 1769480 | tf_op jit(solution)/shard_map/ppermute | solution.py:264
  116.9 0.0 collective-permute-done.1.refs_2_
  116.9 1.9 collective-permute-start.2
  118.8 0.0 all-to-all-done.2
  118.8 1.3 fusion
  120.1 2.1 collective-permute-start.8
  122.2 3.3 %collective-permute-start.11 = (bf16[128,1920]{1,0:T(8,128)(2,1)S(1)}, bf16[128,1920]{1,0:T(8,128)(2,1)S(1)}, u32[]{:S(2)}, u32[]{:S(2)}) collective-permute-start(bf16[128,1920]{1,0:T(8,128)(2,1)S(1)} %bitcast.11), channel_id=1, source_target_pairs={{0,384},{128,0},{256,128},{384,256},{1,385},{129,1},{257,129},{385... | collective-permute-start | bytes 1474568 | tf_op jit(solution)/shard_map/ppermute | solution.py:264
  125.5 2.8 %collective-permute-done.5.refs_6_ = bf16[192,1536]{1,0:T(8,128)(2,1)S(1)} collective-permute-done((bf16[192,1536]{1,0:T(8,128)(2,1)}, bf16[192,1536]{1,0:T(8,128)(2,1)S(1)}, u32[]{:S(2)}, u32[]{:S(2)}) %collective-permute-start.5) | collective-permute-done | bytes 589856 | tf_op jit(solution)/shard_map/ppermute | solution.py:264
  128.3 5.2 %collective-permute-start.7 = (bf16[96,1536]{1,0:T(8,128)(2,1)S(1)}, bf16[96,1536]{1,0:T(8,128)(2,1)S(1)}, u32[]{:S(2)}, u32[]{:S(2)}) collective-permute-start(bf16[96,1536]{1,0:T(8,128)(2,1)S(1)} %slice.25), channel_id=1, source_target_pairs={{0,112},{16,0},{32,16},{48,32},{64,48},{80,64},{96,80},{112,96},{1... | collective-permute-start | bytes 884744 | tf_op jit(solution)/shard_map/ppermute | solution.py:264
  133.6 1.9 collective-permute-start.6
  135.5 2.1 collective-permute-start.13
  137.6 0.0 collective-permute-done.11.refs_3_
  137.6 3.2 %collective-permute-start.14 = (bf16[128,1920]{1,0:T(8,128)(2,1)S(1)}, bf16[128,1920]{1,0:T(8,128)(2,1)S(1)}, u32[]{:S(2)}, u32[]{:S(2)}) collective-permute-start(bf16[128,1920]{1,0:T(8,128)(2,1)S(1)} %collective-permute-done.11.refs_3_), channel_id=1, source_target_pairs={{0,384},{128,0},{256,128},{384,256},{1,385},{129,1},{257,129},{385... | collective-permute-start | bytes 1474568 | tf_op jit(solution)/shard_map/ppermute | solution.py:264
  140.8 2.5 %collective-permute-start.10 = (bf16[128,1920]{1,0:T(8,128)(2,1)S(1)}, bf16[128,1920]{1,0:T(8,128)(2,1)S(1)}, u32[]{:S(2)}, u32[]{:S(2)}) collective-permute-start(bf16[128,1920]{1,0:T(8,128)(2,1)S(1)} %bitcast.15), channel_id=1, source_target_pairs={{0,384},{128,0},{256,128},{384,256},{1,385},{129,1},{257,129},{385... | collective-permute-start | bytes 1474568 | tf_op jit(solution)/shard_map/ppermute | solution.py:264
  143.3 0.0 collective-permute-done.7
  143.3 4.0 %collective-permute-start.9 = (bf16[128,1920]{1,0:T(8,128)(2,1)S(1)}, bf16[128,1920]{1,0:T(8,128)(2,1)S(1)}, u32[]{:S(2)}, u32[]{:S(2)}) collective-permute-start(bf16[128,1920]{1,0:T(8,128)(2,1)S(1)} %bitcast.12), channel_id=1, source_target_pairs={{0,128},{128,256},{256,384},{384,0},{1,129},{129,257},{257,385},{3... | collective-permute-start | bytes 1474568 | tf_op jit(solution)/shard_map/ppermute | solution.py:264
  147.3 0.0 collective-permute-done.6
  147.4 3.7 %shard_map.85 = (bf16[768,1536]{1,0:T(8,128)(2,1)}, bf16[768,1536]{1,0:T(8,128)(2,1)}) custom-call(bf16[192,1536]{1,0:T(8,128)(2,1)S(1)} %get-tuple-element.25.refs_0_, bf16[192,1536]{1,0:T(8,128)(2,1)S(1)} %copy-done.4, bf16[192,1536]{1,0:T(8,128)(2,1)} %collective-permute-done.1.refs_2_, bf16[192,1536]{1,0:T(8,128)(2,1)S(1)} %collective-permute-done.2.refs_3_, ...), custom_call_target="tpu_custom_call" | custom-call | tf_op jit(solution)/shard_map/pallas_call | solution.py:337
  151.1 0.0 collective-permute-done.13.refs_0_
  151.1 0.0 collective-permute-done.14.refs_1_
  151.1 1.7 copy-done
  152.8 4.2 %shard_map.88 = (bf16[128,1920]{1,0:T(8,128)(2,1)S(1)}, bf16[128,1920]{1,0:T(8,128)(2,1)S(1)}) custom-call(bf16[768,1536]{1,0:T(8,128)(2,1)S(1)} %copy-done, bf16[768,1536]{1,0:T(8,128)(2,1)} %get-tuple-element.30.out_ref, bf16[128,1920]{1,0:T(8,128)(2,1)S(1)} %collective-permute-done.13.refs_0_, bf16[128,1920]{1,0:T(8,128)(2,1)S(1)} %collective-permute-done.14.refs_1_), custom_call_target="tpu_custom_call" | custom-call | flops 1509949440 | bytes 6684672 | tf_op jit(solution)/shard_map/pallas_call | solution.py:246
  157.0 2.1 collective-permute-start.15
  159.1 1.9 collective-permute-done.10.refs_2_
  161.0 7.4 %shard_map.87 = (bf16[128,1920]{1,0:T(8,128)(2,1)S(1)}, bf16[128,1920]{1,0:T(8,128)(2,1)S(1)}, bf16[128,1920]{1,0:T(8,128)(2,1)S(1)}, bf16[128,1920]{1,0:T(8,128)(2,1)S(1)}) custom-call(bf16[768,1536]{1,0:T(8,128)(2,1)} %get-tuple-element.29.in_ref, bf16[768,1536]{1,0:T(8,128)(2,1)} %get-tuple-element.30.out_ref, ...), custom_call_target="tpu_custom_call" | custom-call | flops 3019898880 | bytes 8650752 | tf_op jit(solution)/shard_map/pallas_call | solution.py:246
  168.4 2.0 collective-permute-start.12
  170.3 2.5 %collective-permute-start.18 = (bf16[128,1920]{1,0:T(8,128)(2,1)S(1)}, bf16[128,1920]{1,0:T(8,128)(2,1)S(1)}, u32[]{:S(2)}, u32[]{:S(2)}) collective-permute-start(bf16[128,1920]{1,0:T(8,128)(2,1)S(1)} %get-tuple-element.38), channel_id=1, source_target_pairs={{0,384},{128,0},{256,128},{384,256},{1,385},{129,1},{257,129},{385... | collective-permute-start | bytes 1474568 | tf_op jit(solution)/shard_map/ppermute | solution.py:264
  172.8 0.0 collective-permute-done.15
  172.8 0.1 add_convert_fusion.3
  172.9 4.2 %collective-permute-start.16 = (bf16[128,1920]{1,0:T(8,128)(2,1)S(1)}, bf16[128,1920]{1,0:T(8,128)(2,1)S(1)}, u32[]{:S(2)}, u32[]{:S(2)}) collective-permute-start(bf16[128,1920]{1,0:T(8,128)(2,1)S(1)} %add_convert_fusion.3), channel_id=1, source_target_pairs={{0,128},{128,256},{256,384},{384,0},{1,129},{129,257},{257,385},{3... | collective-permute-start | bytes 1474568 | tf_op jit(solution)/shard_map/ppermute | solution.py:264
  177.2 4.2 %shard_map.86 = (bf16[128,1920]{1,0:T(8,128)(2,1)S(1)}, bf16[128,1920]{1,0:T(8,128)(2,1)S(1)}) custom-call(bf16[768,1536]{1,0:T(8,128)(2,1)S(1)} %copy-done.1, bf16[768,1536]{1,0:T(8,128)(2,1)} %get-tuple-element.30.out_ref, bf16[128,1920]{1,0:T(8,128)(2,1)S(1)} %bitcast.16, bf16[128,1920]{1,0:T(8,128)(2,1)S(1)} %bitcast.13), custom_call_target="tpu_custom_call" | custom-call | flops 1509949440 | bytes 6684672 | tf_op jit(solution)/shard_map/pallas_call | solution.py:246
  181.4 3.3 %collective-permute-start.17 = (bf16[128,1920]{1,0:T(8,128)(2,1)S(1)}, bf16[128,1920]{1,0:T(8,128)(2,1)S(1)}, u32[]{:S(2)}, u32[]{:S(2)}) collective-permute-start(bf16[128,1920]{1,0:T(8,128)(2,1)S(1)} %get-tuple-element.36), channel_id=1, source_target_pairs={{0,128},{128,256},{256,384},{384,0},{1,129},{129,257},{257,385},{3... | collective-permute-start | bytes 1474568 | tf_op jit(solution)/shard_map/ppermute | solution.py:264
  184.7 5.0 %collective-permute-done.18 = bf16[128,1920]{1,0:T(8,128)(2,1)S(1)} collective-permute-done((bf16[128,1920]{1,0:T(8,128)(2,1)S(1)}, bf16[128,1920]{1,0:T(8,128)(2,1)S(1)}, u32[]{:S(2)}, u32[]{:S(2)}) %collective-permute-start.18) | collective-permute-done | bytes 491552 | tf_op jit(solution)/shard_map/ppermute | solution.py:264
  189.8 0.1 add_convert_fusion.1
  189.9 1.9 collective-permute-start.19
  191.8 0.0 collective-permute-done.12
  191.8 0.2 add_convert_fusion.2
  192.0 4.2 %collective-permute-done.17 = bf16[128,1920]{1,0:T(8,128)(2,1)S(1)} collective-permute-done((bf16[128,1920]{1,0:T(8,128)(2,1)S(1)}, bf16[128,1920]{1,0:T(8,128)(2,1)S(1)}, u32[]{:S(2)}, u32[]{:S(2)}) %collective-permute-start.17) | collective-permute-done | bytes 491552 | tf_op jit(solution)/shard_map/ppermute | solution.py:264
  196.2 4.4 %collective-permute-done.19 = bf16[128,1920]{1,0:T(8,128)(2,1)S(1)} collective-permute-done((bf16[128,1920]{1,0:T(8,128)(2,1)S(1)}, bf16[128,1920]{1,0:T(8,128)(2,1)S(1)}, u32[]{:S(2)}, u32[]{:S(2)}) %collective-permute-start.19) | collective-permute-done | bytes 491552 | tf_op jit(solution)/shard_map/ppermute | solution.py:264
  200.7 0.2 add_convert_fusion
  200.8 1.0 pad_maximum_fusion
  201.9 13.4 %all-to-all-start.3 = ((bf16[16,16,1920]{2,1,0:T(8,128)(2,1)}), bf16[16,16,1920]{2,1,0:T(8,128)(2,1)S(1)}, u32[]{:S(2)}, u32[]{:S(2)}) async-start(bf16[16,16,1920]{2,1,0:T(8,128)(2,1)} %bitcast.7), calls=%async_computation.3 | async-start | bytes 1966080 | tf_op jit(solution)/shard_map/all_to_all | solution.py:342
  215.3 0.1 copy.11
  215.4 26.5 %all-to-all-done.3 = bf16[16,16,1920]{2,1,0:T(8,128)(2,1)S(1)} async-done(((bf16[16,16,1920]{2,1,0:T(8,128)(2,1)}), bf16[16,16,1920]{2,1,0:T(8,128)(2,1)S(1)}, u32[]{:S(2)}, u32[]{:S(2)}) %all-to-all-start.3) | async-done | bytes 983072 | tf_op jit(solution)/shard_map/all_to_all | solution.py:342
  241.9 1.8 shard_map.89
  (27 shorter events, 0.1 us)
Async XLA Ops:
  0.0 1.3 copy-start.2
  1.3 1.0 copy-start.6
  2.2 1.0 copy-start.7
  43.7 11.1 %copy-start.10 = (s32[1,128,2]{1,2,0:T(2,128)S(1)}, s32[1,128,2]{1,2,0:T(2,128)}, u32[]{:S(2)}) copy-start(s32[1,128,2]{1,2,0:T(2,128)} %param.12) | copy-start | bytes 3076
  43.7 23.2 %copy-start.5 = (bf16[1,128,1536]{2,1,0:T(8,128)(2,1)S(1)}, bf16[1,128,1536]{2,1,0:T(8,128)(2,1)}, u32[]{:S(2)}) copy-start(bf16[1,128,1536]{2,1,0:T(8,128)(2,1)} %param.9) | copy-start | bytes 1179652
  43.7 23.2 %copy-start.8 = (f32[1,1536]{1,0:T(1,128)S(1)}, f32[1,1536]{1,0:T(1,128)}, u32[]{:S(2)}) copy-start(f32[1,1536]{1,0:T(1,128)} %scale_ref.1) | copy-start | bytes 18436
  43.7 23.2 %copy-start.9 = (f32[1,1536]{1,0:T(1,128)S(1)}, f32[1,1536]{1,0:T(1,128)}, u32[]{:S(2)}) copy-start(f32[1,1536]{1,0:T(1,128)} %shift_ref.1) | copy-start | bytes 18436
  51.4 15.6 %all-to-all-start.1 = ((bf16[8,192,128]{2,1,0:T(8,128)(2,1)}), bf16[8,192,128]{2,1,0:T(8,128)(2,1)S(1)}, u32[]{:S(2)}, u32[]{:S(2)}) async-start(bf16[8,192,128]{2,1,0:T(8,128)(2,1)} %shard_map.83), calls=%async_computation.1 | async-start | bytes 786432 | tf_op jit(solution)/shard_map/all_to_all | solution.py:323
  68.7 50.1 %all-to-all-start.2 = ((bf16[16,16,1920]{2,1,0:T(8,128)(2,1)}), bf16[16,16,1920]{2,1,0:T(8,128)(2,1)}, u32[]{:S(2)}, u32[]{:S(2)}) async-start(bf16[16,16,1920]{2,1,0:T(8,128)(2,1)} %bitcast.4), calls=%async_computation.2 | async-start | bytes 1966080 | tf_op jit(solution)/shard_map/all_to_all | solution.py:340
  79.3 16.8 %collective-permute-start.3 = (bf16[192,1536]{1,0:T(8,128)(2,1)S(1)}, bf16[192,1536]{1,0:T(8,128)(2,1)S(1)}, u32[]{:S(2)}, u32[]{:S(2)}) collective-permute-start(bf16[192,1536]{1,0:T(8,128)(2,1)S(1)} %get-tuple-element.25.refs_0_), channel_id=1, source_target_pairs={{0,112},{16,0},{32,16},{48,32},{64,48},{80,64},{96,80},{112,96},{1... | collective-permute-start | bytes 1769480 | tf_op jit(solution)/shard_map/ppermute | solution.py:264
  81.2 18.2 %collective-permute-start = (bf16[192,1536]{1,0:T(8,128)(2,1)S(1)}, bf16[192,1536]{1,0:T(8,128)(2,1)S(1)}, u32[]{:S(2)}, u32[]{:S(2)}) collective-permute-start(bf16[192,1536]{1,0:T(8,128)(2,1)S(1)} %get-tuple-element.25.refs_0_), channel_id=1, source_target_pairs={{0,16},{16,32},{32,48},{48,64},{64,80},{80,96},{96,112},{112,0},{1... | collective-permute-start | bytes 1769480 | tf_op jit(solution)/shard_map/ppermute | solution.py:264
  96.1 16.0 %collective-permute-start.4 = (bf16[192,1536]{1,0:T(8,128)(2,1)S(1)}, bf16[192,1536]{1,0:T(8,128)(2,1)}, u32[]{:S(2)}, u32[]{:S(2)}) collective-permute-start(bf16[192,1536]{1,0:T(8,128)(2,1)S(1)} %collective-permute-done.3.refs_4_), channel_id=1, source_target_pairs={{0,112},{16,0},{32,16},{48,32},{64,48},{80,64},{96,80},{112,96},{1... | collective-permute-start | bytes 1769480 | tf_op jit(solution)/shard_map/ppermute | solution.py:264
  99.4 17.4 %collective-permute-start.1 = (bf16[192,1536]{1,0:T(8,128)(2,1)S(1)}, bf16[192,1536]{1,0:T(8,128)(2,1)}, u32[]{:S(2)}, u32[]{:S(2)}) collective-permute-start(bf16[192,1536]{1,0:T(8,128)(2,1)S(1)} %collective-permute-done.refs_1_), channel_id=1, source_target_pairs={{0,16},{16,32},{32,48},{48,64},{64,80},{80,96},{96,112},{112,0},{1... | collective-permute-start | bytes 1769480 | tf_op jit(solution)/shard_map/ppermute | solution.py:264
  101.4 0.8 copy-start.3
  112.0 16.2 %collective-permute-start.5 = (bf16[192,1536]{1,0:T(8,128)(2,1)}, bf16[192,1536]{1,0:T(8,128)(2,1)S(1)}, u32[]{:S(2)}, u32[]{:S(2)}) collective-permute-start(bf16[192,1536]{1,0:T(8,128)(2,1)} %collective-permute-done.4.refs_5_), channel_id=1, source_target_pairs={{0,112},{16,0},{32,16},{48,32},{64,48},{80,64},{96,80},{112,96},{1... | collective-permute-start | bytes 1769480 | tf_op jit(solution)/shard_map/ppermute | solution.py:264
  116.9 16.7 %collective-permute-start.2 = (bf16[192,1536]{1,0:T(8,128)(2,1)}, bf16[192,1536]{1,0:T(8,128)(2,1)S(1)}, u32[]{:S(2)}, u32[]{:S(2)}) collective-permute-start(bf16[192,1536]{1,0:T(8,128)(2,1)} %collective-permute-done.1.refs_2_), channel_id=1, source_target_pairs={{0,16},{16,32},{32,48},{48,64},{64,80},{80,96},{96,112},{112,0},{1... | collective-permute-start | bytes 1769480 | tf_op jit(solution)/shard_map/ppermute | solution.py:264
  120.1 15.4 %collective-permute-start.8 = (bf16[128,1920]{1,0:T(8,128)(2,1)S(1)}, bf16[128,1920]{1,0:T(8,128)(2,1)S(1)}, u32[]{:S(2)}, u32[]{:S(2)}) collective-permute-start(bf16[128,1920]{1,0:T(8,128)(2,1)S(1)} %bitcast.14), channel_id=1, source_target_pairs={{0,128},{128,256},{256,384},{384,0},{1,129},{129,257},{257,385},{3... | collective-permute-start | bytes 1474568 | tf_op jit(solution)/shard_map/ppermute | solution.py:264
  122.2 25.2 %copy-start.4 = (bf16[192,1536]{1,0:T(8,128)(2,1)S(1)}, bf16[192,1536]{1,0:T(8,128)(2,1)}, u32[]{:S(2)}) copy-start(bf16[192,1536]{1,0:T(8,128)(2,1)} %copy-done.3) | copy-start | bytes 1769476
  122.2 15.4 %collective-permute-start.11 = (bf16[128,1920]{1,0:T(8,128)(2,1)S(1)}, bf16[128,1920]{1,0:T(8,128)(2,1)S(1)}, u32[]{:S(2)}, u32[]{:S(2)}) collective-permute-start(bf16[128,1920]{1,0:T(8,128)(2,1)S(1)} %bitcast.11), channel_id=1, source_target_pairs={{0,384},{128,0},{256,128},{384,256},{1,385},{129,1},{257,129},{385... | collective-permute-start | bytes 1474568 | tf_op jit(solution)/shard_map/ppermute | solution.py:264
  128.3 15.0 %collective-permute-start.7 = (bf16[96,1536]{1,0:T(8,128)(2,1)S(1)}, bf16[96,1536]{1,0:T(8,128)(2,1)S(1)}, u32[]{:S(2)}, u32[]{:S(2)}) collective-permute-start(bf16[96,1536]{1,0:T(8,128)(2,1)S(1)} %slice.25), channel_id=1, source_target_pairs={{0,112},{16,0},{32,16},{48,32},{64,48},{80,64},{96,80},{112,96},{1... | collective-permute-start | bytes 884744 | tf_op jit(solution)/shard_map/ppermute | solution.py:264
  133.6 13.8 %collective-permute-start.6 = (bf16[96,1536]{1,0:T(8,128)(2,1)S(1)}, bf16[96,1536]{1,0:T(8,128)(2,1)S(1)}, u32[]{:S(2)}, u32[]{:S(2)}) collective-permute-start(bf16[96,1536]{1,0:T(8,128)(2,1)S(1)} %slice.24), channel_id=1, source_target_pairs={{0,16},{16,32},{32,48},{48,64},{64,80},{80,96},{96,112},{112,0},{1... | collective-permute-start | bytes 884744 | tf_op jit(solution)/shard_map/ppermute | solution.py:264
  135.5 15.6 %collective-permute-start.13 = (bf16[128,1920]{1,0:T(8,128)(2,1)S(1)}, bf16[128,1920]{1,0:T(8,128)(2,1)S(1)}, u32[]{:S(2)}, u32[]{:S(2)}) collective-permute-start(bf16[128,1920]{1,0:T(8,128)(2,1)S(1)} %collective-permute-done.8.refs_0_), channel_id=1, source_target_pairs={{0,128},{128,256},{256,384},{384,0},{1,129},{129,257},{257,385},{3... | collective-permute-start | bytes 1474568 | tf_op jit(solution)/shard_map/ppermute | solution.py:264
  137.6 13.5 %collective-permute-start.14 = (bf16[128,1920]{1,0:T(8,128)(2,1)S(1)}, bf16[128,1920]{1,0:T(8,128)(2,1)S(1)}, u32[]{:S(2)}, u32[]{:S(2)}) collective-permute-start(bf16[128,1920]{1,0:T(8,128)(2,1)S(1)} %collective-permute-done.11.refs_3_), channel_id=1, source_target_pairs={{0,384},{128,0},{256,128},{384,256},{1,385},{129,1},{257,129},{385... | collective-permute-start | bytes 1474568 | tf_op jit(solution)/shard_map/ppermute | solution.py:264
  140.8 20.2 %collective-permute-start.10 = (bf16[128,1920]{1,0:T(8,128)(2,1)S(1)}, bf16[128,1920]{1,0:T(8,128)(2,1)S(1)}, u32[]{:S(2)}, u32[]{:S(2)}) collective-permute-start(bf16[128,1920]{1,0:T(8,128)(2,1)S(1)} %bitcast.15), channel_id=1, source_target_pairs={{0,384},{128,0},{256,128},{384,256},{1,385},{129,1},{257,129},{385... | collective-permute-start | bytes 1474568 | tf_op jit(solution)/shard_map/ppermute | solution.py:264
  143.3 17.7 %collective-permute-start.9 = (bf16[128,1920]{1,0:T(8,128)(2,1)S(1)}, bf16[128,1920]{1,0:T(8,128)(2,1)S(1)}, u32[]{:S(2)}, u32[]{:S(2)}) collective-permute-start(bf16[128,1920]{1,0:T(8,128)(2,1)S(1)} %bitcast.12), channel_id=1, source_target_pairs={{0,128},{128,256},{256,384},{384,0},{1,129},{129,257},{257,385},{3... | collective-permute-start | bytes 1474568 | tf_op jit(solution)/shard_map/ppermute | solution.py:264
  151.1 1.7 copy-start
  157.0 15.8 %collective-permute-start.15 = (bf16[128,1920]{1,0:T(8,128)(2,1)S(1)}, bf16[128,1920]{1,0:T(8,128)(2,1)S(1)}, u32[]{:S(2)}, u32[]{:S(2)}) collective-permute-start(bf16[128,1920]{1,0:T(8,128)(2,1)S(1)} %get-tuple-element.34), channel_id=1, source_target_pairs={{0,128},{128,256},{256,384},{384,0},{1,129},{129,257},{257,385},{3... | collective-permute-start | bytes 1474568 | tf_op jit(solution)/shard_map/ppermute | solution.py:264
  161.0 16.2 %copy-start.1 = (bf16[768,1536]{1,0:T(8,128)(2,1)S(1)}, bf16[768,1536]{1,0:T(8,128)(2,1)}, u32[]{:S(2)}) copy-start(bf16[768,1536]{1,0:T(8,128)(2,1)} %get-tuple-element.29.in_ref) | copy-start | bytes 7077892
  168.4 23.4 %collective-permute-start.12 = (bf16[128,1920]{1,0:T(8,128)(2,1)S(1)}, bf16[128,1920]{1,0:T(8,128)(2,1)S(1)}, u32[]{:S(2)}, u32[]{:S(2)}) collective-permute-start(bf16[128,1920]{1,0:T(8,128)(2,1)S(1)} %get-tuple-element.32), channel_id=1, source_target_pairs={{0,384},{128,0},{256,128},{384,256},{1,385},{129,1},{257,129},{385... | collective-permute-start | bytes 1474568 | tf_op jit(solution)/shard_map/ppermute | solution.py:264
  170.3 19.4 %collective-permute-start.18 = (bf16[128,1920]{1,0:T(8,128)(2,1)S(1)}, bf16[128,1920]{1,0:T(8,128)(2,1)S(1)}, u32[]{:S(2)}, u32[]{:S(2)}) collective-permute-start(bf16[128,1920]{1,0:T(8,128)(2,1)S(1)} %get-tuple-element.38), channel_id=1, source_target_pairs={{0,384},{128,0},{256,128},{384,256},{1,385},{129,1},{257,129},{385... | collective-permute-start | bytes 1474568 | tf_op jit(solution)/shard_map/ppermute | solution.py:264
  172.9 18.9 %collective-permute-start.16 = (bf16[128,1920]{1,0:T(8,128)(2,1)S(1)}, bf16[128,1920]{1,0:T(8,128)(2,1)S(1)}, u32[]{:S(2)}, u32[]{:S(2)}) collective-permute-start(bf16[128,1920]{1,0:T(8,128)(2,1)S(1)} %add_convert_fusion.3), channel_id=1, source_target_pairs={{0,128},{128,256},{256,384},{384,0},{1,129},{129,257},{257,385},{3... | collective-permute-start | bytes 1474568 | tf_op jit(solution)/shard_map/ppermute | solution.py:264
  181.4 14.8 %collective-permute-start.17 = (bf16[128,1920]{1,0:T(8,128)(2,1)S(1)}, bf16[128,1920]{1,0:T(8,128)(2,1)S(1)}, u32[]{:S(2)}, u32[]{:S(2)}) collective-permute-start(bf16[128,1920]{1,0:T(8,128)(2,1)S(1)} %get-tuple-element.36), channel_id=1, source_target_pairs={{0,128},{128,256},{256,384},{384,0},{1,129},{129,257},{257,385},{3... | collective-permute-start | bytes 1474568 | tf_op jit(solution)/shard_map/ppermute | solution.py:264
  189.9 10.8 %collective-permute-start.19 = (bf16[128,1920]{1,0:T(8,128)(2,1)S(1)}, bf16[128,1920]{1,0:T(8,128)(2,1)S(1)}, u32[]{:S(2)}, u32[]{:S(2)}) collective-permute-start(bf16[128,1920]{1,0:T(8,128)(2,1)S(1)} %add_convert_fusion.1), channel_id=1, source_target_pairs={{0,384},{128,0},{256,128},{384,256},{1,385},{129,1},{257,129},{385... | collective-permute-start | bytes 1474568 | tf_op jit(solution)/shard_map/ppermute | solution.py:264
  201.9 13.4 %copy-start.11 = (f32[1,128,2]{1,2,0:T(2,128)S(1)}, f32[1,128,2]{1,2,0:T(2,128)}, u32[]{:S(2)}) copy-start(f32[1,128,2]{1,2,0:T(2,128)} %param.13) | copy-start | bytes 3076
  201.9 40.0 %all-to-all-start.3 = ((bf16[16,16,1920]{2,1,0:T(8,128)(2,1)}), bf16[16,16,1920]{2,1,0:T(8,128)(2,1)S(1)}, u32[]{:S(2)}, u32[]{:S(2)}) async-start(bf16[16,16,1920]{2,1,0:T(8,128)(2,1)} %bitcast.7), calls=%async_computation.3 | async-start | bytes 1966080 | tf_op jit(solution)/shard_map/all_to_all | solution.py:342

commit v3 on v2

--- a/solution.py
+++ b/solution.py
@@ -22,9 +22,12 @@
     return lax.broadcasted_iota(jnp.int32, (rows, 2 * HD), 1) < HD
 
 
-def pack_kernel(x_ref, in_ref, out_ref, o_ref, w_ref):
+def join_kernel(in_ref, out_ref, w_ref):
     w_ref[: in_ref.shape[1], :] = in_ref[0]
     w_ref[in_ref.shape[1] :, :] = out_ref[0]
+
+
+def pack_kernel(x_ref, o_ref):
     n = o_ref.shape[0]
     t = x_ref.shape[2]
     half = t // 2
@@ -140,15 +143,17 @@
 
 
 def assemble_kernel(*refs):
-    blocks, (in_ref, out_ref) = refs[:-2], refs[-2:]
-    rows = in_ref.shape[0] // len(blocks)
+    far_in, far_out, *blocks, in_ref, out_ref = refs
+    rows = far_in.shape[0]
+    in_ref[len(blocks) * rows :, :] = far_in[...]
+    out_ref[len(blocks) * rows :, :] = far_out[...]
     for i, block in enumerate(blocks):
         in_ref[i * rows : (i + 1) * rows, :] = block[:rows, :]
         out_ref[i * rows : (i + 1) * rows, :] = block[rows:, :]
 
 
 def expert_kernel(pieces, in_ref, out_ref, *refs):
-    x_refs, y_refs, rows_ref = refs[:pieces], refs[pieces:-1], refs[-1]
+    x_refs, plus, y_refs, rows_ref = refs[:pieces], refs[pieces : -pieces - 1], refs[-pieces - 1 : -1], refs[-1]
     rows = x_refs[0].shape[0]
     width = in_ref.shape[1]
     quarter = width // 4
@@ -175,7 +180,7 @@
     picks = [(to == 4 * origin + q).astype(F32).astype(BF) for q in range(4)]
     for p, y_ref in enumerate(y_refs):
         base = p * every
-        y_ref[:, :width] = partial[base : base + rows]
+        main = partial[base : base + rows]
         total = jnp.zeros((rows, quarter), F32)
         for q in range(4):
             total += jnp.dot(
@@ -183,7 +188,12 @@
                 partial[base + rows : base + every, q * quarter : (q + 1) * quarter],
                 preferred_element_type=F32,
             )
-        y_ref[:, width:] = total.astype(BF)
+        total = total.astype(BF)
+        if plus:
+            main = add(main, plus[p][:, :width])
+            total = add(total, plus[p][:, width:])
+        y_ref[:, :width] = main
+        y_ref[:, width:] = total
 
 
 def combine_kernel(experts, cap, s_ref, choice_ref, gate_ref, *refs):
@@ -239,7 +249,7 @@
     )
 
 
-def run_experts(pieces, weight_in, weight_out):
+def run_experts(pieces, weight_in, weight_out, plus=()):
     rows, wide = pieces[0].shape
     hidden, width = weight_in.shape
     work = len(pieces) * rows * 5 // 4
@@ -252,7 +262,7 @@
             bytes_accessed=4 * hidden * width + 4 * len(pieces) * rows * wide,
             transcendentals=work * hidden,
         ),
-    )(weight_in, weight_out, *pieces)
+    )(weight_in, weight_out, *pieces, *plus)
 
 
 def add(*parts):
@@ -268,22 +278,26 @@
     return lax.optimization_barrier((x, *others))[0]
 
 
-def expert_layer(x, weights):
+def ring_in(x):
     half = x.shape[0] // 2
     a, b = x[:half], x[half:]
     left_a, right_b = shift(a, "dp", 1), shift(b, "dp", -1)
     left_b, right_a = shift(b, "dp", 1), shift(a, "dp", -1)
     across_a, across_b = shift(left_a, "dp", 1), shift(right_b, "dp", -1)
-    to_left_a, to_left_b, to_right_a, to_right_b = run_experts(
-        [left_a, left_b, right_a, right_b], *weights
-    )
+    return (a, b), (left_a, left_b, right_a, right_b), (across_a, across_b)
+
+
+def expert_layer(own, near, across, weights):
+    to_left_a, to_left_b, to_right_a, to_right_b = run_experts(near, *weights)
     got_a, got_b = shift(to_left_a, "dp", -1), shift(to_right_b, "dp", 1)
-    to_across_a, to_across_b = run_experts([across_a, across_b], *weights)
+    across = after(across, to_left_a)
+    to_across_a, to_across_b = run_experts(across, *weights)
     via_a, via_b = shift(to_across_a, "dp", 1), shift(to_across_b, "dp", -1)
-    own_a, own_b = run_experts([a, b], *weights)
+    own = after(own, to_across_a)
+    own_a, own_b = run_experts(own, *weights, plus=(got_a, got_b))
     sum_a = shift(add(to_right_a, via_a), "dp", 1)
     sum_b = shift(add(to_left_b, via_b), "dp", -1)
-    return jnp.concatenate([add(own_a, got_a, sum_a), add(own_b, got_b, sum_b)])
+    return jnp.concatenate([add(own_a, sum_a), add(own_b, sum_b)])
 
 
 def per_device(
@@ -301,13 +315,10 @@
     experts = lax.axis_size("expert")
     cap = 5 * t * 2 // (4 * experts)
     slice_rows = expert_in.shape[1]
-    packed, block = local(
-        pack_kernel,
-        [
-            jax.ShapeDtypeStruct((n, t * 9 // 2, 128), BF),
-            jax.ShapeDtypeStruct((2 * slice_rows, width), BF),
-        ],
-    )(projected, expert_in, expert_out)
+    packed = local(pack_kernel, jax.ShapeDtypeStruct((n, t * 9 // 2, 128), BF))(projected)
+    block = local(join_kernel, jax.ShapeDtypeStruct((2 * slice_rows, width), BF))(
+        expert_in, expert_out
+    )
     mixed = lax.all_to_all(packed, "ctx", 0, 0, tiled=True)
     block = after(block, mixed)
     up, down = [shift(block, "ctx", 1)], [shift(block, "ctx", -1)]
@@ -321,6 +332,7 @@
         out_specs=pl.BlockSpec((group, t * 3 // 2, 128), lambda i: (i, 0, 0)),
     )(mixed)
     back = lax.all_to_all(head_output, "ctx", 0, 0, tiled=True)
+    back, up[0], down[0] = lax.optimization_barrier((back, up[0], down[0]))
     part = cap // CHUNKS
     wide = (experts * part * 4 // 5, width * 5 // 4)
     stream, *sends = local(
@@ -328,17 +340,19 @@
         [jax.ShapeDtypeStruct((t, width), F32)] + [jax.ShapeDtypeStruct(wide, BF)] * CHUNKS,
     )(back, residual_in[0], modulation_scale, modulation_shift, expert_choice[0].T)
     up[0], down[0] = after(up[0], *sends), after(down[0], *sends)
+    arrived = [lax.all_to_all(x, "expert", 0, 0, tiled=True) for x in sends]
     for _ in range(n // 2 - 2):
         up.append(shift(up[-1], "ctx", 1))
         down.append(shift(down[-1], "ctx", -1))
+    rings = [ring_in(x) for x in arrived]
+    first = rings[0][0]
+    up[-1], down[-1] = after((up[-1], down[-1]), first)
     far_in = shift(up[-1][:slice_rows], "ctx", 1)
     far_out = shift(down[-1][slice_rows:], "ctx", -1)
-    far = jnp.concatenate([far_in, far_out])
     weights = local(
         assemble_kernel, [jax.ShapeDtypeStruct((n * slice_rows, width), BF)] * 2
-    )(block, *up, *down, far)
-    arrived = [lax.all_to_all(x, "expert", 0, 0, tiled=True) for x in sends]
-    sums = [expert_layer(x, weights) for x in arrived]
+    )(far_in, far_out, block, *up, *down)
+    sums = [expert_layer(*ring, weights) for ring in rings]
     returned = [lax.all_to_all(x, "expert", 0, 0, tiled=True) for x in sums]
     return local(
         functools.partial(combine_kernel, experts, cap),

time: 245 us -> 237 us (0.967)
  starting transfers between devices: 85 us -> 81.4 us
  local copies, waits for them, and re-layouts: 7.27 us -> 4.14 us
    all_to_all x1, waiting for transfers between devices: 11.9 us -> 0.01 us  [per_device(): back = lax.all_to_all(head_output, 'ctx', 0, 0, tiled=True)]
    ppermute x20, waiting for transfers between devices: 39.8 us -> 47.4 us  [shift(): return lax.ppermute(x, axis, [(i, (i + by) % n) for i in range(n)])]
    all_to_all x1, waiting for transfers between devices: 0.01 us -> 3.67 us  [per_device(): arrived = [lax.all_to_all(x, 'expert', 0, 0, tiled=True) for x in sends]]
    unnamed x26 -> x24, local copies, waits for them, and re-layouts: 5.92 us -> 2.73 us
  transfers between devices with their start and end apart: 23 -> 23, of which waited for: 9 -> 9; matrix products, arithmetic and copies ran while one was open for 1% -> 1% of each run, Pallas kernels for 8% -> 6%
where the time goes in v3:
time: 237 us; the launch traced here: 236 us
  starting transfers between devices  81.4 us (34%)
  waiting for transfers between devices  77.6 us (33%)
  blocking collectives  40.4 us (17%)
  Pallas kernels  31 us (13%)
  local copies, waits for them, and re-layouts  4.14 us (2%)
    ppermute x20, starting transfers between devices, shift(): return lax.ppermute(x, axis, [(i, (i + by) % n) for i in range(n)])  57.8 us
    ppermute x20, waiting for transfers between devices, shift(): return lax.ppermute(x, axis, [(i, (i + by) % n) for i in range(n)])  47.4 us
    all_to_all x1, blocking collectives, per_device(): mixed = lax.all_to_all(packed, 'ctx', 0, 0, tiled=True)  40.4 us
    all_to_all x1, waiting for transfers between devices, per_device(): returned = [lax.all_to_all(x, 'expert', 0, 0, tiled=True) for x in sums]  26.5 us
    pallas_call x3, Pallas kernels, run_experts(): local(functools.partial(expert_kernel, len(pieces)), [jax.ShapeDtypeStruc...  15.8 us
    all_to_all x1, starting transfers between devices, per_device(): returned = [lax.all_to_all(x, 'expert', 0, 0, tiled=True) for x in sums]  11.4 us
    all_to_all x1, starting transfers between devices, per_device(): arrived = [lax.all_to_all(x, 'expert', 0, 0, tiled=True) for x in sends]  8.62 us
    pallas_call x1, Pallas kernels, per_device(): local(attend_kernel, jax.ShapeDtypeStruct((n, t * 3 // 2, 128), BF), [plt...  7.62 us
  transfers between devices with their start and end apart: 23, of which 9 were waited for; matrix products, arithmetic and copies ran while one was open for 1% of the time, Pallas kernels for 6%

profile of v3, /device:TPU:7, one launch (start us, length us, event | category | flops | bytes accessed | tf_op | source)
XLA Modules:
  0.0 236.3 jit_solution(12131907135109772029)
XLA Ops:
  0.0 1.3 copy-done.1
  1.3 0.3 shard_map.82
  1.5 0.0 copy-start.5
  1.6 0.0 copy-start.6
  1.6 40.4 %all_to_all.30.m_ref = bf16[8,576,128]{2,1,0:T(8,128)(2,1)S(1)} all-to-all(bf16[8,576,128]{2,1,0:T(8,128)(2,1)S(1)} %shard_map.82), channel_id=1, replica_groups=mesh['dp'=4,'ctx'=8,'expert'=16] {'ctx'}, dimensions={0} | all-to-all | bytes 2359296 | tf_op jit(solution)/shard_map/all_to_all | solution.py:322
  41.9 7.6 %shard_map.83 = bf16[8,192,128]{2,1,0:T(8,128)(2,1)} custom-call(bf16[8,576,128]{2,1,0:T(8,128)(2,1)S(1)} %all_to_all.30.m_ref), custom_call_target="tpu_custom_call" | custom-call | tf_op jit(solution)/shard_map/pallas_call | solution.py:326
  49.6 3.5 %all-to-all-start.1 = ((bf16[8,192,128]{2,1,0:T(8,128)(2,1)}), bf16[8,192,128]{2,1,0:T(8,128)(2,1)S(1)}, u32[]{:S(2)}, u32[]{:S(2)}) async-start(bf16[8,192,128]{2,1,0:T(8,128)(2,1)} %shard_map.83), calls=%async_computation.1 | async-start | bytes 786432 | tf_op jit(solution)/shard_map/all_to_all | solution.py:334
  53.1 3.3 %collective-permute-start = (bf16[192,1536]{1,0:T(8,128)(2,1)S(1)}, bf16[192,1536]{1,0:T(8,128)(2,1)S(1)}, u32[]{:S(2)}, u32[]{:S(2)}) collective-permute-start(bf16[192,1536]{1,0:T(8,128)(2,1)S(1)} %shard_map.84.refs_2_), channel_id=1, source_target_pairs={{0,16},{16,32},{32,48},{48,64},{64,80},{80,96},{96,112},{112,0},{1... | collective-permute-start | bytes 1769480 | tf_op jit(solution)/shard_map/ppermute | solution.py:274
  56.3 3.2 %collective-permute-start.1 = (bf16[192,1536]{1,0:T(8,128)(2,1)S(1)}, bf16[192,1536]{1,0:T(8,128)(2,1)S(1)}, u32[]{:S(2)}, u32[]{:S(2)}) collective-permute-start(bf16[192,1536]{1,0:T(8,128)(2,1)S(1)} %shard_map.84.refs_2_), channel_id=1, source_target_pairs={{0,112},{16,0},{32,16},{48,32},{64,48},{80,64},{96,80},{112,96},{1... | collective-permute-start | bytes 1769480 | tf_op jit(solution)/shard_map/ppermute | solution.py:274
  59.6 0.1 copy.9
  59.7 0.1 copy.10.choice_ref
  59.8 17.3 %collective-permute-done.refs_3_ = bf16[192,1536]{1,0:T(8,128)(2,1)S(1)} collective-permute-done((bf16[192,1536]{1,0:T(8,128)(2,1)S(1)}, bf16[192,1536]{1,0:T(8,128)(2,1)S(1)}, u32[]{:S(2)}, u32[]{:S(2)}) %collective-permute-start) | collective-permute-done | bytes 589856 | tf_op jit(solution)/shard_map/ppermute | solution.py:274
  77.0 0.0 collective-permute-done.1.refs_6_
  77.0 0.0 all-to-all-done.1.b_ref
  77.1 0.0 copy-start.4
  77.1 1.2 copy-done.4
  78.3 1.8 shard_map.85
  80.1 8.6 %all-to-all-start.2 = ((bf16[16,16,1920]{2,1,0:T(8,128)(2,1)}), bf16[16,16,1920]{2,1,0:T(8,128)(2,1)}, u32[]{:S(2)}, u32[]{:S(2)}) async-start(bf16[16,16,1920]{2,1,0:T(8,128)(2,1)} %bitcast.4), calls=%async_computation.2 | async-start | bytes 1966080 | tf_op jit(solution)/shard_map/all_to_all | solution.py:343
  88.7 3.1 %collective-permute-start.4 = (bf16[192,1536]{1,0:T(8,128)(2,1)S(1)}, bf16[192,1536]{1,0:T(8,128)(2,1)}, u32[]{:S(2)}, u32[]{:S(2)}) collective-permute-start(bf16[192,1536]{1,0:T(8,128)(2,1)S(1)} %collective-permute-done.1.refs_6_), channel_id=1, source_target_pairs={{0,112},{16,0},{32,16},{48,32},{64,48},{80,64},{96,80},{112,96},{1... | collective-permute-start | bytes 1769480 | tf_op jit(solution)/shard_map/ppermute | solution.py:274
  91.8 2.2 collective-permute-start.2
  94.0 11.5 %collective-permute-done.4.refs_7_ = bf16[192,1536]{1,0:T(8,128)(2,1)} collective-permute-done((bf16[192,1536]{1,0:T(8,128)(2,1)S(1)}, bf16[192,1536]{1,0:T(8,128)(2,1)}, u32[]{:S(2)}, u32[]{:S(2)}) %collective-permute-start.4) | collective-permute-done | bytes 589856 | tf_op jit(solution)/shard_map/ppermute | solution.py:274
  105.5 4.3 %collective-permute-start.5 = (bf16[192,1536]{1,0:T(8,128)(2,1)}, bf16[192,1536]{1,0:T(8,128)(2,1)S(1)}, u32[]{:S(2)}, u32[]{:S(2)}) collective-permute-start(bf16[192,1536]{1,0:T(8,128)(2,1)} %collective-permute-done.4.refs_7_), channel_id=1, source_target_pairs={{0,112},{16,0},{32,16},{48,32},{64,48},{80,64},{96,80},{112,96},{1... | collective-permute-start | bytes 1769480 | tf_op jit(solution)/shard_map/ppermute | solution.py:274
  109.8 0.0 collective-permute-done.2.refs_4_
  109.8 1.9 collective-permute-start.3
  111.7 3.7 %all-to-all-done.2 = bf16[16,16,1920]{2,1,0:T(8,128)(2,1)} async-done(((bf16[16,16,1920]{2,1,0:T(8,128)(2,1)}), bf16[16,16,1920]{2,1,0:T(8,128)(2,1)}, u32[]{:S(2)}, u32[]{:S(2)}) %all-to-all-start.2) | async-done | bytes 983072 | tf_op jit(solution)/shard_map/all_to_all | solution.py:343
  115.4 1.3 fusion
  116.7 2.5 %collective-permute-start.10 = (bf16[128,1920]{1,0:T(8,128)(2,1)S(1)}, bf16[128,1920]{1,0:T(8,128)(2,1)S(1)}, u32[]{:S(2)}, u32[]{:S(2)}) collective-permute-start(bf16[128,1920]{1,0:T(8,128)(2,1)S(1)} %bitcast.11), channel_id=1, source_target_pairs={{0,384},{128,0},{256,128},{384,256},{1,385},{129,1},{257,129},{385... | collective-permute-start | bytes 1474568 | tf_op jit(solution)/shard_map/ppermute | solution.py:274
  119.2 4.0 %collective-permute-start.8 = (bf16[128,1920]{1,0:T(8,128)(2,1)S(1)}, bf16[128,1920]{1,0:T(8,128)(2,1)S(1)}, u32[]{:S(2)}, u32[]{:S(2)}) collective-permute-start(bf16[128,1920]{1,0:T(8,128)(2,1)S(1)} %bitcast.14), channel_id=1, source_target_pairs={{0,128},{128,256},{256,384},{384,0},{1,129},{129,257},{257,385},{3... | collective-permute-start | bytes 1474568 | tf_op jit(solution)/shard_map/ppermute | solution.py:274
  123.2 0.0 collective-permute-done.5.refs_8_
  123.2 3.5 %collective-permute-done.3.refs_5_ = bf16[192,1536]{1,0:T(8,128)(2,1)S(1)} collective-permute-done((bf16[192,1536]{1,0:T(8,128)(2,1)}, bf16[192,1536]{1,0:T(8,128)(2,1)S(1)}, u32[]{:S(2)}, u32[]{:S(2)}) %collective-permute-start.3) | collective-permute-done | bytes 589856 | tf_op jit(solution)/shard_map/ppermute | solution.py:274
  126.7 1.9 collective-permute-start.6
  128.6 2.1 collective-permute-start.12
  130.7 3.2 %collective-permute-start.13 = (bf16[128,1920]{1,0:T(8,128)(2,1)S(1)}, bf16[128,1920]{1,0:T(8,128)(2,1)S(1)}, u32[]{:S(2)}, u32[]{:S(2)}) collective-permute-start(bf16[128,1920]{1,0:T(8,128)(2,1)S(1)} %bitcast.15), channel_id=1, source_target_pairs={{0,384},{128,0},{256,128},{384,256},{1,385},{129,1},{257,129},{385... | collective-permute-start | bytes 1474568 | tf_op jit(solution)/shard_map/ppermute | solution.py:274
  134.0 2.2 collective-permute-done.6.refs_0_
  136.2 2.4 %collective-permute-start.7 = (bf16[96,1536]{1,0:T(8,128)(2,1)S(1)}, bf16[96,1536]{1,0:T(8,128)(2,1)S(1)}, u32[]{:S(2)}, u32[]{:S(2)}) collective-permute-start(bf16[96,1536]{1,0:T(8,128)(2,1)S(1)} %slice.23), channel_id=1, source_target_pairs={{0,112},{16,0},{32,16},{48,32},{64,48},{80,64},{96,80},{112,96},{1... | collective-permute-start | bytes 884744 | tf_op jit(solution)/shard_map/ppermute | solution.py:274
  138.6 2.5 %collective-permute-start.11 = (bf16[128,1920]{1,0:T(8,128)(2,1)S(1)}, bf16[128,1920]{1,0:T(8,128)(2,1)S(1)}, u32[]{:S(2)}, u32[]{:S(2)}) collective-permute-start(bf16[128,1920]{1,0:T(8,128)(2,1)S(1)} %collective-permute-done.10.refs_3_), channel_id=1, source_target_pairs={{0,384},{128,0},{256,128},{384,256},{1,385},{129,1},{257,129},{385... | collective-permute-start | bytes 1474568 | tf_op jit(solution)/shard_map/ppermute | solution.py:274
  141.0 0.0 collective-permute-done.8.refs_0_
  141.0 4.0 %collective-permute-start.9 = (bf16[128,1920]{1,0:T(8,128)(2,1)S(1)}, bf16[128,1920]{1,0:T(8,128)(2,1)S(1)}, u32[]{:S(2)}, u32[]{:S(2)}) collective-permute-start(bf16[128,1920]{1,0:T(8,128)(2,1)S(1)} %collective-permute-done.8.refs_0_), channel_id=1, source_target_pairs={{0,128},{128,256},{256,384},{384,0},{1,129},{129,257},{257,385},{3... | collective-permute-start | bytes 1474568 | tf_op jit(solution)/shard_map/ppermute | solution.py:274
  145.1 3.7 %shard_map.86 = (bf16[768,1536]{1,0:T(8,128)(2,1)}, bf16[768,1536]{1,0:T(8,128)(2,1)}) custom-call(bf16[96,1536]{1,0:T(8,128)(2,1)S(1)} %collective-permute-done.6.refs_0_, bf16[96,1536]{1,0:T(8,128)(2,1)S(1)} %collective-permute-done.7.refs_1_, bf16[192,1536]{1,0:T(8,128)(2,1)S(1)} %shard_map.84.refs_2_, ...), custom_call_target="tpu_custom_call" | custom-call | tf_op jit(solution)/shard_map/pallas_call | solution.py:352
  148.8 0.0 collective-permute-done.12.refs_1_
  148.8 7.4 %shard_map.87 = (bf16[128,1920]{1,0:T(8,128)(2,1)S(1)}, bf16[128,1920]{1,0:T(8,128)(2,1)S(1)}, bf16[128,1920]{1,0:T(8,128)(2,1)S(1)}, bf16[128,1920]{1,0:T(8,128)(2,1)S(1)}) custom-call(bf16[768,1536]{1,0:T(8,128)(2,1)} %get-tuple-element.39.in_ref, bf16[768,1536]{1,0:T(8,128)(2,1)} %get-tuple-element.40.out_ref, ...), custom_call_target="tpu_custom_call" | custom-call | flops 3019898880 | bytes 8650752 | tf_op jit(solution)/shard_map/pallas_call | solution.py:256
  156.2 0.0 collective-permute-done.9.refs_0_
  156.2 4.2 %shard_map.88 = (bf16[128,1920]{1,0:T(8,128)(2,1)S(1)}, bf16[128,1920]{1,0:T(8,128)(2,1)S(1)}) custom-call(bf16[768,1536]{1,0:T(8,128)(2,1)S(1)} %copy-done, bf16[768,1536]{1,0:T(8,128)(2,1)} %get-tuple-element.40.out_ref, bf16[128,1920]{1,0:T(8,128)(2,1)S(1)} %collective-permute-done.9.refs_0_, bf16[128,1920]{1,0:T(8,128)(2,1)S(1)} %collective-permute-done.11.refs_1_), custom_call_target="tpu_custom_call" | custom-call | flops 1509949440 | bytes 6684672 | tf_op jit(solution)/shard_map/pallas_call | solution.py:256
  160.4 2.1 collective-permute-start.16
  162.5 3.2 %collective-permute-start.18 = (bf16[128,1920]{1,0:T(8,128)(2,1)S(1)}, bf16[128,1920]{1,0:T(8,128)(2,1)S(1)}, u32[]{:S(2)}, u32[]{:S(2)}) collective-permute-start(bf16[128,1920]{1,0:T(8,128)(2,1)S(1)} %get-tuple-element.52), channel_id=1, source_target_pairs={{0,384},{128,0},{256,128},{384,256},{1,385},{129,1},{257,129},{385... | collective-permute-start | bytes 1474568 | tf_op jit(solution)/shard_map/ppermute | solution.py:274
  165.7 1.9 collective-permute-start.14
  167.6 4.6 %collective-permute-start.15 = (bf16[128,1920]{1,0:T(8,128)(2,1)S(1)}, bf16[128,1920]{1,0:T(8,128)(2,1)S(1)}, u32[]{:S(2)}, u32[]{:S(2)}) collective-permute-start(bf16[128,1920]{1,0:T(8,128)(2,1)S(1)} %get-tuple-element.47), channel_id=1, source_target_pairs={{0,128},{128,256},{256,384},{384,0},{1,129},{129,257},{257,385},{3... | collective-permute-start | bytes 1474568 | tf_op jit(solution)/shard_map/ppermute | solution.py:274
  172.2 0.1 add_convert_fusion.3
  172.4 2.2 collective-permute-start.17
  174.6 0.0 collective-permute-done.18
  174.6 0.1 add_convert_fusion.1
  174.8 3.2 %collective-permute-start.19 = (bf16[128,1920]{1,0:T(8,128)(2,1)S(1)}, bf16[128,1920]{1,0:T(8,128)(2,1)S(1)}, u32[]{:S(2)}, u32[]{:S(2)}) collective-permute-start(bf16[128,1920]{1,0:T(8,128)(2,1)S(1)} %add_convert_fusion.1), channel_id=1, source_target_pairs={{0,384},{128,0},{256,128},{384,256},{1,385},{129,1},{257,129},{385... | collective-permute-start | bytes 1474568 | tf_op jit(solution)/shard_map/ppermute | solution.py:274
  178.0 6.8 %collective-permute-done.14.refs_2_ = bf16[128,1920]{1,0:T(8,128)(2,1)S(1)} collective-permute-done((bf16[128,1920]{1,0:T(8,128)(2,1)S(1)}, bf16[128,1920]{1,0:T(8,128)(2,1)S(1)}, u32[]{:S(2)}, u32[]{:S(2)}) %collective-permute-start.14) | collective-permute-done | bytes 491552 | tf_op jit(solution)/shard_map/ppermute | solution.py:274
  184.8 4.2 %shard_map.89 = (bf16[128,1920]{1,0:T(8,128)(2,1)S(1)}, bf16[128,1920]{1,0:T(8,128)(2,1)S(1)}) custom-call(bf16[768,1536]{1,0:T(8,128)(2,1)S(1)} %copy-done, bf16[768,1536]{1,0:T(8,128)(2,1)} %get-tuple-element.40.out_ref, bf16[128,1920]{1,0:T(8,128)(2,1)S(1)} %bitcast.16, bf16[128,1920]{1,0:T(8,128)(2,1)S(1)} %bitcast.13, ...), custom_call_target="tpu_custom_call" | custom-call | flops 1509949440 | bytes 6684672 | tf_op jit(solution)/shard_map/pallas_call | solution.py:256
  189.0 4.4 %collective-permute-done.17 = bf16[128,1920]{1,0:T(8,128)(2,1)S(1)} collective-permute-done((bf16[128,1920]{1,0:T(8,128)(2,1)S(1)}, bf16[128,1920]{1,0:T(8,128)(2,1)S(1)}, u32[]{:S(2)}, u32[]{:S(2)}) %collective-permute-start.17) | collective-permute-done | bytes 491552 | tf_op jit(solution)/shard_map/ppermute | solution.py:274
  193.4 0.1 add_convert_fusion.2
  193.5 1.8 collective-permute-done.19
  195.3 0.1 add_convert_fusion
  195.4 0.0 copy-start.10
  195.4 1.0 pad_maximum_fusion
  196.4 11.4 %all-to-all-start.3 = ((bf16[16,16,1920]{2,1,0:T(8,128)(2,1)}), bf16[16,16,1920]{2,1,0:T(8,128)(2,1)S(1)}, u32[]{:S(2)}, u32[]{:S(2)}) async-start(bf16[16,16,1920]{2,1,0:T(8,128)(2,1)} %bitcast.7), calls=%async_computation.3 | async-start | bytes 1966080 | tf_op jit(solution)/shard_map/all_to_all | solution.py:356
  207.9 0.1 copy.11
  208.0 26.5 %all-to-all-done.3 = bf16[16,16,1920]{2,1,0:T(8,128)(2,1)S(1)} async-done(((bf16[16,16,1920]{2,1,0:T(8,128)(2,1)}), bf16[16,16,1920]{2,1,0:T(8,128)(2,1)S(1)}, u32[]{:S(2)}, u32[]{:S(2)}) %all-to-all-start.3) | async-done | bytes 983072 | tf_op jit(solution)/shard_map/all_to_all | solution.py:356
  234.5 1.8 shard_map.90
  (25 shorter events, 0.1 us)
Async XLA Ops:
  0.0 1.3 copy-start.1
  1.5 51.5 %copy-start.5 = (bf16[1,96,1536]{2,1,0:T(8,128)(2,1)S(1)}, bf16[1,96,1536]{2,1,0:T(8,128)(2,1)}, u32[]{:S(2)}) copy-start(bf16[1,96,1536]{2,1,0:T(8,128)(2,1)} %in_ref.1) | copy-start | bytes 884740
  1.6 51.5 %copy-start.6 = (bf16[1,96,1536]{2,1,0:T(8,128)(2,1)S(1)}, bf16[1,96,1536]{2,1,0:T(8,128)(2,1)}, u32[]{:S(2)}) copy-start(bf16[1,96,1536]{2,1,0:T(8,128)(2,1)} %out_ref.1) | copy-start | bytes 884740
  41.9 17.7 %copy-start.9 = (s32[1,128,2]{1,2,0:T(2,128)S(1)}, s32[1,128,2]{1,2,0:T(2,128)}, u32[]{:S(2)}) copy-start(s32[1,128,2]{1,2,0:T(2,128)} %param.12) | copy-start | bytes 3076
  41.9 35.1 %copy-start.7 = (f32[1,1536]{1,0:T(1,128)S(1)}, f32[1,1536]{1,0:T(1,128)}, u32[]{:S(2)}) copy-start(f32[1,1536]{1,0:T(1,128)} %scale_ref.1) | copy-start | bytes 18436
  41.9 35.1 %copy-start.8 = (f32[1,1536]{1,0:T(1,128)S(1)}, f32[1,1536]{1,0:T(1,128)}, u32[]{:S(2)}) copy-start(f32[1,1536]{1,0:T(1,128)} %shift_ref.1) | copy-start | bytes 18436
  49.6 27.5 %all-to-all-start.1 = ((bf16[8,192,128]{2,1,0:T(8,128)(2,1)}), bf16[8,192,128]{2,1,0:T(8,128)(2,1)S(1)}, u32[]{:S(2)}, u32[]{:S(2)}) async-start(bf16[8,192,128]{2,1,0:T(8,128)(2,1)} %shard_map.83), calls=%async_computation.1 | async-start | bytes 786432 | tf_op jit(solution)/shard_map/all_to_all | solution.py:334
  53.1 23.9 %collective-permute-start = (bf16[192,1536]{1,0:T(8,128)(2,1)S(1)}, bf16[192,1536]{1,0:T(8,128)(2,1)S(1)}, u32[]{:S(2)}, u32[]{:S(2)}) collective-permute-start(bf16[192,1536]{1,0:T(8,128)(2,1)S(1)} %shard_map.84.refs_2_), channel_id=1, source_target_pairs={{0,16},{16,32},{32,48},{48,64},{64,80},{80,96},{96,112},{112,0},{1... | collective-permute-start | bytes 1769480 | tf_op jit(solution)/shard_map/ppermute | solution.py:274
  56.3 20.7 %collective-permute-start.1 = (bf16[192,1536]{1,0:T(8,128)(2,1)S(1)}, bf16[192,1536]{1,0:T(8,128)(2,1)S(1)}, u32[]{:S(2)}, u32[]{:S(2)}) collective-permute-start(bf16[192,1536]{1,0:T(8,128)(2,1)S(1)} %shard_map.84.refs_2_), channel_id=1, source_target_pairs={{0,112},{16,0},{32,16},{48,32},{64,48},{80,64},{96,80},{112,96},{1... | collective-permute-start | bytes 1769480 | tf_op jit(solution)/shard_map/ppermute | solution.py:274
  77.0 16.9 %copy-start.2 = (bf16[192,1536]{1,0:T(8,128)(2,1)}, bf16[192,1536]{1,0:T(8,128)(2,1)S(1)}, u32[]{:S(2)}) copy-start(bf16[192,1536]{1,0:T(8,128)(2,1)S(1)} %collective-permute-done.1.refs_6_) | copy-start | bytes 1769476
  77.1 1.2 copy-start.4
  80.1 35.3 %all-to-all-start.2 = ((bf16[16,16,1920]{2,1,0:T(8,128)(2,1)}), bf16[16,16,1920]{2,1,0:T(8,128)(2,1)}, u32[]{:S(2)}, u32[]{:S(2)}) async-start(bf16[16,16,1920]{2,1,0:T(8,128)(2,1)} %bitcast.4), calls=%async_computation.2 | async-start | bytes 1966080 | tf_op jit(solution)/shard_map/all_to_all | solution.py:343
  88.7 16.8 %collective-permute-start.4 = (bf16[192,1536]{1,0:T(8,128)(2,1)S(1)}, bf16[192,1536]{1,0:T(8,128)(2,1)}, u32[]{:S(2)}, u32[]{:S(2)}) collective-permute-start(bf16[192,1536]{1,0:T(8,128)(2,1)S(1)} %collective-permute-done.1.refs_6_), channel_id=1, source_target_pairs={{0,112},{16,0},{32,16},{48,32},{64,48},{80,64},{96,80},{112,96},{1... | collective-permute-start | bytes 1769480 | tf_op jit(solution)/shard_map/ppermute | solution.py:274
  91.8 18.0 %collective-permute-start.2 = (bf16[192,1536]{1,0:T(8,128)(2,1)S(1)}, bf16[192,1536]{1,0:T(8,128)(2,1)}, u32[]{:S(2)}, u32[]{:S(2)}) collective-permute-start(bf16[192,1536]{1,0:T(8,128)(2,1)S(1)} %collective-permute-done.refs_3_), channel_id=1, source_target_pairs={{0,16},{16,32},{32,48},{48,64},{64,80},{80,96},{96,112},{112,0},{1... | collective-permute-start | bytes 1769480 | tf_op jit(solution)/shard_map/ppermute | solution.py:274
  105.5 17.8 %collective-permute-start.5 = (bf16[192,1536]{1,0:T(8,128)(2,1)}, bf16[192,1536]{1,0:T(8,128)(2,1)S(1)}, u32[]{:S(2)}, u32[]{:S(2)}) collective-permute-start(bf16[192,1536]{1,0:T(8,128)(2,1)} %collective-permute-done.4.refs_7_), channel_id=1, source_target_pairs={{0,112},{16,0},{32,16},{48,32},{64,48},{80,64},{96,80},{112,96},{1... | collective-permute-start | bytes 1769480 | tf_op jit(solution)/shard_map/ppermute | solution.py:274
  109.8 16.9 %collective-permute-start.3 = (bf16[192,1536]{1,0:T(8,128)(2,1)}, bf16[192,1536]{1,0:T(8,128)(2,1)S(1)}, u32[]{:S(2)}, u32[]{:S(2)}) collective-permute-start(bf16[192,1536]{1,0:T(8,128)(2,1)} %collective-permute-done.2.refs_4_), channel_id=1, source_target_pairs={{0,16},{16,32},{32,48},{48,64},{64,80},{80,96},{96,112},{112,0},{1... | collective-permute-start | bytes 1769480 | tf_op jit(solution)/shard_map/ppermute | solution.py:274
  115.4 29.7 %copy-start.3 = (bf16[192,1536]{1,0:T(8,128)(2,1)S(1)}, bf16[192,1536]{1,0:T(8,128)(2,1)}, u32[]{:S(2)}) copy-start(bf16[192,1536]{1,0:T(8,128)(2,1)} %copy-done.2) | copy-start | bytes 1769476
  116.7 21.9 %collective-permute-start.10 = (bf16[128,1920]{1,0:T(8,128)(2,1)S(1)}, bf16[128,1920]{1,0:T(8,128)(2,1)S(1)}, u32[]{:S(2)}, u32[]{:S(2)}) collective-permute-start(bf16[128,1920]{1,0:T(8,128)(2,1)S(1)} %bitcast.11), channel_id=1, source_target_pairs={{0,384},{128,0},{256,128},{384,256},{1,385},{129,1},{257,129},{385... | collective-permute-start | bytes 1474568 | tf_op jit(solution)/shard_map/ppermute | solution.py:274
  119.2 21.9 %collective-permute-start.8 = (bf16[128,1920]{1,0:T(8,128)(2,1)S(1)}, bf16[128,1920]{1,0:T(8,128)(2,1)S(1)}, u32[]{:S(2)}, u32[]{:S(2)}) collective-permute-start(bf16[128,1920]{1,0:T(8,128)(2,1)S(1)} %bitcast.14), channel_id=1, source_target_pairs={{0,128},{128,256},{256,384},{384,0},{1,129},{129,257},{257,385},{3... | collective-permute-start | bytes 1474568 | tf_op jit(solution)/shard_map/ppermute | solution.py:274
  126.7 9.4 %collective-permute-start.6 = (bf16[96,1536]{1,0:T(8,128)(2,1)S(1)}, bf16[96,1536]{1,0:T(8,128)(2,1)S(1)}, u32[]{:S(2)}, u32[]{:S(2)}) collective-permute-start(bf16[96,1536]{1,0:T(8,128)(2,1)S(1)} %slice.22), channel_id=1, source_target_pairs={{0,16},{16,32},{32,48},{48,64},{64,80},{80,96},{96,112},{112,0},{1... | collective-permute-start | bytes 884744 | tf_op jit(solution)/shard_map/ppermute | solution.py:274
  128.6 20.2 %collective-permute-start.12 = (bf16[128,1920]{1,0:T(8,128)(2,1)S(1)}, bf16[128,1920]{1,0:T(8,128)(2,1)S(1)}, u32[]{:S(2)}, u32[]{:S(2)}) collective-permute-start(bf16[128,1920]{1,0:T(8,128)(2,1)S(1)} %bitcast.12), channel_id=1, source_target_pairs={{0,128},{128,256},{256,384},{384,0},{1,129},{129,257},{257,385},{3... | collective-permute-start | bytes 1474568 | tf_op jit(solution)/shard_map/ppermute | solution.py:274
  130.7 18.1 %collective-permute-start.13 = (bf16[128,1920]{1,0:T(8,128)(2,1)S(1)}, bf16[128,1920]{1,0:T(8,128)(2,1)S(1)}, u32[]{:S(2)}, u32[]{:S(2)}) collective-permute-start(bf16[128,1920]{1,0:T(8,128)(2,1)S(1)} %bitcast.15), channel_id=1, source_target_pairs={{0,384},{128,0},{256,128},{384,256},{1,385},{129,1},{257,129},{385... | collective-permute-start | bytes 1474568 | tf_op jit(solution)/shard_map/ppermute | solution.py:274
  136.2 8.9 %collective-permute-start.7 = (bf16[96,1536]{1,0:T(8,128)(2,1)S(1)}, bf16[96,1536]{1,0:T(8,128)(2,1)S(1)}, u32[]{:S(2)}, u32[]{:S(2)}) collective-permute-start(bf16[96,1536]{1,0:T(8,128)(2,1)S(1)} %slice.23), channel_id=1, source_target_pairs={{0,112},{16,0},{32,16},{48,32},{64,48},{80,64},{96,80},{112,96},{1... | collective-permute-start | bytes 884744 | tf_op jit(solution)/shard_map/ppermute | solution.py:274
  138.6 17.6 %collective-permute-start.11 = (bf16[128,1920]{1,0:T(8,128)(2,1)S(1)}, bf16[128,1920]{1,0:T(8,128)(2,1)S(1)}, u32[]{:S(2)}, u32[]{:S(2)}) collective-permute-start(bf16[128,1920]{1,0:T(8,128)(2,1)S(1)} %collective-permute-done.10.refs_3_), channel_id=1, source_target_pairs={{0,384},{128,0},{256,128},{384,256},{1,385},{129,1},{257,129},{385... | collective-permute-start | bytes 1474568 | tf_op jit(solution)/shard_map/ppermute | solution.py:274
  141.0 15.1 %collective-permute-start.9 = (bf16[128,1920]{1,0:T(8,128)(2,1)S(1)}, bf16[128,1920]{1,0:T(8,128)(2,1)S(1)}, u32[]{:S(2)}, u32[]{:S(2)}) collective-permute-start(bf16[128,1920]{1,0:T(8,128)(2,1)S(1)} %collective-permute-done.8.refs_0_), channel_id=1, source_target_pairs={{0,128},{128,256},{256,384},{384,0},{1,129},{129,257},{257,385},{3... | collective-permute-start | bytes 1474568 | tf_op jit(solution)/shard_map/ppermute | solution.py:274
  148.8 7.4 %copy-start = (bf16[768,1536]{1,0:T(8,128)(2,1)S(1)}, bf16[768,1536]{1,0:T(8,128)(2,1)}, u32[]{:S(2)}) copy-start(bf16[768,1536]{1,0:T(8,128)(2,1)} %get-tuple-element.39.in_ref) | copy-start | bytes 7077892
  160.4 11.8 %collective-permute-start.16 = (bf16[128,1920]{1,0:T(8,128)(2,1)S(1)}, bf16[128,1920]{1,0:T(8,128)(2,1)S(1)}, u32[]{:S(2)}, u32[]{:S(2)}) collective-permute-start(bf16[128,1920]{1,0:T(8,128)(2,1)S(1)} %get-tuple-element.44), channel_id=1, source_target_pairs={{0,128},{128,256},{256,384},{384,0},{1,129},{129,257},{257,385},{3... | collective-permute-start | bytes 1474568 | tf_op jit(solution)/shard_map/ppermute | solution.py:274
  162.5 12.1 %collective-permute-start.18 = (bf16[128,1920]{1,0:T(8,128)(2,1)S(1)}, bf16[128,1920]{1,0:T(8,128)(2,1)S(1)}, u32[]{:S(2)}, u32[]{:S(2)}) collective-permute-start(bf16[128,1920]{1,0:T(8,128)(2,1)S(1)} %get-tuple-element.52), channel_id=1, source_target_pairs={{0,384},{128,0},{256,128},{384,256},{1,385},{129,1},{257,129},{385... | collective-permute-start | bytes 1474568 | tf_op jit(solution)/shard_map/ppermute | solution.py:274
  165.7 19.0 %collective-permute-start.14 = (bf16[128,1920]{1,0:T(8,128)(2,1)S(1)}, bf16[128,1920]{1,0:T(8,128)(2,1)S(1)}, u32[]{:S(2)}, u32[]{:S(2)}) collective-permute-start(bf16[128,1920]{1,0:T(8,128)(2,1)S(1)} %get-tuple-element.41), channel_id=1, source_target_pairs={{0,384},{128,0},{256,128},{384,256},{1,385},{129,1},{257,129},{385... | collective-permute-start | bytes 1474568 | tf_op jit(solution)/shard_map/ppermute | solution.py:274
  167.6 17.1 %collective-permute-start.15 = (bf16[128,1920]{1,0:T(8,128)(2,1)S(1)}, bf16[128,1920]{1,0:T(8,128)(2,1)S(1)}, u32[]{:S(2)}, u32[]{:S(2)}) collective-permute-start(bf16[128,1920]{1,0:T(8,128)(2,1)S(1)} %get-tuple-element.47), channel_id=1, source_target_pairs={{0,128},{128,256},{256,384},{384,0},{1,129},{129,257},{257,385},{3... | collective-permute-start | bytes 1474568 | tf_op jit(solution)/shard_map/ppermute | solution.py:274
  172.4 21.0 %collective-permute-start.17 = (bf16[128,1920]{1,0:T(8,128)(2,1)S(1)}, bf16[128,1920]{1,0:T(8,128)(2,1)S(1)}, u32[]{:S(2)}, u32[]{:S(2)}) collective-permute-start(bf16[128,1920]{1,0:T(8,128)(2,1)S(1)} %add_convert_fusion.3), channel_id=1, source_target_pairs={{0,128},{128,256},{256,384},{384,0},{1,129},{129,257},{257,385},{3... | collective-permute-start | bytes 1474568 | tf_op jit(solution)/shard_map/ppermute | solution.py:274
  174.8 20.5 %collective-permute-start.19 = (bf16[128,1920]{1,0:T(8,128)(2,1)S(1)}, bf16[128,1920]{1,0:T(8,128)(2,1)S(1)}, u32[]{:S(2)}, u32[]{:S(2)}) collective-permute-start(bf16[128,1920]{1,0:T(8,128)(2,1)S(1)} %add_convert_fusion.1), channel_id=1, source_target_pairs={{0,384},{128,0},{256,128},{384,256},{1,385},{129,1},{257,129},{385... | collective-permute-start | bytes 1474568 | tf_op jit(solution)/shard_map/ppermute | solution.py:274
  195.4 12.5 %copy-start.10 = (f32[1,128,2]{1,2,0:T(2,128)S(1)}, f32[1,128,2]{1,2,0:T(2,128)}, u32[]{:S(2)}) copy-start(f32[1,128,2]{1,2,0:T(2,128)} %param.13) | copy-start | bytes 3076
  196.4 38.1 %all-to-all-start.3 = ((bf16[16,16,1920]{2,1,0:T(8,128)(2,1)}), bf16[16,16,1920]{2,1,0:T(8,128)(2,1)S(1)}, u32[]{:S(2)}, u32[]{:S(2)}) async-start(bf16[16,16,1920]{2,1,0:T(8,128)(2,1)} %bitcast.7), calls=%async_computation.3 | async-start | bytes 1966080 | tf_op jit(solution)/shard_map/all_to_all | solution.py:356

commit v4 on v3

--- a/solution.py
+++ b/solution.py
@@ -8,10 +8,10 @@
 from jax.sharding import PartitionSpec as P
 
 HD = 64
-CHUNKS = 1
+CHUNKS = 2
 BF = jnp.bfloat16
 F32 = jnp.float32
-LIMIT = 48 * 1024 * 1024
+LIMIT = 24 * 1024 * 1024
 
 
 def swap(x):
@@ -62,8 +62,9 @@
     rows = group * t
     low = low_lanes(rows)
     mine = pl.ds(step * group, group)
-    q01 = m_ref[mine, 0:t, :].reshape(rows, 128)
-    q2 = swap(m_ref[mine, 3 * t : 4 * t, :].reshape(rows, 128))
+    scaling = jnp.asarray(HD ** (-0.5), BF)
+    q01 = m_ref[mine, 0:t, :].reshape(rows, 128) * scaling
+    q2 = swap(m_ref[mine, 3 * t : 4 * t, :].reshape(rows, 128)) * scaling
     k01 = m_ref[:, t : 2 * t, :].reshape(n * t, 128)
     k2 = m_ref[:, 3 * t : 4 * t, :].reshape(n * t, 128)
     v01 = m_ref[:, 2 * t : 3 * t, :].reshape(n * t, 128)
@@ -72,7 +73,6 @@
 
     def head(q, k, v):
         scores = lax.dot_general(q, k, (((1,), (1,)), ((), ())), preferred_element_type=F32)
-        scores = scores * HD ** (-0.5)
         probs = jnp.exp(scores - jnp.max(scores, axis=-1, keepdims=True))
         totals = jnp.sum(probs, axis=-1, keepdims=True)
         return jnp.dot(probs.astype(BF), v, preferred_element_type=F32) / totals
@@ -159,36 +159,31 @@
     quarter = width // 4
     extras = rows // 4
     every = rows + extras
-    row_at = lax.broadcasted_iota(jnp.int32, (extras, rows), 0)
-    source = lax.broadcasted_iota(jnp.int32, (extras, rows), 1)
-    picks = [(source == 4 * row_at + q).astype(F32).astype(BF) for q in range(4)]
+    row_at = lax.broadcasted_iota(jnp.int32, (rows, rows), 0)
+    source = lax.broadcasted_iota(jnp.int32, (rows, rows), 1)
+    pick = (source == 4 * (row_at % extras) + row_at // extras).astype(F32).astype(BF)
     for p, x_ref in enumerate(x_refs):
         base = p * every
         rows_ref[base : base + rows, :] = x_ref[:, :width]
-        packed = x_ref[:, width:]
+        quarters = jnp.dot(pick, x_ref[:, width:], preferred_element_type=F32).astype(BF)
         for q in range(4):
-            rows_ref[base + rows : base + every, q * quarter : (q + 1) * quarter] = jnp.dot(
-                picks[q], packed, preferred_element_type=F32
-            ).astype(BF)
+            rows_ref[base + rows : base + every, q * quarter : (q + 1) * quarter] = quarters[
+                q * extras : (q + 1) * extras
+            ]
     pre_act = lax.dot_general(
         rows_ref[...], in_ref[...], (((1,), (1,)), ((), ())), preferred_element_type=F32
     )
     hidden = jax.nn.gelu(pre_act, approximate=True).astype(BF)
     partial = jnp.dot(hidden, out_ref[...], preferred_element_type=F32).astype(BF)
-    to = lax.broadcasted_iota(jnp.int32, (rows, extras), 0)
-    origin = lax.broadcasted_iota(jnp.int32, (rows, extras), 1)
-    picks = [(to == 4 * origin + q).astype(F32).astype(BF) for q in range(4)]
+    pack = (row_at == 4 * (source % extras) + source // extras).astype(F32).astype(BF)
     for p, y_ref in enumerate(y_refs):
         base = p * every
         main = partial[base : base + rows]
-        total = jnp.zeros((rows, quarter), F32)
-        for q in range(4):
-            total += jnp.dot(
-                picks[q],
-                partial[base + rows : base + every, q * quarter : (q + 1) * quarter],
-                preferred_element_type=F32,
-            )
-        total = total.astype(BF)
+        last = partial[base + rows : base + every]
+        quarters = jnp.concatenate(
+            [last[:, q * quarter : (q + 1) * quarter] for q in range(4)], axis=0
+        )
+        total = jnp.dot(pack, quarters, preferred_element_type=F32).astype(BF)
         if plus:
             main = add(main, plus[p][:, :width])
             total = add(total, plus[p][:, width:])
@@ -278,12 +273,12 @@
     return lax.optimization_barrier((x, *others))[0]
 
 
-def ring_in(x):
-    half = x.shape[0] // 2
-    a, b = x[:half], x[half:]
-    left_a, right_b = shift(a, "dp", 1), shift(b, "dp", -1)
-    left_b, right_a = shift(b, "dp", 1), shift(a, "dp", -1)
-    across_a, across_b = shift(left_a, "dp", 1), shift(right_b, "dp", -1)
+def ring_in(a, b):
+    left_a, right_a = shift(a, "dp", 1), shift(a, "dp", -1)
+    across_a = shift(left_a, "dp", 1)
+    b = after(b, left_a, right_a)
+    left_b, right_b = shift(b, "dp", 1), shift(b, "dp", -1)
+    across_b = shift(right_b, "dp", -1)
     return (a, b), (left_a, left_b, right_a, right_b), (across_a, across_b)
 
 
@@ -293,11 +288,11 @@
     across = after(across, to_left_a)
     to_across_a, to_across_b = run_experts(across, *weights)
     via_a, via_b = shift(to_across_a, "dp", 1), shift(to_across_b, "dp", -1)
-    own = after(own, to_across_a)
+    via_a, via_b = add(to_right_a, via_a), add(to_left_b, via_b)
+    sum_a, sum_b = shift(via_a, "dp", 1), shift(via_b, "dp", -1)
+    own = after(own, via_a, via_b)
     own_a, own_b = run_experts(own, *weights, plus=(got_a, got_b))
-    sum_a = shift(add(to_right_a, via_a), "dp", 1)
-    sum_b = shift(add(to_left_b, via_b), "dp", -1)
-    return jnp.concatenate([add(own_a, sum_a), add(own_b, sum_b)])
+    return add(own_a, sum_a), add(own_b, sum_b)
 
 
 def per_device(
@@ -320,8 +315,6 @@
         expert_in, expert_out
     )
     mixed = lax.all_to_all(packed, "ctx", 0, 0, tiled=True)
-    block = after(block, mixed)
-    up, down = [shift(block, "ctx", 1)], [shift(block, "ctx", -1)]
     group = 2
     head_output = local(
         attend_kernel,
@@ -332,27 +325,25 @@
         out_specs=pl.BlockSpec((group, t * 3 // 2, 128), lambda i: (i, 0, 0)),
     )(mixed)
     back = lax.all_to_all(head_output, "ctx", 0, 0, tiled=True)
-    back, up[0], down[0] = lax.optimization_barrier((back, up[0], down[0]))
     part = cap // CHUNKS
     wide = (experts * part * 4 // 5, width * 5 // 4)
     stream, *sends = local(
         functools.partial(dispatch_kernel, experts, cap),
         [jax.ShapeDtypeStruct((t, width), F32)] + [jax.ShapeDtypeStruct(wide, BF)] * CHUNKS,
     )(back, residual_in[0], modulation_scale, modulation_shift, expert_choice[0].T)
-    up[0], down[0] = after(up[0], *sends), after(down[0], *sends)
+    block = after(block, *sends)
+    up, down = [shift(block, "ctx", 1)], [shift(block, "ctx", -1)]
     arrived = [lax.all_to_all(x, "expert", 0, 0, tiled=True) for x in sends]
     for _ in range(n // 2 - 2):
         up.append(shift(up[-1], "ctx", 1))
         down.append(shift(down[-1], "ctx", -1))
-    rings = [ring_in(x) for x in arrived]
-    first = rings[0][0]
-    up[-1], down[-1] = after((up[-1], down[-1]), first)
+    ring = ring_in(*arrived)
     far_in = shift(up[-1][:slice_rows], "ctx", 1)
     far_out = shift(down[-1][slice_rows:], "ctx", -1)
     weights = local(
         assemble_kernel, [jax.ShapeDtypeStruct((n * slice_rows, width), BF)] * 2
     )(far_in, far_out, block, *up, *down)
-    sums = [expert_layer(*ring, weights) for ring in rings]
+    sums = expert_layer(*ring, weights)
     returned = [lax.all_to_all(x, "expert", 0, 0, tiled=True) for x in sums]
     return local(
         functools.partial(combine_kernel, experts, cap),

time: 237 us -> 242 us (1.021)
  starting transfers between devices: 81.4 us -> 92.2 us
  Pallas kernels: 31 us -> 23 us
    ppermute x20, waiting for transfers between devices: 47.4 us -> 24.2 us  [shift(): return lax.ppermute(x, axis, [(i, (i + by) % n) for i in range(n)])]
    all_to_all x1, waiting for transfers between devices: 0.01 us -> 11.9 us  [per_device(): back = lax.all_to_all(head_output, 'ctx', 0, 0, tiled=True)]
    all_to_all x1 -> x2, waiting for transfers between devices: 3.67 us -> 10 us  [per_device(): arrived = [lax.all_to_all(x, 'expert', 0, 0, tiled=True) for x in sends]]
    ppermute x20, starting transfers between devices: 57.8 us -> 63.6 us  [shift(): return lax.ppermute(x, axis, [(i, (i + by) % n) for i in range(n)])]
    pallas_call x3, Pallas kernels: 15.8 us -> 10.2 us  [run_experts(): local(functools.partial(expert_kernel, len(pieces)), [jax.ShapeDtypeStruc...]
    all_to_all x1 -> x2, starting transfers between devices: 8.62 us -> 14 us  [per_device(): arrived = [lax.all_to_all(x, 'expert', 0, 0, tiled=True) for x in sends]]
    all_to_all x1 -> x2, waiting for transfers between devices: 26.5 us -> 31.6 us  [per_device(): returned = [lax.all_to_all(x, 'expert', 0, 0, tiled=True) for x in sums]]
    all_to_all x1 -> x2, starting transfers between devices: 11.4 us -> 11 us  [per_device(): returned = [lax.all_to_all(x, 'expert', 0, 0, tiled=True) for x in sums]]
  transfers between devices with their start and end apart: 23 -> 25, of which waited for: 9 -> 12; matrix products, arithmetic and copies ran while one was open for 1% -> 1% of each run, Pallas kernels for 6% -> 4%
where the time goes in v4:
time: 242 us; the launch traced here: 240 us
  starting transfers between devices  92.2 us (38%)
  waiting for transfers between devices  77.7 us (32%)
  blocking collectives  40.2 us (17%)
  Pallas kernels  23 us (10%)
  local copies, waits for them, and re-layouts  4.06 us (2%)
    ppermute x20, starting transfers between devices, shift(): return lax.ppermute(x, axis, [(i, (i + by) % n) for i in range(n)])  63.6 us
    all_to_all x1, blocking collectives, per_device(): mixed = lax.all_to_all(packed, 'ctx', 0, 0, tiled=True)  40.2 us
    all_to_all x2, waiting for transfers between devices, per_device(): returned = [lax.all_to_all(x, 'expert', 0, 0, tiled=True) for x in sums]  31.6 us
    ppermute x20, waiting for transfers between devices, shift(): return lax.ppermute(x, axis, [(i, (i + by) % n) for i in range(n)])  24.2 us
    all_to_all x2, starting transfers between devices, per_device(): arrived = [lax.all_to_all(x, 'expert', 0, 0, tiled=True) for x in sends]  14 us
    all_to_all x1, waiting for transfers between devices, per_device(): back = lax.all_to_all(head_output, 'ctx', 0, 0, tiled=True)  11.9 us
    all_to_all x2, starting transfers between devices, per_device(): returned = [lax.all_to_all(x, 'expert', 0, 0, tiled=True) for x in sums]  11 us
    pallas_call x3, Pallas kernels, run_experts(): local(functools.partial(expert_kernel, len(pieces)), [jax.ShapeDtypeStruc...  10.2 us
  transfers between devices with their start and end apart: 25, of which 12 were waited for; matrix products, arithmetic and copies ran while one was open for 1% of the time, Pallas kernels for 4%

profile of v4, /device:TPU:7, one launch (start us, length us, event | category | flops | bytes accessed | tf_op | source)
XLA Modules:
  0.0 239.7 jit_solution(7414666644144877350)
XLA Ops:
  0.0 1.3 copy-done
  1.3 0.3 shard_map.82
  1.5 40.2 %all_to_all.56.m_ref = bf16[8,576,128]{2,1,0:T(8,128)(2,1)S(1)} all-to-all(bf16[8,576,128]{2,1,0:T(8,128)(2,1)S(1)} %shard_map.82), channel_id=1, replica_groups=mesh['dp'=4,'ctx'=8,'expert'=16] {'ctx'}, dimensions={0} | all-to-all | bytes 2359296 | tf_op jit(solution)/shard_map/all_to_all | solution.py:317
  41.8 7.3 %shard_map.83 = bf16[8,192,128]{2,1,0:T(8,128)(2,1)} custom-call(bf16[8,576,128]{2,1,0:T(8,128)(2,1)S(1)} %all_to_all.56.m_ref), custom_call_target="tpu_custom_call" | custom-call | tf_op jit(solution)/shard_map/pallas_call | solution.py:319
  49.1 3.6 %all-to-all-start.1 = ((bf16[8,192,128]{2,1,0:T(8,128)(2,1)}), bf16[8,192,128]{2,1,0:T(8,128)(2,1)S(1)}, u32[]{:S(2)}, u32[]{:S(2)}) async-start(bf16[8,192,128]{2,1,0:T(8,128)(2,1)} %shard_map.83), calls=%async_computation.1 | async-start | bytes 786432 | tf_op jit(solution)/shard_map/all_to_all | solution.py:327
  52.7 0.1 copy.9
  52.8 0.1 copy.10.choice_ref
  52.9 11.9 %all-to-all-done.1.b_ref = bf16[8,192,128]{2,1,0:T(8,128)(2,1)S(1)} async-done(((bf16[8,192,128]{2,1,0:T(8,128)(2,1)}), bf16[8,192,128]{2,1,0:T(8,128)(2,1)S(1)}, u32[]{:S(2)}, u32[]{:S(2)}) %all-to-all-start.1) | async-done | bytes 393248 | tf_op jit(solution)/shard_map/all_to_all | solution.py:327
  64.8 1.4 shard_map.84
  66.3 0.8 copy-done.7
  67.1 10.5 %all-to-all-start.2 = ((bf16[16,8,1920]{2,1,0:T(8,128)(2,1)}), bf16[16,8,1920]{2,1,0:T(8,128)(2,1)S(1)}, u32[]{:S(2)}, u32[]{:S(2)}) async-start(bf16[16,8,1920]{2,1,0:T(8,128)(2,1)} %bitcast.4), calls=%async_computation.2 | async-start | bytes 983040 | tf_op jit(solution)/shard_map/all_to_all | solution.py:336
  77.7 2.2 collective-permute-start
  79.9 4.3 %collective-permute-start.4 = (bf16[192,1536]{1,0:T(8,128)(2,1)S(1)}, bf16[192,1536]{1,0:T(8,128)(2,1)S(1)}, u32[]{:S(2)}, u32[]{:S(2)}) collective-permute-start(bf16[192,1536]{1,0:T(8,128)(2,1)S(1)} %shard_map.85.refs_2_), channel_id=1, source_target_pairs={{0,112},{16,0},{32,16},{48,32},{64,48},{80,64},{96,80},{112,96},{1... | collective-permute-start | bytes 1769480 | tf_op jit(solution)/shard_map/ppermute | solution.py:269
  84.2 10.0 %all-to-all-done.2 = bf16[16,8,1920]{2,1,0:T(8,128)(2,1)S(1)} async-done(((bf16[16,8,1920]{2,1,0:T(8,128)(2,1)}), bf16[16,8,1920]{2,1,0:T(8,128)(2,1)S(1)}, u32[]{:S(2)}, u32[]{:S(2)}) %all-to-all-start.2) | async-done | bytes 491552 | tf_op jit(solution)/shard_map/all_to_all | solution.py:336
  94.3 3.5 %all-to-all-start.3 = ((bf16[16,8,1920]{2,1,0:T(8,128)(2,1)}), bf16[16,8,1920]{2,1,0:T(8,128)(2,1)S(1)}, u32[]{:S(2)}, u32[]{:S(2)}) async-start(bf16[16,8,1920]{2,1,0:T(8,128)(2,1)} %bitcast.25), calls=%async_computation.3 | async-start | bytes 983040 | tf_op jit(solution)/shard_map/all_to_all | solution.py:336
  97.7 0.0 collective-permute-done.refs_3_
  97.7 2.2 collective-permute-start.1
  100.0 0.8 copy-done.1
  100.8 0.0 collective-permute-done.4.refs_6_
  100.8 4.3 %collective-permute-start.5 = (bf16[192,1536]{1,0:T(8,128)(2,1)S(1)}, bf16[192,1536]{1,0:T(8,128)(2,1)}, u32[]{:S(2)}, u32[]{:S(2)}) collective-permute-start(bf16[192,1536]{1,0:T(8,128)(2,1)S(1)} %collective-permute-done.4.refs_6_), channel_id=1, source_target_pairs={{0,112},{16,0},{32,16},{48,32},{64,48},{80,64},{96,80},{112,96},{1... | collective-permute-start | bytes 1769480 | tf_op jit(solution)/shard_map/ppermute | solution.py:269
  105.1 0.8 copy-done.3
  105.9 2.1 collective-permute-start.8
  108.0 3.2 %collective-permute-start.9 = (bf16[128,1920]{1,0:T(8,128)(2,1)S(1)}, bf16[128,1920]{1,0:T(8,128)(2,1)}, u32[]{:S(2)}, u32[]{:S(2)}) collective-permute-start(bf16[128,1920]{1,0:T(8,128)(2,1)S(1)} %bitcast.16), channel_id=1, source_target_pairs={{0,384},{128,0},{256,128},{384,256},{1,385},{129,1},{257,129},{385... | collective-permute-start | bytes 1474568 | tf_op jit(solution)/shard_map/ppermute | solution.py:269
  111.2 5.1 %collective-permute-done.1.refs_4_ = bf16[192,1536]{1,0:T(8,128)(2,1)} collective-permute-done((bf16[192,1536]{1,0:T(8,128)(2,1)S(1)}, bf16[192,1536]{1,0:T(8,128)(2,1)}, u32[]{:S(2)}, u32[]{:S(2)}) %collective-permute-start.1) | collective-permute-done | bytes 589856 | tf_op jit(solution)/shard_map/ppermute | solution.py:269
  116.3 1.9 collective-permute-start.2
  118.2 0.0 collective-permute-done.5.refs_7_
  118.2 5.1 %collective-permute-start.6 = (bf16[192,1536]{1,0:T(8,128)(2,1)}, bf16[192,1536]{1,0:T(8,128)(2,1)S(1)}, u32[]{:S(2)}, u32[]{:S(2)}) collective-permute-start(bf16[192,1536]{1,0:T(8,128)(2,1)} %collective-permute-done.5.refs_7_), channel_id=1, source_target_pairs={{0,112},{16,0},{32,16},{48,32},{64,48},{80,64},{96,80},{112,96},{1... | collective-permute-start | bytes 1769480 | tf_op jit(solution)/shard_map/ppermute | solution.py:269
  123.3 0.0 all-to-all-done.3
  123.4 0.3 collective-permute-done.9.refs_2_
  123.7 2.3 collective-permute-start.11
  126.0 4.3 %collective-permute-start.10 = (bf16[128,1920]{1,0:T(8,128)(2,1)S(1)}, bf16[128,1920]{1,0:T(8,128)(2,1)S(1)}, u32[]{:S(2)}, u32[]{:S(2)}) collective-permute-start(bf16[128,1920]{1,0:T(8,128)(2,1)S(1)} %bitcast.19), channel_id=1, source_target_pairs={{0,128},{128,256},{256,384},{384,0},{1,129},{129,257},{257,385},{3... | collective-permute-start | bytes 1474568 | tf_op jit(solution)/shard_map/ppermute | solution.py:269
  130.3 3.8 %collective-permute-done.2.refs_5_ = bf16[192,1536]{1,0:T(8,128)(2,1)S(1)} collective-permute-done((bf16[192,1536]{1,0:T(8,128)(2,1)}, bf16[192,1536]{1,0:T(8,128)(2,1)S(1)}, u32[]{:S(2)}, u32[]{:S(2)}) %collective-permute-start.2) | collective-permute-done | bytes 589856 | tf_op jit(solution)/shard_map/ppermute | solution.py:269
  134.2 1.9 collective-permute-start.3
  136.1 0.0 collective-permute-done.6.refs_8_
  136.1 4.8 %collective-permute-start.7 = (bf16[96,1536]{1,0:T(8,128)(2,1)S(1)}, bf16[96,1536]{1,0:T(8,128)(2,1)S(1)}, u32[]{:S(2)}, u32[]{:S(2)}) collective-permute-start(bf16[96,1536]{1,0:T(8,128)(2,1)S(1)} %slice.9), channel_id=1, source_target_pairs={{0,112},{16,0},{32,16},{48,32},{64,48},{80,64},{96,80},{112,96},{1... | collective-permute-start | bytes 884744 | tf_op jit(solution)/shard_map/ppermute | solution.py:269
  140.9 2.1 collective-permute-start.12
  143.0 0.0 collective-permute-done.11.refs_3_
  143.0 3.2 %collective-permute-start.13 = (bf16[128,1920]{1,0:T(8,128)(2,1)S(1)}, bf16[128,1920]{1,0:T(8,128)(2,1)S(1)}, u32[]{:S(2)}, u32[]{:S(2)}) collective-permute-start(bf16[128,1920]{1,0:T(8,128)(2,1)S(1)} %collective-permute-done.11.refs_3_), channel_id=1, source_target_pairs={{0,384},{128,0},{256,128},{384,256},{1,385},{129,1},{257,129},{385... | collective-permute-start | bytes 1474568 | tf_op jit(solution)/shard_map/ppermute | solution.py:269
  146.3 1.6 shard_map.86
  147.8 5.5 %shard_map.87 = (bf16[128,1920]{1,0:T(8,128)(2,1)S(1)}, bf16[128,1920]{1,0:T(8,128)(2,1)S(1)}, bf16[128,1920]{1,0:T(8,128)(2,1)S(1)}, bf16[128,1920]{1,0:T(8,128)(2,1)S(1)}) custom-call(bf16[768,1536]{1,0:T(8,128)(2,1)S(1)} %get-tuple-element.28.in_ref, bf16[768,1536]{1,0:T(8,128)(2,1)S(1)} %get-tuple-element.29.out_ref, ...), custom_call_target="tpu_custom_call" | custom-call | flops 3019898880 | bytes 8650752 | tf_op jit(solution)/shard_map/pallas_call | solution.py:251
  153.3 0.6 collective-permute-done.12.refs_0_
  153.9 2.8 %collective-permute-done.13.refs_1_ = bf16[128,1920]{1,0:T(8,128)(2,1)S(1)} collective-permute-done((bf16[128,1920]{1,0:T(8,128)(2,1)S(1)}, bf16[128,1920]{1,0:T(8,128)(2,1)S(1)}, u32[]{:S(2)}, u32[]{:S(2)}) %collective-permute-start.13) | collective-permute-done | bytes 491552 | tf_op jit(solution)/shard_map/ppermute | solution.py:269
  156.8 2.3 shard_map.88
  159.1 2.0 collective-permute-start.15
  161.1 4.5 %collective-permute-start.14 = (bf16[128,1920]{1,0:T(8,128)(2,1)S(1)}, bf16[128,1920]{1,0:T(8,128)(2,1)S(1)}, u32[]{:S(2)}, u32[]{:S(2)}) collective-permute-start(bf16[128,1920]{1,0:T(8,128)(2,1)S(1)} %get-tuple-element.35), channel_id=1, source_target_pairs={{0,128},{128,256},{256,384},{384,0},{1,129},{129,257},{257,385},{3... | collective-permute-start | bytes 1474568 | tf_op jit(solution)/shard_map/ppermute | solution.py:269
  165.6 1.9 collective-permute-start.16
  167.5 4.6 %collective-permute-start.17 = (bf16[128,1920]{1,0:T(8,128)(2,1)S(1)}, bf16[128,1920]{1,0:T(8,128)(2,1)S(1)}, u32[]{:S(2)}, u32[]{:S(2)}) collective-permute-start(bf16[128,1920]{1,0:T(8,128)(2,1)S(1)} %get-tuple-element.40), channel_id=1, source_target_pairs={{0,128},{128,256},{256,384},{384,0},{1,129},{129,257},{257,385},{3... | collective-permute-start | bytes 1474568 | tf_op jit(solution)/shard_map/ppermute | solution.py:269
  172.1 0.1 add_convert_fusion.2
  172.3 1.9 collective-permute-start.19
  174.2 0.1 add_convert_fusion.3
  174.3 4.8 %collective-permute-start.18 = (bf16[128,1920]{1,0:T(8,128)(2,1)S(1)}, bf16[128,1920]{1,0:T(8,128)(2,1)S(1)}, u32[]{:S(2)}, u32[]{:S(2)}) collective-permute-start(bf16[128,1920]{1,0:T(8,128)(2,1)S(1)} %add_convert_fusion.3), channel_id=1, source_target_pairs={{0,128},{128,256},{256,384},{384,0},{1,129},{129,257},{257,385},{3... | collective-permute-start | bytes 1474568 | tf_op jit(solution)/shard_map/ppermute | solution.py:269
  179.1 3.4 %collective-permute-done.16.refs_2_ = bf16[128,1920]{1,0:T(8,128)(2,1)S(1)} collective-permute-done((bf16[128,1920]{1,0:T(8,128)(2,1)S(1)}, bf16[128,1920]{1,0:T(8,128)(2,1)S(1)}, u32[]{:S(2)}, u32[]{:S(2)}) %collective-permute-start.16) | collective-permute-done | bytes 491552 | tf_op jit(solution)/shard_map/ppermute | solution.py:269
  182.4 0.9 collective-permute-done.17.refs_3_
  183.3 2.4 shard_map.89
  185.7 7.3 %collective-permute-done.19 = bf16[128,1920]{1,0:T(8,128)(2,1)S(1)} collective-permute-done((bf16[128,1920]{1,0:T(8,128)(2,1)S(1)}, bf16[128,1920]{1,0:T(8,128)(2,1)S(1)}, u32[]{:S(2)}, u32[]{:S(2)}) %collective-permute-start.19) | collective-permute-done | bytes 491552 | tf_op jit(solution)/shard_map/ppermute | solution.py:269
  193.0 0.9 fusion.1
  193.9 7.6 %all-to-all-start.5 = ((bf16[16,8,1920]{2,1,0:T(8,128)(2,1)}), bf16[16,8,1920]{2,1,0:T(8,128)(2,1)S(1)}, u32[]{:S(2)}, u32[]{:S(2)}) async-start(bf16[16,8,1920]{2,1,0:T(8,128)(2,1)} %fusion.1), calls=%async_computation.5 | async-start | bytes 983040 | tf_op jit(solution)/shard_map/all_to_all | solution.py:347
  201.5 0.0 copy-start.14
  201.5 0.9 fusion
  202.4 15.7 %all-to-all-done.5 = bf16[16,8,1920]{2,1,0:T(8,128)(2,1)S(1)} async-done(((bf16[16,8,1920]{2,1,0:T(8,128)(2,1)}), bf16[16,8,1920]{2,1,0:T(8,128)(2,1)S(1)}, u32[]{:S(2)}, u32[]{:S(2)}) %all-to-all-start.5) | async-done | bytes 491552 | tf_op jit(solution)/shard_map/all_to_all | solution.py:347
  218.1 3.5 %all-to-all-start.4 = ((bf16[16,8,1920]{2,1,0:T(8,128)(2,1)}), bf16[16,8,1920]{2,1,0:T(8,128)(2,1)S(1)}, u32[]{:S(2)}, u32[]{:S(2)}) async-start(bf16[16,8,1920]{2,1,0:T(8,128)(2,1)} %fusion), calls=%async_computation.4 | async-start | bytes 983040 | tf_op jit(solution)/shard_map/all_to_all | solution.py:347
  221.6 0.1 copy.11
  221.7 15.9 %all-to-all-done.4 = bf16[16,8,1920]{2,1,0:T(8,128)(2,1)S(1)} async-done(((bf16[16,8,1920]{2,1,0:T(8,128)(2,1)}), bf16[16,8,1920]{2,1,0:T(8,128)(2,1)S(1)}, u32[]{:S(2)}, u32[]{:S(2)}) %all-to-all-start.4) | async-done | bytes 491552 | tf_op jit(solution)/shard_map/all_to_all | solution.py:347
  237.6 2.2 shard_map.90
  (35 shorter events, 0.1 us)
Async XLA Ops:
  0.0 1.3 copy-start
  41.8 11.0 %copy-start.13 = (s32[1,128,2]{1,2,0:T(2,128)S(1)}, s32[1,128,2]{1,2,0:T(2,128)}, u32[]{:S(2)}) copy-start(s32[1,128,2]{1,2,0:T(2,128)} %param.12) | copy-start | bytes 3076
  41.8 23.1 %copy-start.8 = (bf16[1,128,1536]{2,1,0:T(8,128)(2,1)S(1)}, bf16[1,128,1536]{2,1,0:T(8,128)(2,1)}, u32[]{:S(2)}) copy-start(bf16[1,128,1536]{2,1,0:T(8,128)(2,1)} %param.9) | copy-start | bytes 1179652
  41.8 23.1 %copy-start.11 = (f32[1,1536]{1,0:T(1,128)S(1)}, f32[1,1536]{1,0:T(1,128)}, u32[]{:S(2)}) copy-start(f32[1,1536]{1,0:T(1,128)} %scale_ref.1) | copy-start | bytes 18436
  41.8 23.1 %copy-start.12 = (f32[1,1536]{1,0:T(1,128)S(1)}, f32[1,1536]{1,0:T(1,128)}, u32[]{:S(2)}) copy-start(f32[1,1536]{1,0:T(1,128)} %shift_ref.1) | copy-start | bytes 18436
  49.1 28.5 %copy-start.9 = (bf16[1,96,1536]{2,1,0:T(8,128)(2,1)S(1)}, bf16[1,96,1536]{2,1,0:T(8,128)(2,1)}, u32[]{:S(2)}) copy-start(bf16[1,96,1536]{2,1,0:T(8,128)(2,1)} %in_ref.1) | copy-start | bytes 884740
  49.1 28.5 %copy-start.10 = (bf16[1,96,1536]{2,1,0:T(8,128)(2,1)S(1)}, bf16[1,96,1536]{2,1,0:T(8,128)(2,1)}, u32[]{:S(2)}) copy-start(bf16[1,96,1536]{2,1,0:T(8,128)(2,1)} %out_ref.1) | copy-start | bytes 884740
  49.1 15.7 %all-to-all-start.1 = ((bf16[8,192,128]{2,1,0:T(8,128)(2,1)}), bf16[8,192,128]{2,1,0:T(8,128)(2,1)S(1)}, u32[]{:S(2)}, u32[]{:S(2)}) async-start(bf16[8,192,128]{2,1,0:T(8,128)(2,1)} %shard_map.83), calls=%async_computation.1 | async-start | bytes 786432 | tf_op jit(solution)/shard_map/all_to_all | solution.py:327
  52.8 14.2 %copy-start.5 = (s32[1,128,2]{2,1,0:T(8,128)}, s32[1,128,2]{2,1,0:T(8,128)S(1)}, u32[]{:S(2)}) copy-start(s32[1,128,2]{2,1,0:T(8,128)S(1)} %copy.9) | copy-start | bytes 3076
  66.3 0.8 copy-start.7
  67.1 27.2 %all-to-all-start.2 = ((bf16[16,8,1920]{2,1,0:T(8,128)(2,1)}), bf16[16,8,1920]{2,1,0:T(8,128)(2,1)S(1)}, u32[]{:S(2)}, u32[]{:S(2)}) async-start(bf16[16,8,1920]{2,1,0:T(8,128)(2,1)} %bitcast.4), calls=%async_computation.2 | async-start | bytes 983040 | tf_op jit(solution)/shard_map/all_to_all | solution.py:336
  77.7 20.0 %collective-permute-start = (bf16[192,1536]{1,0:T(8,128)(2,1)S(1)}, bf16[192,1536]{1,0:T(8,128)(2,1)S(1)}, u32[]{:S(2)}, u32[]{:S(2)}) collective-permute-start(bf16[192,1536]{1,0:T(8,128)(2,1)S(1)} %shard_map.85.refs_2_), channel_id=1, source_target_pairs={{0,16},{16,32},{32,48},{48,64},{64,80},{80,96},{96,112},{112,0},{1... | collective-permute-start | bytes 1769480 | tf_op jit(solution)/shard_map/ppermute | solution.py:269
  79.9 20.8 %collective-permute-start.4 = (bf16[192,1536]{1,0:T(8,128)(2,1)S(1)}, bf16[192,1536]{1,0:T(8,128)(2,1)S(1)}, u32[]{:S(2)}, u32[]{:S(2)}) collective-permute-start(bf16[192,1536]{1,0:T(8,128)(2,1)S(1)} %shard_map.85.refs_2_), channel_id=1, source_target_pairs={{0,112},{16,0},{32,16},{48,32},{64,48},{80,64},{96,80},{112,96},{1... | collective-permute-start | bytes 1769480 | tf_op jit(solution)/shard_map/ppermute | solution.py:269
  94.3 29.1 %all-to-all-start.3 = ((bf16[16,8,1920]{2,1,0:T(8,128)(2,1)}), bf16[16,8,1920]{2,1,0:T(8,128)(2,1)S(1)}, u32[]{:S(2)}, u32[]{:S(2)}) async-start(bf16[16,8,1920]{2,1,0:T(8,128)(2,1)} %bitcast.25), calls=%async_computation.3 | async-start | bytes 983040 | tf_op jit(solution)/shard_map/all_to_all | solution.py:336
  97.7 18.5 %collective-permute-start.1 = (bf16[192,1536]{1,0:T(8,128)(2,1)S(1)}, bf16[192,1536]{1,0:T(8,128)(2,1)}, u32[]{:S(2)}, u32[]{:S(2)}) collective-permute-start(bf16[192,1536]{1,0:T(8,128)(2,1)S(1)} %collective-permute-done.refs_3_), channel_id=1, source_target_pairs={{0,16},{16,32},{32,48},{48,64},{64,80},{80,96},{96,112},{112,0},{1... | collective-permute-start | bytes 1769480 | tf_op jit(solution)/shard_map/ppermute | solution.py:269
  100.0 0.8 copy-start.1
  100.8 17.4 %collective-permute-start.5 = (bf16[192,1536]{1,0:T(8,128)(2,1)S(1)}, bf16[192,1536]{1,0:T(8,128)(2,1)}, u32[]{:S(2)}, u32[]{:S(2)}) collective-permute-start(bf16[192,1536]{1,0:T(8,128)(2,1)S(1)} %collective-permute-done.4.refs_6_), channel_id=1, source_target_pairs={{0,112},{16,0},{32,16},{48,32},{64,48},{80,64},{96,80},{112,96},{1... | collective-permute-start | bytes 1769480 | tf_op jit(solution)/shard_map/ppermute | solution.py:269
  105.1 0.8 copy-start.3
  105.9 17.5 %collective-permute-start.8 = (bf16[128,1920]{1,0:T(8,128)(2,1)S(1)}, bf16[128,1920]{1,0:T(8,128)(2,1)}, u32[]{:S(2)}, u32[]{:S(2)}) collective-permute-start(bf16[128,1920]{1,0:T(8,128)(2,1)S(1)} %bitcast.15), channel_id=1, source_target_pairs={{0,128},{128,256},{256,384},{384,0},{1,129},{129,257},{257,385},{3... | collective-permute-start | bytes 1474568 | tf_op jit(solution)/shard_map/ppermute | solution.py:269
  108.0 15.7 %collective-permute-start.9 = (bf16[128,1920]{1,0:T(8,128)(2,1)S(1)}, bf16[128,1920]{1,0:T(8,128)(2,1)}, u32[]{:S(2)}, u32[]{:S(2)}) collective-permute-start(bf16[128,1920]{1,0:T(8,128)(2,1)S(1)} %bitcast.16), channel_id=1, source_target_pairs={{0,384},{128,0},{256,128},{384,256},{1,385},{129,1},{257,129},{385... | collective-permute-start | bytes 1474568 | tf_op jit(solution)/shard_map/ppermute | solution.py:269
  116.3 17.8 %collective-permute-start.2 = (bf16[192,1536]{1,0:T(8,128)(2,1)}, bf16[192,1536]{1,0:T(8,128)(2,1)S(1)}, u32[]{:S(2)}, u32[]{:S(2)}) collective-permute-start(bf16[192,1536]{1,0:T(8,128)(2,1)} %collective-permute-done.1.refs_4_), channel_id=1, source_target_pairs={{0,16},{16,32},{32,48},{48,64},{64,80},{80,96},{96,112},{112,0},{1... | collective-permute-start | bytes 1769480 | tf_op jit(solution)/shard_map/ppermute | solution.py:269
  118.2 17.9 %collective-permute-start.6 = (bf16[192,1536]{1,0:T(8,128)(2,1)}, bf16[192,1536]{1,0:T(8,128)(2,1)S(1)}, u32[]{:S(2)}, u32[]{:S(2)}) collective-permute-start(bf16[192,1536]{1,0:T(8,128)(2,1)} %collective-permute-done.5.refs_7_), channel_id=1, source_target_pairs={{0,112},{16,0},{32,16},{48,32},{64,48},{80,64},{96,80},{112,96},{1... | collective-permute-start | bytes 1769480 | tf_op jit(solution)/shard_map/ppermute | solution.py:269
  123.4 22.9 %copy-start.2 = (bf16[192,1536]{1,0:T(8,128)(2,1)S(1)}, bf16[192,1536]{1,0:T(8,128)(2,1)}, u32[]{:S(2)}) copy-start(bf16[192,1536]{1,0:T(8,128)(2,1)} %copy-done.1) | copy-start | bytes 1769476
  123.4 22.9 %copy-start.4 = (bf16[192,1536]{1,0:T(8,128)(2,1)S(1)}, bf16[192,1536]{1,0:T(8,128)(2,1)}, u32[]{:S(2)}) copy-start(bf16[192,1536]{1,0:T(8,128)(2,1)} %copy-done.3) | copy-start | bytes 1769476
  123.7 19.3 %collective-permute-start.11 = (bf16[128,1920]{1,0:T(8,128)(2,1)S(1)}, bf16[128,1920]{1,0:T(8,128)(2,1)S(1)}, u32[]{:S(2)}, u32[]{:S(2)}) collective-permute-start(bf16[128,1920]{1,0:T(8,128)(2,1)S(1)} %bitcast.18), channel_id=1, source_target_pairs={{0,384},{128,0},{256,128},{384,256},{1,385},{129,1},{257,129},{385... | collective-permute-start | bytes 1474568 | tf_op jit(solution)/shard_map/ppermute | solution.py:269
  126.0 21.8 %collective-permute-start.10 = (bf16[128,1920]{1,0:T(8,128)(2,1)S(1)}, bf16[128,1920]{1,0:T(8,128)(2,1)S(1)}, u32[]{:S(2)}, u32[]{:S(2)}) collective-permute-start(bf16[128,1920]{1,0:T(8,128)(2,1)S(1)} %bitcast.19), channel_id=1, source_target_pairs={{0,128},{128,256},{256,384},{384,0},{1,129},{129,257},{257,385},{3... | collective-permute-start | bytes 1474568 | tf_op jit(solution)/shard_map/ppermute | solution.py:269
  134.2 12.1 %collective-permute-start.3 = (bf16[96,1536]{1,0:T(8,128)(2,1)S(1)}, bf16[96,1536]{1,0:T(8,128)(2,1)S(1)}, u32[]{:S(2)}, u32[]{:S(2)}) collective-permute-start(bf16[96,1536]{1,0:T(8,128)(2,1)S(1)} %slice.8), channel_id=1, source_target_pairs={{0,16},{16,32},{32,48},{48,64},{64,80},{80,96},{96,112},{112,0},{1... | collective-permute-start | bytes 884744 | tf_op jit(solution)/shard_map/ppermute | solution.py:269
  136.1 10.1 %collective-permute-start.7 = (bf16[96,1536]{1,0:T(8,128)(2,1)S(1)}, bf16[96,1536]{1,0:T(8,128)(2,1)S(1)}, u32[]{:S(2)}, u32[]{:S(2)}) collective-permute-start(bf16[96,1536]{1,0:T(8,128)(2,1)S(1)} %slice.9), channel_id=1, source_target_pairs={{0,112},{16,0},{32,16},{48,32},{64,48},{80,64},{96,80},{112,96},{1... | collective-permute-start | bytes 884744 | tf_op jit(solution)/shard_map/ppermute | solution.py:269
  140.9 13.0 %collective-permute-start.12 = (bf16[128,1920]{1,0:T(8,128)(2,1)}, bf16[128,1920]{1,0:T(8,128)(2,1)S(1)}, u32[]{:S(2)}, u32[]{:S(2)}) collective-permute-start(bf16[128,1920]{1,0:T(8,128)(2,1)} %collective-permute-done.8.refs_0_), channel_id=1, source_target_pairs={{0,128},{128,256},{256,384},{384,0},{1,129},{129,257},{257,385},{3... | collective-permute-start | bytes 1474568 | tf_op jit(solution)/shard_map/ppermute | solution.py:269
  143.0 13.7 %collective-permute-start.13 = (bf16[128,1920]{1,0:T(8,128)(2,1)S(1)}, bf16[128,1920]{1,0:T(8,128)(2,1)S(1)}, u32[]{:S(2)}, u32[]{:S(2)}) collective-permute-start(bf16[128,1920]{1,0:T(8,128)(2,1)S(1)} %collective-permute-done.11.refs_3_), channel_id=1, source_target_pairs={{0,384},{128,0},{256,128},{384,256},{1,385},{129,1},{257,129},{385... | collective-permute-start | bytes 1474568 | tf_op jit(solution)/shard_map/ppermute | solution.py:269
  159.1 13.0 %collective-permute-start.15 = (bf16[128,1920]{1,0:T(8,128)(2,1)S(1)}, bf16[128,1920]{1,0:T(8,128)(2,1)S(1)}, u32[]{:S(2)}, u32[]{:S(2)}) collective-permute-start(bf16[128,1920]{1,0:T(8,128)(2,1)S(1)} %get-tuple-element.37), channel_id=1, source_target_pairs={{0,384},{128,0},{256,128},{384,256},{1,385},{129,1},{257,129},{385... | collective-permute-start | bytes 1474568 | tf_op jit(solution)/shard_map/ppermute | solution.py:269
  161.1 13.1 %collective-permute-start.14 = (bf16[128,1920]{1,0:T(8,128)(2,1)S(1)}, bf16[128,1920]{1,0:T(8,128)(2,1)S(1)}, u32[]{:S(2)}, u32[]{:S(2)}) collective-permute-start(bf16[128,1920]{1,0:T(8,128)(2,1)S(1)} %get-tuple-element.35), channel_id=1, source_target_pairs={{0,128},{128,256},{256,384},{384,0},{1,129},{129,257},{257,385},{3... | collective-permute-start | bytes 1474568 | tf_op jit(solution)/shard_map/ppermute | solution.py:269
  165.6 16.8 %collective-permute-start.16 = (bf16[128,1920]{1,0:T(8,128)(2,1)S(1)}, bf16[128,1920]{1,0:T(8,128)(2,1)S(1)}, u32[]{:S(2)}, u32[]{:S(2)}) collective-permute-start(bf16[128,1920]{1,0:T(8,128)(2,1)S(1)} %get-tuple-element.32), channel_id=1, source_target_pairs={{0,384},{128,0},{256,128},{384,256},{1,385},{129,1},{257,129},{385... | collective-permute-start | bytes 1474568 | tf_op jit(solution)/shard_map/ppermute | solution.py:269
  167.5 15.8 %collective-permute-start.17 = (bf16[128,1920]{1,0:T(8,128)(2,1)S(1)}, bf16[128,1920]{1,0:T(8,128)(2,1)S(1)}, u32[]{:S(2)}, u32[]{:S(2)}) collective-permute-start(bf16[128,1920]{1,0:T(8,128)(2,1)S(1)} %get-tuple-element.40), channel_id=1, source_target_pairs={{0,128},{128,256},{256,384},{384,0},{1,129},{129,257},{257,385},{3... | collective-permute-start | bytes 1474568 | tf_op jit(solution)/shard_map/ppermute | solution.py:269
  172.3 20.7 %collective-permute-start.19 = (bf16[128,1920]{1,0:T(8,128)(2,1)S(1)}, bf16[128,1920]{1,0:T(8,128)(2,1)S(1)}, u32[]{:S(2)}, u32[]{:S(2)}) collective-permute-start(bf16[128,1920]{1,0:T(8,128)(2,1)S(1)} %add_convert_fusion.2), channel_id=1, source_target_pairs={{0,384},{128,0},{256,128},{384,256},{1,385},{129,1},{257,129},{385... | collective-permute-start | bytes 1474568 | tf_op jit(solution)/shard_map/ppermute | solution.py:269
  174.3 27.1 %collective-permute-start.18 = (bf16[128,1920]{1,0:T(8,128)(2,1)S(1)}, bf16[128,1920]{1,0:T(8,128)(2,1)S(1)}, u32[]{:S(2)}, u32[]{:S(2)}) collective-permute-start(bf16[128,1920]{1,0:T(8,128)(2,1)S(1)} %add_convert_fusion.3), channel_id=1, source_target_pairs={{0,128},{128,256},{256,384},{384,0},{1,129},{129,257},{257,385},{3... | collective-permute-start | bytes 1474568 | tf_op jit(solution)/shard_map/ppermute | solution.py:269
  193.9 24.2 %all-to-all-start.5 = ((bf16[16,8,1920]{2,1,0:T(8,128)(2,1)}), bf16[16,8,1920]{2,1,0:T(8,128)(2,1)S(1)}, u32[]{:S(2)}, u32[]{:S(2)}) async-start(bf16[16,8,1920]{2,1,0:T(8,128)(2,1)} %fusion.1), calls=%async_computation.5 | async-start | bytes 983040 | tf_op jit(solution)/shard_map/all_to_all | solution.py:347
  201.5 20.1 %copy-start.14 = (f32[1,128,2]{1,2,0:T(2,128)S(1)}, f32[1,128,2]{1,2,0:T(2,128)}, u32[]{:S(2)}) copy-start(f32[1,128,2]{1,2,0:T(2,128)} %param.13) | copy-start | bytes 3076
  201.5 36.1 %copy-start.6 = (s32[1,128,2]{2,1,0:T(8,128)S(1)}, s32[1,128,2]{2,1,0:T(8,128)}, u32[]{:S(2)}) copy-start(s32[1,128,2]{2,1,0:T(8,128)} %copy-done.5) | copy-start | bytes 3076
  218.1 19.5 %all-to-all-start.4 = ((bf16[16,8,1920]{2,1,0:T(8,128)(2,1)}), bf16[16,8,1920]{2,1,0:T(8,128)(2,1)S(1)}, u32[]{:S(2)}, u32[]{:S(2)}) async-start(bf16[16,8,1920]{2,1,0:T(8,128)(2,1)} %fusion), calls=%async_computation.4 | async-start | bytes 983040 | tf_op jit(solution)/shard_map/all_to_all | solution.py:347

commit v5 on v4

--- a/solution.py
+++ b/solution.py
@@ -8,7 +8,7 @@
 from jax.sharding import PartitionSpec as P
 
 HD = 64
-CHUNKS = 2
+CHUNKS = 1
 BF = jnp.bfloat16
 F32 = jnp.float32
 LIMIT = 24 * 1024 * 1024
@@ -143,17 +143,15 @@
 
 
 def assemble_kernel(*refs):
-    far_in, far_out, *blocks, in_ref, out_ref = refs
-    rows = far_in.shape[0]
-    in_ref[len(blocks) * rows :, :] = far_in[...]
-    out_ref[len(blocks) * rows :, :] = far_out[...]
+    *blocks, in_ref, out_ref = refs
+    rows = in_ref.shape[0] // len(blocks)
     for i, block in enumerate(blocks):
         in_ref[i * rows : (i + 1) * rows, :] = block[:rows, :]
         out_ref[i * rows : (i + 1) * rows, :] = block[rows:, :]
 
 
 def expert_kernel(pieces, in_ref, out_ref, *refs):
-    x_refs, plus, y_refs, rows_ref = refs[:pieces], refs[pieces : -pieces - 1], refs[-pieces - 1 : -1], refs[-1]
+    x_refs, y_refs, rows_ref = refs[:pieces], refs[pieces:-1], refs[-1]
     rows = x_refs[0].shape[0]
     width = in_ref.shape[1]
     quarter = width // 4
@@ -184,9 +182,6 @@
             [last[:, q * quarter : (q + 1) * quarter] for q in range(4)], axis=0
         )
         total = jnp.dot(pack, quarters, preferred_element_type=F32).astype(BF)
-        if plus:
-            main = add(main, plus[p][:, :width])
-            total = add(total, plus[p][:, width:])
         y_ref[:, :width] = main
         y_ref[:, width:] = total
 
@@ -244,7 +239,7 @@
     )
 
 
-def run_experts(pieces, weight_in, weight_out, plus=()):
+def run_experts(pieces, weight_in, weight_out):
     rows, wide = pieces[0].shape
     hidden, width = weight_in.shape
     work = len(pieces) * rows * 5 // 4
@@ -257,42 +252,45 @@
             bytes_accessed=4 * hidden * width + 4 * len(pieces) * rows * wide,
             transcendentals=work * hidden,
         ),
-    )(weight_in, weight_out, *pieces, *plus)
+    )(weight_in, weight_out, *pieces)
 
 
 def add(*parts):
     return sum(p.astype(F32) for p in parts).astype(BF)
 
 
-def shift(x, axis, by):
-    n = lax.axis_size(axis)
-    return lax.ppermute(x, axis, [(i, (i + by) % n) for i in range(n)])
+def hop(x, axis):
+    n, experts = lax.axis_size(axis), lax.axis_size("expert")
+    perm = [
+        (i * experts + e, (i + 1 - 2 * (e % 2)) % n * experts + e)
+        for i in range(n)
+        for e in range(experts)
+    ]
+    return lax.ppermute(x, (axis, "expert"), perm)
 
 
 def after(x, *others):
     return lax.optimization_barrier((x, *others))[0]
 
 
-def ring_in(a, b):
-    left_a, right_a = shift(a, "dp", 1), shift(a, "dp", -1)
-    across_a = shift(left_a, "dp", 1)
-    b = after(b, left_a, right_a)
-    left_b, right_b = shift(b, "dp", 1), shift(b, "dp", -1)
-    across_b = shift(right_b, "dp", -1)
-    return (a, b), (left_a, left_b, right_a, right_b), (across_a, across_b)
-
-
-def expert_layer(own, near, across, weights):
-    to_left_a, to_left_b, to_right_a, to_right_b = run_experts(near, *weights)
-    got_a, got_b = shift(to_left_a, "dp", -1), shift(to_right_b, "dp", 1)
-    across = after(across, to_left_a)
-    to_across_a, to_across_b = run_experts(across, *weights)
-    via_a, via_b = shift(to_across_a, "dp", 1), shift(to_across_b, "dp", -1)
-    via_a, via_b = add(to_right_a, via_a), add(to_left_b, via_b)
-    sum_a, sum_b = shift(via_a, "dp", 1), shift(via_b, "dp", -1)
-    own = after(own, via_a, via_b)
-    own_a, own_b = run_experts(own, *weights, plus=(got_a, got_b))
-    return add(own_a, sum_a), add(own_b, sum_b)
+def gather_rows(x):
+    half = x.shape[0] // 2
+    rows = [[x[:half], x[half:]]]
+    for _ in range(lax.axis_size("dp") - 1):
+        rows.append([hop(part, "dp") for part in rows[-1]])
+    return rows
+
+
+def expert_layer(rows, weights):
+    own, *others = rows
+    totals = None
+    for parts in others:
+        partials = run_experts(parts, *weights)
+        if totals is not None:
+            partials = [add(p, total) for p, total in zip(partials, totals)]
+        totals = [hop(p, "dp") for p in partials]
+    partials = run_experts(own, *weights)
+    return jnp.concatenate([add(p, total) for p, total in zip(partials, totals)])
 
 
 def per_device(
@@ -331,19 +329,17 @@
         functools.partial(dispatch_kernel, experts, cap),
         [jax.ShapeDtypeStruct((t, width), F32)] + [jax.ShapeDtypeStruct(wide, BF)] * CHUNKS,
     )(back, residual_in[0], modulation_scale, modulation_shift, expert_choice[0].T)
-    block = after(block, *sends)
-    up, down = [shift(block, "ctx", 1)], [shift(block, "ctx", -1)]
     arrived = [lax.all_to_all(x, "expert", 0, 0, tiled=True) for x in sends]
-    for _ in range(n // 2 - 2):
-        up.append(shift(up[-1], "ctx", 1))
-        down.append(shift(down[-1], "ctx", -1))
-    ring = ring_in(*arrived)
-    far_in = shift(up[-1][:slice_rows], "ctx", 1)
-    far_out = shift(down[-1][slice_rows:], "ctx", -1)
+    rows = gather_rows(arrived[0])
+    gates = {0: [mixed], 1: sends, n - 2: rows[1]}
+    blocks = [block]
+    for step in range(n - 1):
+        last = after(blocks[-1], *gates.get(step, ()))
+        blocks.append(hop(last, "ctx"))
     weights = local(
         assemble_kernel, [jax.ShapeDtypeStruct((n * slice_rows, width), BF)] * 2
-    )(far_in, far_out, block, *up, *down)
-    sums = expert_layer(*ring, weights)
+    )(*blocks)
+    sums = [expert_layer(rows, weights)]
     returned = [lax.all_to_all(x, "expert", 0, 0, tiled=True) for x in sums]
     return local(
         functools.partial(combine_kernel, experts, cap),

time: 242 us -> 252 us (1.041); the launches traced: 240 us -> 247 us
  waiting for transfers between devices: 77.7 us -> 95.5 us
  starting transfers between devices: 92.2 us -> 83.2 us
    ppermute x20 -> x19, waiting for transfers between devices: 24.2 us -> 61.6 us  [hop(): return lax.ppermute(x, (axis, 'expert'), perm)]
    all_to_all x2 -> x1, waiting for transfers between devices: 10 us -> 0.01 us  [per_device(): arrived = [lax.all_to_all(x, 'expert', 0, 0, tiled=True) for x in sends]]
    ppermute x20 -> x19, starting transfers between devices: 63.6 us -> 57.3 us  [hop(): return lax.ppermute(x, (axis, 'expert'), perm)]
    all_to_all x2 -> x1, starting transfers between devices: 14 us -> 8.06 us  [per_device(): arrived = [lax.all_to_all(x, 'expert', 0, 0, tiled=True) for x in sends]]
    all_to_all x2 -> x1, waiting for transfers between devices: 31.6 us -> 26.5 us  [per_device(): returned = [lax.all_to_all(x, 'expert', 0, 0, tiled=True) for x in sums]]
    all_to_all x1, waiting for transfers between devices: 11.9 us -> 7.36 us  [per_device(): back = lax.all_to_all(head_output, 'ctx', 0, 0, tiled=True)]
    all_to_all x2 -> x1, starting transfers between devices: 11 us -> 14.3 us  [per_device(): returned = [lax.all_to_all(x, 'expert', 0, 0, tiled=True) for x in sums]]
    pallas_call x3 -> x4, Pallas kernels: 10.2 us -> 9.39 us  [run_experts(): local(functools.partial(expert_kernel, len(pieces)), [jax.ShapeDtypeStruc...]
  transfers between devices with their start and end apart: 25 -> 22, of which waited for: 12 -> 15; matrix products, arithmetic and copies ran while one was open for 1% -> 1% of each run, Pallas kernels for 4% -> 5%
where the time goes in v5:
time: 252 us; the launch traced here: 247 us
  waiting for transfers between devices  95.5 us (38%)
  starting transfers between devices  83.2 us (33%)
  blocking collectives  40.4 us (16%)
  Pallas kernels  22.2 us (9%)
  local copies, waits for them, and re-layouts  3.72 us (1%)
    ppermute x19, waiting for transfers between devices, hop(): return lax.ppermute(x, (axis, 'expert'), perm)  61.6 us
    ppermute x19, starting transfers between devices, hop(): return lax.ppermute(x, (axis, 'expert'), perm)  57.3 us
    all_to_all x1, blocking collectives, per_device(): mixed = lax.all_to_all(packed, 'ctx', 0, 0, tiled=True)  40.4 us
    all_to_all x1, waiting for transfers between devices, per_device(): returned = [lax.all_to_all(x, 'expert', 0, 0, tiled=True) for x in sums]  26.5 us
    all_to_all x1, starting transfers between devices, per_device(): returned = [lax.all_to_all(x, 'expert', 0, 0, tiled=True) for x in sums]  14.3 us
    pallas_call x4, Pallas kernels, run_experts(): local(functools.partial(expert_kernel, len(pieces)), [jax.ShapeDtypeStruc...  9.39 us
    all_to_all x1, starting transfers between devices, per_device(): arrived = [lax.all_to_all(x, 'expert', 0, 0, tiled=True) for x in sends]  8.06 us
    all_to_all x1, waiting for transfers between devices, per_device(): back = lax.all_to_all(head_output, 'ctx', 0, 0, tiled=True)  7.36 us
  transfers between devices with their start and end apart: 22, of which 15 were waited for; matrix products, arithmetic and copies ran while one was open for 1% of the time, Pallas kernels for 5%

profile of v5, /device:TPU:7, one launch (start us, length us, event | category | flops | bytes accessed | tf_op | source)
XLA Modules:
  0.0 247.0 jit_solution(3957944536916696564)
XLA Ops:
  0.0 1.3 copy-done
  1.3 0.3 shard_map.82
  1.5 0.0 copy-start.6
  1.6 0.0 copy-start.7
  1.6 40.4 %all_to_all.30.m_ref = bf16[8,576,128]{2,1,0:T(8,128)(2,1)S(1)} all-to-all(bf16[8,576,128]{2,1,0:T(8,128)(2,1)S(1)} %shard_map.82), channel_id=1, replica_groups=mesh['dp'=4,'ctx'=8,'expert'=16] {'ctx'}, dimensions={0} | all-to-all | bytes 2359296 | tf_op jit(solution)/shard_map/all_to_all | solution.py:315
  41.9 7.3 %shard_map.83 = bf16[8,192,128]{2,1,0:T(8,128)(2,1)} custom-call(bf16[8,576,128]{2,1,0:T(8,128)(2,1)S(1)} %all_to_all.30.m_ref), custom_call_target="tpu_custom_call" | custom-call | tf_op jit(solution)/shard_map/pallas_call | solution.py:317
  49.3 3.5 %all-to-all-start.1 = ((bf16[8,192,128]{2,1,0:T(8,128)(2,1)}), bf16[8,192,128]{2,1,0:T(8,128)(2,1)S(1)}, u32[]{:S(2)}, u32[]{:S(2)}) async-start(bf16[8,192,128]{2,1,0:T(8,128)(2,1)} %shard_map.83), calls=%async_computation.1 | async-start | bytes 786432 | tf_op jit(solution)/shard_map/all_to_all | solution.py:325
  52.8 4.5 %collective-permute-start = (bf16[192,1536]{1,0:T(8,128)(2,1)S(1)}, bf16[192,1536]{1,0:T(8,128)(2,1)S(1)}, u32[]{:S(2)}, u32[]{:S(2)}) collective-permute-start(bf16[192,1536]{1,0:T(8,128)(2,1)S(1)} %shard_map.85.refs_0_), channel_id=1, source_target_pairs={{0,16},{1,113},{2,18},{3,115},{4,20},{5,117},{6,22},{7,119},{8,24}... | collective-permute-start | bytes 1769480 | tf_op jit(solution)/shard_map/ppermute | solution.py:269
  57.3 0.1 copy.9
  57.4 0.1 copy.10.choice_ref
  57.5 7.4 %all-to-all-done.1.b_ref = bf16[8,192,128]{2,1,0:T(8,128)(2,1)S(1)} async-done(((bf16[8,192,128]{2,1,0:T(8,128)(2,1)}), bf16[8,192,128]{2,1,0:T(8,128)(2,1)S(1)}, u32[]{:S(2)}, u32[]{:S(2)}) %all-to-all-start.1) | async-done | bytes 393248 | tf_op jit(solution)/shard_map/all_to_all | solution.py:325
  64.9 1.8 shard_map.84
  66.7 3.6 %collective-permute-done.refs_1_ = bf16[192,1536]{1,0:T(8,128)(2,1)S(1)} collective-permute-done((bf16[192,1536]{1,0:T(8,128)(2,1)S(1)}, bf16[192,1536]{1,0:T(8,128)(2,1)S(1)}, u32[]{:S(2)}, u32[]{:S(2)}) %collective-permute-start) | collective-permute-done | bytes 589856 | tf_op jit(solution)/shard_map/ppermute | solution.py:269
  70.3 2.9 %collective-permute-start.1 = (bf16[192,1536]{1,0:T(8,128)(2,1)S(1)}, bf16[192,1536]{1,0:T(8,128)(2,1)S(1)}, u32[]{:S(2)}, u32[]{:S(2)}) collective-permute-start(bf16[192,1536]{1,0:T(8,128)(2,1)S(1)} %collective-permute-done.refs_1_), channel_id=1, source_target_pairs={{0,16},{1,113},{2,18},{3,115},{4,20},{5,117},{6,22},{7,119},{8,24}... | collective-permute-start | bytes 1769480 | tf_op jit(solution)/shard_map/ppermute | solution.py:269
  73.2 8.1 %all-to-all-start.2 = ((bf16[16,16,1920]{2,1,0:T(8,128)(2,1)}), bf16[16,16,1920]{2,1,0:T(8,128)(2,1)}, u32[]{:S(2)}, u32[]{:S(2)}) async-start(bf16[16,16,1920]{2,1,0:T(8,128)(2,1)} %bitcast.4), calls=%async_computation.2 | async-start | bytes 1966080 | tf_op jit(solution)/shard_map/all_to_all | solution.py:332
  81.3 0.0 collective-permute-done.1.refs_2_
  81.3 4.5 %collective-permute-start.2 = (bf16[192,1536]{1,0:T(8,128)(2,1)S(1)}, bf16[192,1536]{1,0:T(8,128)(2,1)S(1)}, u32[]{:S(2)}, u32[]{:S(2)}) collective-permute-start(bf16[192,1536]{1,0:T(8,128)(2,1)S(1)} %collective-permute-done.1.refs_2_), channel_id=1, source_target_pairs={{0,16},{1,113},{2,18},{3,115},{4,20},{5,117},{6,22},{7,119},{8,24}... | collective-permute-start | bytes 1769480 | tf_op jit(solution)/shard_map/ppermute | solution.py:269
  85.8 6.8 %collective-permute-done.2.refs_3_ = bf16[192,1536]{1,0:T(8,128)(2,1)S(1)} collective-permute-done((bf16[192,1536]{1,0:T(8,128)(2,1)S(1)}, bf16[192,1536]{1,0:T(8,128)(2,1)S(1)}, u32[]{:S(2)}, u32[]{:S(2)}) %collective-permute-start.2) | collective-permute-done | bytes 589856 | tf_op jit(solution)/shard_map/ppermute | solution.py:269
  92.6 5.4 %collective-permute-start.3 = (bf16[192,1536]{1,0:T(8,128)(2,1)S(1)}, bf16[192,1536]{1,0:T(8,128)(2,1)S(1)}, u32[]{:S(2)}, u32[]{:S(2)}) collective-permute-start(bf16[192,1536]{1,0:T(8,128)(2,1)S(1)} %collective-permute-done.2.refs_3_), channel_id=1, source_target_pairs={{0,16},{1,113},{2,18},{3,115},{4,20},{5,117},{6,22},{7,119},{8,24}... | collective-permute-start | bytes 1769480 | tf_op jit(solution)/shard_map/ppermute | solution.py:269
  98.1 6.8 %collective-permute-done.3.refs_4_ = bf16[192,1536]{1,0:T(8,128)(2,1)S(1)} collective-permute-done((bf16[192,1536]{1,0:T(8,128)(2,1)S(1)}, bf16[192,1536]{1,0:T(8,128)(2,1)S(1)}, u32[]{:S(2)}, u32[]{:S(2)}) %collective-permute-start.3) | collective-permute-done | bytes 589856 | tf_op jit(solution)/shard_map/ppermute | solution.py:269
  104.9 5.4 %collective-permute-start.4 = (bf16[192,1536]{1,0:T(8,128)(2,1)S(1)}, bf16[192,1536]{1,0:T(8,128)(2,1)}, u32[]{:S(2)}, u32[]{:S(2)}) collective-permute-start(bf16[192,1536]{1,0:T(8,128)(2,1)S(1)} %collective-permute-done.3.refs_4_), channel_id=1, source_target_pairs={{0,16},{1,113},{2,18},{3,115},{4,20},{5,117},{6,22},{7,119},{8,24}... | collective-permute-start | bytes 1769480 | tf_op jit(solution)/shard_map/ppermute | solution.py:269
  110.3 0.8 copy-done.1
  111.1 6.0 %collective-permute-done.4.refs_5_ = bf16[192,1536]{1,0:T(8,128)(2,1)} collective-permute-done((bf16[192,1536]{1,0:T(8,128)(2,1)S(1)}, bf16[192,1536]{1,0:T(8,128)(2,1)}, u32[]{:S(2)}, u32[]{:S(2)}) %collective-permute-start.4) | collective-permute-done | bytes 589856 | tf_op jit(solution)/shard_map/ppermute | solution.py:269
  117.1 5.1 %collective-permute-start.5 = (bf16[192,1536]{1,0:T(8,128)(2,1)}, bf16[192,1536]{1,0:T(8,128)(2,1)}, u32[]{:S(2)}, u32[]{:S(2)}) collective-permute-start(bf16[192,1536]{1,0:T(8,128)(2,1)} %collective-permute-done.4.refs_5_), channel_id=1, source_target_pairs={{0,16},{1,113},{2,18},{3,115},{4,20},{5,117},{6,22},{7,119},{8,24}... | collective-permute-start | bytes 1769480 | tf_op jit(solution)/shard_map/ppermute | solution.py:269
  122.2 1.3 fusion
  123.6 2.5 collective-permute-start.6
  126.0 2.2 collective-permute-start.7
  128.2 6.5 %collective-permute-done.6.refs_0_ = bf16[128,1920]{1,0:T(8,128)(2,1)S(1)} collective-permute-done((bf16[128,1920]{1,0:T(8,128)(2,1)S(1)}, bf16[128,1920]{1,0:T(8,128)(2,1)S(1)}, u32[]{:S(2)}, u32[]{:S(2)}) %collective-permute-start.6) | collective-permute-done | bytes 491552 | tf_op jit(solution)/shard_map/ppermute | solution.py:269
  134.7 4.9 %collective-permute-done.7.refs_1_ = bf16[128,1920]{1,0:T(8,128)(2,1)S(1)} collective-permute-done((bf16[128,1920]{1,0:T(8,128)(2,1)S(1)}, bf16[128,1920]{1,0:T(8,128)(2,1)S(1)}, u32[]{:S(2)}, u32[]{:S(2)}) %collective-permute-start.7) | collective-permute-done | bytes 491552 | tf_op jit(solution)/shard_map/ppermute | solution.py:269
  139.6 1.9 collective-permute-start.8
  141.5 1.9 collective-permute-start.11
  143.5 1.9 collective-permute-start.9
  145.4 5.3 %collective-permute-done.8.refs_7_ = bf16[192,1536]{1,0:T(8,128)(2,1)S(1)} collective-permute-done((bf16[192,1536]{1,0:T(8,128)(2,1)}, bf16[192,1536]{1,0:T(8,128)(2,1)S(1)}, u32[]{:S(2)}, u32[]{:S(2)}) %collective-permute-start.8) | collective-permute-done | bytes 589856 | tf_op jit(solution)/shard_map/ppermute | solution.py:269
  150.7 1.5 shard_map.86
  152.3 2.3 shard_map.90
  154.6 1.9 collective-permute-start.13
  156.6 1.0 collective-permute-done.9.refs_0_
  157.6 1.9 collective-permute-start.10
  159.5 1.9 collective-permute-start.12
  161.4 4.4 %collective-permute-start.16 = (bf16[128,1920]{1,0:T(8,128)(2,1)S(1)}, bf16[128,1920]{1,0:T(8,128)(2,1)S(1)}, u32[]{:S(2)}, u32[]{:S(2)}) collective-permute-start(bf16[128,1920]{1,0:T(8,128)(2,1)S(1)} %get-tuple-element.34), channel_id=1, source_target_pairs={{0,128},{1,385},{2,130},{3,387},{4,132},{5,389},{6,134},{7,391},{8... | collective-permute-start | bytes 1474568 | tf_op jit(solution)/shard_map/ppermute | solution.py:269
  165.9 2.3 shard_map.89
  168.2 0.1 add_convert_fusion.5
  168.4 2.9 %collective-permute-start.14 = (bf16[128,1920]{1,0:T(8,128)(2,1)S(1)}, bf16[128,1920]{1,0:T(8,128)(2,1)S(1)}, u32[]{:S(2)}, u32[]{:S(2)}) collective-permute-start(bf16[128,1920]{1,0:T(8,128)(2,1)S(1)} %add_convert_fusion.5), channel_id=1, source_target_pairs={{0,128},{1,385},{2,130},{3,387},{4,132},{5,389},{6,134},{7,391},{8... | collective-permute-start | bytes 1474568 | tf_op jit(solution)/shard_map/ppermute | solution.py:269
  171.3 10.0 %collective-permute-done.16 = bf16[128,1920]{1,0:T(8,128)(2,1)S(1)} collective-permute-done((bf16[128,1920]{1,0:T(8,128)(2,1)S(1)}, bf16[128,1920]{1,0:T(8,128)(2,1)S(1)}, u32[]{:S(2)}, u32[]{:S(2)}) %collective-permute-start.16) | collective-permute-done | bytes 491552 | tf_op jit(solution)/shard_map/ppermute | solution.py:269
  181.2 0.1 add_convert_fusion.2
  181.3 1.9 collective-permute-start.17
  183.3 2.3 shard_map.88
  185.6 0.8 collective-permute-done.14
  186.5 0.1 add_convert_fusion.4
  186.6 1.9 collective-permute-start.15
  188.5 3.6 %collective-permute-done.17 = bf16[128,1920]{1,0:T(8,128)(2,1)S(1)} collective-permute-done((bf16[128,1920]{1,0:T(8,128)(2,1)S(1)}, bf16[128,1920]{1,0:T(8,128)(2,1)S(1)}, u32[]{:S(2)}, u32[]{:S(2)}) %collective-permute-start.17) | collective-permute-done | bytes 491552 | tf_op jit(solution)/shard_map/ppermute | solution.py:269
  192.1 0.1 add_convert_fusion.1
  192.3 2.1 collective-permute-start.18
  194.4 2.3 shard_map.87
  196.7 0.7 collective-permute-done.15
  197.4 0.1 add_convert_fusion.3
  197.5 5.5 %collective-permute-done.18 = bf16[128,1920]{1,0:T(8,128)(2,1)S(1)} collective-permute-done((bf16[128,1920]{1,0:T(8,128)(2,1)S(1)}, bf16[128,1920]{1,0:T(8,128)(2,1)S(1)}, u32[]{:S(2)}, u32[]{:S(2)}) %collective-permute-start.18) | collective-permute-done | bytes 491552 | tf_op jit(solution)/shard_map/ppermute | solution.py:269
  203.0 0.1 add_convert_fusion
  203.2 0.0 copy-start.11
  203.2 1.0 pad_maximum_fusion
  204.2 14.3 %all-to-all-start.3 = ((bf16[16,16,1920]{2,1,0:T(8,128)(2,1)}), bf16[16,16,1920]{2,1,0:T(8,128)(2,1)S(1)}, u32[]{:S(2)}, u32[]{:S(2)}) async-start(bf16[16,16,1920]{2,1,0:T(8,128)(2,1)} %bitcast.7), calls=%async_computation.3 | async-start | bytes 1966080 | tf_op jit(solution)/shard_map/all_to_all | solution.py:343
  218.5 0.1 copy.11
  218.7 26.5 %all-to-all-done.3 = bf16[16,16,1920]{2,1,0:T(8,128)(2,1)S(1)} async-done(((bf16[16,16,1920]{2,1,0:T(8,128)(2,1)}), bf16[16,16,1920]{2,1,0:T(8,128)(2,1)S(1)}, u32[]{:S(2)}, u32[]{:S(2)}) %all-to-all-start.3) | async-done | bytes 983072 | tf_op jit(solution)/shard_map/all_to_all | solution.py:343
  245.2 1.8 shard_map.91
  (26 shorter events, 0.1 us)
Async XLA Ops:
  0.0 1.3 copy-start
  1.5 51.2 %copy-start.6 = (bf16[1,96,1536]{2,1,0:T(8,128)(2,1)S(1)}, bf16[1,96,1536]{2,1,0:T(8,128)(2,1)}, u32[]{:S(2)}) copy-start(bf16[1,96,1536]{2,1,0:T(8,128)(2,1)} %in_ref.1) | copy-start | bytes 884740
  1.6 51.2 %copy-start.7 = (bf16[1,96,1536]{2,1,0:T(8,128)(2,1)S(1)}, bf16[1,96,1536]{2,1,0:T(8,128)(2,1)}, u32[]{:S(2)}) copy-start(bf16[1,96,1536]{2,1,0:T(8,128)(2,1)} %out_ref.1) | copy-start | bytes 884740
  41.9 15.4 %copy-start.10 = (s32[1,128,2]{1,2,0:T(2,128)S(1)}, s32[1,128,2]{1,2,0:T(2,128)}, u32[]{:S(2)}) copy-start(s32[1,128,2]{1,2,0:T(2,128)} %param.12) | copy-start | bytes 3076
  41.9 22.9 %copy-start.5 = (bf16[1,128,1536]{2,1,0:T(8,128)(2,1)S(1)}, bf16[1,128,1536]{2,1,0:T(8,128)(2,1)}, u32[]{:S(2)}) copy-start(bf16[1,128,1536]{2,1,0:T(8,128)(2,1)} %param.9) | copy-start | bytes 1179652
  41.9 22.9 %copy-start.8 = (f32[1,1536]{1,0:T(1,128)S(1)}, f32[1,1536]{1,0:T(1,128)}, u32[]{:S(2)}) copy-start(f32[1,1536]{1,0:T(1,128)} %scale_ref.1) | copy-start | bytes 18436
  41.9 22.9 %copy-start.9 = (f32[1,1536]{1,0:T(1,128)S(1)}, f32[1,1536]{1,0:T(1,128)}, u32[]{:S(2)}) copy-start(f32[1,1536]{1,0:T(1,128)} %shift_ref.1) | copy-start | bytes 18436
  49.3 15.6 %all-to-all-start.1 = ((bf16[8,192,128]{2,1,0:T(8,128)(2,1)}), bf16[8,192,128]{2,1,0:T(8,128)(2,1)S(1)}, u32[]{:S(2)}, u32[]{:S(2)}) async-start(bf16[8,192,128]{2,1,0:T(8,128)(2,1)} %shard_map.83), calls=%async_computation.1 | async-start | bytes 786432 | tf_op jit(solution)/shard_map/all_to_all | solution.py:325
  52.8 17.5 %collective-permute-start = (bf16[192,1536]{1,0:T(8,128)(2,1)S(1)}, bf16[192,1536]{1,0:T(8,128)(2,1)S(1)}, u32[]{:S(2)}, u32[]{:S(2)}) collective-permute-start(bf16[192,1536]{1,0:T(8,128)(2,1)S(1)} %shard_map.85.refs_0_), channel_id=1, source_target_pairs={{0,16},{1,113},{2,18},{3,115},{4,20},{5,117},{6,22},{7,119},{8,24}... | collective-permute-start | bytes 1769480 | tf_op jit(solution)/shard_map/ppermute | solution.py:269
  57.4 7.4 %copy-start.3 = (s32[1,128,2]{2,1,0:T(8,128)}, s32[1,128,2]{2,1,0:T(8,128)S(1)}, u32[]{:S(2)}) copy-start(s32[1,128,2]{2,1,0:T(8,128)S(1)} %copy.9) | copy-start | bytes 3076
  70.3 11.0 %collective-permute-start.1 = (bf16[192,1536]{1,0:T(8,128)(2,1)S(1)}, bf16[192,1536]{1,0:T(8,128)(2,1)S(1)}, u32[]{:S(2)}, u32[]{:S(2)}) collective-permute-start(bf16[192,1536]{1,0:T(8,128)(2,1)S(1)} %collective-permute-done.refs_1_), channel_id=1, source_target_pairs={{0,16},{1,113},{2,18},{3,115},{4,20},{5,117},{6,22},{7,119},{8,24}... | collective-permute-start | bytes 1769480 | tf_op jit(solution)/shard_map/ppermute | solution.py:269
  73.2 49.0 %all-to-all-start.2 = ((bf16[16,16,1920]{2,1,0:T(8,128)(2,1)}), bf16[16,16,1920]{2,1,0:T(8,128)(2,1)}, u32[]{:S(2)}, u32[]{:S(2)}) async-start(bf16[16,16,1920]{2,1,0:T(8,128)(2,1)} %bitcast.4), calls=%async_computation.2 | async-start | bytes 1966080 | tf_op jit(solution)/shard_map/all_to_all | solution.py:332
  81.3 11.3 %collective-permute-start.2 = (bf16[192,1536]{1,0:T(8,128)(2,1)S(1)}, bf16[192,1536]{1,0:T(8,128)(2,1)S(1)}, u32[]{:S(2)}, u32[]{:S(2)}) collective-permute-start(bf16[192,1536]{1,0:T(8,128)(2,1)S(1)} %collective-permute-done.1.refs_2_), channel_id=1, source_target_pairs={{0,16},{1,113},{2,18},{3,115},{4,20},{5,117},{6,22},{7,119},{8,24}... | collective-permute-start | bytes 1769480 | tf_op jit(solution)/shard_map/ppermute | solution.py:269
  92.6 12.2 %collective-permute-start.3 = (bf16[192,1536]{1,0:T(8,128)(2,1)S(1)}, bf16[192,1536]{1,0:T(8,128)(2,1)S(1)}, u32[]{:S(2)}, u32[]{:S(2)}) collective-permute-start(bf16[192,1536]{1,0:T(8,128)(2,1)S(1)} %collective-permute-done.2.refs_3_), channel_id=1, source_target_pairs={{0,16},{1,113},{2,18},{3,115},{4,20},{5,117},{6,22},{7,119},{8,24}... | collective-permute-start | bytes 1769480 | tf_op jit(solution)/shard_map/ppermute | solution.py:269
  104.9 12.2 %collective-permute-start.4 = (bf16[192,1536]{1,0:T(8,128)(2,1)S(1)}, bf16[192,1536]{1,0:T(8,128)(2,1)}, u32[]{:S(2)}, u32[]{:S(2)}) collective-permute-start(bf16[192,1536]{1,0:T(8,128)(2,1)S(1)} %collective-permute-done.3.refs_4_), channel_id=1, source_target_pairs={{0,16},{1,113},{2,18},{3,115},{4,20},{5,117},{6,22},{7,119},{8,24}... | collective-permute-start | bytes 1769480 | tf_op jit(solution)/shard_map/ppermute | solution.py:269
  110.3 0.8 copy-start.1
  117.1 22.5 %collective-permute-start.5 = (bf16[192,1536]{1,0:T(8,128)(2,1)}, bf16[192,1536]{1,0:T(8,128)(2,1)}, u32[]{:S(2)}, u32[]{:S(2)}) collective-permute-start(bf16[192,1536]{1,0:T(8,128)(2,1)} %collective-permute-done.4.refs_5_), channel_id=1, source_target_pairs={{0,16},{1,113},{2,18},{3,115},{4,20},{5,117},{6,22},{7,119},{8,24}... | collective-permute-start | bytes 1769480 | tf_op jit(solution)/shard_map/ppermute | solution.py:269
  122.2 28.5 %copy-start.2 = (bf16[192,1536]{1,0:T(8,128)(2,1)S(1)}, bf16[192,1536]{1,0:T(8,128)(2,1)}, u32[]{:S(2)}) copy-start(bf16[192,1536]{1,0:T(8,128)(2,1)} %copy-done.1) | copy-start | bytes 1769476
  123.6 11.2 %collective-permute-start.6 = (bf16[128,1920]{1,0:T(8,128)(2,1)S(1)}, bf16[128,1920]{1,0:T(8,128)(2,1)S(1)}, u32[]{:S(2)}, u32[]{:S(2)}) collective-permute-start(bf16[128,1920]{1,0:T(8,128)(2,1)S(1)} %bitcast.13), channel_id=1, source_target_pairs={{0,128},{1,385},{2,130},{3,387},{4,132},{5,389},{6,134},{7,391},{8... | collective-permute-start | bytes 1474568 | tf_op jit(solution)/shard_map/ppermute | solution.py:269
  126.0 13.6 %collective-permute-start.7 = (bf16[128,1920]{1,0:T(8,128)(2,1)S(1)}, bf16[128,1920]{1,0:T(8,128)(2,1)S(1)}, u32[]{:S(2)}, u32[]{:S(2)}) collective-permute-start(bf16[128,1920]{1,0:T(8,128)(2,1)S(1)} %bitcast.11), channel_id=1, source_target_pairs={{0,128},{1,385},{2,130},{3,387},{4,132},{5,389},{6,134},{7,391},{8... | collective-permute-start | bytes 1474568 | tf_op jit(solution)/shard_map/ppermute | solution.py:269
  139.6 11.1 %collective-permute-start.8 = (bf16[192,1536]{1,0:T(8,128)(2,1)}, bf16[192,1536]{1,0:T(8,128)(2,1)S(1)}, u32[]{:S(2)}, u32[]{:S(2)}) collective-permute-start(bf16[192,1536]{1,0:T(8,128)(2,1)} %collective-permute-done.5.refs_6_), channel_id=1, source_target_pairs={{0,16},{1,113},{2,18},{3,115},{4,20},{5,117},{6,22},{7,119},{8,24}... | collective-permute-start | bytes 1769480 | tf_op jit(solution)/shard_map/ppermute | solution.py:269
  141.5 18.0 %collective-permute-start.11 = (bf16[128,1920]{1,0:T(8,128)(2,1)S(1)}, bf16[128,1920]{1,0:T(8,128)(2,1)S(1)}, u32[]{:S(2)}, u32[]{:S(2)}) collective-permute-start(bf16[128,1920]{1,0:T(8,128)(2,1)S(1)} %collective-permute-done.7.refs_1_), channel_id=1, source_target_pairs={{0,128},{1,385},{2,130},{3,387},{4,132},{5,389},{6,134},{7,391},{8... | collective-permute-start | bytes 1474568 | tf_op jit(solution)/shard_map/ppermute | solution.py:269
  143.5 14.1 %collective-permute-start.9 = (bf16[128,1920]{1,0:T(8,128)(2,1)S(1)}, bf16[128,1920]{1,0:T(8,128)(2,1)S(1)}, u32[]{:S(2)}, u32[]{:S(2)}) collective-permute-start(bf16[128,1920]{1,0:T(8,128)(2,1)S(1)} %collective-permute-done.6.refs_0_), channel_id=1, source_target_pairs={{0,128},{1,385},{2,130},{3,387},{4,132},{5,389},{6,134},{7,391},{8... | collective-permute-start | bytes 1474568 | tf_op jit(solution)/shard_map/ppermute | solution.py:269
  154.6 13.6 %collective-permute-start.13 = (bf16[128,1920]{1,0:T(8,128)(2,1)S(1)}, bf16[128,1920]{1,0:T(8,128)(2,1)S(1)}, u32[]{:S(2)}, u32[]{:S(2)}) collective-permute-start(bf16[128,1920]{1,0:T(8,128)(2,1)S(1)} %get-tuple-element.30), channel_id=1, source_target_pairs={{0,128},{1,385},{2,130},{3,387},{4,132},{5,389},{6,134},{7,391},{8... | collective-permute-start | bytes 1474568 | tf_op jit(solution)/shard_map/ppermute | solution.py:269
  157.6 25.7 %collective-permute-start.10 = (bf16[128,1920]{1,0:T(8,128)(2,1)S(1)}, bf16[128,1920]{1,0:T(8,128)(2,1)S(1)}, u32[]{:S(2)}, u32[]{:S(2)}) collective-permute-start(bf16[128,1920]{1,0:T(8,128)(2,1)S(1)} %collective-permute-done.9.refs_0_), channel_id=1, source_target_pairs={{0,128},{1,385},{2,130},{3,387},{4,132},{5,389},{6,134},{7,391},{8... | collective-permute-start | bytes 1474568 | tf_op jit(solution)/shard_map/ppermute | solution.py:269
  159.5 23.8 %collective-permute-start.12 = (bf16[128,1920]{1,0:T(8,128)(2,1)S(1)}, bf16[128,1920]{1,0:T(8,128)(2,1)S(1)}, u32[]{:S(2)}, u32[]{:S(2)}) collective-permute-start(bf16[128,1920]{1,0:T(8,128)(2,1)S(1)} %collective-permute-done.11.refs_1_), channel_id=1, source_target_pairs={{0,128},{1,385},{2,130},{3,387},{4,132},{5,389},{6,134},{7,391},{8... | collective-permute-start | bytes 1474568 | tf_op jit(solution)/shard_map/ppermute | solution.py:269
  161.4 19.8 %collective-permute-start.16 = (bf16[128,1920]{1,0:T(8,128)(2,1)S(1)}, bf16[128,1920]{1,0:T(8,128)(2,1)S(1)}, u32[]{:S(2)}, u32[]{:S(2)}) collective-permute-start(bf16[128,1920]{1,0:T(8,128)(2,1)S(1)} %get-tuple-element.34), channel_id=1, source_target_pairs={{0,128},{1,385},{2,130},{3,387},{4,132},{5,389},{6,134},{7,391},{8... | collective-permute-start | bytes 1474568 | tf_op jit(solution)/shard_map/ppermute | solution.py:269
  168.4 18.1 %collective-permute-start.14 = (bf16[128,1920]{1,0:T(8,128)(2,1)S(1)}, bf16[128,1920]{1,0:T(8,128)(2,1)S(1)}, u32[]{:S(2)}, u32[]{:S(2)}) collective-permute-start(bf16[128,1920]{1,0:T(8,128)(2,1)S(1)} %add_convert_fusion.5), channel_id=1, source_target_pairs={{0,128},{1,385},{2,130},{3,387},{4,132},{5,389},{6,134},{7,391},{8... | collective-permute-start | bytes 1474568 | tf_op jit(solution)/shard_map/ppermute | solution.py:269
  181.3 10.8 %collective-permute-start.17 = (bf16[128,1920]{1,0:T(8,128)(2,1)S(1)}, bf16[128,1920]{1,0:T(8,128)(2,1)S(1)}, u32[]{:S(2)}, u32[]{:S(2)}) collective-permute-start(bf16[128,1920]{1,0:T(8,128)(2,1)S(1)} %add_convert_fusion.2), channel_id=1, source_target_pairs={{0,128},{1,385},{2,130},{3,387},{4,132},{5,389},{6,134},{7,391},{8... | collective-permute-start | bytes 1474568 | tf_op jit(solution)/shard_map/ppermute | solution.py:269
  186.6 10.8 %collective-permute-start.15 = (bf16[128,1920]{1,0:T(8,128)(2,1)S(1)}, bf16[128,1920]{1,0:T(8,128)(2,1)S(1)}, u32[]{:S(2)}, u32[]{:S(2)}) collective-permute-start(bf16[128,1920]{1,0:T(8,128)(2,1)S(1)} %add_convert_fusion.4), channel_id=1, source_target_pairs={{0,128},{1,385},{2,130},{3,387},{4,132},{5,389},{6,134},{7,391},{8... | collective-permute-start | bytes 1474568 | tf_op jit(solution)/shard_map/ppermute | solution.py:269
  192.3 10.8 %collective-permute-start.18 = (bf16[128,1920]{1,0:T(8,128)(2,1)S(1)}, bf16[128,1920]{1,0:T(8,128)(2,1)S(1)}, u32[]{:S(2)}, u32[]{:S(2)}) collective-permute-start(bf16[128,1920]{1,0:T(8,128)(2,1)S(1)} %add_convert_fusion.1), channel_id=1, source_target_pairs={{0,128},{1,385},{2,130},{3,387},{4,132},{5,389},{6,134},{7,391},{8... | collective-permute-start | bytes 1474568 | tf_op jit(solution)/shard_map/ppermute | solution.py:269
  203.2 15.4 %copy-start.11 = (f32[1,128,2]{1,2,0:T(2,128)S(1)}, f32[1,128,2]{1,2,0:T(2,128)}, u32[]{:S(2)}) copy-start(f32[1,128,2]{1,2,0:T(2,128)} %param.13) | copy-start | bytes 3076
  203.2 42.0 %copy-start.4 = (s32[1,128,2]{2,1,0:T(8,128)S(1)}, s32[1,128,2]{2,1,0:T(8,128)}, u32[]{:S(2)}) copy-start(s32[1,128,2]{2,1,0:T(8,128)} %copy-done.3) | copy-start | bytes 3076
  204.2 40.9 %all-to-all-start.3 = ((bf16[16,16,1920]{2,1,0:T(8,128)(2,1)}), bf16[16,16,1920]{2,1,0:T(8,128)(2,1)S(1)}, u32[]{:S(2)}, u32[]{:S(2)}) async-start(bf16[16,16,1920]{2,1,0:T(8,128)(2,1)} %bitcast.7), calls=%async_computation.3 | async-start | bytes 1966080 | tf_op jit(solution)/shard_map/all_to_all | solution.py:343

commit v6 on v4

--- a/solution.py
+++ b/solution.py
@@ -8,7 +8,7 @@
 from jax.sharding import PartitionSpec as P
 
 HD = 64
-CHUNKS = 2
+CHUNKS = 1
 BF = jnp.bfloat16
 F32 = jnp.float32
 LIMIT = 24 * 1024 * 1024
@@ -273,12 +273,12 @@
     return lax.optimization_barrier((x, *others))[0]
 
 
-def ring_in(a, b):
-    left_a, right_a = shift(a, "dp", 1), shift(a, "dp", -1)
-    across_a = shift(left_a, "dp", 1)
-    b = after(b, left_a, right_a)
-    left_b, right_b = shift(b, "dp", 1), shift(b, "dp", -1)
-    across_b = shift(right_b, "dp", -1)
+def ring_in(x):
+    half = x.shape[0] // 2
+    a, b = x[:half], x[half:]
+    left_a, right_b = shift(a, "dp", 1), shift(b, "dp", -1)
+    left_b, right_a = shift(b, "dp", 1), shift(a, "dp", -1)
+    across_a, across_b = shift(left_a, "dp", 1), shift(right_b, "dp", -1)
     return (a, b), (left_a, left_b, right_a, right_b), (across_a, across_b)
 
 
@@ -292,7 +292,7 @@
     sum_a, sum_b = shift(via_a, "dp", 1), shift(via_b, "dp", -1)
     own = after(own, via_a, via_b)
     own_a, own_b = run_experts(own, *weights, plus=(got_a, got_b))
-    return add(own_a, sum_a), add(own_b, sum_b)
+    return jnp.concatenate([add(own_a, sum_a), add(own_b, sum_b)])
 
 
 def per_device(
@@ -315,6 +315,8 @@
         expert_in, expert_out
     )
     mixed = lax.all_to_all(packed, "ctx", 0, 0, tiled=True)
+    up, down = [shift(block, "ctx", 1)], [shift(block, "ctx", -1)]
+    mixed, up[0], down[0] = lax.optimization_barrier((mixed, up[0], down[0]))
     group = 2
     head_output = local(
         attend_kernel,
@@ -331,19 +333,19 @@
         functools.partial(dispatch_kernel, experts, cap),
         [jax.ShapeDtypeStruct((t, width), F32)] + [jax.ShapeDtypeStruct(wide, BF)] * CHUNKS,
     )(back, residual_in[0], modulation_scale, modulation_shift, expert_choice[0].T)
-    block = after(block, *sends)
-    up, down = [shift(block, "ctx", 1)], [shift(block, "ctx", -1)]
+    up[0], down[0] = after(up[0], *sends), after(down[0], *sends)
     arrived = [lax.all_to_all(x, "expert", 0, 0, tiled=True) for x in sends]
     for _ in range(n // 2 - 2):
         up.append(shift(up[-1], "ctx", 1))
         down.append(shift(down[-1], "ctx", -1))
     ring = ring_in(*arrived)
+    up[-1], down[-1] = after((up[-1], down[-1]), ring[0])
     far_in = shift(up[-1][:slice_rows], "ctx", 1)
     far_out = shift(down[-1][slice_rows:], "ctx", -1)
     weights = local(
         assemble_kernel, [jax.ShapeDtypeStruct((n * slice_rows, width), BF)] * 2
     )(far_in, far_out, block, *up, *down)
-    sums = expert_layer(*ring, weights)
+    sums = [expert_layer(*ring, weights)]
     returned = [lax.all_to_all(x, "expert", 0, 0, tiled=True) for x in sums]
     return local(
         functools.partial(combine_kernel, experts, cap),

time: 242 us -> 239 us (0.988)
  blocking collectives: 40.2 us -> 0 us
  waiting for transfers between devices: 77.7 us -> 117 us
    ppermute x20, waiting for transfers between devices: 24.2 us -> 71 us  [shift(): return lax.ppermute(x, axis, [(i, (i + by) % n) for i in range(n)])]
    all_to_all x1 -> x0, blocking collectives: 40.2 us -> none  [per_device(): mixed = lax.all_to_all(packed, 'ctx', 0, 0, tiled=True)]
    all_to_all x0 -> x1, starting transfers between devices: none -> 10 us  [per_device(): mixed = lax.all_to_all(packed, 'ctx', 0, 0, tiled=True)]
    all_to_all x2 -> x1, starting transfers between devices: 14 us -> 7.68 us  [per_device(): arrived = [lax.all_to_all(x, 'expert', 0, 0, tiled=True) for x in sends]]
    all_to_all x2 -> x1, waiting for transfers between devices: 10 us -> 4.63 us  [per_device(): arrived = [lax.all_to_all(x, 'expert', 0, 0, tiled=True) for x in sends]]
    ppermute x20, starting transfers between devices: 63.6 us -> 58.5 us  [shift(): return lax.ppermute(x, axis, [(i, (i + by) % n) for i in range(n)])]
    all_to_all x2 -> x1, waiting for transfers between devices: 31.6 us -> 26.5 us  [per_device(): returned = [lax.all_to_all(x, 'expert', 0, 0, tiled=True) for x in sums]]
    all_to_all x1, waiting for transfers between devices: 11.9 us -> 14.9 us  [per_device(): back = lax.all_to_all(head_output, 'ctx', 0, 0, tiled=True)]
  transfers between devices with their start and end apart: 25 -> 24, of which waited for: 12 -> 11; matrix products, arithmetic and copies ran while one was open for 1% -> 1% of each run, Pallas kernels for 4% -> 3%
where the time goes in v6:
time: 239 us; the launch traced here: 238 us
  waiting for transfers between devices  117 us (49%)
  starting transfers between devices  92.2 us (39%)
  Pallas kernels  22.8 us (10%)
  local copies, waits for them, and re-layouts  3.94 us (2%)
    ppermute x20, waiting for transfers between devices, shift(): return lax.ppermute(x, axis, [(i, (i + by) % n) for i in range(n)])  71 us
    ppermute x20, starting transfers between devices, shift(): return lax.ppermute(x, axis, [(i, (i + by) % n) for i in range(n)])  58.5 us
    all_to_all x1, waiting for transfers between devices, per_device(): returned = [lax.all_to_all(x, 'expert', 0, 0, tiled=True) for x in sums]  26.5 us
    all_to_all x1, waiting for transfers between devices, per_device(): back = lax.all_to_all(head_output, 'ctx', 0, 0, tiled=True)  14.9 us
    all_to_all x1, starting transfers between devices, per_device(): returned = [lax.all_to_all(x, 'expert', 0, 0, tiled=True) for x in sums]  10.8 us
    all_to_all x1, starting transfers between devices, per_device(): mixed = lax.all_to_all(packed, 'ctx', 0, 0, tiled=True)  10 us
    pallas_call x3, Pallas kernels, run_experts(): local(functools.partial(expert_kernel, len(pieces)), [jax.ShapeDtypeStruc...  9 us
    all_to_all x1, starting transfers between devices, per_device(): arrived = [lax.all_to_all(x, 'expert', 0, 0, tiled=True) for x in sends]  7.68 us
  transfers between devices with their start and end apart: 24, of which 11 were waited for; matrix products, arithmetic and copies ran while one was open for 1% of the time, Pallas kernels for 3%

profile of v6, /device:TPU:7, one launch (start us, length us, event | category | flops | bytes accessed | tf_op | source)
XLA Modules:
  0.0 237.8 jit_solution(5730197802102969596)
XLA Ops:
  0.0 1.3 copy-done
  1.3 1.3 shard_map.82
  2.6 10.0 %all-to-all-start = ((bf16[8,576,128]{2,1,0:T(8,128)(2,1)}), bf16[8,576,128]{2,1,0:T(8,128)(2,1)S(1)}, u32[]{:S(2)}, u32[]{:S(2)}) async-start(bf16[8,576,128]{2,1,0:T(8,128)(2,1)} %shard_map.82), calls=%async_computation | async-start | bytes 2359296 | tf_op jit(solution)/shard_map/all_to_all | solution.py:317
  12.6 0.0 copy-start.9
  12.6 0.0 copy-start.7
  12.7 0.0 copy-start.8
  12.7 3.4 %collective-permute-start = (bf16[192,1536]{1,0:T(8,128)(2,1)S(1)}, bf16[192,1536]{1,0:T(8,128)(2,1)S(1)}, u32[]{:S(2)}, u32[]{:S(2)}) collective-permute-start(bf16[192,1536]{1,0:T(8,128)(2,1)S(1)} %shard_map.83.refs_2_), channel_id=1, source_target_pairs={{0,16},{16,32},{32,48},{48,64},{64,80},{80,96},{96,112},{112,0},{1... | collective-permute-start | bytes 1769480 | tf_op jit(solution)/shard_map/ppermute | solution.py:269
  16.1 3.1 %collective-permute-start.1 = (bf16[192,1536]{1,0:T(8,128)(2,1)S(1)}, bf16[192,1536]{1,0:T(8,128)(2,1)S(1)}, u32[]{:S(2)}, u32[]{:S(2)}) collective-permute-start(bf16[192,1536]{1,0:T(8,128)(2,1)S(1)} %shard_map.83.refs_2_), channel_id=1, source_target_pairs={{0,112},{16,0},{32,16},{48,32},{64,48},{80,64},{96,80},{112,96},{1... | collective-permute-start | bytes 1769480 | tf_op jit(solution)/shard_map/ppermute | solution.py:269
  19.2 34.4 %collective-permute-done.refs_3_ = bf16[192,1536]{1,0:T(8,128)(2,1)S(1)} collective-permute-done((bf16[192,1536]{1,0:T(8,128)(2,1)S(1)}, bf16[192,1536]{1,0:T(8,128)(2,1)S(1)}, u32[]{:S(2)}, u32[]{:S(2)}) %collective-permute-start) | collective-permute-done | bytes 589856 | tf_op jit(solution)/shard_map/ppermute | solution.py:269
  53.6 0.0 collective-permute-done.1.refs_6_
  53.6 0.0 all-to-all-done.m_ref
  53.6 7.3 %shard_map.84 = bf16[8,192,128]{2,1,0:T(8,128)(2,1)} custom-call(bf16[8,576,128]{2,1,0:T(8,128)(2,1)S(1)} %all-to-all-done.m_ref), custom_call_target="tpu_custom_call" | custom-call | tf_op jit(solution)/shard_map/pallas_call | solution.py:321
  61.0 5.3 %all-to-all-start.1 = ((bf16[8,192,128]{2,1,0:T(8,128)(2,1)}), bf16[8,192,128]{2,1,0:T(8,128)(2,1)S(1)}, u32[]{:S(2)}, u32[]{:S(2)}) async-start(bf16[8,192,128]{2,1,0:T(8,128)(2,1)} %shard_map.84), calls=%async_computation.1 | async-start | bytes 786432 | tf_op jit(solution)/shard_map/all_to_all | solution.py:329
  66.2 0.1 copy.9
  66.3 0.1 copy.10.choice_ref
  66.4 14.9 %all-to-all-done.1.b_ref = bf16[8,192,128]{2,1,0:T(8,128)(2,1)S(1)} async-done(((bf16[8,192,128]{2,1,0:T(8,128)(2,1)}), bf16[8,192,128]{2,1,0:T(8,128)(2,1)S(1)}, u32[]{:S(2)}, u32[]{:S(2)}) %all-to-all-start.1) | async-done | bytes 393248 | tf_op jit(solution)/shard_map/all_to_all | solution.py:329
  81.3 0.0 copy-start.4
  81.3 1.0 copy-done.4
  82.3 1.8 shard_map.85
  84.1 7.7 %all-to-all-start.2 = ((bf16[16,16,1920]{2,1,0:T(8,128)(2,1)}), bf16[16,16,1920]{2,1,0:T(8,128)(2,1)}, u32[]{:S(2)}, u32[]{:S(2)}) async-start(bf16[16,16,1920]{2,1,0:T(8,128)(2,1)} %bitcast.4), calls=%async_computation.2 | async-start | bytes 1966080 | tf_op jit(solution)/shard_map/all_to_all | solution.py:337
  91.8 1.9 collective-permute-start.4
  93.7 3.4 %collective-permute-start.2 = (bf16[192,1536]{1,0:T(8,128)(2,1)S(1)}, bf16[192,1536]{1,0:T(8,128)(2,1)}, u32[]{:S(2)}, u32[]{:S(2)}) collective-permute-start(bf16[192,1536]{1,0:T(8,128)(2,1)S(1)} %collective-permute-done.refs_3_), channel_id=1, source_target_pairs={{0,16},{16,32},{32,48},{48,64},{64,80},{80,96},{96,112},{112,0},{1... | collective-permute-start | bytes 1769480 | tf_op jit(solution)/shard_map/ppermute | solution.py:269
  97.1 11.5 %collective-permute-done.4.refs_7_ = bf16[192,1536]{1,0:T(8,128)(2,1)} collective-permute-done((bf16[192,1536]{1,0:T(8,128)(2,1)S(1)}, bf16[192,1536]{1,0:T(8,128)(2,1)}, u32[]{:S(2)}, u32[]{:S(2)}) %collective-permute-start.4) | collective-permute-done | bytes 589856 | tf_op jit(solution)/shard_map/ppermute | solution.py:269
  108.5 3.4 %collective-permute-start.5 = (bf16[192,1536]{1,0:T(8,128)(2,1)}, bf16[192,1536]{1,0:T(8,128)(2,1)S(1)}, u32[]{:S(2)}, u32[]{:S(2)}) collective-permute-start(bf16[192,1536]{1,0:T(8,128)(2,1)} %collective-permute-done.4.refs_7_), channel_id=1, source_target_pairs={{0,112},{16,0},{32,16},{48,32},{64,48},{80,64},{96,80},{112,96},{1... | collective-permute-start | bytes 1769480 | tf_op jit(solution)/shard_map/ppermute | solution.py:269
  111.9 0.0 collective-permute-done.2.refs_4_
  111.9 1.9 collective-permute-start.3
  113.8 4.6 %all-to-all-done.2 = bf16[16,16,1920]{2,1,0:T(8,128)(2,1)} async-done(((bf16[16,16,1920]{2,1,0:T(8,128)(2,1)}), bf16[16,16,1920]{2,1,0:T(8,128)(2,1)}, u32[]{:S(2)}, u32[]{:S(2)}) %all-to-all-start.2) | async-done | bytes 983072 | tf_op jit(solution)/shard_map/all_to_all | solution.py:337
  118.5 1.3 fusion
  119.8 2.1 collective-permute-start.8
  121.9 3.2 %collective-permute-start.11 = (bf16[128,1920]{1,0:T(8,128)(2,1)S(1)}, bf16[128,1920]{1,0:T(8,128)(2,1)S(1)}, u32[]{:S(2)}, u32[]{:S(2)}) collective-permute-start(bf16[128,1920]{1,0:T(8,128)(2,1)S(1)} %bitcast.11), channel_id=1, source_target_pairs={{0,384},{128,0},{256,128},{384,256},{1,385},{129,1},{257,129},{385... | collective-permute-start | bytes 1474568 | tf_op jit(solution)/shard_map/ppermute | solution.py:269
  125.1 0.0 collective-permute-done.5.refs_8_
  125.1 3.9 %collective-permute-done.3.refs_5_ = bf16[192,1536]{1,0:T(8,128)(2,1)S(1)} collective-permute-done((bf16[192,1536]{1,0:T(8,128)(2,1)}, bf16[192,1536]{1,0:T(8,128)(2,1)S(1)}, u32[]{:S(2)}, u32[]{:S(2)}) %collective-permute-start.3) | collective-permute-done | bytes 589856 | tf_op jit(solution)/shard_map/ppermute | solution.py:269
  129.1 1.9 collective-permute-start.6
  131.0 2.5 %collective-permute-start.10 = (bf16[128,1920]{1,0:T(8,128)(2,1)S(1)}, bf16[128,1920]{1,0:T(8,128)(2,1)S(1)}, u32[]{:S(2)}, u32[]{:S(2)}) collective-permute-start(bf16[128,1920]{1,0:T(8,128)(2,1)S(1)} %bitcast.15), channel_id=1, source_target_pairs={{0,384},{128,0},{256,128},{384,256},{1,385},{129,1},{257,129},{385... | collective-permute-start | bytes 1474568 | tf_op jit(solution)/shard_map/ppermute | solution.py:269
  133.5 4.0 %collective-permute-start.9 = (bf16[128,1920]{1,0:T(8,128)(2,1)S(1)}, bf16[128,1920]{1,0:T(8,128)(2,1)S(1)}, u32[]{:S(2)}, u32[]{:S(2)}) collective-permute-start(bf16[128,1920]{1,0:T(8,128)(2,1)S(1)} %bitcast.12), channel_id=1, source_target_pairs={{0,128},{128,256},{256,384},{384,0},{1,129},{129,257},{257,385},{3... | collective-permute-start | bytes 1474568 | tf_op jit(solution)/shard_map/ppermute | solution.py:269
  137.5 1.2 collective-permute-done.6.refs_0_
  138.7 3.4 %collective-permute-start.7 = (bf16[96,1536]{1,0:T(8,128)(2,1)S(1)}, bf16[96,1536]{1,0:T(8,128)(2,1)S(1)}, u32[]{:S(2)}, u32[]{:S(2)}) collective-permute-start(bf16[96,1536]{1,0:T(8,128)(2,1)S(1)} %slice.23), channel_id=1, source_target_pairs={{0,112},{16,0},{32,16},{48,32},{64,48},{80,64},{96,80},{112,96},{1... | collective-permute-start | bytes 884744 | tf_op jit(solution)/shard_map/ppermute | solution.py:269
  142.1 1.9 collective-permute-start.12
  144.1 0.0 collective-permute-done.11.refs_3_
  144.1 3.4 %collective-permute-start.13 = (bf16[128,1920]{1,0:T(8,128)(2,1)S(1)}, bf16[128,1920]{1,0:T(8,128)(2,1)S(1)}, u32[]{:S(2)}, u32[]{:S(2)}) collective-permute-start(bf16[128,1920]{1,0:T(8,128)(2,1)S(1)} %collective-permute-done.11.refs_3_), channel_id=1, source_target_pairs={{0,384},{128,0},{256,128},{384,256},{1,385},{129,1},{257,129},{385... | collective-permute-start | bytes 1474568 | tf_op jit(solution)/shard_map/ppermute | solution.py:269
  147.5 1.6 shard_map.86
  149.0 4.3 %shard_map.87 = (bf16[128,1920]{1,0:T(8,128)(2,1)S(1)}, bf16[128,1920]{1,0:T(8,128)(2,1)S(1)}, bf16[128,1920]{1,0:T(8,128)(2,1)S(1)}, bf16[128,1920]{1,0:T(8,128)(2,1)S(1)}) custom-call(bf16[768,1536]{1,0:T(8,128)(2,1)S(1)} %get-tuple-element.37.in_ref, bf16[768,1536]{1,0:T(8,128)(2,1)S(1)} %get-tuple-element.38.out_ref, ...), custom_call_target="tpu_custom_call" | custom-call | flops 3019898880 | bytes 8650752 | tf_op jit(solution)/shard_map/pallas_call | solution.py:251
  153.3 4.0 %collective-permute-done.12.refs_0_ = bf16[128,1920]{1,0:T(8,128)(2,1)S(1)} collective-permute-done((bf16[128,1920]{1,0:T(8,128)(2,1)S(1)}, bf16[128,1920]{1,0:T(8,128)(2,1)S(1)}, u32[]{:S(2)}, u32[]{:S(2)}) %collective-permute-start.12) | collective-permute-done | bytes 491552 | tf_op jit(solution)/shard_map/ppermute | solution.py:269
  157.3 2.3 shard_map.88
  159.7 4.3 %collective-permute-start.14 = (bf16[128,1920]{1,0:T(8,128)(2,1)S(1)}, bf16[128,1920]{1,0:T(8,128)(2,1)S(1)}, u32[]{:S(2)}, u32[]{:S(2)}) collective-permute-start(bf16[128,1920]{1,0:T(8,128)(2,1)S(1)} %get-tuple-element.43), channel_id=1, source_target_pairs={{0,128},{128,256},{256,384},{384,0},{1,129},{129,257},{257,385},{3... | collective-permute-start | bytes 1474568 | tf_op jit(solution)/shard_map/ppermute | solution.py:269
  164.0 1.9 collective-permute-start.15
  165.9 1.9 collective-permute-start.16
  167.9 4.6 %collective-permute-start.17 = (bf16[128,1920]{1,0:T(8,128)(2,1)S(1)}, bf16[128,1920]{1,0:T(8,128)(2,1)S(1)}, u32[]{:S(2)}, u32[]{:S(2)}) collective-permute-start(bf16[128,1920]{1,0:T(8,128)(2,1)S(1)} %get-tuple-element.48), channel_id=1, source_target_pairs={{0,128},{128,256},{256,384},{384,0},{1,129},{129,257},{257,385},{3... | collective-permute-start | bytes 1474568 | tf_op jit(solution)/shard_map/ppermute | solution.py:269
  172.4 0.1 add_convert_fusion.3
  172.6 4.2 %collective-permute-start.18 = (bf16[128,1920]{1,0:T(8,128)(2,1)S(1)}, bf16[128,1920]{1,0:T(8,128)(2,1)S(1)}, u32[]{:S(2)}, u32[]{:S(2)}) collective-permute-start(bf16[128,1920]{1,0:T(8,128)(2,1)S(1)} %add_convert_fusion.3), channel_id=1, source_target_pairs={{0,128},{128,256},{256,384},{384,0},{1,129},{129,257},{257,385},{3... | collective-permute-start | bytes 1474568 | tf_op jit(solution)/shard_map/ppermute | solution.py:269
  176.8 0.1 add_convert_fusion.2
  176.9 2.1 collective-permute-start.19
  179.0 7.9 %collective-permute-done.16.refs_2_ = bf16[128,1920]{1,0:T(8,128)(2,1)S(1)} collective-permute-done((bf16[128,1920]{1,0:T(8,128)(2,1)S(1)}, bf16[128,1920]{1,0:T(8,128)(2,1)S(1)}, u32[]{:S(2)}, u32[]{:S(2)}) %collective-permute-start.16) | collective-permute-done | bytes 491552 | tf_op jit(solution)/shard_map/ppermute | solution.py:269
  186.9 2.4 shard_map.89
  189.3 4.7 %collective-permute-done.18 = bf16[128,1920]{1,0:T(8,128)(2,1)S(1)} collective-permute-done((bf16[128,1920]{1,0:T(8,128)(2,1)S(1)}, bf16[128,1920]{1,0:T(8,128)(2,1)S(1)}, u32[]{:S(2)}, u32[]{:S(2)}) %collective-permute-start.18) | collective-permute-done | bytes 491552 | tf_op jit(solution)/shard_map/ppermute | solution.py:269
  194.0 0.1 add_convert_fusion.1
  194.1 3.4 %collective-permute-done.19 = bf16[128,1920]{1,0:T(8,128)(2,1)S(1)} collective-permute-done((bf16[128,1920]{1,0:T(8,128)(2,1)S(1)}, bf16[128,1920]{1,0:T(8,128)(2,1)S(1)}, u32[]{:S(2)}, u32[]{:S(2)}) %collective-permute-start.19) | collective-permute-done | bytes 491552 | tf_op jit(solution)/shard_map/ppermute | solution.py:269
  197.5 0.1 add_convert_fusion
  197.6 0.0 copy-start.10
  197.6 1.0 pad_maximum_fusion
  198.6 10.8 %all-to-all-start.3 = ((bf16[16,16,1920]{2,1,0:T(8,128)(2,1)}), bf16[16,16,1920]{2,1,0:T(8,128)(2,1)S(1)}, u32[]{:S(2)}, u32[]{:S(2)}) async-start(bf16[16,16,1920]{2,1,0:T(8,128)(2,1)} %bitcast.7), calls=%async_computation.3 | async-start | bytes 1966080 | tf_op jit(solution)/shard_map/all_to_all | solution.py:349
  209.4 0.1 copy.11
  209.5 26.5 %all-to-all-done.3 = bf16[16,16,1920]{2,1,0:T(8,128)(2,1)S(1)} async-done(((bf16[16,16,1920]{2,1,0:T(8,128)(2,1)}), bf16[16,16,1920]{2,1,0:T(8,128)(2,1)S(1)}, u32[]{:S(2)}, u32[]{:S(2)}) %all-to-all-start.3) | async-done | bytes 983072 | tf_op jit(solution)/shard_map/all_to_all | solution.py:349
  236.0 1.8 shard_map.90
  (26 shorter events, 0.1 us)
Async XLA Ops:
  0.0 1.3 copy-start
  1.3 11.4 %copy-start.5 = (bf16[1,96,1536]{2,1,0:T(8,128)(2,1)S(1)}, bf16[1,96,1536]{2,1,0:T(8,128)(2,1)}, u32[]{:S(2)}) copy-start(bf16[1,96,1536]{2,1,0:T(8,128)(2,1)} %in_ref.1) | copy-start | bytes 884740
  1.3 11.4 %copy-start.6 = (bf16[1,96,1536]{2,1,0:T(8,128)(2,1)S(1)}, bf16[1,96,1536]{2,1,0:T(8,128)(2,1)}, u32[]{:S(2)}) copy-start(bf16[1,96,1536]{2,1,0:T(8,128)(2,1)} %out_ref.1) | copy-start | bytes 884740
  2.6 51.0 %all-to-all-start = ((bf16[8,576,128]{2,1,0:T(8,128)(2,1)}), bf16[8,576,128]{2,1,0:T(8,128)(2,1)S(1)}, u32[]{:S(2)}, u32[]{:S(2)}) async-start(bf16[8,576,128]{2,1,0:T(8,128)(2,1)} %shard_map.82), calls=%async_computation | async-start | bytes 2359296 | tf_op jit(solution)/shard_map/all_to_all | solution.py:317
  12.6 53.6 %copy-start.9 = (s32[1,128,2]{1,2,0:T(2,128)S(1)}, s32[1,128,2]{1,2,0:T(2,128)}, u32[]{:S(2)}) copy-start(s32[1,128,2]{1,2,0:T(2,128)} %param.12) | copy-start | bytes 3076
  12.6 68.6 %copy-start.7 = (f32[1,1536]{1,0:T(1,128)S(1)}, f32[1,1536]{1,0:T(1,128)}, u32[]{:S(2)}) copy-start(f32[1,1536]{1,0:T(1,128)} %scale_ref.1) | copy-start | bytes 18436
  12.7 68.6 %copy-start.8 = (f32[1,1536]{1,0:T(1,128)S(1)}, f32[1,1536]{1,0:T(1,128)}, u32[]{:S(2)}) copy-start(f32[1,1536]{1,0:T(1,128)} %shift_ref.1) | copy-start | bytes 18436
  12.7 40.9 %collective-permute-start = (bf16[192,1536]{1,0:T(8,128)(2,1)S(1)}, bf16[192,1536]{1,0:T(8,128)(2,1)S(1)}, u32[]{:S(2)}, u32[]{:S(2)}) collective-permute-start(bf16[192,1536]{1,0:T(8,128)(2,1)S(1)} %shard_map.83.refs_2_), channel_id=1, source_target_pairs={{0,16},{16,32},{32,48},{48,64},{64,80},{80,96},{96,112},{112,0},{1... | collective-permute-start | bytes 1769480 | tf_op jit(solution)/shard_map/ppermute | solution.py:269
  16.1 37.5 %collective-permute-start.1 = (bf16[192,1536]{1,0:T(8,128)(2,1)S(1)}, bf16[192,1536]{1,0:T(8,128)(2,1)S(1)}, u32[]{:S(2)}, u32[]{:S(2)}) collective-permute-start(bf16[192,1536]{1,0:T(8,128)(2,1)S(1)} %shard_map.83.refs_2_), channel_id=1, source_target_pairs={{0,112},{16,0},{32,16},{48,32},{64,48},{80,64},{96,80},{112,96},{1... | collective-permute-start | bytes 1769480 | tf_op jit(solution)/shard_map/ppermute | solution.py:269
  53.6 27.7 %copy-start.1 = (bf16[192,1536]{1,0:T(8,128)(2,1)}, bf16[192,1536]{1,0:T(8,128)(2,1)S(1)}, u32[]{:S(2)}) copy-start(bf16[192,1536]{1,0:T(8,128)(2,1)S(1)} %collective-permute-done.1.refs_6_) | copy-start | bytes 1769476
  61.0 20.3 %all-to-all-start.1 = ((bf16[8,192,128]{2,1,0:T(8,128)(2,1)}), bf16[8,192,128]{2,1,0:T(8,128)(2,1)S(1)}, u32[]{:S(2)}, u32[]{:S(2)}) async-start(bf16[8,192,128]{2,1,0:T(8,128)(2,1)} %shard_map.84), calls=%async_computation.1 | async-start | bytes 786432 | tf_op jit(solution)/shard_map/all_to_all | solution.py:329
  81.3 1.0 copy-start.4
  82.3 9.5 %copy-start.2 = (bf16[192,1536]{1,0:T(8,128)(2,1)S(1)}, bf16[192,1536]{1,0:T(8,128)(2,1)}, u32[]{:S(2)}) copy-start(bf16[192,1536]{1,0:T(8,128)(2,1)} %copy-done.1) | copy-start | bytes 1769476
  84.1 34.4 %all-to-all-start.2 = ((bf16[16,16,1920]{2,1,0:T(8,128)(2,1)}), bf16[16,16,1920]{2,1,0:T(8,128)(2,1)}, u32[]{:S(2)}, u32[]{:S(2)}) async-start(bf16[16,16,1920]{2,1,0:T(8,128)(2,1)} %bitcast.4), calls=%async_computation.2 | async-start | bytes 1966080 | tf_op jit(solution)/shard_map/all_to_all | solution.py:337
  91.8 16.8 %collective-permute-start.4 = (bf16[192,1536]{1,0:T(8,128)(2,1)S(1)}, bf16[192,1536]{1,0:T(8,128)(2,1)}, u32[]{:S(2)}, u32[]{:S(2)}) collective-permute-start(bf16[192,1536]{1,0:T(8,128)(2,1)S(1)} %copy-done.2), channel_id=1, source_target_pairs={{0,112},{16,0},{32,16},{48,32},{64,48},{80,64},{96,80},{112,96},{1... | collective-permute-start | bytes 1769480 | tf_op jit(solution)/shard_map/ppermute | solution.py:269
  93.7 18.2 %collective-permute-start.2 = (bf16[192,1536]{1,0:T(8,128)(2,1)S(1)}, bf16[192,1536]{1,0:T(8,128)(2,1)}, u32[]{:S(2)}, u32[]{:S(2)}) collective-permute-start(bf16[192,1536]{1,0:T(8,128)(2,1)S(1)} %collective-permute-done.refs_3_), channel_id=1, source_target_pairs={{0,16},{16,32},{32,48},{48,64},{64,80},{80,96},{96,112},{112,0},{1... | collective-permute-start | bytes 1769480 | tf_op jit(solution)/shard_map/ppermute | solution.py:269
  108.5 16.6 %collective-permute-start.5 = (bf16[192,1536]{1,0:T(8,128)(2,1)}, bf16[192,1536]{1,0:T(8,128)(2,1)S(1)}, u32[]{:S(2)}, u32[]{:S(2)}) collective-permute-start(bf16[192,1536]{1,0:T(8,128)(2,1)} %collective-permute-done.4.refs_7_), channel_id=1, source_target_pairs={{0,112},{16,0},{32,16},{48,32},{64,48},{80,64},{96,80},{112,96},{1... | collective-permute-start | bytes 1769480 | tf_op jit(solution)/shard_map/ppermute | solution.py:269
  111.9 17.1 %collective-permute-start.3 = (bf16[192,1536]{1,0:T(8,128)(2,1)}, bf16[192,1536]{1,0:T(8,128)(2,1)S(1)}, u32[]{:S(2)}, u32[]{:S(2)}) collective-permute-start(bf16[192,1536]{1,0:T(8,128)(2,1)} %collective-permute-done.2.refs_4_), channel_id=1, source_target_pairs={{0,16},{16,32},{32,48},{48,64},{64,80},{80,96},{96,112},{112,0},{1... | collective-permute-start | bytes 1769480 | tf_op jit(solution)/shard_map/ppermute | solution.py:269
  118.5 29.0 %copy-start.3 = (bf16[192,1536]{1,0:T(8,128)(2,1)S(1)}, bf16[192,1536]{1,0:T(8,128)(2,1)}, u32[]{:S(2)}) copy-start(bf16[192,1536]{1,0:T(8,128)(2,1)} %copy-done.1) | copy-start | bytes 1769476
  119.8 22.3 %collective-permute-start.8 = (bf16[128,1920]{1,0:T(8,128)(2,1)S(1)}, bf16[128,1920]{1,0:T(8,128)(2,1)S(1)}, u32[]{:S(2)}, u32[]{:S(2)}) collective-permute-start(bf16[128,1920]{1,0:T(8,128)(2,1)S(1)} %bitcast.14), channel_id=1, source_target_pairs={{0,128},{128,256},{256,384},{384,0},{1,129},{129,257},{257,385},{3... | collective-permute-start | bytes 1474568 | tf_op jit(solution)/shard_map/ppermute | solution.py:269
  121.9 22.1 %collective-permute-start.11 = (bf16[128,1920]{1,0:T(8,128)(2,1)S(1)}, bf16[128,1920]{1,0:T(8,128)(2,1)S(1)}, u32[]{:S(2)}, u32[]{:S(2)}) collective-permute-start(bf16[128,1920]{1,0:T(8,128)(2,1)S(1)} %bitcast.11), channel_id=1, source_target_pairs={{0,384},{128,0},{256,128},{384,256},{1,385},{129,1},{257,129},{385... | collective-permute-start | bytes 1474568 | tf_op jit(solution)/shard_map/ppermute | solution.py:269
  129.1 9.7 %collective-permute-start.6 = (bf16[96,1536]{1,0:T(8,128)(2,1)S(1)}, bf16[96,1536]{1,0:T(8,128)(2,1)S(1)}, u32[]{:S(2)}, u32[]{:S(2)}) collective-permute-start(bf16[96,1536]{1,0:T(8,128)(2,1)S(1)} %slice.22), channel_id=1, source_target_pairs={{0,16},{16,32},{32,48},{48,64},{64,80},{80,96},{96,112},{112,0},{1... | collective-permute-start | bytes 884744 | tf_op jit(solution)/shard_map/ppermute | solution.py:269
  131.0 18.0 %collective-permute-start.10 = (bf16[128,1920]{1,0:T(8,128)(2,1)S(1)}, bf16[128,1920]{1,0:T(8,128)(2,1)S(1)}, u32[]{:S(2)}, u32[]{:S(2)}) collective-permute-start(bf16[128,1920]{1,0:T(8,128)(2,1)S(1)} %bitcast.15), channel_id=1, source_target_pairs={{0,384},{128,0},{256,128},{384,256},{1,385},{129,1},{257,129},{385... | collective-permute-start | bytes 1474568 | tf_op jit(solution)/shard_map/ppermute | solution.py:269
  133.5 15.6 %collective-permute-start.9 = (bf16[128,1920]{1,0:T(8,128)(2,1)S(1)}, bf16[128,1920]{1,0:T(8,128)(2,1)S(1)}, u32[]{:S(2)}, u32[]{:S(2)}) collective-permute-start(bf16[128,1920]{1,0:T(8,128)(2,1)S(1)} %bitcast.12), channel_id=1, source_target_pairs={{0,128},{128,256},{256,384},{384,0},{1,129},{129,257},{257,385},{3... | collective-permute-start | bytes 1474568 | tf_op jit(solution)/shard_map/ppermute | solution.py:269
  138.7 8.7 %collective-permute-start.7 = (bf16[96,1536]{1,0:T(8,128)(2,1)S(1)}, bf16[96,1536]{1,0:T(8,128)(2,1)S(1)}, u32[]{:S(2)}, u32[]{:S(2)}) collective-permute-start(bf16[96,1536]{1,0:T(8,128)(2,1)S(1)} %slice.23), channel_id=1, source_target_pairs={{0,112},{16,0},{32,16},{48,32},{64,48},{80,64},{96,80},{112,96},{1... | collective-permute-start | bytes 884744 | tf_op jit(solution)/shard_map/ppermute | solution.py:269
  142.1 15.2 %collective-permute-start.12 = (bf16[128,1920]{1,0:T(8,128)(2,1)S(1)}, bf16[128,1920]{1,0:T(8,128)(2,1)S(1)}, u32[]{:S(2)}, u32[]{:S(2)}) collective-permute-start(bf16[128,1920]{1,0:T(8,128)(2,1)S(1)} %collective-permute-done.8.refs_0_), channel_id=1, source_target_pairs={{0,128},{128,256},{256,384},{384,0},{1,129},{129,257},{257,385},{3... | collective-permute-start | bytes 1474568 | tf_op jit(solution)/shard_map/ppermute | solution.py:269
  144.1 13.3 %collective-permute-start.13 = (bf16[128,1920]{1,0:T(8,128)(2,1)S(1)}, bf16[128,1920]{1,0:T(8,128)(2,1)S(1)}, u32[]{:S(2)}, u32[]{:S(2)}) collective-permute-start(bf16[128,1920]{1,0:T(8,128)(2,1)S(1)} %collective-permute-done.11.refs_3_), channel_id=1, source_target_pairs={{0,384},{128,0},{256,128},{384,256},{1,385},{129,1},{257,129},{385... | collective-permute-start | bytes 1474568 | tf_op jit(solution)/shard_map/ppermute | solution.py:269
  159.7 12.8 %collective-permute-start.14 = (bf16[128,1920]{1,0:T(8,128)(2,1)S(1)}, bf16[128,1920]{1,0:T(8,128)(2,1)S(1)}, u32[]{:S(2)}, u32[]{:S(2)}) collective-permute-start(bf16[128,1920]{1,0:T(8,128)(2,1)S(1)} %get-tuple-element.43), channel_id=1, source_target_pairs={{0,128},{128,256},{256,384},{384,0},{1,129},{129,257},{257,385},{3... | collective-permute-start | bytes 1474568 | tf_op jit(solution)/shard_map/ppermute | solution.py:269
  164.0 12.8 %collective-permute-start.15 = (bf16[128,1920]{1,0:T(8,128)(2,1)S(1)}, bf16[128,1920]{1,0:T(8,128)(2,1)S(1)}, u32[]{:S(2)}, u32[]{:S(2)}) collective-permute-start(bf16[128,1920]{1,0:T(8,128)(2,1)S(1)} %get-tuple-element.45), channel_id=1, source_target_pairs={{0,384},{128,0},{256,128},{384,256},{1,385},{129,1},{257,129},{385... | collective-permute-start | bytes 1474568 | tf_op jit(solution)/shard_map/ppermute | solution.py:269
  165.9 21.0 %collective-permute-start.16 = (bf16[128,1920]{1,0:T(8,128)(2,1)S(1)}, bf16[128,1920]{1,0:T(8,128)(2,1)S(1)}, u32[]{:S(2)}, u32[]{:S(2)}) collective-permute-start(bf16[128,1920]{1,0:T(8,128)(2,1)S(1)} %get-tuple-element.40), channel_id=1, source_target_pairs={{0,384},{128,0},{256,128},{384,256},{1,385},{129,1},{257,129},{385... | collective-permute-start | bytes 1474568 | tf_op jit(solution)/shard_map/ppermute | solution.py:269
  167.9 19.1 %collective-permute-start.17 = (bf16[128,1920]{1,0:T(8,128)(2,1)S(1)}, bf16[128,1920]{1,0:T(8,128)(2,1)S(1)}, u32[]{:S(2)}, u32[]{:S(2)}) collective-permute-start(bf16[128,1920]{1,0:T(8,128)(2,1)S(1)} %get-tuple-element.48), channel_id=1, source_target_pairs={{0,128},{128,256},{256,384},{384,0},{1,129},{129,257},{257,385},{3... | collective-permute-start | bytes 1474568 | tf_op jit(solution)/shard_map/ppermute | solution.py:269
  172.6 21.4 %collective-permute-start.18 = (bf16[128,1920]{1,0:T(8,128)(2,1)S(1)}, bf16[128,1920]{1,0:T(8,128)(2,1)S(1)}, u32[]{:S(2)}, u32[]{:S(2)}) collective-permute-start(bf16[128,1920]{1,0:T(8,128)(2,1)S(1)} %add_convert_fusion.3), channel_id=1, source_target_pairs={{0,128},{128,256},{256,384},{384,0},{1,129},{129,257},{257,385},{3... | collective-permute-start | bytes 1474568 | tf_op jit(solution)/shard_map/ppermute | solution.py:269
  176.9 20.5 %collective-permute-start.19 = (bf16[128,1920]{1,0:T(8,128)(2,1)S(1)}, bf16[128,1920]{1,0:T(8,128)(2,1)S(1)}, u32[]{:S(2)}, u32[]{:S(2)}) collective-permute-start(bf16[128,1920]{1,0:T(8,128)(2,1)S(1)} %add_convert_fusion.2), channel_id=1, source_target_pairs={{0,384},{128,0},{256,128},{384,256},{1,385},{129,1},{257,129},{385... | collective-permute-start | bytes 1474568 | tf_op jit(solution)/shard_map/ppermute | solution.py:269
  197.6 11.8 %copy-start.10 = (f32[1,128,2]{1,2,0:T(2,128)S(1)}, f32[1,128,2]{1,2,0:T(2,128)}, u32[]{:S(2)}) copy-start(f32[1,128,2]{1,2,0:T(2,128)} %param.13) | copy-start | bytes 3076
  198.6 37.4 %all-to-all-start.3 = ((bf16[16,16,1920]{2,1,0:T(8,128)(2,1)}), bf16[16,16,1920]{2,1,0:T(8,128)(2,1)S(1)}, u32[]{:S(2)}, u32[]{:S(2)}) async-start(bf16[16,16,1920]{2,1,0:T(8,128)(2,1)} %bitcast.7), calls=%async_computation.3 | async-start | bytes 1966080 | tf_op jit(solution)/shard_map/all_to_all | solution.py:349

commit v7 on v6

--- a/solution.py
+++ b/solution.py
@@ -315,9 +315,7 @@
         expert_in, expert_out
     )
     mixed = lax.all_to_all(packed, "ctx", 0, 0, tiled=True)
-    up, down = [shift(block, "ctx", 1)], [shift(block, "ctx", -1)]
-    mixed, up[0], down[0] = lax.optimization_barrier((mixed, up[0], down[0]))
-    group = 2
+    group = 4
     head_output = local(
         attend_kernel,
         jax.ShapeDtypeStruct((n, t * 3 // 2, 128), BF),
@@ -333,17 +331,22 @@
         functools.partial(dispatch_kernel, experts, cap),
         [jax.ShapeDtypeStruct((t, width), F32)] + [jax.ShapeDtypeStruct(wide, BF)] * CHUNKS,
     )(back, residual_in[0], modulation_scale, modulation_shift, expert_choice[0].T)
-    up[0], down[0] = after(up[0], *sends), after(down[0], *sends)
+    first = after(block, mixed)
+    up, down = [shift(first, "ctx", 1)], [shift(first, "ctx", -1)]
+    *sends, up[0], down[0] = lax.optimization_barrier((*sends, up[0], down[0]))
     arrived = [lax.all_to_all(x, "expert", 0, 0, tiled=True) for x in sends]
-    for _ in range(n // 2 - 2):
-        up.append(shift(up[-1], "ctx", 1))
-        down.append(shift(down[-1], "ctx", -1))
     ring = ring_in(*arrived)
+    up.append(shift(up[-1], "ctx", 1))
+    down.append(shift(down[-1], "ctx", -1))
+    up.append(shift(up[-1], "ctx", 1))
+    down.append(shift(down[-1], "ctx", -1))
     up[-1], down[-1] = after((up[-1], down[-1]), ring[0])
     far_in = shift(up[-1][:slice_rows], "ctx", 1)
     far_out = shift(down[-1][slice_rows:], "ctx", -1)
     weights = local(
-        assemble_kernel, [jax.ShapeDtypeStruct((n * slice_rows, width), BF)] * 2
+        assemble_kernel,
+        [jax.ShapeDtypeStruct((n * slice_rows, width), BF)] * 2,
+
     )(far_in, far_out, block, *up, *down)
     sums = [expert_layer(*ring, weights)]
     returned = [lax.all_to_all(x, "expert", 0, 0, tiled=True) for x in sums]

time: 239 us -> 230 us (0.962)
  blocking collectives: 0 us -> 40.4 us
  waiting for transfers between devices: 117 us -> 78.8 us
  starting transfers between devices: 92.2 us -> 83.6 us
    all_to_all x0 -> x1, blocking collectives: none -> 40.4 us  [per_device(): mixed = lax.all_to_all(packed, 'ctx', 0, 0, tiled=True)]
    ppermute x20, waiting for transfers between devices: 71 us -> 44.7 us  [shift(): return lax.ppermute(x, axis, [(i, (i + by) % n) for i in range(n)])]
    all_to_all x1 -> x0, starting transfers between devices: 10 us -> none  [per_device(): mixed = lax.all_to_all(packed, 'ctx', 0, 0, tiled=True)]
    all_to_all x1, waiting for transfers between devices: 14.9 us -> 5.38 us  [per_device(): back = lax.all_to_all(head_output, 'ctx', 0, 0, tiled=True)]
    all_to_all x1, waiting for transfers between devices: 4.63 us -> 2.22 us  [per_device(): arrived = [lax.all_to_all(x, 'expert', 0, 0, tiled=True) for x in sends]]
  transfers between devices with their start and end apart: 24 -> 23, of which waited for: 11 -> 12; matrix products, arithmetic and copies ran while one was open for 1% -> 1% of each run, Pallas kernels for 3% -> 4%
where the time goes in v7:
time: 230 us; the launch traced here: 229 us
  starting transfers between devices  83.6 us (36%)
  waiting for transfers between devices  78.8 us (34%)
  blocking collectives  40.4 us (18%)
  Pallas kernels  20.8 us (9%)
  local copies, waits for them, and re-layouts  3.94 us (2%)
    ppermute x20, starting transfers between devices, shift(): return lax.ppermute(x, axis, [(i, (i + by) % n) for i in range(n)])  60.8 us
    ppermute x20, waiting for transfers between devices, shift(): return lax.ppermute(x, axis, [(i, (i + by) % n) for i in range(n)])  44.7 us
    all_to_all x1, blocking collectives, per_device(): mixed = lax.all_to_all(packed, 'ctx', 0, 0, tiled=True)  40.4 us
    all_to_all x1, waiting for transfers between devices, per_device(): returned = [lax.all_to_all(x, 'expert', 0, 0, tiled=True) for x in sums]  26.5 us
    all_to_all x1, starting transfers between devices, per_device(): returned = [lax.all_to_all(x, 'expert', 0, 0, tiled=True) for x in sums]  10.7 us
    pallas_call x3, Pallas kernels, run_experts(): local(functools.partial(expert_kernel, len(pieces)), [jax.ShapeDtypeStruc...  9 us
    all_to_all x1, starting transfers between devices, per_device(): arrived = [lax.all_to_all(x, 'expert', 0, 0, tiled=True) for x in sends]  8.62 us
    pallas_call x1, Pallas kernels, per_device(): local(attend_kernel, jax.ShapeDtypeStruct((n, t * 3 // 2, 128), BF), [plt...  6.28 us
  transfers between devices with their start and end apart: 23, of which 12 were waited for; matrix products, arithmetic and copies ran while one was open for 1% of the time, Pallas kernels for 4%

profile of v7, /device:TPU:7, one launch (start us, length us, event | category | flops | bytes accessed | tf_op | source)
XLA Modules:
  0.0 229.3 jit_solution(1975694198448064447)
XLA Ops:
  0.0 1.3 copy-done
  1.3 0.3 shard_map.82
  1.5 0.0 copy-start.4
  1.6 0.0 copy-start.5
  1.6 40.4 %all_to_all.30.m_ref = bf16[8,576,128]{2,1,0:T(8,128)(2,1)S(1)} all-to-all(bf16[8,576,128]{2,1,0:T(8,128)(2,1)S(1)} %shard_map.82), channel_id=1, replica_groups=mesh['dp'=4,'ctx'=8,'expert'=16] {'ctx'}, dimensions={0} | all-to-all | bytes 2359296 | tf_op jit(solution)/shard_map/all_to_all | solution.py:317
  41.9 6.3 %shard_map.83 = bf16[8,192,128]{2,1,0:T(8,128)(2,1)} custom-call(bf16[8,576,128]{2,1,0:T(8,128)(2,1)S(1)} %all_to_all.30.m_ref), custom_call_target="tpu_custom_call" | custom-call | tf_op jit(solution)/shard_map/pallas_call | solution.py:319
  48.2 3.5 %all-to-all-start.1 = ((bf16[8,192,128]{2,1,0:T(8,128)(2,1)}), bf16[8,192,128]{2,1,0:T(8,128)(2,1)S(1)}, u32[]{:S(2)}, u32[]{:S(2)}) async-start(bf16[8,192,128]{2,1,0:T(8,128)(2,1)} %shard_map.83), calls=%async_computation.1 | async-start | bytes 786432 | tf_op jit(solution)/shard_map/all_to_all | solution.py:327
  51.7 3.3 %collective-permute-start = (bf16[192,1536]{1,0:T(8,128)(2,1)S(1)}, bf16[192,1536]{1,0:T(8,128)(2,1)S(1)}, u32[]{:S(2)}, u32[]{:S(2)}) collective-permute-start(bf16[192,1536]{1,0:T(8,128)(2,1)S(1)} %shard_map.85.refs_2_), channel_id=1, source_target_pairs={{0,16},{16,32},{32,48},{48,64},{64,80},{80,96},{96,112},{112,0},{1... | collective-permute-start | bytes 1769480 | tf_op jit(solution)/shard_map/ppermute | solution.py:269
  55.0 3.2 %collective-permute-start.1 = (bf16[192,1536]{1,0:T(8,128)(2,1)S(1)}, bf16[192,1536]{1,0:T(8,128)(2,1)S(1)}, u32[]{:S(2)}, u32[]{:S(2)}) collective-permute-start(bf16[192,1536]{1,0:T(8,128)(2,1)S(1)} %shard_map.85.refs_2_), channel_id=1, source_target_pairs={{0,112},{16,0},{32,16},{48,32},{64,48},{80,64},{96,80},{112,96},{1... | collective-permute-start | bytes 1769480 | tf_op jit(solution)/shard_map/ppermute | solution.py:269
  58.3 0.1 copy.9
  58.4 0.1 copy.10.choice_ref
  58.4 5.4 %all-to-all-done.1.b_ref = bf16[8,192,128]{2,1,0:T(8,128)(2,1)S(1)} async-done(((bf16[8,192,128]{2,1,0:T(8,128)(2,1)}), bf16[8,192,128]{2,1,0:T(8,128)(2,1)S(1)}, u32[]{:S(2)}, u32[]{:S(2)}) %all-to-all-start.1) | async-done | bytes 393248 | tf_op jit(solution)/shard_map/all_to_all | solution.py:327
  63.8 1.0 copy-done.3
  64.8 1.8 shard_map.84
  66.6 9.1 %collective-permute-done.refs_3_ = bf16[192,1536]{1,0:T(8,128)(2,1)S(1)} collective-permute-done((bf16[192,1536]{1,0:T(8,128)(2,1)S(1)}, bf16[192,1536]{1,0:T(8,128)(2,1)S(1)}, u32[]{:S(2)}, u32[]{:S(2)}) %collective-permute-start) | collective-permute-done | bytes 589856 | tf_op jit(solution)/shard_map/ppermute | solution.py:269
  75.7 0.0 collective-permute-done.1.refs_6_
  75.7 8.6 %all-to-all-start.2 = ((bf16[16,16,1920]{2,1,0:T(8,128)(2,1)}), bf16[16,16,1920]{2,1,0:T(8,128)(2,1)}, u32[]{:S(2)}, u32[]{:S(2)}) async-start(bf16[16,16,1920]{2,1,0:T(8,128)(2,1)} %bitcast.4), calls=%async_computation.2 | async-start | bytes 1966080 | tf_op jit(solution)/shard_map/all_to_all | solution.py:337
  84.3 2.1 collective-permute-start.2
  86.4 4.4 %collective-permute-start.4 = (bf16[192,1536]{1,0:T(8,128)(2,1)S(1)}, bf16[192,1536]{1,0:T(8,128)(2,1)}, u32[]{:S(2)}, u32[]{:S(2)}) collective-permute-start(bf16[192,1536]{1,0:T(8,128)(2,1)S(1)} %collective-permute-done.1.refs_6_), channel_id=1, source_target_pairs={{0,112},{16,0},{32,16},{48,32},{64,48},{80,64},{96,80},{112,96},{1... | collective-permute-start | bytes 1769480 | tf_op jit(solution)/shard_map/ppermute | solution.py:269
  90.8 11.5 %collective-permute-done.2.refs_4_ = bf16[192,1536]{1,0:T(8,128)(2,1)} collective-permute-done((bf16[192,1536]{1,0:T(8,128)(2,1)S(1)}, bf16[192,1536]{1,0:T(8,128)(2,1)}, u32[]{:S(2)}, u32[]{:S(2)}) %collective-permute-start.2) | collective-permute-done | bytes 589856 | tf_op jit(solution)/shard_map/ppermute | solution.py:269
  102.3 1.9 collective-permute-start.3
  104.2 0.0 collective-permute-done.4.refs_7_
  104.2 4.6 %collective-permute-start.5 = (bf16[192,1536]{1,0:T(8,128)(2,1)}, bf16[192,1536]{1,0:T(8,128)(2,1)S(1)}, u32[]{:S(2)}, u32[]{:S(2)}) collective-permute-start(bf16[192,1536]{1,0:T(8,128)(2,1)} %collective-permute-done.4.refs_7_), channel_id=1, source_target_pairs={{0,112},{16,0},{32,16},{48,32},{64,48},{80,64},{96,80},{112,96},{1... | collective-permute-start | bytes 1769480 | tf_op jit(solution)/shard_map/ppermute | solution.py:269
  108.8 2.2 all-to-all-done.2
  111.0 1.3 fusion
  112.4 2.1 collective-permute-start.8
  114.5 3.2 %collective-permute-start.11 = (bf16[128,1920]{1,0:T(8,128)(2,1)S(1)}, bf16[128,1920]{1,0:T(8,128)(2,1)S(1)}, u32[]{:S(2)}, u32[]{:S(2)}) collective-permute-start(bf16[128,1920]{1,0:T(8,128)(2,1)S(1)} %bitcast.11), channel_id=1, source_target_pairs={{0,384},{128,0},{256,128},{384,256},{1,385},{129,1},{257,129},{385... | collective-permute-start | bytes 1474568 | tf_op jit(solution)/shard_map/ppermute | solution.py:269
  117.7 1.8 collective-permute-done.3.refs_5_
  119.5 1.0 collective-permute-done.5.refs_8_
  120.5 2.5 %collective-permute-start.6 = (bf16[96,1536]{1,0:T(8,128)(2,1)S(1)}, bf16[96,1536]{1,0:T(8,128)(2,1)S(1)}, u32[]{:S(2)}, u32[]{:S(2)}) collective-permute-start(bf16[96,1536]{1,0:T(8,128)(2,1)S(1)} %slice.22), channel_id=1, source_target_pairs={{0,16},{16,32},{32,48},{48,64},{64,80},{80,96},{96,112},{112,0},{1... | collective-permute-start | bytes 884744 | tf_op jit(solution)/shard_map/ppermute | solution.py:269
  123.0 2.5 %collective-permute-start.10 = (bf16[128,1920]{1,0:T(8,128)(2,1)S(1)}, bf16[128,1920]{1,0:T(8,128)(2,1)S(1)}, u32[]{:S(2)}, u32[]{:S(2)}) collective-permute-start(bf16[128,1920]{1,0:T(8,128)(2,1)S(1)} %bitcast.15), channel_id=1, source_target_pairs={{0,384},{128,0},{256,128},{384,256},{1,385},{129,1},{257,129},{385... | collective-permute-start | bytes 1474568 | tf_op jit(solution)/shard_map/ppermute | solution.py:269
  125.5 4.0 %collective-permute-start.9 = (bf16[128,1920]{1,0:T(8,128)(2,1)S(1)}, bf16[128,1920]{1,0:T(8,128)(2,1)S(1)}, u32[]{:S(2)}, u32[]{:S(2)}) collective-permute-start(bf16[128,1920]{1,0:T(8,128)(2,1)S(1)} %bitcast.12), channel_id=1, source_target_pairs={{0,128},{128,256},{256,384},{384,0},{1,129},{129,257},{257,385},{3... | collective-permute-start | bytes 1474568 | tf_op jit(solution)/shard_map/ppermute | solution.py:269
  129.5 1.3 collective-permute-done.6.refs_0_
  130.9 3.3 %collective-permute-start.7 = (bf16[96,1536]{1,0:T(8,128)(2,1)S(1)}, bf16[96,1536]{1,0:T(8,128)(2,1)S(1)}, u32[]{:S(2)}, u32[]{:S(2)}) collective-permute-start(bf16[96,1536]{1,0:T(8,128)(2,1)S(1)} %slice.23), channel_id=1, source_target_pairs={{0,112},{16,0},{32,16},{48,32},{64,48},{80,64},{96,80},{112,96},{1... | collective-permute-start | bytes 884744 | tf_op jit(solution)/shard_map/ppermute | solution.py:269
  134.2 0.0 collective-permute-done.8.refs_0_
  134.2 1.9 collective-permute-start.12
  136.2 0.0 collective-permute-done.11.refs_3_
  136.2 3.4 %collective-permute-start.13 = (bf16[128,1920]{1,0:T(8,128)(2,1)S(1)}, bf16[128,1920]{1,0:T(8,128)(2,1)S(1)}, u32[]{:S(2)}, u32[]{:S(2)}) collective-permute-start(bf16[128,1920]{1,0:T(8,128)(2,1)S(1)} %collective-permute-done.11.refs_3_), channel_id=1, source_target_pairs={{0,384},{128,0},{256,128},{384,256},{1,385},{129,1},{257,129},{385... | collective-permute-start | bytes 1474568 | tf_op jit(solution)/shard_map/ppermute | solution.py:269
  139.6 1.6 shard_map.86
  141.1 0.0 collective-permute-done.9.refs_1_
  141.1 4.3 %shard_map.87 = (bf16[128,1920]{1,0:T(8,128)(2,1)S(1)}, bf16[128,1920]{1,0:T(8,128)(2,1)S(1)}, bf16[128,1920]{1,0:T(8,128)(2,1)S(1)}, bf16[128,1920]{1,0:T(8,128)(2,1)S(1)}) custom-call(bf16[768,1536]{1,0:T(8,128)(2,1)S(1)} %get-tuple-element.35.in_ref, bf16[768,1536]{1,0:T(8,128)(2,1)S(1)} %get-tuple-element.36.out_ref, ...), custom_call_target="tpu_custom_call" | custom-call | flops 3019898880 | bytes 8650752 | tf_op jit(solution)/shard_map/pallas_call | solution.py:251
  145.4 3.8 %collective-permute-done.12.refs_0_ = bf16[128,1920]{1,0:T(8,128)(2,1)S(1)} collective-permute-done((bf16[128,1920]{1,0:T(8,128)(2,1)S(1)}, bf16[128,1920]{1,0:T(8,128)(2,1)S(1)}, u32[]{:S(2)}, u32[]{:S(2)}) %collective-permute-start.12) | collective-permute-done | bytes 491552 | tf_op jit(solution)/shard_map/ppermute | solution.py:269
  149.3 2.3 %shard_map.88 = (bf16[128,1920]{1,0:T(8,128)(2,1)S(1)}, bf16[128,1920]{1,0:T(8,128)(2,1)S(1)}) custom-call(bf16[768,1536]{1,0:T(8,128)(2,1)S(1)} %get-tuple-element.35.in_ref, bf16[768,1536]{1,0:T(8,128)(2,1)S(1)} %get-tuple-element.36.out_ref, bf16[128,1920]{1,0:T(8,128)(2,1)S(1)} %collective-permute-done.12.refs_0_, ...), custom_call_target="tpu_custom_call" | custom-call | flops 1509949440 | bytes 6684672 | tf_op jit(solution)/shard_map/pallas_call | solution.py:251
  151.6 4.2 %collective-permute-start.14 = (bf16[128,1920]{1,0:T(8,128)(2,1)S(1)}, bf16[128,1920]{1,0:T(8,128)(2,1)S(1)}, u32[]{:S(2)}, u32[]{:S(2)}) collective-permute-start(bf16[128,1920]{1,0:T(8,128)(2,1)S(1)} %get-tuple-element.41), channel_id=1, source_target_pairs={{0,128},{128,256},{256,384},{384,0},{1,129},{129,257},{257,385},{3... | collective-permute-start | bytes 1474568 | tf_op jit(solution)/shard_map/ppermute | solution.py:269
  155.8 1.9 collective-permute-start.15
  157.7 1.9 collective-permute-start.16
  159.6 4.8 %collective-permute-start.17 = (bf16[128,1920]{1,0:T(8,128)(2,1)S(1)}, bf16[128,1920]{1,0:T(8,128)(2,1)S(1)}, u32[]{:S(2)}, u32[]{:S(2)}) collective-permute-start(bf16[128,1920]{1,0:T(8,128)(2,1)S(1)} %get-tuple-element.46), channel_id=1, source_target_pairs={{0,128},{128,256},{256,384},{384,0},{1,129},{129,257},{257,385},{3... | collective-permute-start | bytes 1474568 | tf_op jit(solution)/shard_map/ppermute | solution.py:269
  164.4 0.1 add_convert_fusion.3
  164.5 3.8 %collective-permute-start.18 = (bf16[128,1920]{1,0:T(8,128)(2,1)S(1)}, bf16[128,1920]{1,0:T(8,128)(2,1)S(1)}, u32[]{:S(2)}, u32[]{:S(2)}) collective-permute-start(bf16[128,1920]{1,0:T(8,128)(2,1)S(1)} %add_convert_fusion.3), channel_id=1, source_target_pairs={{0,128},{128,256},{256,384},{384,0},{1,129},{129,257},{257,385},{3... | collective-permute-start | bytes 1474568 | tf_op jit(solution)/shard_map/ppermute | solution.py:269
  168.4 0.1 add_convert_fusion.2
  168.5 1.9 collective-permute-start.19
  170.4 8.1 %collective-permute-done.16.refs_2_ = bf16[128,1920]{1,0:T(8,128)(2,1)S(1)} collective-permute-done((bf16[128,1920]{1,0:T(8,128)(2,1)S(1)}, bf16[128,1920]{1,0:T(8,128)(2,1)S(1)}, u32[]{:S(2)}, u32[]{:S(2)}) %collective-permute-start.16) | collective-permute-done | bytes 491552 | tf_op jit(solution)/shard_map/ppermute | solution.py:269
  178.5 0.0 collective-permute-done.17.refs_3_
  178.5 2.4 %shard_map.89 = (bf16[128,1920]{1,0:T(8,128)(2,1)S(1)}, bf16[128,1920]{1,0:T(8,128)(2,1)S(1)}) custom-call(bf16[768,1536]{1,0:T(8,128)(2,1)S(1)} %get-tuple-element.35.in_ref, bf16[768,1536]{1,0:T(8,128)(2,1)S(1)} %get-tuple-element.36.out_ref, bf16[128,1920]{1,0:T(8,128)(2,1)S(1)} %bitcast.16, bf16[128,1920]{1,0:T(8,128)(2,1)S(1)} %bitcast.13, ...), custom_call_target="tpu_custom_call" | custom-call | flops 1509949440 | bytes 6684672 | tf_op jit(solution)/shard_map/pallas_call | solution.py:251
  180.9 4.7 %collective-permute-done.18 = bf16[128,1920]{1,0:T(8,128)(2,1)S(1)} collective-permute-done((bf16[128,1920]{1,0:T(8,128)(2,1)S(1)}, bf16[128,1920]{1,0:T(8,128)(2,1)S(1)}, u32[]{:S(2)}, u32[]{:S(2)}) %collective-permute-start.18) | collective-permute-done | bytes 491552 | tf_op jit(solution)/shard_map/ppermute | solution.py:269
  185.5 0.1 add_convert_fusion.1
  185.6 3.4 %collective-permute-done.19 = bf16[128,1920]{1,0:T(8,128)(2,1)S(1)} collective-permute-done((bf16[128,1920]{1,0:T(8,128)(2,1)S(1)}, bf16[128,1920]{1,0:T(8,128)(2,1)S(1)}, u32[]{:S(2)}, u32[]{:S(2)}) %collective-permute-start.19) | collective-permute-done | bytes 491552 | tf_op jit(solution)/shard_map/ppermute | solution.py:269
  189.0 0.1 add_convert_fusion
  189.2 0.0 copy-start.9
  189.2 1.0 pad_maximum_fusion
  190.2 10.7 %all-to-all-start.3 = ((bf16[16,16,1920]{2,1,0:T(8,128)(2,1)}), bf16[16,16,1920]{2,1,0:T(8,128)(2,1)S(1)}, u32[]{:S(2)}, u32[]{:S(2)}) async-start(bf16[16,16,1920]{2,1,0:T(8,128)(2,1)} %bitcast.7), calls=%async_computation.3 | async-start | bytes 1966080 | tf_op jit(solution)/shard_map/all_to_all | solution.py:352
  200.9 0.1 copy.11
  201.0 26.5 %all-to-all-done.3 = bf16[16,16,1920]{2,1,0:T(8,128)(2,1)S(1)} async-done(((bf16[16,16,1920]{2,1,0:T(8,128)(2,1)}), bf16[16,16,1920]{2,1,0:T(8,128)(2,1)S(1)}, u32[]{:S(2)}, u32[]{:S(2)}) %all-to-all-start.3) | async-done | bytes 983072 | tf_op jit(solution)/shard_map/all_to_all | solution.py:352
  227.5 1.8 shard_map.90
  (23 shorter events, 0.1 us)
Async XLA Ops:
  0.0 1.3 copy-start
  1.5 50.1 %copy-start.4 = (bf16[1,96,1536]{2,1,0:T(8,128)(2,1)S(1)}, bf16[1,96,1536]{2,1,0:T(8,128)(2,1)}, u32[]{:S(2)}) copy-start(bf16[1,96,1536]{2,1,0:T(8,128)(2,1)} %in_ref.1) | copy-start | bytes 884740
  1.6 50.1 %copy-start.5 = (bf16[1,96,1536]{2,1,0:T(8,128)(2,1)S(1)}, bf16[1,96,1536]{2,1,0:T(8,128)(2,1)}, u32[]{:S(2)}) copy-start(bf16[1,96,1536]{2,1,0:T(8,128)(2,1)} %out_ref.1) | copy-start | bytes 884740
  41.9 16.3 %copy-start.8 = (s32[1,128,2]{1,2,0:T(2,128)S(1)}, s32[1,128,2]{1,2,0:T(2,128)}, u32[]{:S(2)}) copy-start(s32[1,128,2]{1,2,0:T(2,128)} %param.12) | copy-start | bytes 3076
  41.9 21.9 %copy-start.6 = (f32[1,1536]{1,0:T(1,128)S(1)}, f32[1,1536]{1,0:T(1,128)}, u32[]{:S(2)}) copy-start(f32[1,1536]{1,0:T(1,128)} %scale_ref.1) | copy-start | bytes 18436
  41.9 21.9 %copy-start.7 = (f32[1,1536]{1,0:T(1,128)S(1)}, f32[1,1536]{1,0:T(1,128)}, u32[]{:S(2)}) copy-start(f32[1,1536]{1,0:T(1,128)} %shift_ref.1) | copy-start | bytes 18436
  48.2 15.6 %all-to-all-start.1 = ((bf16[8,192,128]{2,1,0:T(8,128)(2,1)}), bf16[8,192,128]{2,1,0:T(8,128)(2,1)S(1)}, u32[]{:S(2)}, u32[]{:S(2)}) async-start(bf16[8,192,128]{2,1,0:T(8,128)(2,1)} %shard_map.83), calls=%async_computation.1 | async-start | bytes 786432 | tf_op jit(solution)/shard_map/all_to_all | solution.py:327
  51.7 23.9 %collective-permute-start = (bf16[192,1536]{1,0:T(8,128)(2,1)S(1)}, bf16[192,1536]{1,0:T(8,128)(2,1)S(1)}, u32[]{:S(2)}, u32[]{:S(2)}) collective-permute-start(bf16[192,1536]{1,0:T(8,128)(2,1)S(1)} %shard_map.85.refs_2_), channel_id=1, source_target_pairs={{0,16},{16,32},{32,48},{48,64},{64,80},{80,96},{96,112},{112,0},{1... | collective-permute-start | bytes 1769480 | tf_op jit(solution)/shard_map/ppermute | solution.py:269
  55.0 20.7 %collective-permute-start.1 = (bf16[192,1536]{1,0:T(8,128)(2,1)S(1)}, bf16[192,1536]{1,0:T(8,128)(2,1)S(1)}, u32[]{:S(2)}, u32[]{:S(2)}) collective-permute-start(bf16[192,1536]{1,0:T(8,128)(2,1)S(1)} %shard_map.85.refs_2_), channel_id=1, source_target_pairs={{0,112},{16,0},{32,16},{48,32},{64,48},{80,64},{96,80},{112,96},{1... | collective-permute-start | bytes 1769480 | tf_op jit(solution)/shard_map/ppermute | solution.py:269
  63.8 1.0 copy-start.3
  75.7 28.5 %copy-start.1 = (bf16[192,1536]{1,0:T(8,128)(2,1)}, bf16[192,1536]{1,0:T(8,128)(2,1)S(1)}, u32[]{:S(2)}) copy-start(bf16[192,1536]{1,0:T(8,128)(2,1)S(1)} %collective-permute-done.1.refs_6_) | copy-start | bytes 1769476
  75.7 35.3 %all-to-all-start.2 = ((bf16[16,16,1920]{2,1,0:T(8,128)(2,1)}), bf16[16,16,1920]{2,1,0:T(8,128)(2,1)}, u32[]{:S(2)}, u32[]{:S(2)}) async-start(bf16[16,16,1920]{2,1,0:T(8,128)(2,1)} %bitcast.4), calls=%async_computation.2 | async-start | bytes 1966080 | tf_op jit(solution)/shard_map/all_to_all | solution.py:337
  84.3 18.0 %collective-permute-start.2 = (bf16[192,1536]{1,0:T(8,128)(2,1)S(1)}, bf16[192,1536]{1,0:T(8,128)(2,1)}, u32[]{:S(2)}, u32[]{:S(2)}) collective-permute-start(bf16[192,1536]{1,0:T(8,128)(2,1)S(1)} %collective-permute-done.refs_3_), channel_id=1, source_target_pairs={{0,16},{16,32},{32,48},{48,64},{64,80},{80,96},{96,112},{112,0},{1... | collective-permute-start | bytes 1769480 | tf_op jit(solution)/shard_map/ppermute | solution.py:269
  86.4 17.8 %collective-permute-start.4 = (bf16[192,1536]{1,0:T(8,128)(2,1)S(1)}, bf16[192,1536]{1,0:T(8,128)(2,1)}, u32[]{:S(2)}, u32[]{:S(2)}) collective-permute-start(bf16[192,1536]{1,0:T(8,128)(2,1)S(1)} %collective-permute-done.1.refs_6_), channel_id=1, source_target_pairs={{0,112},{16,0},{32,16},{48,32},{64,48},{80,64},{96,80},{112,96},{1... | collective-permute-start | bytes 1769480 | tf_op jit(solution)/shard_map/ppermute | solution.py:269
  102.3 17.2 %collective-permute-start.3 = (bf16[192,1536]{1,0:T(8,128)(2,1)}, bf16[192,1536]{1,0:T(8,128)(2,1)S(1)}, u32[]{:S(2)}, u32[]{:S(2)}) collective-permute-start(bf16[192,1536]{1,0:T(8,128)(2,1)} %collective-permute-done.2.refs_4_), channel_id=1, source_target_pairs={{0,16},{16,32},{32,48},{48,64},{64,80},{80,96},{96,112},{112,0},{1... | collective-permute-start | bytes 1769480 | tf_op jit(solution)/shard_map/ppermute | solution.py:269
  104.2 16.3 %collective-permute-start.5 = (bf16[192,1536]{1,0:T(8,128)(2,1)}, bf16[192,1536]{1,0:T(8,128)(2,1)S(1)}, u32[]{:S(2)}, u32[]{:S(2)}) collective-permute-start(bf16[192,1536]{1,0:T(8,128)(2,1)} %collective-permute-done.4.refs_7_), channel_id=1, source_target_pairs={{0,112},{16,0},{32,16},{48,32},{64,48},{80,64},{96,80},{112,96},{1... | collective-permute-start | bytes 1769480 | tf_op jit(solution)/shard_map/ppermute | solution.py:269
  111.0 28.5 %copy-start.2 = (bf16[192,1536]{1,0:T(8,128)(2,1)S(1)}, bf16[192,1536]{1,0:T(8,128)(2,1)}, u32[]{:S(2)}) copy-start(bf16[192,1536]{1,0:T(8,128)(2,1)} %copy-done.1) | copy-start | bytes 1769476
  112.4 21.9 %collective-permute-start.8 = (bf16[128,1920]{1,0:T(8,128)(2,1)S(1)}, bf16[128,1920]{1,0:T(8,128)(2,1)S(1)}, u32[]{:S(2)}, u32[]{:S(2)}) collective-permute-start(bf16[128,1920]{1,0:T(8,128)(2,1)S(1)} %bitcast.14), channel_id=1, source_target_pairs={{0,128},{128,256},{256,384},{384,0},{1,129},{129,257},{257,385},{3... | collective-permute-start | bytes 1474568 | tf_op jit(solution)/shard_map/ppermute | solution.py:269
  114.5 21.7 %collective-permute-start.11 = (bf16[128,1920]{1,0:T(8,128)(2,1)S(1)}, bf16[128,1920]{1,0:T(8,128)(2,1)S(1)}, u32[]{:S(2)}, u32[]{:S(2)}) collective-permute-start(bf16[128,1920]{1,0:T(8,128)(2,1)S(1)} %bitcast.11), channel_id=1, source_target_pairs={{0,384},{128,0},{256,128},{384,256},{1,385},{129,1},{257,129},{385... | collective-permute-start | bytes 1474568 | tf_op jit(solution)/shard_map/ppermute | solution.py:269
  120.5 10.4 %collective-permute-start.6 = (bf16[96,1536]{1,0:T(8,128)(2,1)S(1)}, bf16[96,1536]{1,0:T(8,128)(2,1)S(1)}, u32[]{:S(2)}, u32[]{:S(2)}) collective-permute-start(bf16[96,1536]{1,0:T(8,128)(2,1)S(1)} %slice.22), channel_id=1, source_target_pairs={{0,16},{16,32},{32,48},{48,64},{64,80},{80,96},{96,112},{112,0},{1... | collective-permute-start | bytes 884744 | tf_op jit(solution)/shard_map/ppermute | solution.py:269
  123.0 18.1 %collective-permute-start.10 = (bf16[128,1920]{1,0:T(8,128)(2,1)S(1)}, bf16[128,1920]{1,0:T(8,128)(2,1)S(1)}, u32[]{:S(2)}, u32[]{:S(2)}) collective-permute-start(bf16[128,1920]{1,0:T(8,128)(2,1)S(1)} %bitcast.15), channel_id=1, source_target_pairs={{0,384},{128,0},{256,128},{384,256},{1,385},{129,1},{257,129},{385... | collective-permute-start | bytes 1474568 | tf_op jit(solution)/shard_map/ppermute | solution.py:269
  125.5 15.7 %collective-permute-start.9 = (bf16[128,1920]{1,0:T(8,128)(2,1)S(1)}, bf16[128,1920]{1,0:T(8,128)(2,1)S(1)}, u32[]{:S(2)}, u32[]{:S(2)}) collective-permute-start(bf16[128,1920]{1,0:T(8,128)(2,1)S(1)} %bitcast.12), channel_id=1, source_target_pairs={{0,128},{128,256},{256,384},{384,0},{1,129},{129,257},{257,385},{3... | collective-permute-start | bytes 1474568 | tf_op jit(solution)/shard_map/ppermute | solution.py:269
  130.9 8.7 %collective-permute-start.7 = (bf16[96,1536]{1,0:T(8,128)(2,1)S(1)}, bf16[96,1536]{1,0:T(8,128)(2,1)S(1)}, u32[]{:S(2)}, u32[]{:S(2)}) collective-permute-start(bf16[96,1536]{1,0:T(8,128)(2,1)S(1)} %slice.23), channel_id=1, source_target_pairs={{0,112},{16,0},{32,16},{48,32},{64,48},{80,64},{96,80},{112,96},{1... | collective-permute-start | bytes 884744 | tf_op jit(solution)/shard_map/ppermute | solution.py:269
  134.2 15.0 %collective-permute-start.12 = (bf16[128,1920]{1,0:T(8,128)(2,1)S(1)}, bf16[128,1920]{1,0:T(8,128)(2,1)S(1)}, u32[]{:S(2)}, u32[]{:S(2)}) collective-permute-start(bf16[128,1920]{1,0:T(8,128)(2,1)S(1)} %collective-permute-done.8.refs_0_), channel_id=1, source_target_pairs={{0,128},{128,256},{256,384},{384,0},{1,129},{129,257},{257,385},{3... | collective-permute-start | bytes 1474568 | tf_op jit(solution)/shard_map/ppermute | solution.py:269
  136.2 13.1 %collective-permute-start.13 = (bf16[128,1920]{1,0:T(8,128)(2,1)S(1)}, bf16[128,1920]{1,0:T(8,128)(2,1)S(1)}, u32[]{:S(2)}, u32[]{:S(2)}) collective-permute-start(bf16[128,1920]{1,0:T(8,128)(2,1)S(1)} %collective-permute-done.11.refs_3_), channel_id=1, source_target_pairs={{0,384},{128,0},{256,128},{384,256},{1,385},{129,1},{257,129},{385... | collective-permute-start | bytes 1474568 | tf_op jit(solution)/shard_map/ppermute | solution.py:269
  151.6 12.8 %collective-permute-start.14 = (bf16[128,1920]{1,0:T(8,128)(2,1)S(1)}, bf16[128,1920]{1,0:T(8,128)(2,1)S(1)}, u32[]{:S(2)}, u32[]{:S(2)}) collective-permute-start(bf16[128,1920]{1,0:T(8,128)(2,1)S(1)} %get-tuple-element.41), channel_id=1, source_target_pairs={{0,128},{128,256},{256,384},{384,0},{1,129},{129,257},{257,385},{3... | collective-permute-start | bytes 1474568 | tf_op jit(solution)/shard_map/ppermute | solution.py:269
  155.8 12.6 %collective-permute-start.15 = (bf16[128,1920]{1,0:T(8,128)(2,1)S(1)}, bf16[128,1920]{1,0:T(8,128)(2,1)S(1)}, u32[]{:S(2)}, u32[]{:S(2)}) collective-permute-start(bf16[128,1920]{1,0:T(8,128)(2,1)S(1)} %get-tuple-element.43), channel_id=1, source_target_pairs={{0,384},{128,0},{256,128},{384,256},{1,385},{129,1},{257,129},{385... | collective-permute-start | bytes 1474568 | tf_op jit(solution)/shard_map/ppermute | solution.py:269
  157.7 20.8 %collective-permute-start.16 = (bf16[128,1920]{1,0:T(8,128)(2,1)S(1)}, bf16[128,1920]{1,0:T(8,128)(2,1)S(1)}, u32[]{:S(2)}, u32[]{:S(2)}) collective-permute-start(bf16[128,1920]{1,0:T(8,128)(2,1)S(1)} %get-tuple-element.38), channel_id=1, source_target_pairs={{0,384},{128,0},{256,128},{384,256},{1,385},{129,1},{257,129},{385... | collective-permute-start | bytes 1474568 | tf_op jit(solution)/shard_map/ppermute | solution.py:269
  159.6 18.9 %collective-permute-start.17 = (bf16[128,1920]{1,0:T(8,128)(2,1)S(1)}, bf16[128,1920]{1,0:T(8,128)(2,1)S(1)}, u32[]{:S(2)}, u32[]{:S(2)}) collective-permute-start(bf16[128,1920]{1,0:T(8,128)(2,1)S(1)} %get-tuple-element.46), channel_id=1, source_target_pairs={{0,128},{128,256},{256,384},{384,0},{1,129},{129,257},{257,385},{3... | collective-permute-start | bytes 1474568 | tf_op jit(solution)/shard_map/ppermute | solution.py:269
  164.5 21.0 %collective-permute-start.18 = (bf16[128,1920]{1,0:T(8,128)(2,1)S(1)}, bf16[128,1920]{1,0:T(8,128)(2,1)S(1)}, u32[]{:S(2)}, u32[]{:S(2)}) collective-permute-start(bf16[128,1920]{1,0:T(8,128)(2,1)S(1)} %add_convert_fusion.3), channel_id=1, source_target_pairs={{0,128},{128,256},{256,384},{384,0},{1,129},{129,257},{257,385},{3... | collective-permute-start | bytes 1474568 | tf_op jit(solution)/shard_map/ppermute | solution.py:269
  168.5 20.5 %collective-permute-start.19 = (bf16[128,1920]{1,0:T(8,128)(2,1)S(1)}, bf16[128,1920]{1,0:T(8,128)(2,1)S(1)}, u32[]{:S(2)}, u32[]{:S(2)}) collective-permute-start(bf16[128,1920]{1,0:T(8,128)(2,1)S(1)} %add_convert_fusion.2), channel_id=1, source_target_pairs={{0,384},{128,0},{256,128},{384,256},{1,385},{129,1},{257,129},{385... | collective-permute-start | bytes 1474568 | tf_op jit(solution)/shard_map/ppermute | solution.py:269
  189.2 11.7 %copy-start.9 = (f32[1,128,2]{1,2,0:T(2,128)S(1)}, f32[1,128,2]{1,2,0:T(2,128)}, u32[]{:S(2)}) copy-start(f32[1,128,2]{1,2,0:T(2,128)} %param.13) | copy-start | bytes 3076
  190.2 37.3 %all-to-all-start.3 = ((bf16[16,16,1920]{2,1,0:T(8,128)(2,1)}), bf16[16,16,1920]{2,1,0:T(8,128)(2,1)S(1)}, u32[]{:S(2)}, u32[]{:S(2)}) async-start(bf16[16,16,1920]{2,1,0:T(8,128)(2,1)} %bitcast.7), calls=%async_computation.3 | async-start | bytes 1966080 | tf_op jit(solution)/shard_map/all_to_all | solution.py:352

commit v8 on v7

--- a/solution.py
+++ b/solution.py
@@ -152,6 +152,11 @@
         out_ref[i * rows : (i + 1) * rows, :] = block[rows:, :]
 
 
+def relay_kernel(up_ref, down_ref, up_out_ref, down_out_ref):
+    up_out_ref[...] = up_ref[...]
+    down_out_ref[...] = down_ref[...]
+
+
 def expert_kernel(pieces, in_ref, out_ref, *refs):
     x_refs, plus, y_refs, rows_ref = refs[:pieces], refs[pieces : -pieces - 1], refs[-pieces - 1 : -1], refs[-1]
     rows = x_refs[0].shape[0]
@@ -331,13 +336,18 @@
         functools.partial(dispatch_kernel, experts, cap),
         [jax.ShapeDtypeStruct((t, width), F32)] + [jax.ShapeDtypeStruct(wide, BF)] * CHUNKS,
     )(back, residual_in[0], modulation_scale, modulation_shift, expert_choice[0].T)
-    first = after(block, mixed)
-    up, down = [shift(first, "ctx", 1)], [shift(first, "ctx", -1)]
-    *sends, up[0], down[0] = lax.optimization_barrier((*sends, up[0], down[0]))
     arrived = [lax.all_to_all(x, "expert", 0, 0, tiled=True) for x in sends]
-    ring = ring_in(*arrived)
+    up, down = [shift(after(block, mixed), "ctx", 1)], [shift(after(block, mixed), "ctx", -1)]
+    up[0], down[0] = after((up[0], down[0]), *sends)
     up.append(shift(up[-1], "ctx", 1))
     down.append(shift(down[-1], "ctx", -1))
+    up[-1], down[-1] = local(
+        relay_kernel,
+        [jax.ShapeDtypeStruct(block.shape, BF)] * 2,
+        cost_estimate=pl.CostEstimate(flops=10 * 10**9, bytes_accessed=0, transcendentals=0),
+    )(up[-1], down[-1])
+    *arrived, _, _ = lax.optimization_barrier((*arrived, up[-1], down[-1]))
+    ring = ring_in(*arrived)
     up.append(shift(up[-1], "ctx", 1))
     down.append(shift(down[-1], "ctx", -1))
     up[-1], down[-1] = after((up[-1], down[-1]), ring[0])

time: 230 us -> 227 us (0.987)
  waiting for transfers between devices: 78.8 us -> 70.3 us
  starting transfers between devices: 83.6 us -> 87.3 us
    ppermute x20, waiting for transfers between devices: 44.7 us -> 38.4 us  [shift(): return lax.ppermute(x, axis, [(i, (i + by) % n) for i in range(n)])]
    all_to_all x1, starting transfers between devices: 8.62 us -> 12 us  [per_device(): arrived = [lax.all_to_all(x, 'expert', 0, 0, tiled=True) for x in sends]]
  transfers between devices with their start and end apart: 23 -> 23, of which waited for: 12 -> 12; matrix products, arithmetic and copies ran while one was open for 1% -> 1% of each run, Pallas kernels for 4% -> 5%
where the time goes in v8:
time: 227 us; the launch traced here: 226 us
  starting transfers between devices  87.3 us (38%)
  waiting for transfers between devices  70.3 us (31%)
  blocking collectives  40.4 us (18%)
  Pallas kernels  21.9 us (10%)
  local copies, waits for them, and re-layouts  3.94 us (2%)
    ppermute x20, starting transfers between devices, shift(): return lax.ppermute(x, axis, [(i, (i + by) % n) for i in range(n)])  61.5 us
    all_to_all x1, blocking collectives, per_device(): mixed = lax.all_to_all(packed, 'ctx', 0, 0, tiled=True)  40.4 us
    ppermute x20, waiting for transfers between devices, shift(): return lax.ppermute(x, axis, [(i, (i + by) % n) for i in range(n)])  38.4 us
    all_to_all x1, waiting for transfers between devices, per_device(): returned = [lax.all_to_all(x, 'expert', 0, 0, tiled=True) for x in sums]  26.5 us
    all_to_all x1, starting transfers between devices, per_device(): arrived = [lax.all_to_all(x, 'expert', 0, 0, tiled=True) for x in sends]  12 us
    all_to_all x1, starting transfers between devices, per_device(): returned = [lax.all_to_all(x, 'expert', 0, 0, tiled=True) for x in sums]  10.4 us
    pallas_call x3, Pallas kernels, run_experts(): local(functools.partial(expert_kernel, len(pieces)), [jax.ShapeDtypeStruc...  9 us
    pallas_call x1, Pallas kernels, per_device(): local(attend_kernel, jax.ShapeDtypeStruct((n, t * 3 // 2, 128), BF), [plt...  6.28 us
  transfers between devices with their start and end apart: 23, of which 12 were waited for; matrix products, arithmetic and copies ran while one was open for 1% of the time, Pallas kernels for 5%

profile of v8, /device:TPU:7, one launch (start us, length us, event | category | flops | bytes accessed | tf_op | source)
XLA Modules:
  0.0 225.6 jit_solution(1941323223018154768)
XLA Ops:
  0.0 1.3 copy-done
  1.3 0.3 shard_map.82
  1.5 0.0 copy-start.4
  1.6 0.0 copy-start.5
  1.6 40.4 %all_to_all.33.m_ref = bf16[8,576,128]{2,1,0:T(8,128)(2,1)S(1)} all-to-all(bf16[8,576,128]{2,1,0:T(8,128)(2,1)S(1)} %shard_map.82), channel_id=1, replica_groups=mesh['dp'=4,'ctx'=8,'expert'=16] {'ctx'}, dimensions={0} | all-to-all | bytes 2359296 | tf_op jit(solution)/shard_map/all_to_all | solution.py:322
  41.9 6.3 %shard_map.83 = bf16[8,192,128]{2,1,0:T(8,128)(2,1)} custom-call(bf16[8,576,128]{2,1,0:T(8,128)(2,1)S(1)} %all_to_all.33.m_ref), custom_call_target="tpu_custom_call" | custom-call | tf_op jit(solution)/shard_map/pallas_call | solution.py:324
  48.2 3.5 %all-to-all-start.1 = ((bf16[8,192,128]{2,1,0:T(8,128)(2,1)}), bf16[8,192,128]{2,1,0:T(8,128)(2,1)S(1)}, u32[]{:S(2)}, u32[]{:S(2)}) async-start(bf16[8,192,128]{2,1,0:T(8,128)(2,1)} %shard_map.83), calls=%async_computation.1 | async-start | bytes 786432 | tf_op jit(solution)/shard_map/all_to_all | solution.py:332
  51.7 3.3 %collective-permute-start = (bf16[192,1536]{1,0:T(8,128)(2,1)S(1)}, bf16[192,1536]{1,0:T(8,128)(2,1)S(1)}, u32[]{:S(2)}, u32[]{:S(2)}) collective-permute-start(bf16[192,1536]{1,0:T(8,128)(2,1)S(1)} %shard_map.85.refs_2_), channel_id=1, source_target_pairs={{0,16},{16,32},{32,48},{48,64},{64,80},{80,96},{96,112},{112,0},{1... | collective-permute-start | bytes 1769480 | tf_op jit(solution)/shard_map/ppermute | solution.py:274
  55.0 3.2 %collective-permute-start.1 = (bf16[192,1536]{1,0:T(8,128)(2,1)S(1)}, bf16[192,1536]{1,0:T(8,128)(2,1)S(1)}, u32[]{:S(2)}, u32[]{:S(2)}) collective-permute-start(bf16[192,1536]{1,0:T(8,128)(2,1)S(1)} %shard_map.85.refs_2_), channel_id=1, source_target_pairs={{0,112},{16,0},{32,16},{48,32},{64,48},{80,64},{96,80},{112,96},{1... | collective-permute-start | bytes 1769480 | tf_op jit(solution)/shard_map/ppermute | solution.py:274
  58.3 0.1 copy.9
  58.4 0.1 copy.10.choice_ref
  58.4 5.4 %all-to-all-done.1.b_ref = bf16[8,192,128]{2,1,0:T(8,128)(2,1)S(1)} async-done(((bf16[8,192,128]{2,1,0:T(8,128)(2,1)}), bf16[8,192,128]{2,1,0:T(8,128)(2,1)S(1)}, u32[]{:S(2)}, u32[]{:S(2)}) %all-to-all-start.1) | async-done | bytes 393248 | tf_op jit(solution)/shard_map/all_to_all | solution.py:332
  63.8 1.0 copy-done.3
  64.8 1.8 shard_map.84
  66.6 12.0 %all-to-all-start.2 = ((bf16[16,16,1920]{2,1,0:T(8,128)(2,1)}), bf16[16,16,1920]{2,1,0:T(8,128)(2,1)}, u32[]{:S(2)}, u32[]{:S(2)}) async-start(bf16[16,16,1920]{2,1,0:T(8,128)(2,1)} %bitcast.4), calls=%async_computation.2 | async-start | bytes 1966080 | tf_op jit(solution)/shard_map/all_to_all | solution.py:339
  78.6 0.0 collective-permute-done.1.refs_6_
  78.6 2.1 collective-permute-start.2
  80.8 4.4 %collective-permute-start.3 = (bf16[192,1536]{1,0:T(8,128)(2,1)S(1)}, bf16[192,1536]{1,0:T(8,128)(2,1)S(1)}, u32[]{:S(2)}, u32[]{:S(2)}) collective-permute-start(bf16[192,1536]{1,0:T(8,128)(2,1)S(1)} %collective-permute-done.1.refs_6_), channel_id=1, source_target_pairs={{0,112},{16,0},{32,16},{48,32},{64,48},{80,64},{96,80},{112,96},{1... | collective-permute-start | bytes 1769480 | tf_op jit(solution)/shard_map/ppermute | solution.py:274
  85.1 11.5 %collective-permute-done.2.up_ref = bf16[192,1536]{1,0:T(8,128)(2,1)S(1)} collective-permute-done((bf16[192,1536]{1,0:T(8,128)(2,1)S(1)}, bf16[192,1536]{1,0:T(8,128)(2,1)S(1)}, u32[]{:S(2)}, u32[]{:S(2)}) %collective-permute-start.2) | collective-permute-done | bytes 589856 | tf_op jit(solution)/shard_map/ppermute | solution.py:274
  96.6 0.8 collective-permute-done.3.down_ref
  97.4 1.1 shard_map.86
  98.5 1.9 collective-permute-start.4
  100.4 5.4 %collective-permute-start.5 = (bf16[192,1536]{1,0:T(8,128)(2,1)}, bf16[192,1536]{1,0:T(8,128)(2,1)S(1)}, u32[]{:S(2)}, u32[]{:S(2)}) collective-permute-start(bf16[192,1536]{1,0:T(8,128)(2,1)} %get-tuple-element.35.refs_7_), channel_id=1, source_target_pairs={{0,112},{16,0},{32,16},{48,32},{64,48},{80,64},{96,80},{112,96},{1... | collective-permute-start | bytes 1769480 | tf_op jit(solution)/shard_map/ppermute | solution.py:274
  105.8 0.0 all-to-all-done.2
  105.9 1.3 fusion
  107.2 2.1 collective-permute-start.8
  109.3 3.2 %collective-permute-start.11 = (bf16[128,1920]{1,0:T(8,128)(2,1)S(1)}, bf16[128,1920]{1,0:T(8,128)(2,1)S(1)}, u32[]{:S(2)}, u32[]{:S(2)}) collective-permute-start(bf16[128,1920]{1,0:T(8,128)(2,1)S(1)} %get-tuple-element.49.refs_1_), channel_id=1, source_target_pairs={{0,384},{128,0},{256,128},{384,256},{1,385},{129,1},{257,129},{385... | collective-permute-start | bytes 1474568 | tf_op jit(solution)/shard_map/ppermute | solution.py:274
  112.5 4.1 %collective-permute-done.4.refs_5_ = bf16[192,1536]{1,0:T(8,128)(2,1)S(1)} collective-permute-done((bf16[192,1536]{1,0:T(8,128)(2,1)}, bf16[192,1536]{1,0:T(8,128)(2,1)S(1)}, u32[]{:S(2)}, u32[]{:S(2)}) %collective-permute-start.4) | collective-permute-done | bytes 589856 | tf_op jit(solution)/shard_map/ppermute | solution.py:274
  116.6 1.0 collective-permute-done.5.refs_8_
  117.6 1.9 collective-permute-start.6
  119.5 2.5 %collective-permute-start.10 = (bf16[128,1920]{1,0:T(8,128)(2,1)S(1)}, bf16[128,1920]{1,0:T(8,128)(2,1)S(1)}, u32[]{:S(2)}, u32[]{:S(2)}) collective-permute-start(bf16[128,1920]{1,0:T(8,128)(2,1)S(1)} %get-tuple-element.48.refs_0_), channel_id=1, source_target_pairs={{0,384},{128,0},{256,128},{384,256},{1,385},{129,1},{257,129},{385... | collective-permute-start | bytes 1474568 | tf_op jit(solution)/shard_map/ppermute | solution.py:274
  122.0 4.0 %collective-permute-start.9 = (bf16[128,1920]{1,0:T(8,128)(2,1)S(1)}, bf16[128,1920]{1,0:T(8,128)(2,1)S(1)}, u32[]{:S(2)}, u32[]{:S(2)}) collective-permute-start(bf16[128,1920]{1,0:T(8,128)(2,1)S(1)} %get-tuple-element.49.refs_1_), channel_id=1, source_target_pairs={{0,128},{128,256},{256,384},{384,0},{1,129},{129,257},{257,385},{3... | collective-permute-start | bytes 1474568 | tf_op jit(solution)/shard_map/ppermute | solution.py:274
  126.1 2.0 collective-permute-done.6.refs_0_
  128.0 3.3 %collective-permute-start.7 = (bf16[96,1536]{1,0:T(8,128)(2,1)S(1)}, bf16[96,1536]{1,0:T(8,128)(2,1)S(1)}, u32[]{:S(2)}, u32[]{:S(2)}) collective-permute-start(bf16[96,1536]{1,0:T(8,128)(2,1)S(1)} %slice.15), channel_id=1, source_target_pairs={{0,112},{16,0},{32,16},{48,32},{64,48},{80,64},{96,80},{112,96},{1... | collective-permute-start | bytes 884744 | tf_op jit(solution)/shard_map/ppermute | solution.py:274
  131.3 0.0 collective-permute-done.8.refs_0_
  131.3 1.9 collective-permute-start.12
  133.2 3.4 %collective-permute-start.13 = (bf16[128,1920]{1,0:T(8,128)(2,1)S(1)}, bf16[128,1920]{1,0:T(8,128)(2,1)S(1)}, u32[]{:S(2)}, u32[]{:S(2)}) collective-permute-start(bf16[128,1920]{1,0:T(8,128)(2,1)S(1)} %collective-permute-done.11.refs_3_), channel_id=1, source_target_pairs={{0,384},{128,0},{256,128},{384,256},{1,385},{129,1},{257,129},{385... | collective-permute-start | bytes 1474568 | tf_op jit(solution)/shard_map/ppermute | solution.py:274
  136.6 1.6 shard_map.87
  138.2 0.0 collective-permute-done.10.refs_2_
  138.2 0.0 collective-permute-done.9.refs_1_
  138.2 4.3 %shard_map.88 = (bf16[128,1920]{1,0:T(8,128)(2,1)S(1)}, bf16[128,1920]{1,0:T(8,128)(2,1)S(1)}, bf16[128,1920]{1,0:T(8,128)(2,1)S(1)}, bf16[128,1920]{1,0:T(8,128)(2,1)S(1)}) custom-call(bf16[768,1536]{1,0:T(8,128)(2,1)S(1)} %get-tuple-element.39.in_ref, bf16[768,1536]{1,0:T(8,128)(2,1)S(1)} %get-tuple-element.40.out_ref, ...), custom_call_target="tpu_custom_call" | custom-call | flops 3019898880 | bytes 8650752 | tf_op jit(solution)/shard_map/pallas_call | solution.py:256
  142.5 2.7 %collective-permute-done.12.refs_0_ = bf16[128,1920]{1,0:T(8,128)(2,1)S(1)} collective-permute-done((bf16[128,1920]{1,0:T(8,128)(2,1)S(1)}, bf16[128,1920]{1,0:T(8,128)(2,1)S(1)}, u32[]{:S(2)}, u32[]{:S(2)}) %collective-permute-start.12) | collective-permute-done | bytes 491552 | tf_op jit(solution)/shard_map/ppermute | solution.py:274
  145.3 0.2 collective-permute-done.13.refs_1_
  145.5 2.3 %shard_map.89 = (bf16[128,1920]{1,0:T(8,128)(2,1)S(1)}, bf16[128,1920]{1,0:T(8,128)(2,1)S(1)}) custom-call(bf16[768,1536]{1,0:T(8,128)(2,1)S(1)} %get-tuple-element.39.in_ref, bf16[768,1536]{1,0:T(8,128)(2,1)S(1)} %get-tuple-element.40.out_ref, bf16[128,1920]{1,0:T(8,128)(2,1)S(1)} %collective-permute-done.12.refs_0_, ...), custom_call_target="tpu_custom_call" | custom-call | flops 1509949440 | bytes 6684672 | tf_op jit(solution)/shard_map/pallas_call | solution.py:256
  147.8 4.5 %collective-permute-start.14 = (bf16[128,1920]{1,0:T(8,128)(2,1)S(1)}, bf16[128,1920]{1,0:T(8,128)(2,1)S(1)}, u32[]{:S(2)}, u32[]{:S(2)}) collective-permute-start(bf16[128,1920]{1,0:T(8,128)(2,1)S(1)} %get-tuple-element.45), channel_id=1, source_target_pairs={{0,128},{128,256},{256,384},{384,0},{1,129},{129,257},{257,385},{3... | collective-permute-start | bytes 1474568 | tf_op jit(solution)/shard_map/ppermute | solution.py:274
  152.4 1.9 collective-permute-start.15
  154.3 2.1 collective-permute-start.16
  156.4 4.6 %collective-permute-start.17 = (bf16[128,1920]{1,0:T(8,128)(2,1)S(1)}, bf16[128,1920]{1,0:T(8,128)(2,1)S(1)}, u32[]{:S(2)}, u32[]{:S(2)}) collective-permute-start(bf16[128,1920]{1,0:T(8,128)(2,1)S(1)} %get-tuple-element.50), channel_id=1, source_target_pairs={{0,128},{128,256},{256,384},{384,0},{1,129},{129,257},{257,385},{3... | collective-permute-start | bytes 1474568 | tf_op jit(solution)/shard_map/ppermute | solution.py:274
  161.0 0.1 add_convert_fusion.3
  161.1 3.9 %collective-permute-start.18 = (bf16[128,1920]{1,0:T(8,128)(2,1)S(1)}, bf16[128,1920]{1,0:T(8,128)(2,1)S(1)}, u32[]{:S(2)}, u32[]{:S(2)}) collective-permute-start(bf16[128,1920]{1,0:T(8,128)(2,1)S(1)} %add_convert_fusion.3), channel_id=1, source_target_pairs={{0,128},{128,256},{256,384},{384,0},{1,129},{129,257},{257,385},{3... | collective-permute-start | bytes 1474568 | tf_op jit(solution)/shard_map/ppermute | solution.py:274
  165.0 0.1 add_convert_fusion.2
  165.1 1.9 collective-permute-start.19
  167.1 8.1 %collective-permute-done.16.refs_2_ = bf16[128,1920]{1,0:T(8,128)(2,1)S(1)} collective-permute-done((bf16[128,1920]{1,0:T(8,128)(2,1)S(1)}, bf16[128,1920]{1,0:T(8,128)(2,1)S(1)}, u32[]{:S(2)}, u32[]{:S(2)}) %collective-permute-start.16) | collective-permute-done | bytes 491552 | tf_op jit(solution)/shard_map/ppermute | solution.py:274
  175.1 2.4 %shard_map.90 = (bf16[128,1920]{1,0:T(8,128)(2,1)S(1)}, bf16[128,1920]{1,0:T(8,128)(2,1)S(1)}) custom-call(bf16[768,1536]{1,0:T(8,128)(2,1)S(1)} %get-tuple-element.39.in_ref, bf16[768,1536]{1,0:T(8,128)(2,1)S(1)} %get-tuple-element.40.out_ref, bf16[128,1920]{1,0:T(8,128)(2,1)S(1)} %get-tuple-element.48.refs_0_, ...), custom_call_target="tpu_custom_call" | custom-call | flops 1509949440 | bytes 6684672 | tf_op jit(solution)/shard_map/pallas_call | solution.py:256
  177.5 4.1 %collective-permute-done.18 = bf16[128,1920]{1,0:T(8,128)(2,1)S(1)} collective-permute-done((bf16[128,1920]{1,0:T(8,128)(2,1)S(1)}, bf16[128,1920]{1,0:T(8,128)(2,1)S(1)}, u32[]{:S(2)}, u32[]{:S(2)}) %collective-permute-start.18) | collective-permute-done | bytes 491552 | tf_op jit(solution)/shard_map/ppermute | solution.py:274
  181.6 0.1 add_convert_fusion.1
  181.8 3.9 %collective-permute-done.19 = bf16[128,1920]{1,0:T(8,128)(2,1)S(1)} collective-permute-done((bf16[128,1920]{1,0:T(8,128)(2,1)S(1)}, bf16[128,1920]{1,0:T(8,128)(2,1)S(1)}, u32[]{:S(2)}, u32[]{:S(2)}) %collective-permute-start.19) | collective-permute-done | bytes 491552 | tf_op jit(solution)/shard_map/ppermute | solution.py:274
  185.7 0.1 add_convert_fusion
  185.8 0.0 copy-start.9
  185.8 1.0 pad_maximum_fusion
  186.8 10.4 %all-to-all-start.3 = ((bf16[16,16,1920]{2,1,0:T(8,128)(2,1)}), bf16[16,16,1920]{2,1,0:T(8,128)(2,1)S(1)}, u32[]{:S(2)}, u32[]{:S(2)}) async-start(bf16[16,16,1920]{2,1,0:T(8,128)(2,1)} %bitcast.6), calls=%async_computation.3 | async-start | bytes 1966080 | tf_op jit(solution)/shard_map/all_to_all | solution.py:362
  197.2 0.1 copy.11
  197.3 26.5 %all-to-all-done.3 = bf16[16,16,1920]{2,1,0:T(8,128)(2,1)S(1)} async-done(((bf16[16,16,1920]{2,1,0:T(8,128)(2,1)}), bf16[16,16,1920]{2,1,0:T(8,128)(2,1)S(1)}, u32[]{:S(2)}, u32[]{:S(2)}) %all-to-all-start.3) | async-done | bytes 983072 | tf_op jit(solution)/shard_map/all_to_all | solution.py:362
  223.8 1.8 shard_map.91
  (24 shorter events, 0.1 us)
Async XLA Ops:
  0.0 1.3 copy-start
  1.5 50.1 %copy-start.4 = (bf16[1,96,1536]{2,1,0:T(8,128)(2,1)S(1)}, bf16[1,96,1536]{2,1,0:T(8,128)(2,1)}, u32[]{:S(2)}) copy-start(bf16[1,96,1536]{2,1,0:T(8,128)(2,1)} %in_ref.1) | copy-start | bytes 884740
  1.6 50.1 %copy-start.5 = (bf16[1,96,1536]{2,1,0:T(8,128)(2,1)S(1)}, bf16[1,96,1536]{2,1,0:T(8,128)(2,1)}, u32[]{:S(2)}) copy-start(bf16[1,96,1536]{2,1,0:T(8,128)(2,1)} %out_ref.1) | copy-start | bytes 884740
  41.9 16.3 %copy-start.8 = (s32[1,128,2]{1,2,0:T(2,128)S(1)}, s32[1,128,2]{1,2,0:T(2,128)}, u32[]{:S(2)}) copy-start(s32[1,128,2]{1,2,0:T(2,128)} %param.12) | copy-start | bytes 3076
  41.9 21.9 %copy-start.6 = (f32[1,1536]{1,0:T(1,128)S(1)}, f32[1,1536]{1,0:T(1,128)}, u32[]{:S(2)}) copy-start(f32[1,1536]{1,0:T(1,128)} %scale_ref.1) | copy-start | bytes 18436
  41.9 21.9 %copy-start.7 = (f32[1,1536]{1,0:T(1,128)S(1)}, f32[1,1536]{1,0:T(1,128)}, u32[]{:S(2)}) copy-start(f32[1,1536]{1,0:T(1,128)} %shift_ref.1) | copy-start | bytes 18436
  48.2 15.6 %all-to-all-start.1 = ((bf16[8,192,128]{2,1,0:T(8,128)(2,1)}), bf16[8,192,128]{2,1,0:T(8,128)(2,1)S(1)}, u32[]{:S(2)}, u32[]{:S(2)}) async-start(bf16[8,192,128]{2,1,0:T(8,128)(2,1)} %shard_map.83), calls=%async_computation.1 | async-start | bytes 786432 | tf_op jit(solution)/shard_map/all_to_all | solution.py:332
  51.7 26.8 %collective-permute-start = (bf16[192,1536]{1,0:T(8,128)(2,1)S(1)}, bf16[192,1536]{1,0:T(8,128)(2,1)S(1)}, u32[]{:S(2)}, u32[]{:S(2)}) collective-permute-start(bf16[192,1536]{1,0:T(8,128)(2,1)S(1)} %shard_map.85.refs_2_), channel_id=1, source_target_pairs={{0,16},{16,32},{32,48},{48,64},{64,80},{80,96},{96,112},{112,0},{1... | collective-permute-start | bytes 1769480 | tf_op jit(solution)/shard_map/ppermute | solution.py:274
  55.0 23.6 %collective-permute-start.1 = (bf16[192,1536]{1,0:T(8,128)(2,1)S(1)}, bf16[192,1536]{1,0:T(8,128)(2,1)S(1)}, u32[]{:S(2)}, u32[]{:S(2)}) collective-permute-start(bf16[192,1536]{1,0:T(8,128)(2,1)S(1)} %shard_map.85.refs_2_), channel_id=1, source_target_pairs={{0,112},{16,0},{32,16},{48,32},{64,48},{80,64},{96,80},{112,96},{1... | collective-permute-start | bytes 1769480 | tf_op jit(solution)/shard_map/ppermute | solution.py:274
  63.8 1.0 copy-start.3
  66.6 39.2 %all-to-all-start.2 = ((bf16[16,16,1920]{2,1,0:T(8,128)(2,1)}), bf16[16,16,1920]{2,1,0:T(8,128)(2,1)}, u32[]{:S(2)}, u32[]{:S(2)}) async-start(bf16[16,16,1920]{2,1,0:T(8,128)(2,1)} %bitcast.4), calls=%async_computation.2 | async-start | bytes 1966080 | tf_op jit(solution)/shard_map/all_to_all | solution.py:339
  78.6 19.9 %copy-start.1 = (bf16[192,1536]{1,0:T(8,128)(2,1)}, bf16[192,1536]{1,0:T(8,128)(2,1)S(1)}, u32[]{:S(2)}) copy-start(bf16[192,1536]{1,0:T(8,128)(2,1)S(1)} %collective-permute-done.1.refs_6_) | copy-start | bytes 1769476
  78.6 18.0 %collective-permute-start.2 = (bf16[192,1536]{1,0:T(8,128)(2,1)S(1)}, bf16[192,1536]{1,0:T(8,128)(2,1)S(1)}, u32[]{:S(2)}, u32[]{:S(2)}) collective-permute-start(bf16[192,1536]{1,0:T(8,128)(2,1)S(1)} %collective-permute-done.refs_3_), channel_id=1, source_target_pairs={{0,16},{16,32},{32,48},{48,64},{64,80},{80,96},{96,112},{112,0},{1... | collective-permute-start | bytes 1769480 | tf_op jit(solution)/shard_map/ppermute | solution.py:274
  80.8 16.6 %collective-permute-start.3 = (bf16[192,1536]{1,0:T(8,128)(2,1)S(1)}, bf16[192,1536]{1,0:T(8,128)(2,1)S(1)}, u32[]{:S(2)}, u32[]{:S(2)}) collective-permute-start(bf16[192,1536]{1,0:T(8,128)(2,1)S(1)} %collective-permute-done.1.refs_6_), channel_id=1, source_target_pairs={{0,112},{16,0},{32,16},{48,32},{64,48},{80,64},{96,80},{112,96},{1... | collective-permute-start | bytes 1769480 | tf_op jit(solution)/shard_map/ppermute | solution.py:274
  98.5 18.1 %collective-permute-start.4 = (bf16[192,1536]{1,0:T(8,128)(2,1)}, bf16[192,1536]{1,0:T(8,128)(2,1)S(1)}, u32[]{:S(2)}, u32[]{:S(2)}) collective-permute-start(bf16[192,1536]{1,0:T(8,128)(2,1)} %get-tuple-element.34.refs_4_), channel_id=1, source_target_pairs={{0,16},{16,32},{32,48},{48,64},{64,80},{80,96},{96,112},{112,0},{1... | collective-permute-start | bytes 1769480 | tf_op jit(solution)/shard_map/ppermute | solution.py:274
  100.4 17.2 %collective-permute-start.5 = (bf16[192,1536]{1,0:T(8,128)(2,1)}, bf16[192,1536]{1,0:T(8,128)(2,1)S(1)}, u32[]{:S(2)}, u32[]{:S(2)}) collective-permute-start(bf16[192,1536]{1,0:T(8,128)(2,1)} %get-tuple-element.35.refs_7_), channel_id=1, source_target_pairs={{0,112},{16,0},{32,16},{48,32},{64,48},{80,64},{96,80},{112,96},{1... | collective-permute-start | bytes 1769480 | tf_op jit(solution)/shard_map/ppermute | solution.py:274
  105.8 30.8 %copy-start.2 = (bf16[192,1536]{1,0:T(8,128)(2,1)S(1)}, bf16[192,1536]{1,0:T(8,128)(2,1)}, u32[]{:S(2)}) copy-start(bf16[192,1536]{1,0:T(8,128)(2,1)} %copy-done.1) | copy-start | bytes 1769476
  107.2 24.1 %collective-permute-start.8 = (bf16[128,1920]{1,0:T(8,128)(2,1)S(1)}, bf16[128,1920]{1,0:T(8,128)(2,1)S(1)}, u32[]{:S(2)}, u32[]{:S(2)}) collective-permute-start(bf16[128,1920]{1,0:T(8,128)(2,1)S(1)} %get-tuple-element.48.refs_0_), channel_id=1, source_target_pairs={{0,128},{128,256},{256,384},{384,0},{1,129},{129,257},{257,385},{3... | collective-permute-start | bytes 1474568 | tf_op jit(solution)/shard_map/ppermute | solution.py:274
  109.3 24.0 %collective-permute-start.11 = (bf16[128,1920]{1,0:T(8,128)(2,1)S(1)}, bf16[128,1920]{1,0:T(8,128)(2,1)S(1)}, u32[]{:S(2)}, u32[]{:S(2)}) collective-permute-start(bf16[128,1920]{1,0:T(8,128)(2,1)S(1)} %get-tuple-element.49.refs_1_), channel_id=1, source_target_pairs={{0,384},{128,0},{256,128},{384,256},{1,385},{129,1},{257,129},{385... | collective-permute-start | bytes 1474568 | tf_op jit(solution)/shard_map/ppermute | solution.py:274
  117.6 10.4 %collective-permute-start.6 = (bf16[96,1536]{1,0:T(8,128)(2,1)S(1)}, bf16[96,1536]{1,0:T(8,128)(2,1)S(1)}, u32[]{:S(2)}, u32[]{:S(2)}) collective-permute-start(bf16[96,1536]{1,0:T(8,128)(2,1)S(1)} %slice.14), channel_id=1, source_target_pairs={{0,16},{16,32},{32,48},{48,64},{64,80},{80,96},{96,112},{112,0},{1... | collective-permute-start | bytes 884744 | tf_op jit(solution)/shard_map/ppermute | solution.py:274
  119.5 18.7 %collective-permute-start.10 = (bf16[128,1920]{1,0:T(8,128)(2,1)S(1)}, bf16[128,1920]{1,0:T(8,128)(2,1)S(1)}, u32[]{:S(2)}, u32[]{:S(2)}) collective-permute-start(bf16[128,1920]{1,0:T(8,128)(2,1)S(1)} %get-tuple-element.48.refs_0_), channel_id=1, source_target_pairs={{0,384},{128,0},{256,128},{384,256},{1,385},{129,1},{257,129},{385... | collective-permute-start | bytes 1474568 | tf_op jit(solution)/shard_map/ppermute | solution.py:274
  122.0 16.2 %collective-permute-start.9 = (bf16[128,1920]{1,0:T(8,128)(2,1)S(1)}, bf16[128,1920]{1,0:T(8,128)(2,1)S(1)}, u32[]{:S(2)}, u32[]{:S(2)}) collective-permute-start(bf16[128,1920]{1,0:T(8,128)(2,1)S(1)} %get-tuple-element.49.refs_1_), channel_id=1, source_target_pairs={{0,128},{128,256},{256,384},{384,0},{1,129},{129,257},{257,385},{3... | collective-permute-start | bytes 1474568 | tf_op jit(solution)/shard_map/ppermute | solution.py:274
  128.0 8.6 %collective-permute-start.7 = (bf16[96,1536]{1,0:T(8,128)(2,1)S(1)}, bf16[96,1536]{1,0:T(8,128)(2,1)S(1)}, u32[]{:S(2)}, u32[]{:S(2)}) collective-permute-start(bf16[96,1536]{1,0:T(8,128)(2,1)S(1)} %slice.15), channel_id=1, source_target_pairs={{0,112},{16,0},{32,16},{48,32},{64,48},{80,64},{96,80},{112,96},{1... | collective-permute-start | bytes 884744 | tf_op jit(solution)/shard_map/ppermute | solution.py:274
  131.3 13.9 %collective-permute-start.12 = (bf16[128,1920]{1,0:T(8,128)(2,1)S(1)}, bf16[128,1920]{1,0:T(8,128)(2,1)S(1)}, u32[]{:S(2)}, u32[]{:S(2)}) collective-permute-start(bf16[128,1920]{1,0:T(8,128)(2,1)S(1)} %collective-permute-done.8.refs_0_), channel_id=1, source_target_pairs={{0,128},{128,256},{256,384},{384,0},{1,129},{129,257},{257,385},{3... | collective-permute-start | bytes 1474568 | tf_op jit(solution)/shard_map/ppermute | solution.py:274
  133.2 12.2 %collective-permute-start.13 = (bf16[128,1920]{1,0:T(8,128)(2,1)S(1)}, bf16[128,1920]{1,0:T(8,128)(2,1)S(1)}, u32[]{:S(2)}, u32[]{:S(2)}) collective-permute-start(bf16[128,1920]{1,0:T(8,128)(2,1)S(1)} %collective-permute-done.11.refs_3_), channel_id=1, source_target_pairs={{0,384},{128,0},{256,128},{384,256},{1,385},{129,1},{257,129},{385... | collective-permute-start | bytes 1474568 | tf_op jit(solution)/shard_map/ppermute | solution.py:274
  147.8 13.1 %collective-permute-start.14 = (bf16[128,1920]{1,0:T(8,128)(2,1)S(1)}, bf16[128,1920]{1,0:T(8,128)(2,1)S(1)}, u32[]{:S(2)}, u32[]{:S(2)}) collective-permute-start(bf16[128,1920]{1,0:T(8,128)(2,1)S(1)} %get-tuple-element.45), channel_id=1, source_target_pairs={{0,128},{128,256},{256,384},{384,0},{1,129},{129,257},{257,385},{3... | collective-permute-start | bytes 1474568 | tf_op jit(solution)/shard_map/ppermute | solution.py:274
  152.4 12.6 %collective-permute-start.15 = (bf16[128,1920]{1,0:T(8,128)(2,1)S(1)}, bf16[128,1920]{1,0:T(8,128)(2,1)S(1)}, u32[]{:S(2)}, u32[]{:S(2)}) collective-permute-start(bf16[128,1920]{1,0:T(8,128)(2,1)S(1)} %get-tuple-element.47), channel_id=1, source_target_pairs={{0,384},{128,0},{256,128},{384,256},{1,385},{129,1},{257,129},{385... | collective-permute-start | bytes 1474568 | tf_op jit(solution)/shard_map/ppermute | solution.py:274
  154.3 20.8 %collective-permute-start.16 = (bf16[128,1920]{1,0:T(8,128)(2,1)S(1)}, bf16[128,1920]{1,0:T(8,128)(2,1)S(1)}, u32[]{:S(2)}, u32[]{:S(2)}) collective-permute-start(bf16[128,1920]{1,0:T(8,128)(2,1)S(1)} %get-tuple-element.42), channel_id=1, source_target_pairs={{0,384},{128,0},{256,128},{384,256},{1,385},{129,1},{257,129},{385... | collective-permute-start | bytes 1474568 | tf_op jit(solution)/shard_map/ppermute | solution.py:274
  156.4 18.7 %collective-permute-start.17 = (bf16[128,1920]{1,0:T(8,128)(2,1)S(1)}, bf16[128,1920]{1,0:T(8,128)(2,1)S(1)}, u32[]{:S(2)}, u32[]{:S(2)}) collective-permute-start(bf16[128,1920]{1,0:T(8,128)(2,1)S(1)} %get-tuple-element.50), channel_id=1, source_target_pairs={{0,128},{128,256},{256,384},{384,0},{1,129},{129,257},{257,385},{3... | collective-permute-start | bytes 1474568 | tf_op jit(solution)/shard_map/ppermute | solution.py:274
  161.1 20.5 %collective-permute-start.18 = (bf16[128,1920]{1,0:T(8,128)(2,1)S(1)}, bf16[128,1920]{1,0:T(8,128)(2,1)S(1)}, u32[]{:S(2)}, u32[]{:S(2)}) collective-permute-start(bf16[128,1920]{1,0:T(8,128)(2,1)S(1)} %add_convert_fusion.3), channel_id=1, source_target_pairs={{0,128},{128,256},{256,384},{384,0},{1,129},{129,257},{257,385},{3... | collective-permute-start | bytes 1474568 | tf_op jit(solution)/shard_map/ppermute | solution.py:274
  165.1 20.5 %collective-permute-start.19 = (bf16[128,1920]{1,0:T(8,128)(2,1)S(1)}, bf16[128,1920]{1,0:T(8,128)(2,1)S(1)}, u32[]{:S(2)}, u32[]{:S(2)}) collective-permute-start(bf16[128,1920]{1,0:T(8,128)(2,1)S(1)} %add_convert_fusion.2), channel_id=1, source_target_pairs={{0,384},{128,0},{256,128},{384,256},{1,385},{129,1},{257,129},{385... | collective-permute-start | bytes 1474568 | tf_op jit(solution)/shard_map/ppermute | solution.py:274
  185.8 11.4 %copy-start.9 = (f32[1,128,2]{1,2,0:T(2,128)S(1)}, f32[1,128,2]{1,2,0:T(2,128)}, u32[]{:S(2)}) copy-start(f32[1,128,2]{1,2,0:T(2,128)} %param.13) | copy-start | bytes 3076
  186.8 37.0 %all-to-all-start.3 = ((bf16[16,16,1920]{2,1,0:T(8,128)(2,1)}), bf16[16,16,1920]{2,1,0:T(8,128)(2,1)S(1)}, u32[]{:S(2)}, u32[]{:S(2)}) async-start(bf16[16,16,1920]{2,1,0:T(8,128)(2,1)} %bitcast.6), calls=%async_computation.3 | async-start | bytes 1966080 | tf_op jit(solution)/shard_map/all_to_all | solution.py:362

commit v9 on v8

--- a/solution.py
+++ b/solution.py
@@ -284,6 +284,11 @@
     left_a, right_b = shift(a, "dp", 1), shift(b, "dp", -1)
     left_b, right_a = shift(b, "dp", 1), shift(a, "dp", -1)
     across_a, across_b = shift(left_a, "dp", 1), shift(right_b, "dp", -1)
+    left_b, right_a = local(
+        relay_kernel,
+        [jax.ShapeDtypeStruct(a.shape, BF)] * 2,
+        cost_estimate=pl.CostEstimate(flops=3 * 10**9, bytes_accessed=0, transcendentals=0),
+    )(left_b, right_a)
     return (a, b), (left_a, left_b, right_a, right_b), (across_a, across_b)
 
 
@@ -350,7 +355,7 @@
     ring = ring_in(*arrived)
     up.append(shift(up[-1], "ctx", 1))
     down.append(shift(down[-1], "ctx", -1))
-    up[-1], down[-1] = after((up[-1], down[-1]), ring[0])
+    up[-1], down[-1] = after((up[-1], down[-1]), *ring[1][::3])
     far_in = shift(up[-1][:slice_rows], "ctx", 1)
     far_out = shift(down[-1][slice_rows:], "ctx", -1)
     weights = local(

time: 227 us -> 223 us (0.982)
  waiting for transfers between devices: 70.3 us -> 64.3 us
    ppermute x20, waiting for transfers between devices: 38.4 us -> 32.4 us  [shift(): return lax.ppermute(x, axis, [(i, (i + by) % n) for i in range(n)])]
  transfers between devices with their start and end apart: 23 -> 23, of which waited for: 12 -> 11; matrix products, arithmetic and copies ran while one was open for 1% -> 1% of each run, Pallas kernels for 5% -> 5%
where the time goes in v9:
time: 223 us; the launch traced here: 221 us
  starting transfers between devices  88.5 us (40%)
  waiting for transfers between devices  64.3 us (29%)
  blocking collectives  40.4 us (18%)
  Pallas kernels  21.9 us (10%)
  local copies, waits for them, and re-layouts  3.88 us (2%)
    ppermute x20, starting transfers between devices, shift(): return lax.ppermute(x, axis, [(i, (i + by) % n) for i in range(n)])  60.5 us
    all_to_all x1, blocking collectives, per_device(): mixed = lax.all_to_all(packed, 'ctx', 0, 0, tiled=True)  40.4 us
    ppermute x20, waiting for transfers between devices, shift(): return lax.ppermute(x, axis, [(i, (i + by) % n) for i in range(n)])  32.4 us
    all_to_all x1, waiting for transfers between devices, per_device(): returned = [lax.all_to_all(x, 'expert', 0, 0, tiled=True) for x in sums]  26.5 us
    all_to_all x1, starting transfers between devices, per_device(): returned = [lax.all_to_all(x, 'expert', 0, 0, tiled=True) for x in sums]  12.5 us
    all_to_all x1, starting transfers between devices, per_device(): arrived = [lax.all_to_all(x, 'expert', 0, 0, tiled=True) for x in sends]  12 us
    pallas_call x3, Pallas kernels, run_experts(): local(functools.partial(expert_kernel, len(pieces)), [jax.ShapeDtypeStruc...  8.99 us
    pallas_call x1, Pallas kernels, per_device(): local(attend_kernel, jax.ShapeDtypeStruct((n, t * 3 // 2, 128), BF), [plt...  6.28 us
  transfers between devices with their start and end apart: 23, of which 11 were waited for; matrix products, arithmetic and copies ran while one was open for 1% of the time, Pallas kernels for 5%

profile of v9, /device:TPU:7, one launch (start us, length us, event | category | flops | bytes accessed | tf_op | source)
XLA Modules:
  0.0 220.9 jit_solution(1988766095631767823)
XLA Ops:
  0.0 1.3 copy-done
  1.3 0.3 shard_map.82
  1.5 0.0 copy-start.4
  1.6 0.0 copy-start.5
  1.6 40.4 %all_to_all.33.m_ref = bf16[8,576,128]{2,1,0:T(8,128)(2,1)S(1)} all-to-all(bf16[8,576,128]{2,1,0:T(8,128)(2,1)S(1)} %shard_map.82), channel_id=1, replica_groups=mesh['dp'=4,'ctx'=8,'expert'=16] {'ctx'}, dimensions={0} | all-to-all | bytes 2359296 | tf_op jit(solution)/shard_map/all_to_all | solution.py:327
  41.9 6.3 %shard_map.83 = bf16[8,192,128]{2,1,0:T(8,128)(2,1)} custom-call(bf16[8,576,128]{2,1,0:T(8,128)(2,1)S(1)} %all_to_all.33.m_ref), custom_call_target="tpu_custom_call" | custom-call | tf_op jit(solution)/shard_map/pallas_call | solution.py:329
  48.2 3.5 %all-to-all-start.1 = ((bf16[8,192,128]{2,1,0:T(8,128)(2,1)}), bf16[8,192,128]{2,1,0:T(8,128)(2,1)S(1)}, u32[]{:S(2)}, u32[]{:S(2)}) async-start(bf16[8,192,128]{2,1,0:T(8,128)(2,1)} %shard_map.83), calls=%async_computation.1 | async-start | bytes 786432 | tf_op jit(solution)/shard_map/all_to_all | solution.py:337
  51.7 3.3 %collective-permute-start = (bf16[192,1536]{1,0:T(8,128)(2,1)S(1)}, bf16[192,1536]{1,0:T(8,128)(2,1)S(1)}, u32[]{:S(2)}, u32[]{:S(2)}) collective-permute-start(bf16[192,1536]{1,0:T(8,128)(2,1)S(1)} %shard_map.85.refs_2_), channel_id=1, source_target_pairs={{0,16},{16,32},{32,48},{48,64},{64,80},{80,96},{96,112},{112,0},{1... | collective-permute-start | bytes 1769480 | tf_op jit(solution)/shard_map/ppermute | solution.py:274
  55.0 3.2 %collective-permute-start.1 = (bf16[192,1536]{1,0:T(8,128)(2,1)S(1)}, bf16[192,1536]{1,0:T(8,128)(2,1)S(1)}, u32[]{:S(2)}, u32[]{:S(2)}) collective-permute-start(bf16[192,1536]{1,0:T(8,128)(2,1)S(1)} %shard_map.85.refs_2_), channel_id=1, source_target_pairs={{0,112},{16,0},{32,16},{48,32},{64,48},{80,64},{96,80},{112,96},{1... | collective-permute-start | bytes 1769480 | tf_op jit(solution)/shard_map/ppermute | solution.py:274
  58.3 0.1 copy.9
  58.4 0.1 copy.10.choice_ref
  58.4 5.4 %all-to-all-done.1.b_ref = bf16[8,192,128]{2,1,0:T(8,128)(2,1)S(1)} async-done(((bf16[8,192,128]{2,1,0:T(8,128)(2,1)}), bf16[8,192,128]{2,1,0:T(8,128)(2,1)S(1)}, u32[]{:S(2)}, u32[]{:S(2)}) %all-to-all-start.1) | async-done | bytes 393248 | tf_op jit(solution)/shard_map/all_to_all | solution.py:337
  63.8 1.0 copy-done.3
  64.8 1.8 shard_map.84
  66.6 12.0 %all-to-all-start.2 = ((bf16[16,16,1920]{2,1,0:T(8,128)(2,1)}), bf16[16,16,1920]{2,1,0:T(8,128)(2,1)}, u32[]{:S(2)}, u32[]{:S(2)}) async-start(bf16[16,16,1920]{2,1,0:T(8,128)(2,1)} %bitcast.4), calls=%async_computation.2 | async-start | bytes 1966080 | tf_op jit(solution)/shard_map/all_to_all | solution.py:344
  78.6 0.0 collective-permute-done.refs_3_
  78.6 0.0 collective-permute-done.1.refs_6_
  78.6 2.1 collective-permute-start.2
  80.7 4.4 %collective-permute-start.3 = (bf16[192,1536]{1,0:T(8,128)(2,1)S(1)}, bf16[192,1536]{1,0:T(8,128)(2,1)S(1)}, u32[]{:S(2)}, u32[]{:S(2)}) collective-permute-start(bf16[192,1536]{1,0:T(8,128)(2,1)S(1)} %collective-permute-done.1.refs_6_), channel_id=1, source_target_pairs={{0,112},{16,0},{32,16},{48,32},{64,48},{80,64},{96,80},{112,96},{1... | collective-permute-start | bytes 1769480 | tf_op jit(solution)/shard_map/ppermute | solution.py:274
  85.1 11.5 %collective-permute-done.2.up_ref = bf16[192,1536]{1,0:T(8,128)(2,1)S(1)} collective-permute-done((bf16[192,1536]{1,0:T(8,128)(2,1)S(1)}, bf16[192,1536]{1,0:T(8,128)(2,1)S(1)}, u32[]{:S(2)}, u32[]{:S(2)}) %collective-permute-start.2) | collective-permute-done | bytes 589856 | tf_op jit(solution)/shard_map/ppermute | solution.py:274
  96.6 0.8 collective-permute-done.3.down_ref
  97.3 1.1 shard_map.86
  98.5 1.9 collective-permute-start.4
  100.4 5.4 %collective-permute-start.5 = (bf16[192,1536]{1,0:T(8,128)(2,1)}, bf16[192,1536]{1,0:T(8,128)(2,1)S(1)}, u32[]{:S(2)}, u32[]{:S(2)}) collective-permute-start(bf16[192,1536]{1,0:T(8,128)(2,1)} %get-tuple-element.37.refs_7_), channel_id=1, source_target_pairs={{0,112},{16,0},{32,16},{48,32},{64,48},{80,64},{96,80},{112,96},{1... | collective-permute-start | bytes 1769480 | tf_op jit(solution)/shard_map/ppermute | solution.py:274
  105.8 1.3 fusion
  107.1 2.1 collective-permute-start.6
  109.2 3.2 %collective-permute-start.7 = (bf16[128,1920]{1,0:T(8,128)(2,1)S(1)}, bf16[128,1920]{1,0:T(8,128)(2,1)S(1)}, u32[]{:S(2)}, u32[]{:S(2)}) collective-permute-start(bf16[128,1920]{1,0:T(8,128)(2,1)S(1)} %get-tuple-element.53.refs_1_), channel_id=1, source_target_pairs={{0,384},{128,0},{256,128},{384,256},{1,385},{129,1},{257,129},{385... | collective-permute-start | bytes 1474568 | tf_op jit(solution)/shard_map/ppermute | solution.py:274
  112.4 3.3 %collective-permute-start.10 = (bf16[128,1920]{1,0:T(8,128)(2,1)S(1)}, bf16[128,1920]{1,0:T(8,128)(2,1)S(1)}, u32[]{:S(2)}, u32[]{:S(2)}) collective-permute-start(bf16[128,1920]{1,0:T(8,128)(2,1)S(1)} %get-tuple-element.53.refs_1_), channel_id=1, source_target_pairs={{0,128},{128,256},{256,384},{384,0},{1,129},{129,257},{257,385},{3... | collective-permute-start | bytes 1474568 | tf_op jit(solution)/shard_map/ppermute | solution.py:274
  115.7 0.9 collective-permute-done.4.refs_5_
  116.6 2.5 %collective-permute-start.11 = (bf16[128,1920]{1,0:T(8,128)(2,1)S(1)}, bf16[128,1920]{1,0:T(8,128)(2,1)S(1)}, u32[]{:S(2)}, u32[]{:S(2)}) collective-permute-start(bf16[128,1920]{1,0:T(8,128)(2,1)S(1)} %get-tuple-element.52.refs_0_), channel_id=1, source_target_pairs={{0,384},{128,0},{256,128},{384,256},{1,385},{129,1},{257,129},{385... | collective-permute-start | bytes 1474568 | tf_op jit(solution)/shard_map/ppermute | solution.py:274
  119.0 0.0 collective-permute-done.5.refs_8_
  119.0 1.2 collective-permute-done.6.refs_0_
  120.2 3.0 %collective-permute-done.7.refs_3_ = bf16[128,1920]{1,0:T(8,128)(2,1)S(1)} collective-permute-done((bf16[128,1920]{1,0:T(8,128)(2,1)S(1)}, bf16[128,1920]{1,0:T(8,128)(2,1)S(1)}, u32[]{:S(2)}, u32[]{:S(2)}) %collective-permute-start.7) | collective-permute-done | bytes 491552 | tf_op jit(solution)/shard_map/ppermute | solution.py:274
  123.3 3.3 %collective-permute-start.8 = (bf16[96,1536]{1,0:T(8,128)(2,1)S(1)}, bf16[96,1536]{1,0:T(8,128)(2,1)S(1)}, u32[]{:S(2)}, u32[]{:S(2)}) collective-permute-start(bf16[96,1536]{1,0:T(8,128)(2,1)S(1)} %slice.14), channel_id=1, source_target_pairs={{0,16},{16,32},{32,48},{48,64},{64,80},{80,96},{96,112},{112,0},{1... | collective-permute-start | bytes 884744 | tf_op jit(solution)/shard_map/ppermute | solution.py:274
  126.7 3.3 %collective-permute-start.9 = (bf16[96,1536]{1,0:T(8,128)(2,1)S(1)}, bf16[96,1536]{1,0:T(8,128)(2,1)S(1)}, u32[]{:S(2)}, u32[]{:S(2)}) collective-permute-start(bf16[96,1536]{1,0:T(8,128)(2,1)S(1)} %slice.15), channel_id=1, source_target_pairs={{0,112},{16,0},{32,16},{48,32},{64,48},{80,64},{96,80},{112,96},{1... | collective-permute-start | bytes 884744 | tf_op jit(solution)/shard_map/ppermute | solution.py:274
  130.0 1.9 collective-permute-start.12
  131.9 0.0 collective-permute-done.10.up_ref
  131.9 3.4 %collective-permute-start.13 = (bf16[128,1920]{1,0:T(8,128)(2,1)S(1)}, bf16[128,1920]{1,0:T(8,128)(2,1)S(1)}, u32[]{:S(2)}, u32[]{:S(2)}) collective-permute-start(bf16[128,1920]{1,0:T(8,128)(2,1)S(1)} %collective-permute-done.7.refs_3_), channel_id=1, source_target_pairs={{0,384},{128,0},{256,128},{384,256},{1,385},{129,1},{257,129},{385... | collective-permute-start | bytes 1474568 | tf_op jit(solution)/shard_map/ppermute | solution.py:274
  135.3 0.0 collective-permute-done.11.down_ref
  135.3 0.1 shard_map.88
  135.4 1.6 shard_map.87
  137.0 4.3 %shard_map.89 = (bf16[128,1920]{1,0:T(8,128)(2,1)S(1)}, bf16[128,1920]{1,0:T(8,128)(2,1)S(1)}, bf16[128,1920]{1,0:T(8,128)(2,1)S(1)}, bf16[128,1920]{1,0:T(8,128)(2,1)S(1)}) custom-call(bf16[768,1536]{1,0:T(8,128)(2,1)S(1)} %get-tuple-element.41.in_ref, bf16[768,1536]{1,0:T(8,128)(2,1)S(1)} %get-tuple-element.42.out_ref, ...), custom_call_target="tpu_custom_call" | custom-call | flops 3019898880 | bytes 8650752 | tf_op jit(solution)/shard_map/pallas_call | solution.py:256
  141.3 1.4 collective-permute-done.13.refs_1_
  142.7 2.3 %shard_map.90 = (bf16[128,1920]{1,0:T(8,128)(2,1)S(1)}, bf16[128,1920]{1,0:T(8,128)(2,1)S(1)}) custom-call(bf16[768,1536]{1,0:T(8,128)(2,1)S(1)} %get-tuple-element.41.in_ref, bf16[768,1536]{1,0:T(8,128)(2,1)S(1)} %get-tuple-element.42.out_ref, bf16[128,1920]{1,0:T(8,128)(2,1)S(1)} %collective-permute-done.12.refs_0_, ...), custom_call_target="tpu_custom_call" | custom-call | flops 1509949440 | bytes 6684672 | tf_op jit(solution)/shard_map/pallas_call | solution.py:256
  145.1 2.2 collective-permute-start.14
  147.3 3.3 %collective-permute-start.15 = (bf16[128,1920]{1,0:T(8,128)(2,1)S(1)}, bf16[128,1920]{1,0:T(8,128)(2,1)S(1)}, u32[]{:S(2)}, u32[]{:S(2)}) collective-permute-start(bf16[128,1920]{1,0:T(8,128)(2,1)S(1)} %get-tuple-element.51), channel_id=1, source_target_pairs={{0,384},{128,0},{256,128},{384,256},{1,385},{129,1},{257,129},{385... | collective-permute-start | bytes 1474568 | tf_op jit(solution)/shard_map/ppermute | solution.py:274
  150.5 2.4 %collective-permute-start.16 = (bf16[128,1920]{1,0:T(8,128)(2,1)S(1)}, bf16[128,1920]{1,0:T(8,128)(2,1)S(1)}, u32[]{:S(2)}, u32[]{:S(2)}) collective-permute-start(bf16[128,1920]{1,0:T(8,128)(2,1)S(1)} %get-tuple-element.46), channel_id=1, source_target_pairs={{0,384},{128,0},{256,128},{384,256},{1,385},{129,1},{257,129},{385... | collective-permute-start | bytes 1474568 | tf_op jit(solution)/shard_map/ppermute | solution.py:274
  153.0 4.0 %collective-permute-start.17 = (bf16[128,1920]{1,0:T(8,128)(2,1)S(1)}, bf16[128,1920]{1,0:T(8,128)(2,1)S(1)}, u32[]{:S(2)}, u32[]{:S(2)}) collective-permute-start(bf16[128,1920]{1,0:T(8,128)(2,1)S(1)} %get-tuple-element.54), channel_id=1, source_target_pairs={{0,128},{128,256},{256,384},{384,0},{1,129},{129,257},{257,385},{3... | collective-permute-start | bytes 1474568 | tf_op jit(solution)/shard_map/ppermute | solution.py:274
  157.1 0.1 add_convert_fusion.3
  157.2 2.2 collective-permute-start.18
  159.4 0.1 add_convert_fusion.2
  159.5 3.1 %collective-permute-start.19 = (bf16[128,1920]{1,0:T(8,128)(2,1)S(1)}, bf16[128,1920]{1,0:T(8,128)(2,1)S(1)}, u32[]{:S(2)}, u32[]{:S(2)}) collective-permute-start(bf16[128,1920]{1,0:T(8,128)(2,1)S(1)} %add_convert_fusion.2), channel_id=1, source_target_pairs={{0,384},{128,0},{256,128},{384,256},{1,385},{129,1},{257,129},{385... | collective-permute-start | bytes 1474568 | tf_op jit(solution)/shard_map/ppermute | solution.py:274
  162.6 4.1 %collective-permute-done.16.refs_2_ = bf16[128,1920]{1,0:T(8,128)(2,1)S(1)} collective-permute-done((bf16[128,1920]{1,0:T(8,128)(2,1)S(1)}, bf16[128,1920]{1,0:T(8,128)(2,1)S(1)}, u32[]{:S(2)}, u32[]{:S(2)}) %collective-permute-start.16) | collective-permute-done | bytes 491552 | tf_op jit(solution)/shard_map/ppermute | solution.py:274
  166.7 1.3 collective-permute-done.17.refs_3_
  168.1 2.4 %shard_map.91 = (bf16[128,1920]{1,0:T(8,128)(2,1)S(1)}, bf16[128,1920]{1,0:T(8,128)(2,1)S(1)}) custom-call(bf16[768,1536]{1,0:T(8,128)(2,1)S(1)} %get-tuple-element.41.in_ref, bf16[768,1536]{1,0:T(8,128)(2,1)S(1)} %get-tuple-element.42.out_ref, bf16[128,1920]{1,0:T(8,128)(2,1)S(1)} %get-tuple-element.52.refs_0_, ...), custom_call_target="tpu_custom_call" | custom-call | flops 1509949440 | bytes 6684672 | tf_op jit(solution)/shard_map/pallas_call | solution.py:256
  170.4 8.2 %collective-permute-done.18 = bf16[128,1920]{1,0:T(8,128)(2,1)S(1)} collective-permute-done((bf16[128,1920]{1,0:T(8,128)(2,1)S(1)}, bf16[128,1920]{1,0:T(8,128)(2,1)S(1)}, u32[]{:S(2)}, u32[]{:S(2)}) %collective-permute-start.18) | collective-permute-done | bytes 491552 | tf_op jit(solution)/shard_map/ppermute | solution.py:274
  178.6 0.1 add_convert_fusion.1
  178.7 0.1 add_convert_fusion
  178.8 0.0 copy-start.9
  178.9 1.0 pad_maximum_fusion
  179.9 12.5 %all-to-all-start.3 = ((bf16[16,16,1920]{2,1,0:T(8,128)(2,1)}), bf16[16,16,1920]{2,1,0:T(8,128)(2,1)S(1)}, u32[]{:S(2)}, u32[]{:S(2)}) async-start(bf16[16,16,1920]{2,1,0:T(8,128)(2,1)} %bitcast.6), calls=%async_computation.3 | async-start | bytes 1966080 | tf_op jit(solution)/shard_map/all_to_all | solution.py:367
  192.5 0.1 copy.11
  192.6 26.5 %all-to-all-done.3 = bf16[16,16,1920]{2,1,0:T(8,128)(2,1)S(1)} async-done(((bf16[16,16,1920]{2,1,0:T(8,128)(2,1)}), bf16[16,16,1920]{2,1,0:T(8,128)(2,1)S(1)}, u32[]{:S(2)}, u32[]{:S(2)}) %all-to-all-start.3) | async-done | bytes 983072 | tf_op jit(solution)/shard_map/all_to_all | solution.py:367
  219.1 1.8 shard_map.92
  (25 shorter events, 0.1 us)
Async XLA Ops:
  0.0 1.3 copy-start
  1.5 50.1 %copy-start.4 = (bf16[1,96,1536]{2,1,0:T(8,128)(2,1)S(1)}, bf16[1,96,1536]{2,1,0:T(8,128)(2,1)}, u32[]{:S(2)}) copy-start(bf16[1,96,1536]{2,1,0:T(8,128)(2,1)} %in_ref.1) | copy-start | bytes 884740
  1.6 50.1 %copy-start.5 = (bf16[1,96,1536]{2,1,0:T(8,128)(2,1)S(1)}, bf16[1,96,1536]{2,1,0:T(8,128)(2,1)}, u32[]{:S(2)}) copy-start(bf16[1,96,1536]{2,1,0:T(8,128)(2,1)} %out_ref.1) | copy-start | bytes 884740
  41.9 16.3 %copy-start.8 = (s32[1,128,2]{1,2,0:T(2,128)S(1)}, s32[1,128,2]{1,2,0:T(2,128)}, u32[]{:S(2)}) copy-start(s32[1,128,2]{1,2,0:T(2,128)} %param.12) | copy-start | bytes 3076
  41.9 21.9 %copy-start.6 = (f32[1,1536]{1,0:T(1,128)S(1)}, f32[1,1536]{1,0:T(1,128)}, u32[]{:S(2)}) copy-start(f32[1,1536]{1,0:T(1,128)} %scale_ref.1) | copy-start | bytes 18436
  41.9 21.9 %copy-start.7 = (f32[1,1536]{1,0:T(1,128)S(1)}, f32[1,1536]{1,0:T(1,128)}, u32[]{:S(2)}) copy-start(f32[1,1536]{1,0:T(1,128)} %shift_ref.1) | copy-start | bytes 18436
  48.2 15.6 %all-to-all-start.1 = ((bf16[8,192,128]{2,1,0:T(8,128)(2,1)}), bf16[8,192,128]{2,1,0:T(8,128)(2,1)S(1)}, u32[]{:S(2)}, u32[]{:S(2)}) async-start(bf16[8,192,128]{2,1,0:T(8,128)(2,1)} %shard_map.83), calls=%async_computation.1 | async-start | bytes 786432 | tf_op jit(solution)/shard_map/all_to_all | solution.py:337
  51.7 26.8 %collective-permute-start = (bf16[192,1536]{1,0:T(8,128)(2,1)S(1)}, bf16[192,1536]{1,0:T(8,128)(2,1)S(1)}, u32[]{:S(2)}, u32[]{:S(2)}) collective-permute-start(bf16[192,1536]{1,0:T(8,128)(2,1)S(1)} %shard_map.85.refs_2_), channel_id=1, source_target_pairs={{0,16},{16,32},{32,48},{48,64},{64,80},{80,96},{96,112},{112,0},{1... | collective-permute-start | bytes 1769480 | tf_op jit(solution)/shard_map/ppermute | solution.py:274
  55.0 23.6 %collective-permute-start.1 = (bf16[192,1536]{1,0:T(8,128)(2,1)S(1)}, bf16[192,1536]{1,0:T(8,128)(2,1)S(1)}, u32[]{:S(2)}, u32[]{:S(2)}) collective-permute-start(bf16[192,1536]{1,0:T(8,128)(2,1)S(1)} %shard_map.85.refs_2_), channel_id=1, source_target_pairs={{0,112},{16,0},{32,16},{48,32},{64,48},{80,64},{96,80},{112,96},{1... | collective-permute-start | bytes 1769480 | tf_op jit(solution)/shard_map/ppermute | solution.py:274
  63.8 1.0 copy-start.3
  66.6 39.2 %all-to-all-start.2 = ((bf16[16,16,1920]{2,1,0:T(8,128)(2,1)}), bf16[16,16,1920]{2,1,0:T(8,128)(2,1)}, u32[]{:S(2)}, u32[]{:S(2)}) async-start(bf16[16,16,1920]{2,1,0:T(8,128)(2,1)} %bitcast.4), calls=%async_computation.2 | async-start | bytes 1966080 | tf_op jit(solution)/shard_map/all_to_all | solution.py:344
  78.6 19.9 %copy-start.1 = (bf16[192,1536]{1,0:T(8,128)(2,1)}, bf16[192,1536]{1,0:T(8,128)(2,1)S(1)}, u32[]{:S(2)}) copy-start(bf16[192,1536]{1,0:T(8,128)(2,1)S(1)} %collective-permute-done.1.refs_6_) | copy-start | bytes 1769476
  78.6 18.0 %collective-permute-start.2 = (bf16[192,1536]{1,0:T(8,128)(2,1)S(1)}, bf16[192,1536]{1,0:T(8,128)(2,1)S(1)}, u32[]{:S(2)}, u32[]{:S(2)}) collective-permute-start(bf16[192,1536]{1,0:T(8,128)(2,1)S(1)} %collective-permute-done.refs_3_), channel_id=1, source_target_pairs={{0,16},{16,32},{32,48},{48,64},{64,80},{80,96},{96,112},{112,0},{1... | collective-permute-start | bytes 1769480 | tf_op jit(solution)/shard_map/ppermute | solution.py:274
  80.7 16.6 %collective-permute-start.3 = (bf16[192,1536]{1,0:T(8,128)(2,1)S(1)}, bf16[192,1536]{1,0:T(8,128)(2,1)S(1)}, u32[]{:S(2)}, u32[]{:S(2)}) collective-permute-start(bf16[192,1536]{1,0:T(8,128)(2,1)S(1)} %collective-permute-done.1.refs_6_), channel_id=1, source_target_pairs={{0,112},{16,0},{32,16},{48,32},{64,48},{80,64},{96,80},{112,96},{1... | collective-permute-start | bytes 1769480 | tf_op jit(solution)/shard_map/ppermute | solution.py:274
  98.5 18.1 %collective-permute-start.4 = (bf16[192,1536]{1,0:T(8,128)(2,1)}, bf16[192,1536]{1,0:T(8,128)(2,1)S(1)}, u32[]{:S(2)}, u32[]{:S(2)}) collective-permute-start(bf16[192,1536]{1,0:T(8,128)(2,1)} %get-tuple-element.36.refs_4_), channel_id=1, source_target_pairs={{0,16},{16,32},{32,48},{48,64},{64,80},{80,96},{96,112},{112,0},{1... | collective-permute-start | bytes 1769480 | tf_op jit(solution)/shard_map/ppermute | solution.py:274
  100.4 18.6 %collective-permute-start.5 = (bf16[192,1536]{1,0:T(8,128)(2,1)}, bf16[192,1536]{1,0:T(8,128)(2,1)S(1)}, u32[]{:S(2)}, u32[]{:S(2)}) collective-permute-start(bf16[192,1536]{1,0:T(8,128)(2,1)} %get-tuple-element.37.refs_7_), channel_id=1, source_target_pairs={{0,112},{16,0},{32,16},{48,32},{64,48},{80,64},{96,80},{112,96},{1... | collective-permute-start | bytes 1769480 | tf_op jit(solution)/shard_map/ppermute | solution.py:274
  107.1 13.1 %collective-permute-start.6 = (bf16[128,1920]{1,0:T(8,128)(2,1)S(1)}, bf16[128,1920]{1,0:T(8,128)(2,1)S(1)}, u32[]{:S(2)}, u32[]{:S(2)}) collective-permute-start(bf16[128,1920]{1,0:T(8,128)(2,1)S(1)} %get-tuple-element.52.refs_0_), channel_id=1, source_target_pairs={{0,128},{128,256},{256,384},{384,0},{1,129},{129,257},{257,385},{3... | collective-permute-start | bytes 1474568 | tf_op jit(solution)/shard_map/ppermute | solution.py:274
  109.2 14.1 %collective-permute-start.7 = (bf16[128,1920]{1,0:T(8,128)(2,1)S(1)}, bf16[128,1920]{1,0:T(8,128)(2,1)S(1)}, u32[]{:S(2)}, u32[]{:S(2)}) collective-permute-start(bf16[128,1920]{1,0:T(8,128)(2,1)S(1)} %get-tuple-element.53.refs_1_), channel_id=1, source_target_pairs={{0,384},{128,0},{256,128},{384,256},{1,385},{129,1},{257,129},{385... | collective-permute-start | bytes 1474568 | tf_op jit(solution)/shard_map/ppermute | solution.py:274
  112.4 19.5 %collective-permute-start.10 = (bf16[128,1920]{1,0:T(8,128)(2,1)S(1)}, bf16[128,1920]{1,0:T(8,128)(2,1)S(1)}, u32[]{:S(2)}, u32[]{:S(2)}) collective-permute-start(bf16[128,1920]{1,0:T(8,128)(2,1)S(1)} %get-tuple-element.53.refs_1_), channel_id=1, source_target_pairs={{0,128},{128,256},{256,384},{384,0},{1,129},{129,257},{257,385},{3... | collective-permute-start | bytes 1474568 | tf_op jit(solution)/shard_map/ppermute | solution.py:274
  116.6 18.7 %collective-permute-start.11 = (bf16[128,1920]{1,0:T(8,128)(2,1)S(1)}, bf16[128,1920]{1,0:T(8,128)(2,1)S(1)}, u32[]{:S(2)}, u32[]{:S(2)}) collective-permute-start(bf16[128,1920]{1,0:T(8,128)(2,1)S(1)} %get-tuple-element.52.refs_0_), channel_id=1, source_target_pairs={{0,384},{128,0},{256,128},{384,256},{1,385},{129,1},{257,129},{385... | collective-permute-start | bytes 1474568 | tf_op jit(solution)/shard_map/ppermute | solution.py:274
  123.3 12.1 %collective-permute-start.8 = (bf16[96,1536]{1,0:T(8,128)(2,1)S(1)}, bf16[96,1536]{1,0:T(8,128)(2,1)S(1)}, u32[]{:S(2)}, u32[]{:S(2)}) collective-permute-start(bf16[96,1536]{1,0:T(8,128)(2,1)S(1)} %slice.14), channel_id=1, source_target_pairs={{0,16},{16,32},{32,48},{48,64},{64,80},{80,96},{96,112},{112,0},{1... | collective-permute-start | bytes 884744 | tf_op jit(solution)/shard_map/ppermute | solution.py:274
  126.6 8.8 %copy-start.2 = (bf16[192,1536]{1,0:T(8,128)(2,1)S(1)}, bf16[192,1536]{1,0:T(8,128)(2,1)}, u32[]{:S(2)}) copy-start(bf16[192,1536]{1,0:T(8,128)(2,1)} %copy-done.1) | copy-start | bytes 1769476
  126.7 8.7 %collective-permute-start.9 = (bf16[96,1536]{1,0:T(8,128)(2,1)S(1)}, bf16[96,1536]{1,0:T(8,128)(2,1)S(1)}, u32[]{:S(2)}, u32[]{:S(2)}) collective-permute-start(bf16[96,1536]{1,0:T(8,128)(2,1)S(1)} %slice.15), channel_id=1, source_target_pairs={{0,112},{16,0},{32,16},{48,32},{64,48},{80,64},{96,80},{112,96},{1... | collective-permute-start | bytes 884744 | tf_op jit(solution)/shard_map/ppermute | solution.py:274
  130.0 11.3 %collective-permute-start.12 = (bf16[128,1920]{1,0:T(8,128)(2,1)S(1)}, bf16[128,1920]{1,0:T(8,128)(2,1)S(1)}, u32[]{:S(2)}, u32[]{:S(2)}) collective-permute-start(bf16[128,1920]{1,0:T(8,128)(2,1)S(1)} %collective-permute-done.6.refs_0_), channel_id=1, source_target_pairs={{0,128},{128,256},{256,384},{384,0},{1,129},{129,257},{257,385},{3... | collective-permute-start | bytes 1474568 | tf_op jit(solution)/shard_map/ppermute | solution.py:274
  131.9 10.8 %collective-permute-start.13 = (bf16[128,1920]{1,0:T(8,128)(2,1)S(1)}, bf16[128,1920]{1,0:T(8,128)(2,1)S(1)}, u32[]{:S(2)}, u32[]{:S(2)}) collective-permute-start(bf16[128,1920]{1,0:T(8,128)(2,1)S(1)} %collective-permute-done.7.refs_3_), channel_id=1, source_target_pairs={{0,384},{128,0},{256,128},{384,256},{1,385},{129,1},{257,129},{385... | collective-permute-start | bytes 1474568 | tf_op jit(solution)/shard_map/ppermute | solution.py:274
  145.1 12.0 %collective-permute-start.14 = (bf16[128,1920]{1,0:T(8,128)(2,1)S(1)}, bf16[128,1920]{1,0:T(8,128)(2,1)S(1)}, u32[]{:S(2)}, u32[]{:S(2)}) collective-permute-start(bf16[128,1920]{1,0:T(8,128)(2,1)S(1)} %get-tuple-element.49), channel_id=1, source_target_pairs={{0,128},{128,256},{256,384},{384,0},{1,129},{129,257},{257,385},{3... | collective-permute-start | bytes 1474568 | tf_op jit(solution)/shard_map/ppermute | solution.py:274
  147.3 12.1 %collective-permute-start.15 = (bf16[128,1920]{1,0:T(8,128)(2,1)S(1)}, bf16[128,1920]{1,0:T(8,128)(2,1)S(1)}, u32[]{:S(2)}, u32[]{:S(2)}) collective-permute-start(bf16[128,1920]{1,0:T(8,128)(2,1)S(1)} %get-tuple-element.51), channel_id=1, source_target_pairs={{0,384},{128,0},{256,128},{384,256},{1,385},{129,1},{257,129},{385... | collective-permute-start | bytes 1474568 | tf_op jit(solution)/shard_map/ppermute | solution.py:274
  150.5 16.2 %collective-permute-start.16 = (bf16[128,1920]{1,0:T(8,128)(2,1)S(1)}, bf16[128,1920]{1,0:T(8,128)(2,1)S(1)}, u32[]{:S(2)}, u32[]{:S(2)}) collective-permute-start(bf16[128,1920]{1,0:T(8,128)(2,1)S(1)} %get-tuple-element.46), channel_id=1, source_target_pairs={{0,384},{128,0},{256,128},{384,256},{1,385},{129,1},{257,129},{385... | collective-permute-start | bytes 1474568 | tf_op jit(solution)/shard_map/ppermute | solution.py:274
  153.0 15.1 %collective-permute-start.17 = (bf16[128,1920]{1,0:T(8,128)(2,1)S(1)}, bf16[128,1920]{1,0:T(8,128)(2,1)S(1)}, u32[]{:S(2)}, u32[]{:S(2)}) collective-permute-start(bf16[128,1920]{1,0:T(8,128)(2,1)S(1)} %get-tuple-element.54), channel_id=1, source_target_pairs={{0,128},{128,256},{256,384},{384,0},{1,129},{129,257},{257,385},{3... | collective-permute-start | bytes 1474568 | tf_op jit(solution)/shard_map/ppermute | solution.py:274
  157.2 21.4 %collective-permute-start.18 = (bf16[128,1920]{1,0:T(8,128)(2,1)S(1)}, bf16[128,1920]{1,0:T(8,128)(2,1)S(1)}, u32[]{:S(2)}, u32[]{:S(2)}) collective-permute-start(bf16[128,1920]{1,0:T(8,128)(2,1)S(1)} %add_convert_fusion.3), channel_id=1, source_target_pairs={{0,128},{128,256},{256,384},{384,0},{1,129},{129,257},{257,385},{3... | collective-permute-start | bytes 1474568 | tf_op jit(solution)/shard_map/ppermute | solution.py:274
  159.5 19.2 %collective-permute-start.19 = (bf16[128,1920]{1,0:T(8,128)(2,1)S(1)}, bf16[128,1920]{1,0:T(8,128)(2,1)S(1)}, u32[]{:S(2)}, u32[]{:S(2)}) collective-permute-start(bf16[128,1920]{1,0:T(8,128)(2,1)S(1)} %add_convert_fusion.2), channel_id=1, source_target_pairs={{0,384},{128,0},{256,128},{384,256},{1,385},{129,1},{257,129},{385... | collective-permute-start | bytes 1474568 | tf_op jit(solution)/shard_map/ppermute | solution.py:274
  178.8 13.6 %copy-start.9 = (f32[1,128,2]{1,2,0:T(2,128)S(1)}, f32[1,128,2]{1,2,0:T(2,128)}, u32[]{:S(2)}) copy-start(f32[1,128,2]{1,2,0:T(2,128)} %param.13) | copy-start | bytes 3076
  179.9 39.2 %all-to-all-start.3 = ((bf16[16,16,1920]{2,1,0:T(8,128)(2,1)}), bf16[16,16,1920]{2,1,0:T(8,128)(2,1)S(1)}, u32[]{:S(2)}, u32[]{:S(2)}) async-start(bf16[16,16,1920]{2,1,0:T(8,128)(2,1)} %bitcast.6), calls=%async_computation.3 | async-start | bytes 1966080 | tf_op jit(solution)/shard_map/all_to_all | solution.py:367

commit v10 on v9

--- a/solution.py
+++ b/solution.py
@@ -294,7 +294,11 @@
 
 def expert_layer(own, near, across, weights):
     to_left_a, to_left_b, to_right_a, to_right_b = run_experts(near, *weights)
-    got_a, got_b = shift(to_left_a, "dp", -1), shift(to_right_b, "dp", 1)
+    got_a, got_b = local(
+        relay_kernel,
+        [jax.ShapeDtypeStruct(to_left_a.shape, BF)] * 2,
+        cost_estimate=pl.CostEstimate(flops=12 * 10**9, bytes_accessed=0, transcendentals=0),
+    )(shift(to_left_a, "dp", -1), shift(to_right_b, "dp", 1))
     across = after(across, to_left_a)
     to_across_a, to_across_b = run_experts(across, *weights)
     via_a, via_b = shift(to_across_a, "dp", 1), shift(to_across_b, "dp", -1)

time: 223 us -> 226 us (1.013)
  starting transfers between devices: 88.5 us -> 92.3 us
    all_to_all x1, starting transfers between devices: 12.5 us -> 16.4 us  [per_device(): returned = [lax.all_to_all(x, 'expert', 0, 0, tiled=True) for x in sums]]
  transfers between devices with their start and end apart: 23 -> 23, of which waited for: 11 -> 10; matrix products, arithmetic and copies ran while one was open for 1% -> 1% of each run, Pallas kernels for 5% -> 6%
where the time goes in v10:
time: 226 us; the launch traced here: 225 us
  starting transfers between devices  92.3 us (41%)
  waiting for transfers between devices  64.3 us (28%)
  blocking collectives  40.4 us (18%)
  Pallas kernels  22 us (10%)
  local copies, waits for them, and re-layouts  3.88 us (2%)
    ppermute x20, starting transfers between devices, shift(): return lax.ppermute(x, axis, [(i, (i + by) % n) for i in range(n)])  60.5 us
    all_to_all x1, blocking collectives, per_device(): mixed = lax.all_to_all(packed, 'ctx', 0, 0, tiled=True)  40.4 us
    ppermute x20, waiting for transfers between devices, shift(): return lax.ppermute(x, axis, [(i, (i + by) % n) for i in range(n)])  32.5 us
    all_to_all x1, waiting for transfers between devices, per_device(): returned = [lax.all_to_all(x, 'expert', 0, 0, tiled=True) for x in sums]  26.5 us
    all_to_all x1, starting transfers between devices, per_device(): returned = [lax.all_to_all(x, 'expert', 0, 0, tiled=True) for x in sums]  16.4 us
    all_to_all x1, starting transfers between devices, per_device(): arrived = [lax.all_to_all(x, 'expert', 0, 0, tiled=True) for x in sends]  12 us
    pallas_call x3, Pallas kernels, run_experts(): local(functools.partial(expert_kernel, len(pieces)), [jax.ShapeDtypeStruc...  9 us
    pallas_call x1, Pallas kernels, per_device(): local(attend_kernel, jax.ShapeDtypeStruct((n, t * 3 // 2, 128), BF), [plt...  6.28 us
  transfers between devices with their start and end apart: 23, of which 10 were waited for; matrix products, arithmetic and copies ran while one was open for 1% of the time, Pallas kernels for 6%

profile of v10, /device:TPU:7, one launch (start us, length us, event | category | flops | bytes accessed | tf_op | source)
XLA Modules:
  0.0 224.8 jit_solution(6839726082655353750)
XLA Ops:
  0.0 1.3 copy-done
  1.3 0.3 shard_map.82
  1.5 0.0 copy-start.4
  1.6 0.0 copy-start.5
  1.6 40.4 %all_to_all.33.m_ref = bf16[8,576,128]{2,1,0:T(8,128)(2,1)S(1)} all-to-all(bf16[8,576,128]{2,1,0:T(8,128)(2,1)S(1)} %shard_map.82), channel_id=1, replica_groups=mesh['dp'=4,'ctx'=8,'expert'=16] {'ctx'}, dimensions={0} | all-to-all | bytes 2359296 | tf_op jit(solution)/shard_map/all_to_all | solution.py:331
  41.9 6.3 %shard_map.83 = bf16[8,192,128]{2,1,0:T(8,128)(2,1)} custom-call(bf16[8,576,128]{2,1,0:T(8,128)(2,1)S(1)} %all_to_all.33.m_ref), custom_call_target="tpu_custom_call" | custom-call | tf_op jit(solution)/shard_map/pallas_call | solution.py:333
  48.2 3.5 %all-to-all-start.1 = ((bf16[8,192,128]{2,1,0:T(8,128)(2,1)}), bf16[8,192,128]{2,1,0:T(8,128)(2,1)S(1)}, u32[]{:S(2)}, u32[]{:S(2)}) async-start(bf16[8,192,128]{2,1,0:T(8,128)(2,1)} %shard_map.83), calls=%async_computation.1 | async-start | bytes 786432 | tf_op jit(solution)/shard_map/all_to_all | solution.py:341
  51.7 3.3 %collective-permute-start = (bf16[192,1536]{1,0:T(8,128)(2,1)S(1)}, bf16[192,1536]{1,0:T(8,128)(2,1)S(1)}, u32[]{:S(2)}, u32[]{:S(2)}) collective-permute-start(bf16[192,1536]{1,0:T(8,128)(2,1)S(1)} %shard_map.85.refs_2_), channel_id=1, source_target_pairs={{0,16},{16,32},{32,48},{48,64},{64,80},{80,96},{96,112},{112,0},{1... | collective-permute-start | bytes 1769480 | tf_op jit(solution)/shard_map/ppermute | solution.py:274
  55.0 3.2 %collective-permute-start.1 = (bf16[192,1536]{1,0:T(8,128)(2,1)S(1)}, bf16[192,1536]{1,0:T(8,128)(2,1)S(1)}, u32[]{:S(2)}, u32[]{:S(2)}) collective-permute-start(bf16[192,1536]{1,0:T(8,128)(2,1)S(1)} %shard_map.85.refs_2_), channel_id=1, source_target_pairs={{0,112},{16,0},{32,16},{48,32},{64,48},{80,64},{96,80},{112,96},{1... | collective-permute-start | bytes 1769480 | tf_op jit(solution)/shard_map/ppermute | solution.py:274
  58.3 0.1 copy.9
  58.4 0.1 copy.10.choice_ref
  58.4 5.4 %all-to-all-done.1.b_ref = bf16[8,192,128]{2,1,0:T(8,128)(2,1)S(1)} async-done(((bf16[8,192,128]{2,1,0:T(8,128)(2,1)}), bf16[8,192,128]{2,1,0:T(8,128)(2,1)S(1)}, u32[]{:S(2)}, u32[]{:S(2)}) %all-to-all-start.1) | async-done | bytes 393248 | tf_op jit(solution)/shard_map/all_to_all | solution.py:341
  63.8 1.0 copy-done.3
  64.8 1.8 shard_map.84
  66.6 12.0 %all-to-all-start.2 = ((bf16[16,16,1920]{2,1,0:T(8,128)(2,1)}), bf16[16,16,1920]{2,1,0:T(8,128)(2,1)}, u32[]{:S(2)}, u32[]{:S(2)}) async-start(bf16[16,16,1920]{2,1,0:T(8,128)(2,1)} %bitcast.4), calls=%async_computation.2 | async-start | bytes 1966080 | tf_op jit(solution)/shard_map/all_to_all | solution.py:348
  78.6 0.0 collective-permute-done.refs_3_
  78.6 2.1 collective-permute-start.2
  80.7 4.4 %collective-permute-start.3 = (bf16[192,1536]{1,0:T(8,128)(2,1)S(1)}, bf16[192,1536]{1,0:T(8,128)(2,1)S(1)}, u32[]{:S(2)}, u32[]{:S(2)}) collective-permute-start(bf16[192,1536]{1,0:T(8,128)(2,1)S(1)} %collective-permute-done.1.refs_6_), channel_id=1, source_target_pairs={{0,112},{16,0},{32,16},{48,32},{64,48},{80,64},{96,80},{112,96},{1... | collective-permute-start | bytes 1769480 | tf_op jit(solution)/shard_map/ppermute | solution.py:274
  85.1 11.5 %collective-permute-done.2.up_ref = bf16[192,1536]{1,0:T(8,128)(2,1)S(1)} collective-permute-done((bf16[192,1536]{1,0:T(8,128)(2,1)S(1)}, bf16[192,1536]{1,0:T(8,128)(2,1)S(1)}, u32[]{:S(2)}, u32[]{:S(2)}) %collective-permute-start.2) | collective-permute-done | bytes 589856 | tf_op jit(solution)/shard_map/ppermute | solution.py:274
  96.6 0.8 collective-permute-done.3.down_ref
  97.3 1.1 shard_map.86
  98.5 1.9 collective-permute-start.4
  100.4 5.4 %collective-permute-start.5 = (bf16[192,1536]{1,0:T(8,128)(2,1)}, bf16[192,1536]{1,0:T(8,128)(2,1)S(1)}, u32[]{:S(2)}, u32[]{:S(2)}) collective-permute-start(bf16[192,1536]{1,0:T(8,128)(2,1)} %get-tuple-element.39.refs_7_), channel_id=1, source_target_pairs={{0,112},{16,0},{32,16},{48,32},{64,48},{80,64},{96,80},{112,96},{1... | collective-permute-start | bytes 1769480 | tf_op jit(solution)/shard_map/ppermute | solution.py:274
  105.8 0.0 all-to-all-done.2
  105.8 1.3 fusion
  107.1 2.1 collective-permute-start.6
  109.2 3.2 %collective-permute-start.7 = (bf16[128,1920]{1,0:T(8,128)(2,1)S(1)}, bf16[128,1920]{1,0:T(8,128)(2,1)S(1)}, u32[]{:S(2)}, u32[]{:S(2)}) collective-permute-start(bf16[128,1920]{1,0:T(8,128)(2,1)S(1)} %get-tuple-element.55.refs_1_), channel_id=1, source_target_pairs={{0,384},{128,0},{256,128},{384,256},{1,385},{129,1},{257,129},{385... | collective-permute-start | bytes 1474568 | tf_op jit(solution)/shard_map/ppermute | solution.py:274
  112.4 3.3 %collective-permute-start.10 = (bf16[128,1920]{1,0:T(8,128)(2,1)S(1)}, bf16[128,1920]{1,0:T(8,128)(2,1)S(1)}, u32[]{:S(2)}, u32[]{:S(2)}) collective-permute-start(bf16[128,1920]{1,0:T(8,128)(2,1)S(1)} %get-tuple-element.55.refs_1_), channel_id=1, source_target_pairs={{0,128},{128,256},{256,384},{384,0},{1,129},{129,257},{257,385},{3... | collective-permute-start | bytes 1474568 | tf_op jit(solution)/shard_map/ppermute | solution.py:274
  115.7 0.9 collective-permute-done.4.refs_5_
  116.6 2.5 %collective-permute-start.11 = (bf16[128,1920]{1,0:T(8,128)(2,1)S(1)}, bf16[128,1920]{1,0:T(8,128)(2,1)S(1)}, u32[]{:S(2)}, u32[]{:S(2)}) collective-permute-start(bf16[128,1920]{1,0:T(8,128)(2,1)S(1)} %get-tuple-element.54.refs_0_), channel_id=1, source_target_pairs={{0,384},{128,0},{256,128},{384,256},{1,385},{129,1},{257,129},{385... | collective-permute-start | bytes 1474568 | tf_op jit(solution)/shard_map/ppermute | solution.py:274
  119.0 1.2 collective-permute-done.6.refs_0_
  120.2 3.0 %collective-permute-done.7.refs_3_ = bf16[128,1920]{1,0:T(8,128)(2,1)S(1)} collective-permute-done((bf16[128,1920]{1,0:T(8,128)(2,1)S(1)}, bf16[128,1920]{1,0:T(8,128)(2,1)S(1)}, u32[]{:S(2)}, u32[]{:S(2)}) %collective-permute-start.7) | collective-permute-done | bytes 491552 | tf_op jit(solution)/shard_map/ppermute | solution.py:274
  123.3 3.3 %collective-permute-start.8 = (bf16[96,1536]{1,0:T(8,128)(2,1)S(1)}, bf16[96,1536]{1,0:T(8,128)(2,1)S(1)}, u32[]{:S(2)}, u32[]{:S(2)}) collective-permute-start(bf16[96,1536]{1,0:T(8,128)(2,1)S(1)} %slice.14), channel_id=1, source_target_pairs={{0,16},{16,32},{32,48},{48,64},{64,80},{80,96},{96,112},{112,0},{1... | collective-permute-start | bytes 884744 | tf_op jit(solution)/shard_map/ppermute | solution.py:274
  126.7 3.3 %collective-permute-start.9 = (bf16[96,1536]{1,0:T(8,128)(2,1)S(1)}, bf16[96,1536]{1,0:T(8,128)(2,1)S(1)}, u32[]{:S(2)}, u32[]{:S(2)}) collective-permute-start(bf16[96,1536]{1,0:T(8,128)(2,1)S(1)} %slice.15), channel_id=1, source_target_pairs={{0,112},{16,0},{32,16},{48,32},{64,48},{80,64},{96,80},{112,96},{1... | collective-permute-start | bytes 884744 | tf_op jit(solution)/shard_map/ppermute | solution.py:274
  130.0 1.9 collective-permute-start.12
  131.9 3.4 %collective-permute-start.13 = (bf16[128,1920]{1,0:T(8,128)(2,1)S(1)}, bf16[128,1920]{1,0:T(8,128)(2,1)S(1)}, u32[]{:S(2)}, u32[]{:S(2)}) collective-permute-start(bf16[128,1920]{1,0:T(8,128)(2,1)S(1)} %collective-permute-done.7.refs_3_), channel_id=1, source_target_pairs={{0,384},{128,0},{256,128},{384,256},{1,385},{129,1},{257,129},{385... | collective-permute-start | bytes 1474568 | tf_op jit(solution)/shard_map/ppermute | solution.py:274
  135.3 0.0 collective-permute-done.11.down_ref
  135.3 0.1 shard_map.88
  135.4 0.0 collective-permute-done.8.refs_0_
  135.4 0.0 collective-permute-done.9.refs_1_
  135.4 1.6 shard_map.87
  137.0 4.3 %shard_map.89 = (bf16[128,1920]{1,0:T(8,128)(2,1)S(1)}, bf16[128,1920]{1,0:T(8,128)(2,1)S(1)}, bf16[128,1920]{1,0:T(8,128)(2,1)S(1)}, bf16[128,1920]{1,0:T(8,128)(2,1)S(1)}) custom-call(bf16[768,1536]{1,0:T(8,128)(2,1)S(1)} %get-tuple-element.43.in_ref, bf16[768,1536]{1,0:T(8,128)(2,1)S(1)} %get-tuple-element.44.out_ref, ...), custom_call_target="tpu_custom_call" | custom-call | flops 3019898880 | bytes 8650752 | tf_op jit(solution)/shard_map/pallas_call | solution.py:256
  141.3 2.0 collective-permute-start.16
  143.2 4.7 %collective-permute-start.17 = (bf16[128,1920]{1,0:T(8,128)(2,1)S(1)}, bf16[128,1920]{1,0:T(8,128)(2,1)S(1)}, u32[]{:S(2)}, u32[]{:S(2)}) collective-permute-start(bf16[128,1920]{1,0:T(8,128)(2,1)S(1)} %get-tuple-element.56), channel_id=1, source_target_pairs={{0,128},{128,256},{256,384},{384,0},{1,129},{129,257},{257,385},{3... | collective-permute-start | bytes 1474568 | tf_op jit(solution)/shard_map/ppermute | solution.py:274
  148.0 2.3 %shard_map.90 = (bf16[128,1920]{1,0:T(8,128)(2,1)S(1)}, bf16[128,1920]{1,0:T(8,128)(2,1)S(1)}) custom-call(bf16[768,1536]{1,0:T(8,128)(2,1)S(1)} %get-tuple-element.43.in_ref, bf16[768,1536]{1,0:T(8,128)(2,1)S(1)} %get-tuple-element.44.out_ref, bf16[128,1920]{1,0:T(8,128)(2,1)S(1)} %collective-permute-done.12.refs_0_, ...), custom_call_target="tpu_custom_call" | custom-call | flops 1509949440 | bytes 6684672 | tf_op jit(solution)/shard_map/pallas_call | solution.py:256
  150.3 1.9 collective-permute-start.14
  152.2 3.4 %collective-permute-start.15 = (bf16[128,1920]{1,0:T(8,128)(2,1)S(1)}, bf16[128,1920]{1,0:T(8,128)(2,1)S(1)}, u32[]{:S(2)}, u32[]{:S(2)}) collective-permute-start(bf16[128,1920]{1,0:T(8,128)(2,1)S(1)} %get-tuple-element.53), channel_id=1, source_target_pairs={{0,384},{128,0},{256,128},{384,256},{1,385},{129,1},{257,129},{385... | collective-permute-start | bytes 1474568 | tf_op jit(solution)/shard_map/ppermute | solution.py:274
  155.6 0.1 shard_map.91
  155.7 9.7 %collective-permute-done.14 = bf16[128,1920]{1,0:T(8,128)(2,1)S(1)} collective-permute-done((bf16[128,1920]{1,0:T(8,128)(2,1)S(1)}, bf16[128,1920]{1,0:T(8,128)(2,1)S(1)}, u32[]{:S(2)}, u32[]{:S(2)}) %collective-permute-start.14) | collective-permute-done | bytes 491552 | tf_op jit(solution)/shard_map/ppermute | solution.py:274
  165.5 0.1 add_convert_fusion.3
  165.6 2.3 %collective-permute-start.18 = (bf16[128,1920]{1,0:T(8,128)(2,1)S(1)}, bf16[128,1920]{1,0:T(8,128)(2,1)S(1)}, u32[]{:S(2)}, u32[]{:S(2)}) collective-permute-start(bf16[128,1920]{1,0:T(8,128)(2,1)S(1)} %add_convert_fusion.3), channel_id=1, source_target_pairs={{0,128},{128,256},{256,384},{384,0},{1,129},{129,257},{257,385},{3... | collective-permute-start | bytes 1474568 | tf_op jit(solution)/shard_map/ppermute | solution.py:274
  167.9 0.1 add_convert_fusion.2
  168.1 2.9 %collective-permute-start.19 = (bf16[128,1920]{1,0:T(8,128)(2,1)S(1)}, bf16[128,1920]{1,0:T(8,128)(2,1)S(1)}, u32[]{:S(2)}, u32[]{:S(2)}) collective-permute-start(bf16[128,1920]{1,0:T(8,128)(2,1)S(1)} %add_convert_fusion.2), channel_id=1, source_target_pairs={{0,384},{128,0},{256,128},{384,256},{1,385},{129,1},{257,129},{385... | collective-permute-start | bytes 1474568 | tf_op jit(solution)/shard_map/ppermute | solution.py:274
  171.0 2.4 %shard_map.92 = (bf16[128,1920]{1,0:T(8,128)(2,1)S(1)}, bf16[128,1920]{1,0:T(8,128)(2,1)S(1)}) custom-call(bf16[768,1536]{1,0:T(8,128)(2,1)S(1)} %get-tuple-element.43.in_ref, bf16[768,1536]{1,0:T(8,128)(2,1)S(1)} %get-tuple-element.44.out_ref, bf16[128,1920]{1,0:T(8,128)(2,1)S(1)} %get-tuple-element.54.refs_0_, ...), custom_call_target="tpu_custom_call" | custom-call | flops 1509949440 | bytes 6684672 | tf_op jit(solution)/shard_map/pallas_call | solution.py:256
  173.4 2.0 collective-permute-done.18
  175.4 0.1 add_convert_fusion.1
  175.5 3.3 %collective-permute-done.19 = bf16[128,1920]{1,0:T(8,128)(2,1)S(1)} collective-permute-done((bf16[128,1920]{1,0:T(8,128)(2,1)S(1)}, bf16[128,1920]{1,0:T(8,128)(2,1)S(1)}, u32[]{:S(2)}, u32[]{:S(2)}) %collective-permute-start.19) | collective-permute-done | bytes 491552 | tf_op jit(solution)/shard_map/ppermute | solution.py:274
  178.8 0.1 add_convert_fusion
  179.0 0.0 copy-start.9
  179.0 1.0 pad_maximum_fusion
  180.0 16.4 %all-to-all-start.3 = ((bf16[16,16,1920]{2,1,0:T(8,128)(2,1)}), bf16[16,16,1920]{2,1,0:T(8,128)(2,1)S(1)}, u32[]{:S(2)}, u32[]{:S(2)}) async-start(bf16[16,16,1920]{2,1,0:T(8,128)(2,1)} %bitcast.6), calls=%async_computation.3 | async-start | bytes 1966080 | tf_op jit(solution)/shard_map/all_to_all | solution.py:371
  196.4 0.1 copy.11
  196.5 26.5 %all-to-all-done.3 = bf16[16,16,1920]{2,1,0:T(8,128)(2,1)S(1)} async-done(((bf16[16,16,1920]{2,1,0:T(8,128)(2,1)}), bf16[16,16,1920]{2,1,0:T(8,128)(2,1)S(1)}, u32[]{:S(2)}, u32[]{:S(2)}) %all-to-all-start.3) | async-done | bytes 983072 | tf_op jit(solution)/shard_map/all_to_all | solution.py:371
  223.0 1.8 shard_map.93
  (26 shorter events, 0.1 us)
Async XLA Ops:
  0.0 1.3 copy-start
  1.5 50.1 %copy-start.4 = (bf16[1,96,1536]{2,1,0:T(8,128)(2,1)S(1)}, bf16[1,96,1536]{2,1,0:T(8,128)(2,1)}, u32[]{:S(2)}) copy-start(bf16[1,96,1536]{2,1,0:T(8,128)(2,1)} %in_ref.1) | copy-start | bytes 884740
  1.6 50.1 %copy-start.5 = (bf16[1,96,1536]{2,1,0:T(8,128)(2,1)S(1)}, bf16[1,96,1536]{2,1,0:T(8,128)(2,1)}, u32[]{:S(2)}) copy-start(bf16[1,96,1536]{2,1,0:T(8,128)(2,1)} %out_ref.1) | copy-start | bytes 884740
  41.9 16.3 %copy-start.8 = (s32[1,128,2]{1,2,0:T(2,128)S(1)}, s32[1,128,2]{1,2,0:T(2,128)}, u32[]{:S(2)}) copy-start(s32[1,128,2]{1,2,0:T(2,128)} %param.12) | copy-start | bytes 3076
  41.9 21.9 %copy-start.6 = (f32[1,1536]{1,0:T(1,128)S(1)}, f32[1,1536]{1,0:T(1,128)}, u32[]{:S(2)}) copy-start(f32[1,1536]{1,0:T(1,128)} %scale_ref.1) | copy-start | bytes 18436
  41.9 21.9 %copy-start.7 = (f32[1,1536]{1,0:T(1,128)S(1)}, f32[1,1536]{1,0:T(1,128)}, u32[]{:S(2)}) copy-start(f32[1,1536]{1,0:T(1,128)} %shift_ref.1) | copy-start | bytes 18436
  48.2 15.6 %all-to-all-start.1 = ((bf16[8,192,128]{2,1,0:T(8,128)(2,1)}), bf16[8,192,128]{2,1,0:T(8,128)(2,1)S(1)}, u32[]{:S(2)}, u32[]{:S(2)}) async-start(bf16[8,192,128]{2,1,0:T(8,128)(2,1)} %shard_map.83), calls=%async_computation.1 | async-start | bytes 786432 | tf_op jit(solution)/shard_map/all_to_all | solution.py:341
  51.7 26.8 %collective-permute-start = (bf16[192,1536]{1,0:T(8,128)(2,1)S(1)}, bf16[192,1536]{1,0:T(8,128)(2,1)S(1)}, u32[]{:S(2)}, u32[]{:S(2)}) collective-permute-start(bf16[192,1536]{1,0:T(8,128)(2,1)S(1)} %shard_map.85.refs_2_), channel_id=1, source_target_pairs={{0,16},{16,32},{32,48},{48,64},{64,80},{80,96},{96,112},{112,0},{1... | collective-permute-start | bytes 1769480 | tf_op jit(solution)/shard_map/ppermute | solution.py:274
  55.0 23.6 %collective-permute-start.1 = (bf16[192,1536]{1,0:T(8,128)(2,1)S(1)}, bf16[192,1536]{1,0:T(8,128)(2,1)S(1)}, u32[]{:S(2)}, u32[]{:S(2)}) collective-permute-start(bf16[192,1536]{1,0:T(8,128)(2,1)S(1)} %shard_map.85.refs_2_), channel_id=1, source_target_pairs={{0,112},{16,0},{32,16},{48,32},{64,48},{80,64},{96,80},{112,96},{1... | collective-permute-start | bytes 1769480 | tf_op jit(solution)/shard_map/ppermute | solution.py:274
  63.8 1.0 copy-start.3
  66.6 39.2 %all-to-all-start.2 = ((bf16[16,16,1920]{2,1,0:T(8,128)(2,1)}), bf16[16,16,1920]{2,1,0:T(8,128)(2,1)}, u32[]{:S(2)}, u32[]{:S(2)}) async-start(bf16[16,16,1920]{2,1,0:T(8,128)(2,1)} %bitcast.4), calls=%async_computation.2 | async-start | bytes 1966080 | tf_op jit(solution)/shard_map/all_to_all | solution.py:348
  78.6 19.9 %copy-start.1 = (bf16[192,1536]{1,0:T(8,128)(2,1)}, bf16[192,1536]{1,0:T(8,128)(2,1)S(1)}, u32[]{:S(2)}) copy-start(bf16[192,1536]{1,0:T(8,128)(2,1)S(1)} %collective-permute-done.1.refs_6_) | copy-start | bytes 1769476
  78.6 18.0 %collective-permute-start.2 = (bf16[192,1536]{1,0:T(8,128)(2,1)S(1)}, bf16[192,1536]{1,0:T(8,128)(2,1)S(1)}, u32[]{:S(2)}, u32[]{:S(2)}) collective-permute-start(bf16[192,1536]{1,0:T(8,128)(2,1)S(1)} %collective-permute-done.refs_3_), channel_id=1, source_target_pairs={{0,16},{16,32},{32,48},{48,64},{64,80},{80,96},{96,112},{112,0},{1... | collective-permute-start | bytes 1769480 | tf_op jit(solution)/shard_map/ppermute | solution.py:274
  80.7 16.6 %collective-permute-start.3 = (bf16[192,1536]{1,0:T(8,128)(2,1)S(1)}, bf16[192,1536]{1,0:T(8,128)(2,1)S(1)}, u32[]{:S(2)}, u32[]{:S(2)}) collective-permute-start(bf16[192,1536]{1,0:T(8,128)(2,1)S(1)} %collective-permute-done.1.refs_6_), channel_id=1, source_target_pairs={{0,112},{16,0},{32,16},{48,32},{64,48},{80,64},{96,80},{112,96},{1... | collective-permute-start | bytes 1769480 | tf_op jit(solution)/shard_map/ppermute | solution.py:274
  98.5 18.1 %collective-permute-start.4 = (bf16[192,1536]{1,0:T(8,128)(2,1)}, bf16[192,1536]{1,0:T(8,128)(2,1)S(1)}, u32[]{:S(2)}, u32[]{:S(2)}) collective-permute-start(bf16[192,1536]{1,0:T(8,128)(2,1)} %get-tuple-element.38.refs_4_), channel_id=1, source_target_pairs={{0,16},{16,32},{32,48},{48,64},{64,80},{80,96},{96,112},{112,0},{1... | collective-permute-start | bytes 1769480 | tf_op jit(solution)/shard_map/ppermute | solution.py:274
  100.4 18.6 %collective-permute-start.5 = (bf16[192,1536]{1,0:T(8,128)(2,1)}, bf16[192,1536]{1,0:T(8,128)(2,1)S(1)}, u32[]{:S(2)}, u32[]{:S(2)}) collective-permute-start(bf16[192,1536]{1,0:T(8,128)(2,1)} %get-tuple-element.39.refs_7_), channel_id=1, source_target_pairs={{0,112},{16,0},{32,16},{48,32},{64,48},{80,64},{96,80},{112,96},{1... | collective-permute-start | bytes 1769480 | tf_op jit(solution)/shard_map/ppermute | solution.py:274
  107.1 13.1 %collective-permute-start.6 = (bf16[128,1920]{1,0:T(8,128)(2,1)S(1)}, bf16[128,1920]{1,0:T(8,128)(2,1)S(1)}, u32[]{:S(2)}, u32[]{:S(2)}) collective-permute-start(bf16[128,1920]{1,0:T(8,128)(2,1)S(1)} %get-tuple-element.54.refs_0_), channel_id=1, source_target_pairs={{0,128},{128,256},{256,384},{384,0},{1,129},{129,257},{257,385},{3... | collective-permute-start | bytes 1474568 | tf_op jit(solution)/shard_map/ppermute | solution.py:274
  109.2 14.1 %collective-permute-start.7 = (bf16[128,1920]{1,0:T(8,128)(2,1)S(1)}, bf16[128,1920]{1,0:T(8,128)(2,1)S(1)}, u32[]{:S(2)}, u32[]{:S(2)}) collective-permute-start(bf16[128,1920]{1,0:T(8,128)(2,1)S(1)} %get-tuple-element.55.refs_1_), channel_id=1, source_target_pairs={{0,384},{128,0},{256,128},{384,256},{1,385},{129,1},{257,129},{385... | collective-permute-start | bytes 1474568 | tf_op jit(solution)/shard_map/ppermute | solution.py:274
  112.4 19.5 %collective-permute-start.10 = (bf16[128,1920]{1,0:T(8,128)(2,1)S(1)}, bf16[128,1920]{1,0:T(8,128)(2,1)S(1)}, u32[]{:S(2)}, u32[]{:S(2)}) collective-permute-start(bf16[128,1920]{1,0:T(8,128)(2,1)S(1)} %get-tuple-element.55.refs_1_), channel_id=1, source_target_pairs={{0,128},{128,256},{256,384},{384,0},{1,129},{129,257},{257,385},{3... | collective-permute-start | bytes 1474568 | tf_op jit(solution)/shard_map/ppermute | solution.py:274
  116.6 18.7 %collective-permute-start.11 = (bf16[128,1920]{1,0:T(8,128)(2,1)S(1)}, bf16[128,1920]{1,0:T(8,128)(2,1)S(1)}, u32[]{:S(2)}, u32[]{:S(2)}) collective-permute-start(bf16[128,1920]{1,0:T(8,128)(2,1)S(1)} %get-tuple-element.54.refs_0_), channel_id=1, source_target_pairs={{0,384},{128,0},{256,128},{384,256},{1,385},{129,1},{257,129},{385... | collective-permute-start | bytes 1474568 | tf_op jit(solution)/shard_map/ppermute | solution.py:274
  123.3 12.1 %collective-permute-start.8 = (bf16[96,1536]{1,0:T(8,128)(2,1)S(1)}, bf16[96,1536]{1,0:T(8,128)(2,1)S(1)}, u32[]{:S(2)}, u32[]{:S(2)}) collective-permute-start(bf16[96,1536]{1,0:T(8,128)(2,1)S(1)} %slice.14), channel_id=1, source_target_pairs={{0,16},{16,32},{32,48},{48,64},{64,80},{80,96},{96,112},{112,0},{1... | collective-permute-start | bytes 884744 | tf_op jit(solution)/shard_map/ppermute | solution.py:274
  126.6 8.8 %copy-start.2 = (bf16[192,1536]{1,0:T(8,128)(2,1)S(1)}, bf16[192,1536]{1,0:T(8,128)(2,1)}, u32[]{:S(2)}) copy-start(bf16[192,1536]{1,0:T(8,128)(2,1)} %copy-done.1) | copy-start | bytes 1769476
  126.7 8.7 %collective-permute-start.9 = (bf16[96,1536]{1,0:T(8,128)(2,1)S(1)}, bf16[96,1536]{1,0:T(8,128)(2,1)S(1)}, u32[]{:S(2)}, u32[]{:S(2)}) collective-permute-start(bf16[96,1536]{1,0:T(8,128)(2,1)S(1)} %slice.15), channel_id=1, source_target_pairs={{0,112},{16,0},{32,16},{48,32},{64,48},{80,64},{96,80},{112,96},{1... | collective-permute-start | bytes 884744 | tf_op jit(solution)/shard_map/ppermute | solution.py:274
  130.0 18.0 %collective-permute-start.12 = (bf16[128,1920]{1,0:T(8,128)(2,1)S(1)}, bf16[128,1920]{1,0:T(8,128)(2,1)S(1)}, u32[]{:S(2)}, u32[]{:S(2)}) collective-permute-start(bf16[128,1920]{1,0:T(8,128)(2,1)S(1)} %collective-permute-done.6.refs_0_), channel_id=1, source_target_pairs={{0,128},{128,256},{256,384},{384,0},{1,129},{129,257},{257,385},{3... | collective-permute-start | bytes 1474568 | tf_op jit(solution)/shard_map/ppermute | solution.py:274
  131.9 16.0 %collective-permute-start.13 = (bf16[128,1920]{1,0:T(8,128)(2,1)S(1)}, bf16[128,1920]{1,0:T(8,128)(2,1)S(1)}, u32[]{:S(2)}, u32[]{:S(2)}) collective-permute-start(bf16[128,1920]{1,0:T(8,128)(2,1)S(1)} %collective-permute-done.7.refs_3_), channel_id=1, source_target_pairs={{0,384},{128,0},{256,128},{384,256},{1,385},{129,1},{257,129},{385... | collective-permute-start | bytes 1474568 | tf_op jit(solution)/shard_map/ppermute | solution.py:274
  141.3 14.4 %collective-permute-start.16 = (bf16[128,1920]{1,0:T(8,128)(2,1)S(1)}, bf16[128,1920]{1,0:T(8,128)(2,1)S(1)}, u32[]{:S(2)}, u32[]{:S(2)}) collective-permute-start(bf16[128,1920]{1,0:T(8,128)(2,1)S(1)} %get-tuple-element.48), channel_id=1, source_target_pairs={{0,384},{128,0},{256,128},{384,256},{1,385},{129,1},{257,129},{385... | collective-permute-start | bytes 1474568 | tf_op jit(solution)/shard_map/ppermute | solution.py:274
  143.2 12.4 %collective-permute-start.17 = (bf16[128,1920]{1,0:T(8,128)(2,1)S(1)}, bf16[128,1920]{1,0:T(8,128)(2,1)S(1)}, u32[]{:S(2)}, u32[]{:S(2)}) collective-permute-start(bf16[128,1920]{1,0:T(8,128)(2,1)S(1)} %get-tuple-element.56), channel_id=1, source_target_pairs={{0,128},{128,256},{256,384},{384,0},{1,129},{129,257},{257,385},{3... | collective-permute-start | bytes 1474568 | tf_op jit(solution)/shard_map/ppermute | solution.py:274
  150.3 15.1 %collective-permute-start.14 = (bf16[128,1920]{1,0:T(8,128)(2,1)S(1)}, bf16[128,1920]{1,0:T(8,128)(2,1)S(1)}, u32[]{:S(2)}, u32[]{:S(2)}) collective-permute-start(bf16[128,1920]{1,0:T(8,128)(2,1)S(1)} %get-tuple-element.51), channel_id=1, source_target_pairs={{0,128},{128,256},{256,384},{384,0},{1,129},{129,257},{257,385},{3... | collective-permute-start | bytes 1474568 | tf_op jit(solution)/shard_map/ppermute | solution.py:274
  152.2 15.7 %collective-permute-start.15 = (bf16[128,1920]{1,0:T(8,128)(2,1)S(1)}, bf16[128,1920]{1,0:T(8,128)(2,1)S(1)}, u32[]{:S(2)}, u32[]{:S(2)}) collective-permute-start(bf16[128,1920]{1,0:T(8,128)(2,1)S(1)} %get-tuple-element.53), channel_id=1, source_target_pairs={{0,384},{128,0},{256,128},{384,256},{1,385},{129,1},{257,129},{385... | collective-permute-start | bytes 1474568 | tf_op jit(solution)/shard_map/ppermute | solution.py:274
  165.6 9.8 %collective-permute-start.18 = (bf16[128,1920]{1,0:T(8,128)(2,1)S(1)}, bf16[128,1920]{1,0:T(8,128)(2,1)S(1)}, u32[]{:S(2)}, u32[]{:S(2)}) collective-permute-start(bf16[128,1920]{1,0:T(8,128)(2,1)S(1)} %add_convert_fusion.3), channel_id=1, source_target_pairs={{0,128},{128,256},{256,384},{384,0},{1,129},{129,257},{257,385},{3... | collective-permute-start | bytes 1474568 | tf_op jit(solution)/shard_map/ppermute | solution.py:274
  168.1 10.8 %collective-permute-start.19 = (bf16[128,1920]{1,0:T(8,128)(2,1)S(1)}, bf16[128,1920]{1,0:T(8,128)(2,1)S(1)}, u32[]{:S(2)}, u32[]{:S(2)}) collective-permute-start(bf16[128,1920]{1,0:T(8,128)(2,1)S(1)} %add_convert_fusion.2), channel_id=1, source_target_pairs={{0,384},{128,0},{256,128},{384,256},{1,385},{129,1},{257,129},{385... | collective-permute-start | bytes 1474568 | tf_op jit(solution)/shard_map/ppermute | solution.py:274
  179.0 17.4 %copy-start.9 = (f32[1,128,2]{1,2,0:T(2,128)S(1)}, f32[1,128,2]{1,2,0:T(2,128)}, u32[]{:S(2)}) copy-start(f32[1,128,2]{1,2,0:T(2,128)} %param.13) | copy-start | bytes 3076
  180.0 43.0 %all-to-all-start.3 = ((bf16[16,16,1920]{2,1,0:T(8,128)(2,1)}), bf16[16,16,1920]{2,1,0:T(8,128)(2,1)S(1)}, u32[]{:S(2)}, u32[]{:S(2)}) async-start(bf16[16,16,1920]{2,1,0:T(8,128)(2,1)} %bitcast.6), calls=%async_computation.3 | async-start | bytes 1966080 | tf_op jit(solution)/shard_map/all_to_all | solution.py:371
